TPU v7x, 32 devices: a whole 2x2x4 slice. The times are simulated.
32 devices in a mesh: band: 16 (over z, x, core), tile: 2 (over y).
Axes of the slice: x: 2, y: 2, z: 4, core: 2. Of those that a mesh axis runs over, the one named last changes fastest.
Arguments:
- alm: bfloat16 [1024, 9, 2, 1024], P('band', None, None, 'tile'), may hold values from -22 to 22
- legendre: bfloat16 [1024, 1024, 256], P('band', 'tile'), may hold values from -0.1875 to 0.1875
- order_of_slot: int32 [1024], replicated, may hold values from 0 to 1023, each once
Outputs:
- ilc_map: float32 [256, 4096], P('band', 'tile')
- ilc_alm: float32 [1024, 2, 1024], P('band', None, 'tile')
Inputs may be any that keep to these rules, and one draw needn't show every extreme that they name: `order_of_slot`: every order 0 to 1023 stands in exactly one slot.
All inputs are finite; a program needn't handle non-finite values.
Results may differ from a plain program's by a relative error of at most 0.02.
Values may be sent and summed in bfloat16 or wider, within the bound.
No kernel may reach another device: no remote copies, remote signals or barrier semaphores. Data moves between devices by JAX's collectives and lax.ppermute only.
A program may use at most 128 MiB of HBM per device.

v0:
```python
import functools
import math

import jax
import jax.numpy as jnp
from jax import lax
from jax.experimental import pallas as pl
from jax.experimental.pallas import tpu as pltpu
from jax.sharding import PartitionSpec as P

C = 9
L = 1024
NLON = 4096
HALO = 32

RIDGE = 0.1
EPSILON = 1e-06

WINDOW = 2 * HALO + 1
LANES = NLON // HALO
HALF = LANES // 2
PAIRS = [(a_at, b_at) for a_at in range(C) for b_at in range(a_at, C)]
VMEM_LIMIT = 48 * 1024 * 1024


def round_up(value, multiple):
    return (value + multiple - 1) // multiple * multiple


def cos_turns(turns):
    away = jnp.abs(turns - jnp.floor(turns + 0.5))
    quarter = 1.0 - 4.0 * away
    square = quarter * quarter
    tail = square * (1.6044118478736e-04 - square * 3.598843235e-06)
    tail = square * (-4.68175413531868e-03 + tail)
    tail = square * (7.96926262461670e-02 + tail)
    tail = square * (-6.45964097506246e-01 + tail)
    return quarter * (1.57079632679490 + tail)


def basis_kernel(order_ref, basis_ref):
    rows = order_ref.shape[0]
    order = jnp.broadcast_to(order_ref[...], (rows, LANES))
    row = lax.broadcasted_iota(jnp.int32, (rows, LANES), 0)
    lane = lax.broadcasted_iota(jnp.int32, (rows, LANES), 1)
    cell = HALO * (lane % HALF) + lane // HALF
    turns = order * (cell.astype(jnp.float32) / NLON) + (row % 2).astype(jnp.float32) * 0.25
    step = order * (2.0 / NLON)
    scaling = 1.0 / math.sqrt(L)
    before = cos_turns(turns) * scaling
    now = cos_turns(turns + step) * scaling
    twice = 2.0 * cos_turns(step)
    for at in range(HALO // 2):
        basis_ref[at // 2, :, at % 2 * LANES : (at % 2 + 1) * LANES] = before.astype(jnp.bfloat16)
        if at < HALO // 2 - 1:
            before, now = now, twice * now - before


def make_basis(order_rows):
    rows = order_rows.shape[0]
    block = 128
    chunks = HALO // 4
    return pl.pallas_call(
        basis_kernel,
        grid=(rows // block,),
        in_specs=[pl.BlockSpec((block, 1), lambda at: (at, 0))],
        out_specs=pl.BlockSpec((chunks, block, 2 * LANES), lambda at: (0, at, 0)),
        out_shape=jax.ShapeDtypeStruct((chunks, rows, 2 * LANES), jnp.bfloat16),
        cost_estimate=pl.CostEstimate(
            flops=rows * chunks * 2 * LANES * 8, bytes_accessed=rows * chunks * 4 * LANES, transcendentals=0
        ),
        compiler_params=pltpu.CompilerParams(vmem_limit_bytes=VMEM_LIMIT),
    )(order_rows)


def combine(entries, maps):
    entries = dict(entries)
    trace = entries[0, 0]
    for at in range(1, C):
        trace = trace + entries[at, at]
    ridge = RIDGE * (trace * (1.0 / C) + WINDOW * EPSILON)
    for at in range(C):
        entries[at, at] = entries[at, at] + ridge
    ones = [None] * C
    maps = list(maps)
    top = bottom = None
    for at in range(C):
        inverse = 1.0 / entries[at, at]
        scaled = inverse if at == 0 else inverse * ones[at]
        term = scaled * maps[at]
        top = term if top is None else top + term
        term = scaled if at == 0 else scaled * ones[at]
        bottom = term if bottom is None else bottom + term
        for row in range(at + 1, C):
            ratio = entries[at, row] * inverse
            ones[row] = 1.0 - ratio if at == 0 else ones[row] - ratio * ones[at]
            maps[row] = maps[row] - ratio * maps[at]
            for col in range(row, C):
                entries[row, col] = entries[row, col] - ratio * entries[at, col]
    return top / bottom


def ilc_kernel(modes_ref, odd_ref, basis_hbm, ilc_ref, spectra_ref, basis_ref, lhs_ref, maps_ref, sums_ref, low_ref, sems):
    groups, rows, width = modes_ref.shape
    chunks = basis_ref.shape[0]
    cycles = rows // C
    second = round_up(rows, 16)
    for chunk in range(chunks):
        pltpu.make_async_copy(basis_hbm.at[chunk], basis_ref.at[chunk], sems.at[chunk]).start()
    for group in range(groups):
        span = slice(group * width, (group + 1) * width)
        odd = odd_ref[:, span]
        values = modes_ref[group].astype(jnp.float32)
        lhs_ref[0:rows, span] = (values * (1.0 - odd)).astype(jnp.bfloat16)
        lhs_ref[second : second + rows, span] = (values * odd).astype(jnp.bfloat16)
    low_half = lax.broadcasted_iota(jnp.int32, (cycles, LANES), 1) < HALF
    for chunk in range(chunks):
        pltpu.make_async_copy(basis_hbm.at[chunk], basis_ref.at[chunk], sems.at[chunk]).wait()
        result = jnp.dot(lhs_ref[...], basis_ref[chunk], preferred_element_type=jnp.float32)
        for part in range(2):
            at = 4 * chunk + 2 * part
            even_part = result[0:rows, part * LANES : (part + 1) * LANES]
            odd_part = result[second : second + rows, part * LANES : (part + 1) * LANES]
            near = even_part + odd_part
            far = even_part - odd_part
            wide = jnp.concatenate([low_half] * C, axis=0)
            maps_ref[at] = jnp.where(wide, near, pltpu.roll(far, HALF, 1))
            maps_ref[at + 1] = jnp.where(wide, pltpu.roll(near, HALF, 1), far)

    def maps_at(at):
        return [maps_ref[at, chan * cycles : (chan + 1) * cycles, :] for chan in range(C)]

    for first in range(0, len(PAIRS), 15):
        some = PAIRS[first : first + 15]

        def add(at, totals, some=some):
            values = maps_at(at)
            return tuple(total + values[a_at] * values[b_at] for total, (a_at, b_at) in zip(totals, some))

        zero = jnp.zeros((cycles, LANES), jnp.float32)
        totals = lax.fori_loop(0, HALO, add, (zero,) * len(some))
        for pair, total in enumerate(totals):
            sums_ref[first + pair] = total + pltpu.roll(total, 1, 1)

    def smooth(at, leaves):
        ahead = [pltpu.roll(value, LANES - 1, 1) for value in maps_at(at)]
        behind = [pltpu.roll(value, 1, 1) for value in maps_at(jnp.maximum(at - 1, 0))]
        behind = [value * leaves for value in behind]
        entries = {}
        for pair, (a_at, b_at) in enumerate(PAIRS):
            total = sums_ref[pair] + (ahead[a_at] * ahead[b_at] - behind[a_at] * behind[b_at])
            sums_ref[pair] = total
            entries[a_at, b_at] = total
        return entries

    def two_vectors(pair_at, carry):
        at = 2 * pair_at
        found = []
        for part in range(2):
            leaves = jnp.where(at == 0, 0.0, 1.0) if part == 0 else 1.0
            value = combine(smooth(at + part, leaves), maps_at(at + part))
            ilc_ref[at + part] = value
            found.append(value)
        near = jnp.where(low_half, found[0], pltpu.roll(found[1], HALF, 1))
        far = jnp.where(low_half, pltpu.roll(found[0], HALF, 1), found[1])
        low_ref[pair_at] = jnp.concatenate([near, far], axis=0).astype(jnp.bfloat16)
        return carry

    lax.fori_loop(0, HALO // 2, two_vectors, 0)

    result = jnp.zeros((2 * cycles, groups * width), jnp.float32)
    for chunk in range(chunks):
        lhs = jnp.concatenate([low_ref[2 * chunk], low_ref[2 * chunk + 1]], axis=1)
        result = result + lax.dot_general(
            lhs, basis_ref[chunk], (((1,), (1,)), ((), ())), preferred_element_type=jnp.float32
        )
    for group in range(groups):
        span = slice(group * width, (group + 1) * width)
        sign = 1.0 - 2.0 * odd_ref[:, span]
        spectra_ref[group] = (result[0:cycles, span] + sign * result[cycles:, span]).astype(jnp.bfloat16)


def run_ilc(modes, odd, basis):
    groups, rows, width = modes.shape
    chunks, depth, columns = basis.shape
    cycles = rows // C
    vmem = pl.BlockSpec(memory_space=pltpu.VMEM)
    return pl.pallas_call(
        ilc_kernel,
        in_specs=[vmem, vmem, pl.BlockSpec(memory_space=pl.ANY)],
        out_specs=[vmem, vmem],
        out_shape=[
            jax.ShapeDtypeStruct((HALO, cycles, LANES), jnp.float32),
            jax.ShapeDtypeStruct((groups, cycles, width), jnp.bfloat16),
        ],
        scratch_shapes=[
            pltpu.VMEM((chunks, depth, columns), jnp.bfloat16),
            pltpu.VMEM((2 * round_up(rows, 16), depth), jnp.bfloat16),
            pltpu.VMEM((HALO, rows, LANES), jnp.float32),
            pltpu.VMEM((len(PAIRS), cycles, LANES), jnp.float32),
            pltpu.VMEM((HALO // 2, 2 * cycles, LANES), jnp.bfloat16),
            pltpu.SemaphoreType.DMA((chunks,)),
        ],
        cost_estimate=pl.CostEstimate(
            flops=2 * chunks * depth * columns * (2 * rows + 2 * cycles),
            bytes_accessed=chunks * depth * columns * 2,
            transcendentals=0,
        ),
        compiler_params=pltpu.CompilerParams(vmem_limit_bytes=VMEM_LIMIT),
    )(modes, odd, basis)


def from_other_tiles(send):
    count = lax.axis_size("tile")
    got = [send(0)]
    for hop in range(1, count):
        got.append(lax.ppermute(send(hop), "tile", [(at, (at + hop) % count) for at in range(count)]))
    return got


def in_tile_order(got):
    count = len(got)
    tile_at = lax.axis_index("tile")
    stacked = jnp.stack(got)
    return jnp.stack(
        [lax.dynamic_index_in_dim(stacked, (tile_at - at) % count, 0, keepdims=False) for at in range(count)]
    )


def body(alm, legendre, order_of_slot):
    tile_count = lax.axis_size("tile")
    band_count = lax.axis_size("band")
    tile_at = lax.axis_index("tile")
    slot_count = alm.shape[0]
    cycles = legendre.shape[2] // (band_count * tile_count)
    padded = round_up(cycles, 8)
    depth = 2 * L
    width = 2 * slot_count
    group_width = math.lcm(width, LANES)
    groups = depth // group_width

    partial = jnp.einsum("scel,slr->scer", alm, legendre, preferred_element_type=jnp.float32)
    partial = partial.astype(jnp.bfloat16).reshape(slot_count, C, 2, band_count, tile_count, cycles)
    partial = partial.transpose(4, 3, 1, 5, 0, 2).reshape(tile_count, band_count, C * cycles, width)
    got = from_other_tiles(
        lambda hop: lax.dynamic_index_in_dim(partial, (tile_at + hop) % tile_count, 0, keepdims=False)
    )
    total = got[0].astype(jnp.float32)
    for other in got[1:]:
        total = total + other.astype(jnp.float32)
    modes = lax.all_to_all(total.astype(jnp.bfloat16), "band", split_axis=0, concat_axis=0, tiled=True)
    if group_width != width:
        modes = modes.reshape(groups, group_width // width, C * cycles, width)
        modes = modes.transpose(0, 2, 1, 3).reshape(groups, C * cycles, group_width)
    if padded != cycles:
        modes = modes.reshape(groups, C, cycles, group_width)
        modes = jnp.pad(modes, ((0, 0), (0, 0), (0, padded - cycles), (0, 0)))
        modes = modes.reshape(groups, C * padded, group_width)

    order_rows = jnp.repeat(order_of_slot, 2)
    basis = make_basis(order_rows.astype(jnp.float32)[:, None])
    odd = (order_rows % 2).astype(jnp.float32)[None, :]
    vectors, spectra = run_ilc(modes, odd, basis)

    spectra = spectra[:, :cycles]
    if group_width != width:
        spectra = spectra.reshape(groups, cycles, group_width // width, width)
        spectra = spectra.transpose(0, 2, 1, 3).reshape(band_count, cycles, width)
    routed = lax.all_to_all(spectra, "band", split_axis=0, concat_axis=0, tiled=True)
    cycle_spectra = in_tile_order(from_other_tiles(lambda hop: routed))
    cycle_spectra = cycle_spectra.transpose(1, 0, 2, 3).reshape(band_count * tile_count * cycles, slot_count, 2)
    ilc_alm = jnp.einsum("slr,rse->sel", legendre, cycle_spectra, preferred_element_type=jnp.float32)

    own = vectors[:, :cycles].transpose(1, 2, 0).reshape(cycles, tile_count, NLON // tile_count)
    own = own.transpose(1, 0, 2)
    ilc_map = in_tile_order(
        from_other_tiles(lambda hop: lax.dynamic_index_in_dim(own, (tile_at + hop) % tile_count, 0, keepdims=False))
    )
    return (ilc_map.reshape(tile_count * cycles, NLON // tile_count), ilc_alm)


def solution(mesh):
    placed = (P("band", None, None, "tile"), P("band", "tile", None), P())
    return jax.shard_map(
        body,
        mesh=mesh,
        in_specs=placed,
        out_specs=(P("band", "tile"), P("band", None, "tile")),
        check_vma=False,
    )
```

profile of v0, /device:TPU:0, one launch (start us, length us, event | category | flops | bytes accessed | tf_op | source)
XLA Modules:
  0.0 97.8 jit_solution(4221631306891276698)
XLA Ops:
  0.7 9.1 %fusion.3 = bf16[64,9,2,256]{3,1,2,0:T(8,128)(2,1)S(1)} fusion(bf16[64,512,256]{2,1,0:T(8,128)(2,1)} %param.4, bf16[64,9,2,512]{3,2,1,0:T(2,128)(2,1)} %param.3), kind=kOutput, calls=%fused_computation.3 | convolution fusion | flops 302284800 | bytes 18546688 | tf_op jit(solution)/shard_map/scel,slr->scer/dot_general | solution.py:242
  9.8 1.0 copy.8
  10.7 4.1 %copy.9 = bf16[2,16,9,8,64,2]{1,3,2,5,4,0:T(8,128)(2,1)} copy(bf16[2,16,9,8,64,2]{4,3,0,1,5,2:T(8,128)(2,1)S(1)} %bitcast.35) | data formatting | bytes 1179648 | tf_op jit(solution)/shard_map/transpose | solution.py:244
  14.8 4.6 %constant_dynamic-slice_fusion.3 = (bf16[1,16,72,128]{1,2,3,0:T(8,128)(2,1)S(1)}, bf16[1,16,72,128]{1,2,3,0:T(8,128)(2,1)}) fusion(bf16[2,16,72,128]{1,2,3,0:T(8,128)(2,1)} %bitcast.34, s32[]{:T(128)S(6)} %select_n.56, s32[]{:T(128)S(6)} %select_n.58), kind=kLoop, calls=%fused_computation.30 | loop fusion | bytes 1179656 | tf_op jit(solution)/shard_map/jit(dynamic_index_in_dim)/dynamic_slice | solution.py:246
  19.4 2.9 %copy.11 = bf16[1,16,72,128]{3,2,1,0:T(8,128)(2,1)S(1)} copy(bf16[1,16,72,128]{1,2,3,0:T(8,128)(2,1)} %get-tuple-element.7) | data formatting | bytes 589824 | tf_op jit(solution)/shard_map/jit(dynamic_index_in_dim)/dynamic_slice | solution.py:246
  22.4 0.0 copy-start
  22.4 3.0 %collective-permute-start = (bf16[16,72,128]{2,1,0:T(8,128)(2,1)S(1)}, bf16[16,72,128]{2,1,0:T(8,128)(2,1)S(1)}, u32[]{:S(2)}, u32[]{:S(2)}) collective-permute-start(bf16[16,72,128]{2,1,0:T(8,128)(2,1)S(1)} %bitcast.36), channel_id=1, source_target_pairs={{0,1},{1,0},{2,3},{3,2},{4,5},{5,4},{6,7},{7,6},{8,9},{9,8},{10,11... | collective-permute-start | bytes 884744 | tf_op jit(solution)/shard_map/ppermute | solution.py:217
  25.4 1.9 %copy.18 = bf16[1,16,72,128]{3,2,1,0:T(8,128)(2,1)S(1)} copy(bf16[1,16,72,128]{1,2,3,0:T(8,128)(2,1)S(1)} %get-tuple-element.6) | data formatting | bytes 589824
  27.3 5.1 %collective-permute-done = bf16[16,72,128]{2,1,0:T(8,128)(2,1)S(1)} collective-permute-done((bf16[16,72,128]{2,1,0:T(8,128)(2,1)S(1)}, bf16[16,72,128]{2,1,0:T(8,128)(2,1)S(1)}, u32[]{:S(2)}, u32[]{:S(2)}) %collective-permute-start) | collective-permute-done | bytes 294944 | tf_op jit(solution)/shard_map/ppermute | solution.py:217
  32.4 0.8 fusion.8
  33.2 6.1 %all-to-all-start = ((bf16[16,72,128]{2,1,0:T(8,128)(2,1)}), bf16[16,72,128]{2,1,0:T(8,128)(2,1)S(1)}, u32[]{:S(2)}, u32[]{:S(2)}) async-start(bf16[16,72,128]{2,1,0:T(8,128)(2,1)} %fusion.8), calls=%async_computation | async-start | bytes 589824 | tf_op jit(solution)/shard_map/all_to_all | solution.py:251
  39.4 0.0 copy-done
  39.4 0.2 broadcast_in_dim.8
  39.6 0.2 convert_element_type.48.order_ref
  39.8 0.2 broadcast_in_dim.7
  40.0 0.3 reshape.95
  40.3 9.4 %shard_map.50.basis_hbm = bf16[8,2048,256]{2,1,0:T(8,128)(2,1)} custom-call(f32[2048,1]{1,0:T(8,128)S(1)} %convert_element_type.48.order_ref), custom_call_target="tpu_custom_call" | custom-call | flops 33554432 | bytes 8388608 | tf_op jit(solution)/shard_map/pallas_call | solution.py:63
  49.8 0.1 all-to-all-done.modes_ref
  49.9 16.0 %shard_map.51 = (f32[32,8,128]{2,1,0:T(8,128)S(1)}, bf16[16,8,128]{2,1,0:T(8,128)(2,1)}) custom-call(bf16[16,72,128]{2,1,0:T(8,128)(2,1)S(1)} %all-to-all-done.modes_ref, f32[1,2048]{1,0:T(1,128)S(1)} %fusion.13.odd_ref, bf16[8,2048,256]{2,1,0:T(8,128)(2,1)} %shard_map.50.basis_hbm), custom_call_target="tpu_custom_call" | custom-call | flops 1342177280 | bytes 8388608 | tf_op jit(solution)/shard_map/pallas_call | solution.py:188
  65.9 0.2 copy.13
  66.1 0.3 reshape.96
  66.4 0.1 constant_dynamic-slice_fusion
  66.6 1.6 %collective-permute-start.1 = (f32[8,2048]{1,0:T(8,128)S(1)}, f32[8,2048]{1,0:T(8,128)S(1)}, u32[]{:S(2)}, u32[]{:S(2)}) collective-permute-start(f32[8,2048]{1,0:T(8,128)S(1)} %bitcast.39), channel_id=1, source_target_pairs={{0,1},{1,0},{2,3},{3,2},{4,5},{5,4},{6,7},{7,6},{8,9},{9,8},{10,11... | collective-permute-start | bytes 196616 | tf_op jit(solution)/shard_map/ppermute | solution.py:217
  68.2 6.1 %all-to-all-start.1 = ((bf16[16,8,128]{2,1,0:T(8,128)(2,1)}), bf16[16,8,128]{2,1,0:T(8,128)(2,1)S(1)}, u32[]{:S(2)}, u32[]{:S(2)}) async-start(bf16[16,8,128]{2,1,0:T(8,128)(2,1)} %get-tuple-element.5), calls=%async_computation.1 | async-start | bytes 65536 | tf_op jit(solution)/shard_map/all_to_all | solution.py:269
  74.3 6.6 %all-to-all-done.1 = bf16[16,8,128]{2,1,0:T(8,128)(2,1)S(1)} async-done(((bf16[16,8,128]{2,1,0:T(8,128)(2,1)}), bf16[16,8,128]{2,1,0:T(8,128)(2,1)S(1)}, u32[]{:S(2)}, u32[]{:S(2)}) %all-to-all-start.1) | async-done | bytes 32800 | tf_op jit(solution)/shard_map/all_to_all | solution.py:269
  80.9 0.5 collective-permute-start.2
  81.4 0.0 collective-permute-done.1
  81.4 0.7 maximum_bitcast_fusion
  82.1 2.7 %collective-permute-done.2 = bf16[16,8,128]{2,1,0:T(8,128)(2,1)S(1)} collective-permute-done((bf16[16,8,128]{2,1,0:T(8,128)(2,1)S(1)}, bf16[16,8,128]{2,1,0:T(8,128)(2,1)S(1)}, u32[]{:S(2)}, u32[]{:S(2)}) %collective-permute-start.2) | collective-permute-done | bytes 32800 | tf_op jit(solution)/shard_map/ppermute | solution.py:217
  84.9 0.9 copy.14
  85.8 1.1 %reshape.98 = bf16[256,64,2]{0,2,1:T(2,128)(2,1)S(1)} reshape(bf16[16,2,8,128]{2,1,0,3:T(2,128)(2,1)S(1)} %copy.14) | data formatting | bytes 131072 | tf_op jit(solution)/shard_map/reshape | solution.py:271
  86.9 10.9 %fusion.15 = f32[64,2,512]{2,1,0:T(2,128)} fusion(bf16[256,64,2]{0,2,1:T(2,128)(2,1)S(1)} %reshape.98, bf16[64,512,256]{2,1,0:T(8,128)(2,1)} %param.4), kind=kOutput, calls=%fused_computation.31 | convolution fusion | flops 33554432 | bytes 17104896 | tf_op jit(solution)/shard_map/slr,rse->sel/dot_general | solution.py:272
  (7 shorter events, 0.2 us)
Async XLA Ops:
  22.4 17.0 %copy-start = (s32[1024]{0:T(1024)S(1)}, s32[1024]{0:T(1024)}, u32[]{:S(2)}) copy-start(s32[1024]{0:T(1024)} %param.5) | copy-start | bytes 12292
  22.4 10.0 %collective-permute-start = (bf16[16,72,128]{2,1,0:T(8,128)(2,1)S(1)}, bf16[16,72,128]{2,1,0:T(8,128)(2,1)S(1)}, u32[]{:S(2)}, u32[]{:S(2)}) collective-permute-start(bf16[16,72,128]{2,1,0:T(8,128)(2,1)S(1)} %bitcast.36), channel_id=1, source_target_pairs={{0,1},{1,0},{2,3},{3,2},{4,5},{5,4},{6,7},{7,6},{8,9},{9,8},{10,11... | collective-permute-start | bytes 884744 | tf_op jit(solution)/shard_map/ppermute | solution.py:217
  33.2 16.7 %all-to-all-start = ((bf16[16,72,128]{2,1,0:T(8,128)(2,1)}), bf16[16,72,128]{2,1,0:T(8,128)(2,1)S(1)}, u32[]{:S(2)}, u32[]{:S(2)}) async-start(bf16[16,72,128]{2,1,0:T(8,128)(2,1)} %fusion.8), calls=%async_computation | async-start | bytes 589824 | tf_op jit(solution)/shard_map/all_to_all | solution.py:251
  66.6 14.8 %collective-permute-start.1 = (f32[8,2048]{1,0:T(8,128)S(1)}, f32[8,2048]{1,0:T(8,128)S(1)}, u32[]{:S(2)}, u32[]{:S(2)}) collective-permute-start(f32[8,2048]{1,0:T(8,128)S(1)} %bitcast.39), channel_id=1, source_target_pairs={{0,1},{1,0},{2,3},{3,2},{4,5},{5,4},{6,7},{7,6},{8,9},{9,8},{10,11... | collective-permute-start | bytes 196616 | tf_op jit(solution)/shard_map/ppermute | solution.py:217
  68.2 12.7 %all-to-all-start.1 = ((bf16[16,8,128]{2,1,0:T(8,128)(2,1)}), bf16[16,8,128]{2,1,0:T(8,128)(2,1)S(1)}, u32[]{:S(2)}, u32[]{:S(2)}) async-start(bf16[16,8,128]{2,1,0:T(8,128)(2,1)} %get-tuple-element.5), calls=%async_computation.1 | async-start | bytes 65536 | tf_op jit(solution)/shard_map/all_to_all | solution.py:269
  80.9 3.9 %collective-permute-start.2 = (bf16[16,8,128]{2,1,0:T(8,128)(2,1)S(1)}, bf16[16,8,128]{2,1,0:T(8,128)(2,1)S(1)}, u32[]{:S(2)}, u32[]{:S(2)}) collective-permute-start(bf16[16,8,128]{2,1,0:T(8,128)(2,1)S(1)} %all-to-all-done.1), channel_id=1, source_target_pairs={{0,1},{1,0},{2,3},{3,2},{4,5},{5,4},{6,7},{7,6},{8,9},{9,8},{10,11... | collective-permute-start | bytes 98312 | tf_op jit(solution)/shard_map/ppermute | solution.py:217
where the time goes:
time: 98.2 us; the launch traced here: 97.8 us
  Pallas kernels  25.4 us (26%)
  matrix products  20 us (20%)
  local copies, waits for them, and re-layouts  18.1 us (18%)
  starting transfers between devices  17.3 us (18%)
  waiting for transfers between devices  14.6 us (15%)
  other arithmetic  1.58 us (2%)
    pallas_call x1, Pallas kernels, run_ilc(): pl.pallas_call(ilc_kernel, in_specs=[vmem, vmem, pl.BlockSpec(memory_spac...  16 us
    dot_general x1, matrix products, body(): jnp.einsum('slr,rse->sel', legendre, cycle_spectra, preferred_element_typ...  10.9 us
    pallas_call x1, Pallas kernels, make_basis(): pl.pallas_call(basis_kernel, grid=(rows // block,), in_specs=[pl.BlockSpe...  9.45 us
    dot_general x1, matrix products, body(): jnp.einsum('scel,slr->scer', alm, legendre, preferred_element_type=jnp.fl...  9.1 us
    ppermute x3, waiting for transfers between devices, from_other_tiles(): lax.ppermute(send(hop), 'tile', [(at, (at + hop) % count) for at in range...  7.85 us
    dynamic_slice x2, local copies, waits for them, and re-layouts, body(): lax.dynamic_index_in_dim(partial, (tile_at + hop) % tile_count, 0, keepdi...  7.57 us
    all_to_all x1, waiting for transfers between devices, body(): lax.all_to_all(spectra, 'band', split_axis=0, concat_axis=0, tiled=True)  6.58 us
    all_to_all x1, starting transfers between devices, body(): lax.all_to_all(total.astype(jnp.bfloat16), 'band', split_axis=0, concat_a...  6.13 us
  transfers between devices with their start and end apart: 5, of which 4 were waited for; matrix products, arithmetic and copies ran while one was open for 4% of the time, Pallas kernels for 10%

commit v1 on v0

--- a/solution.py
+++ b/solution.py
@@ -210,11 +210,120 @@
     )(modes, odd, basis)
 
 
-def from_other_tiles(send):
-    count = lax.axis_size("tile")
-    got = [send(0)]
+def modes_kernel(alm_ref, table_ref, *refs):
+    out_refs, (lhs_ref, held_ref, turned_ref) = refs[:-3], refs[-3:]
+    tile_count = len(out_refs)
+    slots = table_ref.shape[0]
+    bands, rows = out_refs[0].shape[:2]
+    cycles = rows // C
+    step = pl.program_id(0)
+    for slot in range(slots):
+        for chan in range(C):
+            lhs_ref[slot, 2 * chan : 2 * chan + 2, :] = alm_ref[slot, chan].astype(jnp.float32)
+        result = jnp.dot(
+            lhs_ref[slot].astype(jnp.bfloat16), table_ref[slot], preferred_element_type=jnp.float32
+        )
+        for chan in range(C):
+            held_ref[chan, step, 2 * slot : 2 * slot + 2, :] = result[2 * chan : 2 * chan + 2]
+
+    @pl.when(step == pl.num_programs(0) - 1)
+    def _():
+        for chan in range(C):
+            turned_ref[chan] = held_ref[chan].reshape(turned_ref.shape[2], turned_ref.shape[1]).T
+        tile_at = lax.axis_index("tile")
+        for hop in range(tile_count):
+            begin = (tile_at + hop) % tile_count * cycles
+            for band in range(bands):
+                at = band * tile_count * cycles + begin
+                if cycles % 8 == 0:
+                    at = pl.multiple_of(at, 8)
+                block = jnp.concatenate([turned_ref[chan, pl.ds(at, cycles), :] for chan in range(C)], axis=0)
+                out_refs[hop][band] = block.astype(jnp.bfloat16)
+
+
+def make_modes(alm, legendre, band_count, tile_count):
+    slot_count, degrees, total = legendre.shape
+    slots = 8
+    width = 2 * slot_count
+    cycles = total // (band_count * tile_count)
+    one = jax.ShapeDtypeStruct((band_count, C * cycles, width), jnp.bfloat16)
+    whole = pl.BlockSpec(one.shape, lambda at: (0, 0, 0))
+    return pl.pallas_call(
+        modes_kernel,
+        grid=(slot_count // slots,),
+        in_specs=[
+            pl.BlockSpec((slots, C, 2, degrees), lambda at: (at, 0, 0, 0)),
+            pl.BlockSpec((slots, degrees, total), lambda at: (at, 0, 0)),
+        ],
+        out_specs=[whole] * tile_count,
+        out_shape=[one] * tile_count,
+        scratch_shapes=[
+            pltpu.VMEM((slots, 2 * C, degrees), jnp.float32),
+            pltpu.VMEM((C, slot_count // slots, 2 * slots, total), jnp.float32),
+            pltpu.VMEM((C, total, width), jnp.float32),
+        ],
+        cost_estimate=pl.CostEstimate(
+            flops=2 * slot_count * degrees * total * 2 * C,
+            bytes_accessed=slot_count * degrees * (total + 2 * C) * 2,
+            transcendentals=0,
+        ),
+        compiler_params=pltpu.CompilerParams(vmem_limit_bytes=VMEM_LIMIT),
+    )(alm, legendre)
+
+
+def analysis_kernel(table_ref, *refs):
+    spectra_refs, (out_ref, gathered_ref, turned_ref) = refs[:-3], refs[-3:]
+    tile_count = len(spectra_refs)
+    slots = table_ref.shape[0]
+    bands, cycles = spectra_refs[0].shape[:2]
+    step = pl.program_id(0)
+
+    @pl.when(step == 0)
+    def _():
+        tile_at = lax.axis_index("tile")
+        for hop in range(tile_count):
+            begin = (tile_at + tile_count - hop) % tile_count * cycles
+            for band in range(bands):
+                at = band * tile_count * cycles + begin
+                if cycles % 8 == 0:
+                    at = pl.multiple_of(at, 8)
+                gathered_ref[pl.ds(at, cycles), :] = spectra_refs[hop][band].astype(jnp.float32)
+        turned_ref[...] = gathered_ref[...].T.astype(jnp.bfloat16)
+
+    lhs = turned_ref[pl.ds(pl.multiple_of(step * 2 * slots, 2 * slots), 2 * slots), :]
+    for slot in range(slots):
+        result = lax.dot_general(
+            lhs, table_ref[slot], (((1,), (1,)), ((), ())), preferred_element_type=jnp.float32
+        )
+        out_ref[slot] = result[2 * slot : 2 * slot + 2]
+
+
+def analyse(legendre, spectra):
+    slot_count, degrees, total = legendre.shape
+    slots = 8
+    width = 2 * slot_count
+    whole = pl.BlockSpec(spectra[0].shape, lambda at: (0, 0, 0))
+    return pl.pallas_call(
+        analysis_kernel,
+        grid=(slot_count // slots,),
+        in_specs=[pl.BlockSpec((slots, degrees, total), lambda at: (at, 0, 0))] + [whole] * len(spectra),
+        out_specs=pl.BlockSpec((slots, 2, degrees), lambda at: (at, 0, 0)),
+        out_shape=jax.ShapeDtypeStruct((slot_count, 2, degrees), jnp.float32),
+        scratch_shapes=[pltpu.VMEM((total, width), jnp.float32), pltpu.VMEM((width, total), jnp.bfloat16)],
+        cost_estimate=pl.CostEstimate(
+            flops=2 * slot_count * degrees * total * 16,
+            bytes_accessed=slot_count * degrees * total * 2,
+            transcendentals=0,
+        ),
+        compiler_params=pltpu.CompilerParams(vmem_limit_bytes=VMEM_LIMIT),
+    )(legendre, *spectra)
+
+
+def from_other_tiles(sends):
+    count = len(sends)
+    got = [sends[0]]
     for hop in range(1, count):
-        got.append(lax.ppermute(send(hop), "tile", [(at, (at + hop) % count) for at in range(count)]))
+        got.append(lax.ppermute(sends[hop], "tile", [(at, (at + hop) % count) for at in range(count)]))
     return got
 
 
@@ -239,12 +348,7 @@
     group_width = math.lcm(width, LANES)
     groups = depth // group_width
 
-    partial = jnp.einsum("scel,slr->scer", alm, legendre, preferred_element_type=jnp.float32)
-    partial = partial.astype(jnp.bfloat16).reshape(slot_count, C, 2, band_count, tile_count, cycles)
-    partial = partial.transpose(4, 3, 1, 5, 0, 2).reshape(tile_count, band_count, C * cycles, width)
-    got = from_other_tiles(
-        lambda hop: lax.dynamic_index_in_dim(partial, (tile_at + hop) % tile_count, 0, keepdims=False)
-    )
+    got = from_other_tiles(make_modes(alm, legendre, band_count, tile_count))
     total = got[0].astype(jnp.float32)
     for other in got[1:]:
         total = total + other.astype(jnp.float32)
@@ -267,15 +371,14 @@
         spectra = spectra.reshape(groups, cycles, group_width // width, width)
         spectra = spectra.transpose(0, 2, 1, 3).reshape(band_count, cycles, width)
     routed = lax.all_to_all(spectra, "band", split_axis=0, concat_axis=0, tiled=True)
-    cycle_spectra = in_tile_order(from_other_tiles(lambda hop: routed))
-    cycle_spectra = cycle_spectra.transpose(1, 0, 2, 3).reshape(band_count * tile_count * cycles, slot_count, 2)
-    ilc_alm = jnp.einsum("slr,rse->sel", legendre, cycle_spectra, preferred_element_type=jnp.float32)
+    ilc_alm = analyse(legendre, from_other_tiles([routed] * tile_count))
 
     own = vectors[:, :cycles].transpose(1, 2, 0).reshape(cycles, tile_count, NLON // tile_count)
     own = own.transpose(1, 0, 2)
-    ilc_map = in_tile_order(
-        from_other_tiles(lambda hop: lax.dynamic_index_in_dim(own, (tile_at + hop) % tile_count, 0, keepdims=False))
-    )
+    sends = [
+        lax.dynamic_index_in_dim(own, (tile_at + hop) % tile_count, 0, keepdims=False) for hop in range(tile_count)
+    ]
+    ilc_map = in_tile_order(from_other_tiles(sends))
     return (ilc_map.reshape(tile_count * cycles, NLON // tile_count), ilc_alm)
 
 

time: 98.2 us -> 85.5 us (0.87)
  Pallas kernels: 25.4 us -> 46.2 us
  matrix products: 20 us -> 0 us
  local copies, waits for them, and re-layouts: 18.1 us -> 2.86 us
  waiting for transfers between devices: 14.6 us -> 16.4 us
    pallas_call x0 -> x2, Pallas kernels: none -> 20.8 us  [the longest x1 10.9 us: analyse(): pl.pallas_call(analysis_kernel, grid=(slot_count // slots,), in_specs=[pl...]
    dot_general x2 -> x0, matrix products: 20 us -> none  [the longest x1 10.9 us: body(): jnp.einsum('slr,rse->sel', legendre, cycle_spectra, preferred_element_typ...]
    dynamic_slice x2 -> x0, local copies, waits for them, and re-layouts: 7.57 us -> none  [body(): lax.dynamic_index_in_dim(partial, (tile_at + hop) % tile_count, 0, keepdi...]
    transpose x2 -> x0, local copies, waits for them, and re-layouts: 4.97 us -> none  [the longest x1 4.06 us: body(): partial.transpose(4, 3, 1, 5, 0, 2)]
    ppermute x3, waiting for transfers between devices: 7.85 us -> 9.71 us  [from_other_tiles(): lax.ppermute(sends[hop], 'tile', [(at, (at + hop) % count) for at in rang...]
    reshape x1 -> x0, local copies, waits for them, and re-layouts: 1.14 us -> none  [body(): cycle_spectra.transpose(1, 0, 2, 3)]
  transfers between devices with their start and end apart: 5 -> 5, of which waited for: 4 -> 4; matrix products, arithmetic and copies ran while one was open for 4% -> 2% of each run, Pallas kernels for 10% -> 11%
where the time goes in v1:
time: 85.5 us; the launch traced here: 85 us
  Pallas kernels  46.2 us (54%)
  starting transfers between devices  17.1 us (20%)
  waiting for transfers between devices  16.4 us (19%)
  local copies, waits for them, and re-layouts  2.86 us (3%)
  other arithmetic  1.55 us (2%)
    pallas_call x1, Pallas kernels, run_ilc(): pl.pallas_call(ilc_kernel, in_specs=[vmem, vmem, pl.BlockSpec(memory_spac...  16 us
    pallas_call x1, Pallas kernels, analyse(): pl.pallas_call(analysis_kernel, grid=(slot_count // slots,), in_specs=[pl...  10.9 us
    pallas_call x1, Pallas kernels, make_modes(): pl.pallas_call(modes_kernel, grid=(slot_count // slots,), in_specs=[pl.Bl...  9.85 us
    ppermute x3, waiting for transfers between devices, from_other_tiles(): lax.ppermute(sends[hop], 'tile', [(at, (at + hop) % count) for at in rang...  9.71 us
    pallas_call x1, Pallas kernels, make_basis(): pl.pallas_call(basis_kernel, grid=(rows // block,), in_specs=[pl.BlockSpe...  9.45 us
    all_to_all x1, waiting for transfers between devices, body(): lax.all_to_all(spectra, 'band', split_axis=0, concat_axis=0, tiled=True)  6.58 us
    all_to_all x1, starting transfers between devices, body(): lax.all_to_all(total.astype(jnp.bfloat16), 'band', split_axis=0, concat_a...  6.13 us
    all_to_all x1, starting transfers between devices, body(): lax.all_to_all(spectra, 'band', split_axis=0, concat_axis=0, tiled=True)  5.89 us
  transfers between devices with their start and end apart: 5, of which 4 were waited for; matrix products, arithmetic and copies ran while one was open for 2% of the time, Pallas kernels for 11%

profile of v1, /device:TPU:0, one launch (start us, length us, event | category | flops | bytes accessed | tf_op | source)
XLA Modules:
  0.0 85.0 jit_solution(2666475519802627988)
XLA Ops:
  0.6 0.0 copy-start
  0.6 1.3 %copy-done = bf16[64,9,2,512]{3,2,1,0:T(2,128)(2,1)S(1)} copy-done((bf16[64,9,2,512]{3,2,1,0:T(2,128)(2,1)S(1)}, bf16[64,9,2,512]{3,2,1,0:T(2,128)(2,1)}, u32[]{:S(2)}) %copy-start) | copy-done | bytes 1179672
  1.9 0.0 copy-start.1
  1.9 9.9 %shard_map.50 = (bf16[16,72,128]{2,1,0:T(8,128)(2,1)S(1)}, bf16[16,72,128]{2,1,0:T(8,128)(2,1)S(1)}) custom-call(bf16[64,9,2,512]{3,2,1,0:T(2,128)(2,1)S(1)} %copy-done, bf16[64,512,256]{2,1,0:T(8,128)(2,1)} %table_ref.3), custom_call_target="tpu_custom_call" | custom-call | flops 301989888 | bytes 17956864 | tf_op jit(solution)/shard_map/pallas_call | solution.py:251
  11.8 3.0 %collective-permute-start = (bf16[16,72,128]{2,1,0:T(8,128)(2,1)S(1)}, bf16[16,72,128]{2,1,0:T(8,128)(2,1)S(1)}, u32[]{:S(2)}, u32[]{:S(2)}) collective-permute-start(bf16[16,72,128]{2,1,0:T(8,128)(2,1)S(1)} %get-tuple-element.7), channel_id=1, source_target_pairs={{0,1},{1,0},{2,3},{3,2},{4,5},{5,4},{6,7},{7,6},{8,9},{9,8},{10,11... | collective-permute-start | bytes 884744 | tf_op jit(solution)/shard_map/ppermute | solution.py:326
  14.8 7.0 %collective-permute-done = bf16[16,72,128]{2,1,0:T(8,128)(2,1)S(1)} collective-permute-done((bf16[16,72,128]{2,1,0:T(8,128)(2,1)S(1)}, bf16[16,72,128]{2,1,0:T(8,128)(2,1)S(1)}, u32[]{:S(2)}, u32[]{:S(2)}) %collective-permute-start) | collective-permute-done | bytes 294944 | tf_op jit(solution)/shard_map/ppermute | solution.py:326
  21.8 0.8 add_convert_fusion
  22.6 6.1 %all-to-all-start = ((bf16[16,72,128]{2,1,0:T(8,128)(2,1)}), bf16[16,72,128]{2,1,0:T(8,128)(2,1)S(1)}, u32[]{:S(2)}, u32[]{:S(2)}) async-start(bf16[16,72,128]{2,1,0:T(8,128)(2,1)} %add_convert_fusion), calls=%async_computation | async-start | bytes 589824 | tf_op jit(solution)/shard_map/all_to_all | solution.py:355
  28.8 0.0 copy-done.1
  28.8 0.2 broadcast_in_dim.8
  29.0 0.2 convert_element_type.39.order_ref
  29.2 0.2 broadcast_in_dim.7
  29.4 0.3 reshape.82
  29.8 9.4 %shard_map.51.basis_hbm = bf16[8,2048,256]{2,1,0:T(8,128)(2,1)} custom-call(f32[2048,1]{1,0:T(8,128)S(1)} %convert_element_type.39.order_ref), custom_call_target="tpu_custom_call" | custom-call | flops 33554432 | bytes 8388608 | tf_op jit(solution)/shard_map/pallas_call | solution.py:63
  39.2 0.1 all-to-all-done.modes_ref
  39.3 16.0 %shard_map.52 = (f32[32,8,128]{2,1,0:T(8,128)S(1)}, bf16[16,8,128]{2,1,0:T(8,128)(2,1)}) custom-call(bf16[16,72,128]{2,1,0:T(8,128)(2,1)S(1)} %all-to-all-done.modes_ref, f32[1,2048]{1,0:T(1,128)S(1)} %fusion.2.odd_ref, bf16[8,2048,256]{2,1,0:T(8,128)(2,1)} %shard_map.51.basis_hbm), custom_call_target="tpu_custom_call" | custom-call | flops 1342177280 | bytes 8388608 | tf_op jit(solution)/shard_map/pallas_call | solution.py:188
  55.3 0.2 copy.6
  55.5 0.3 reshape.83
  55.8 0.1 constant_dynamic-slice_fusion
  56.0 1.6 %collective-permute-start.1 = (f32[8,2048]{1,0:T(8,128)S(1)}, f32[8,2048]{1,0:T(8,128)S(1)}, u32[]{:S(2)}, u32[]{:S(2)}) collective-permute-start(f32[8,2048]{1,0:T(8,128)S(1)} %bitcast.12), channel_id=1, source_target_pairs={{0,1},{1,0},{2,3},{3,2},{4,5},{5,4},{6,7},{7,6},{8,9},{9,8},{10,11... | collective-permute-start | bytes 196616 | tf_op jit(solution)/shard_map/ppermute | solution.py:326
  57.6 5.9 %all-to-all-start.1 = ((bf16[16,8,128]{2,1,0:T(8,128)(2,1)}), bf16[16,8,128]{2,1,0:T(8,128)(2,1)S(1)}, u32[]{:S(2)}, u32[]{:S(2)}) async-start(bf16[16,8,128]{2,1,0:T(8,128)(2,1)} %get-tuple-element.9), calls=%async_computation.1 | async-start | bytes 65536 | tf_op jit(solution)/shard_map/all_to_all | solution.py:373
  63.5 6.6 %all-to-all-done.1.refs_0_ = bf16[16,8,128]{2,1,0:T(8,128)(2,1)S(1)} async-done(((bf16[16,8,128]{2,1,0:T(8,128)(2,1)}), bf16[16,8,128]{2,1,0:T(8,128)(2,1)S(1)}, u32[]{:S(2)}, u32[]{:S(2)}) %all-to-all-start.1) | async-done | bytes 32800 | tf_op jit(solution)/shard_map/all_to_all | solution.py:373
  70.1 0.5 collective-permute-start.2
  70.6 0.0 collective-permute-done.1
  70.7 0.7 maximum_bitcast_fusion
  71.3 2.7 %collective-permute-done.2.refs_1_ = bf16[16,8,128]{2,1,0:T(8,128)(2,1)S(1)} collective-permute-done((bf16[16,8,128]{2,1,0:T(8,128)(2,1)S(1)}, bf16[16,8,128]{2,1,0:T(8,128)(2,1)S(1)}, u32[]{:S(2)}, u32[]{:S(2)}) %collective-permute-start.2) | collective-permute-done | bytes 32800 | tf_op jit(solution)/shard_map/ppermute | solution.py:326
  74.0 10.9 %shard_map.53 = f32[64,2,512]{2,1,0:T(2,128)} custom-call(bf16[64,512,256]{2,1,0:T(8,128)(2,1)} %table_ref.3, bf16[16,8,128]{2,1,0:T(8,128)(2,1)S(1)} %all-to-all-done.1.refs_0_, bf16[16,8,128]{2,1,0:T(8,128)(2,1)S(1)} %collective-permute-done.2.refs_1_), custom_call_target="tpu_custom_call" | custom-call | flops 268435456 | bytes 16777216 | tf_op jit(solution)/shard_map/pallas_call | solution.py:306
  (5 shorter events, 0.1 us)
Async XLA Ops:
  0.6 1.3 %copy-start = (bf16[64,9,2,512]{3,2,1,0:T(2,128)(2,1)S(1)}, bf16[64,9,2,512]{3,2,1,0:T(2,128)(2,1)}, u32[]{:S(2)}) copy-start(bf16[64,9,2,512]{3,2,1,0:T(2,128)(2,1)} %alm_ref.1) | copy-start | bytes 3538948
  1.9 26.9 %copy-start.1 = (s32[1024]{0:T(1024)S(1)}, s32[1024]{0:T(1024)}, u32[]{:S(2)}) copy-start(s32[1024]{0:T(1024)} %param.5) | copy-start | bytes 12292
  11.8 10.0 %collective-permute-start = (bf16[16,72,128]{2,1,0:T(8,128)(2,1)S(1)}, bf16[16,72,128]{2,1,0:T(8,128)(2,1)S(1)}, u32[]{:S(2)}, u32[]{:S(2)}) collective-permute-start(bf16[16,72,128]{2,1,0:T(8,128)(2,1)S(1)} %get-tuple-element.7), channel_id=1, source_target_pairs={{0,1},{1,0},{2,3},{3,2},{4,5},{5,4},{6,7},{7,6},{8,9},{9,8},{10,11... | collective-permute-start | bytes 884744 | tf_op jit(solution)/shard_map/ppermute | solution.py:326
  22.6 16.7 %all-to-all-start = ((bf16[16,72,128]{2,1,0:T(8,128)(2,1)}), bf16[16,72,128]{2,1,0:T(8,128)(2,1)S(1)}, u32[]{:S(2)}, u32[]{:S(2)}) async-start(bf16[16,72,128]{2,1,0:T(8,128)(2,1)} %add_convert_fusion), calls=%async_computation | async-start | bytes 589824 | tf_op jit(solution)/shard_map/all_to_all | solution.py:355
  56.0 14.6 %collective-permute-start.1 = (f32[8,2048]{1,0:T(8,128)S(1)}, f32[8,2048]{1,0:T(8,128)S(1)}, u32[]{:S(2)}, u32[]{:S(2)}) collective-permute-start(f32[8,2048]{1,0:T(8,128)S(1)} %bitcast.12), channel_id=1, source_target_pairs={{0,1},{1,0},{2,3},{3,2},{4,5},{5,4},{6,7},{7,6},{8,9},{9,8},{10,11... | collective-permute-start | bytes 196616 | tf_op jit(solution)/shard_map/ppermute | solution.py:326
  57.6 12.5 %all-to-all-start.1 = ((bf16[16,8,128]{2,1,0:T(8,128)(2,1)}), bf16[16,8,128]{2,1,0:T(8,128)(2,1)S(1)}, u32[]{:S(2)}, u32[]{:S(2)}) async-start(bf16[16,8,128]{2,1,0:T(8,128)(2,1)} %get-tuple-element.9), calls=%async_computation.1 | async-start | bytes 65536 | tf_op jit(solution)/shard_map/all_to_all | solution.py:373
  70.1 3.9 %collective-permute-start.2 = (bf16[16,8,128]{2,1,0:T(8,128)(2,1)S(1)}, bf16[16,8,128]{2,1,0:T(8,128)(2,1)S(1)}, u32[]{:S(2)}, u32[]{:S(2)}) collective-permute-start(bf16[16,8,128]{2,1,0:T(8,128)(2,1)S(1)} %all-to-all-done.1.refs_0_), channel_id=1, source_target_pairs={{0,1},{1,0},{2,3},{3,2},{4,5},{5,4},{6,7},{7,6},{8,9},{9,8},{10,11... | collective-permute-start | bytes 98312 | tf_op jit(solution)/shard_map/ppermute | solution.py:326

commit v2 on v0

--- a/solution.py
+++ b/solution.py
@@ -20,7 +20,7 @@
 LANES = NLON // HALO
 HALF = LANES // 2
 PAIRS = [(a_at, b_at) for a_at in range(C) for b_at in range(a_at, C)]
-VMEM_LIMIT = 48 * 1024 * 1024
+VMEM_LIMIT = 24 * 1024 * 1024
 
 
 def round_up(value, multiple):
@@ -28,8 +28,8 @@
 
 
 def cos_turns(turns):
-    away = jnp.abs(turns - jnp.floor(turns + 0.5))
-    quarter = 1.0 - 4.0 * away
+    nearest = (turns + 12582912.0) - 12582912.0
+    quarter = 1.0 - 4.0 * jnp.abs(turns - nearest)
     square = quarter * quarter
     tail = square * (1.6044118478736e-04 - square * 3.598843235e-06)
     tail = square * (-4.68175413531868e-03 + tail)
@@ -39,26 +39,34 @@
 
 
 def basis_kernel(order_ref, basis_ref):
-    rows = order_ref.shape[0]
-    order = jnp.broadcast_to(order_ref[...], (rows, LANES))
+    rows = 32
     row = lax.broadcasted_iota(jnp.int32, (rows, LANES), 0)
     lane = lax.broadcasted_iota(jnp.int32, (rows, LANES), 1)
-    cell = HALO * (lane % HALF) + lane // HALF
-    turns = order * (cell.astype(jnp.float32) / NLON) + (row % 2).astype(jnp.float32) * 0.25
-    step = order * (2.0 / NLON)
+    cell = (HALO * (lane % HALF) + lane // HALF).astype(jnp.float32) / NLON
+    offset = (row % 2).astype(jnp.float32) * 0.25
     scaling = 1.0 / math.sqrt(L)
-    before = cos_turns(turns) * scaling
-    now = cos_turns(turns + step) * scaling
-    twice = 2.0 * cos_turns(step)
-    for at in range(HALO // 2):
-        basis_ref[at // 2, :, at % 2 * LANES : (at % 2 + 1) * LANES] = before.astype(jnp.bfloat16)
-        if at < HALO // 2 - 1:
-            before, now = now, twice * now - before
+
+    def block(at, carry):
+        span = pl.ds(pl.multiple_of(at * rows, rows), rows)
+        order = jnp.broadcast_to(order_ref[span, :], (rows, LANES))
+        turns = order * cell + offset
+        step = order * (2.0 / NLON)
+        before = cos_turns(turns) * scaling
+        now = cos_turns(turns + step) * scaling
+        twice = 2.0 * cos_turns(step)
+        for column in range(HALO // 2):
+            lanes = slice(column % 2 * LANES, (column % 2 + 1) * LANES)
+            basis_ref[column // 2, span, lanes] = before.astype(jnp.bfloat16)
+            if column < HALO // 2 - 1:
+                before, now = now, twice * now - before
+        return carry
+
+    lax.fori_loop(0, order_ref.shape[0] // rows, block, 0)
 
 
 def make_basis(order_rows):
     rows = order_rows.shape[0]
-    block = 128
+    block = 256
     chunks = HALO // 4
     return pl.pallas_call(
         basis_kernel,
@@ -100,7 +108,7 @@
     return top / bottom
 
 
-def ilc_kernel(modes_ref, odd_ref, basis_hbm, ilc_ref, spectra_ref, basis_ref, lhs_ref, maps_ref, sums_ref, low_ref, sems):
+def ilc_kernel(modes_ref, odd_ref, basis_hbm, ilc_ref, spectra_ref, basis_ref, lhs_ref, maps_ref, sums_ref, low_ref, found_ref, sems):
     groups, rows, width = modes_ref.shape
     chunks = basis_ref.shape[0]
     cycles = rows // C
@@ -163,21 +171,21 @@
             found.append(value)
         near = jnp.where(low_half, found[0], pltpu.roll(found[1], HALF, 1))
         far = jnp.where(low_half, pltpu.roll(found[0], HALF, 1), found[1])
-        low_ref[pair_at] = jnp.concatenate([near, far], axis=0).astype(jnp.bfloat16)
+        low_ref[pair_at] = jnp.concatenate([near, far], axis=0).T.astype(jnp.bfloat16)
         return carry
 
     lax.fori_loop(0, HALO // 2, two_vectors, 0)
 
-    result = jnp.zeros((2 * cycles, groups * width), jnp.float32)
-    for chunk in range(chunks):
-        lhs = jnp.concatenate([low_ref[2 * chunk], low_ref[2 * chunk + 1]], axis=1)
-        result = result + lax.dot_general(
-            lhs, basis_ref[chunk], (((1,), (1,)), ((), ())), preferred_element_type=jnp.float32
-        )
+    for chunk in range(0, chunks, 2):
+        lhs = jnp.concatenate([basis_ref[chunk], basis_ref[chunk + 1]], axis=1)
+        rhs = jnp.concatenate([low_ref[2 * chunk + part] for part in range(4)], axis=0)
+        term = jnp.dot(lhs, rhs, preferred_element_type=jnp.float32)
+        found_ref[...] = term if chunk == 0 else found_ref[...] + term
     for group in range(groups):
         span = slice(group * width, (group + 1) * width)
         sign = 1.0 - 2.0 * odd_ref[:, span]
-        spectra_ref[group] = (result[0:cycles, span] + sign * result[cycles:, span]).astype(jnp.bfloat16)
+        result = found_ref[span, :].T
+        spectra_ref[group] = (result[0:cycles] + sign * result[cycles:]).astype(jnp.bfloat16)
 
 
 def run_ilc(modes, odd, basis):
@@ -198,7 +206,8 @@
             pltpu.VMEM((2 * round_up(rows, 16), depth), jnp.bfloat16),
             pltpu.VMEM((HALO, rows, LANES), jnp.float32),
             pltpu.VMEM((len(PAIRS), cycles, LANES), jnp.float32),
-            pltpu.VMEM((HALO // 2, 2 * cycles, LANES), jnp.bfloat16),
+            pltpu.VMEM((HALO // 2, LANES, 2 * cycles), jnp.bfloat16),
+            pltpu.VMEM((depth, 2 * cycles), jnp.float32),
             pltpu.SemaphoreType.DMA((chunks,)),
         ],
         cost_estimate=pl.CostEstimate(
@@ -210,11 +219,155 @@
     )(modes, odd, basis)
 
 
-def from_other_tiles(send):
-    count = lax.axis_size("tile")
-    got = [send(0)]
+def start_table(table_hbm, table_ref, sems):
+    parts = sems.shape[0]
+    slots = table_ref.shape[0] // parts
+    for part in range(parts):
+        span = slice(part * slots, (part + 1) * slots)
+        pltpu.make_async_copy(table_hbm.at[span], table_ref.at[span], sems.at[part]).start()
+
+
+def wait_table(table_hbm, table_ref, sems, part):
+    slots = table_ref.shape[0] // sems.shape[0]
+    span = pl.ds(part * slots, slots)
+    pltpu.make_async_copy(table_hbm.at[span], table_ref.at[span], sems.at[part]).wait()
+
+
+def tile_rows(band, tile, tile_count, cycles):
+    at = (band * tile_count + tile) * cycles
+    return pl.ds(pl.multiple_of(at, 8) if cycles % 8 == 0 else at, cycles)
+
+
+def modes_kernel(alm_hbm, table_hbm, *refs):
+    out_refs, (alm_ref, table_ref, lhs_ref, held_ref, turned_ref, alm_sem, sems) = refs[:-7], refs[-7:]
+    tile_count = len(out_refs)
+    parts = sems.shape[0]
+    slots = table_ref.shape[0] // parts
+    bands, rows = out_refs[0].shape[:2]
+    cycles = rows // C
+    alm_copy = pltpu.make_async_copy(alm_hbm, alm_ref, alm_sem)
+    alm_copy.start()
+    start_table(table_hbm, table_ref, sems)
+    alm_copy.wait()
+
+    def some_slots(part, carry):
+        wait_table(table_hbm, table_ref, sems, part)
+        for slot in range(slots):
+            at = part * slots + slot
+            for chan in range(C):
+                lhs_ref[slot, 2 * chan : 2 * chan + 2, :] = alm_ref[at, chan].astype(jnp.float32)
+            result = jnp.dot(
+                lhs_ref[slot].astype(jnp.bfloat16), table_ref[at], preferred_element_type=jnp.float32
+            )
+            for chan in range(C):
+                held_ref[chan, part, 2 * slot : 2 * slot + 2, :] = result[2 * chan : 2 * chan + 2]
+        return carry
+
+    lax.fori_loop(0, parts, some_slots, 0)
+    for chan in range(C):
+        turned_ref[chan] = held_ref[chan].reshape(turned_ref.shape[2], turned_ref.shape[1]).T
+    tile_at = lax.axis_index("tile")
+    for hop in range(tile_count):
+        for band in range(bands):
+            span = tile_rows(band, (tile_at + hop) % tile_count, tile_count, cycles)
+            block = jnp.concatenate([turned_ref[chan, span, :] for chan in range(C)], axis=0)
+            out_refs[hop][band] = block.astype(jnp.bfloat16)
+
+
+def make_modes(alm, legendre, band_count, tile_count):
+    slot_count, degrees, total = legendre.shape
+    slots = 8
+    parts = slot_count // slots
+    width = 2 * slot_count
+    cycles = total // (band_count * tile_count)
+    one = jax.ShapeDtypeStruct((band_count, C * cycles, width), jnp.bfloat16)
+    vmem = pl.BlockSpec(memory_space=pltpu.VMEM)
+    return pl.pallas_call(
+        modes_kernel,
+        in_specs=[pl.BlockSpec(memory_space=pl.ANY)] * 2,
+        out_specs=[vmem] * tile_count,
+        out_shape=[one] * tile_count,
+        scratch_shapes=[
+            pltpu.VMEM(alm.shape, jnp.bfloat16),
+            pltpu.VMEM(legendre.shape, jnp.bfloat16),
+            pltpu.VMEM((slots, 2 * C, degrees), jnp.float32),
+            pltpu.VMEM((C, parts, 2 * slots, total), jnp.float32),
+            pltpu.VMEM((C, total, width), jnp.float32),
+            pltpu.SemaphoreType.DMA,
+            pltpu.SemaphoreType.DMA((parts,)),
+        ],
+        cost_estimate=pl.CostEstimate(
+            flops=2 * slot_count * degrees * total * 2 * C,
+            bytes_accessed=slot_count * degrees * (total + 2 * C) * 2,
+            transcendentals=0,
+        ),
+        compiler_params=pltpu.CompilerParams(vmem_limit_bytes=61 * 1024 * 1024),
+    )(alm, legendre)
+
+
+def analysis_kernel(table_hbm, *refs):
+    spectra_refs = refs[:-6]
+    out_ref, table_ref, gathered_ref, rhs_ref, total_ref, sems = refs[-6:]
+    tile_count = len(spectra_refs)
+    parts = sems.shape[0]
+    slots = table_ref.shape[0] // parts
+    bands, cycles = spectra_refs[0].shape[:2]
+    count = bands * tile_count * cycles
+    start_table(table_hbm, table_ref, sems)
+    tile_at = lax.axis_index("tile")
+    for hop in range(tile_count):
+        for band in range(bands):
+            span = tile_rows(band, (tile_at + tile_count - hop) % tile_count, tile_count, cycles)
+            gathered_ref[span, :] = spectra_refs[hop][band].astype(jnp.float32)
+    lane = lax.broadcasted_iota(jnp.int32, gathered_ref.shape, 1) // 2
+    total_ref[...] = jnp.zeros_like(total_ref)
+
+    def some_slots(part, carry):
+        for slot in range(slots):
+            own = jnp.where(lane == part * slots + slot, gathered_ref[...], 0.0)
+            rhs_ref[slot * count : (slot + 1) * count, :] = own.astype(jnp.bfloat16)
+        wait_table(table_hbm, table_ref, sems, part)
+        lhs = jnp.concatenate([table_ref[part * slots + slot] for slot in range(slots)], axis=1)
+        total_ref[...] += jnp.dot(lhs, rhs_ref[...], preferred_element_type=jnp.float32)
+        return carry
+
+    lax.fori_loop(0, parts, some_slots, 0)
+    turned = total_ref[...].T
+    for slot in range(out_ref.shape[0]):
+        out_ref[slot] = turned[2 * slot : 2 * slot + 2]
+
+
+def analyse(legendre, spectra):
+    slot_count, degrees, total = legendre.shape
+    slots = 4
+    width = 2 * slot_count
+    vmem = pl.BlockSpec(memory_space=pltpu.VMEM)
+    return pl.pallas_call(
+        analysis_kernel,
+        in_specs=[pl.BlockSpec(memory_space=pl.ANY)] + [vmem] * len(spectra),
+        out_specs=vmem,
+        out_shape=jax.ShapeDtypeStruct((slot_count, 2, degrees), jnp.float32),
+        scratch_shapes=[
+            pltpu.VMEM(legendre.shape, jnp.bfloat16),
+            pltpu.VMEM((total, width), jnp.float32),
+            pltpu.VMEM((slots * total, width), jnp.bfloat16),
+            pltpu.VMEM((degrees, width), jnp.float32),
+            pltpu.SemaphoreType.DMA((slot_count // slots,)),
+        ],
+        cost_estimate=pl.CostEstimate(
+            flops=2 * slot_count * degrees * total * width,
+            bytes_accessed=slot_count * degrees * total * 2,
+            transcendentals=0,
+        ),
+        compiler_params=pltpu.CompilerParams(vmem_limit_bytes=24 * 1024 * 1024),
+    )(legendre, *spectra)
+
+
+def from_other_tiles(sends):
+    count = len(sends)
+    got = [sends[0]]
     for hop in range(1, count):
-        got.append(lax.ppermute(send(hop), "tile", [(at, (at + hop) % count) for at in range(count)]))
+        got.append(lax.ppermute(sends[hop], "tile", [(at, (at + hop) % count) for at in range(count)]))
     return got
 
 
@@ -239,12 +392,7 @@
     group_width = math.lcm(width, LANES)
     groups = depth // group_width
 
-    partial = jnp.einsum("scel,slr->scer", alm, legendre, preferred_element_type=jnp.float32)
-    partial = partial.astype(jnp.bfloat16).reshape(slot_count, C, 2, band_count, tile_count, cycles)
-    partial = partial.transpose(4, 3, 1, 5, 0, 2).reshape(tile_count, band_count, C * cycles, width)
-    got = from_other_tiles(
-        lambda hop: lax.dynamic_index_in_dim(partial, (tile_at + hop) % tile_count, 0, keepdims=False)
-    )
+    got = from_other_tiles(make_modes(alm, legendre, band_count, tile_count))
     total = got[0].astype(jnp.float32)
     for other in got[1:]:
         total = total + other.astype(jnp.float32)
@@ -267,15 +415,14 @@
         spectra = spectra.reshape(groups, cycles, group_width // width, width)
         spectra = spectra.transpose(0, 2, 1, 3).reshape(band_count, cycles, width)
     routed = lax.all_to_all(spectra, "band", split_axis=0, concat_axis=0, tiled=True)
-    cycle_spectra = in_tile_order(from_other_tiles(lambda hop: routed))
-    cycle_spectra = cycle_spectra.transpose(1, 0, 2, 3).reshape(band_count * tile_count * cycles, slot_count, 2)
-    ilc_alm = jnp.einsum("slr,rse->sel", legendre, cycle_spectra, preferred_element_type=jnp.float32)
+    ilc_alm = analyse(legendre, from_other_tiles([routed] * tile_count))
 
     own = vectors[:, :cycles].transpose(1, 2, 0).reshape(cycles, tile_count, NLON // tile_count)
     own = own.transpose(1, 0, 2)
-    ilc_map = in_tile_order(
-        from_other_tiles(lambda hop: lax.dynamic_index_in_dim(own, (tile_at + hop) % tile_count, 0, keepdims=False))
-    )
+    sends = [
+        lax.dynamic_index_in_dim(own, (tile_at + hop) % tile_count, 0, keepdims=False) for hop in range(tile_count)
+    ]
+    ilc_map = in_tile_order(from_other_tiles(sends))
     return (ilc_map.reshape(tile_count * cycles, NLON // tile_count), ilc_alm)
 
 

time: 98.2 us -> 99.5 us (1.013)
  Pallas kernels: 25.4 us -> 48.1 us
  matrix products: 20 us -> 0 us
  local copies, waits for them, and re-layouts: 18.1 us -> 14 us
  waiting for transfers between devices: 14.6 us -> 16.5 us
    pallas_call x0 -> x2, Pallas kernels: none -> 20.4 us  [the longest x1 10.7 us: make_modes(): pl.pallas_call(modes_kernel, in_specs=[pl.BlockSpec(memory_space=pl.ANY)]...]
    dot_general x2 -> x0, matrix products: 20 us -> none  [the longest x1 10.9 us: body(): jnp.einsum('slr,rse->sel', legendre, cycle_spectra, preferred_element_typ...]
    unnamed x5 -> x10, local copies, waits for them, and re-layouts: 1.92 us -> 12.4 us
    dynamic_slice x2 -> x0, local copies, waits for them, and re-layouts: 7.57 us -> none  [body(): lax.dynamic_index_in_dim(partial, (tile_at + hop) % tile_count, 0, keepdi...]
    transpose x2 -> x0, local copies, waits for them, and re-layouts: 4.97 us -> none  [the longest x1 4.06 us: body(): partial.transpose(4, 3, 1, 5, 0, 2)]
    ppermute x3, waiting for transfers between devices: 7.85 us -> 9.92 us  [from_other_tiles(): lax.ppermute(sends[hop], 'tile', [(at, (at + hop) % count) for at in rang...]
    pallas_call x1, Pallas kernels: 16 us -> 17.6 us  [run_ilc(): pl.pallas_call(ilc_kernel, in_specs=[vmem, vmem, pl.BlockSpec(memory_spac...]
    reshape x1 -> x0, local copies, waits for them, and re-layouts: 1.14 us -> none  [body(): cycle_spectra.transpose(1, 0, 2, 3)]
  transfers between devices with their start and end apart: 5 -> 5, of which waited for: 4 -> 3; matrix products, arithmetic and copies ran while one was open for 4% -> 2% of each run, Pallas kernels for 10% -> 10%
where the time goes in v2:
time: 99.5 us; the launch traced here: 99.1 us
  Pallas kernels  48.1 us (48%)
  starting transfers between devices  17.2 us (17%)
  waiting for transfers between devices  16.5 us (17%)
  local copies, waits for them, and re-layouts  14 us (14%)
  other arithmetic  2.51 us (3%)
    pallas_call x1, Pallas kernels, run_ilc(): pl.pallas_call(ilc_kernel, in_specs=[vmem, vmem, pl.BlockSpec(memory_spac...  17.6 us
    unnamed x10, local copies, waits for them, and re-layouts  12.4 us
    pallas_call x1, Pallas kernels, make_modes(): pl.pallas_call(modes_kernel, in_specs=[pl.BlockSpec(memory_space=pl.ANY)]...  10.7 us
    pallas_call x1, Pallas kernels, make_basis(): pl.pallas_call(basis_kernel, grid=(rows // block,), in_specs=[pl.BlockSpe...  10.1 us
    ppermute x3, waiting for transfers between devices, from_other_tiles(): lax.ppermute(sends[hop], 'tile', [(at, (at + hop) % count) for at in rang...  9.92 us
    pallas_call x1, Pallas kernels, analyse(): pl.pallas_call(analysis_kernel, in_specs=[pl.BlockSpec(memory_space=pl.AN...  9.67 us
    all_to_all x1, waiting for transfers between devices, body(): lax.all_to_all(spectra, 'band', split_axis=0, concat_axis=0, tiled=True)  6.58 us
    all_to_all x1, starting transfers between devices, body(): lax.all_to_all(total.astype(jnp.bfloat16), 'band', split_axis=0, concat_a...  6.13 us
  transfers between devices with their start and end apart: 5, of which 3 were waited for; matrix products, arithmetic and copies ran while one was open for 2% of the time, Pallas kernels for 10%

profile of v2, /device:TPU:0, one launch (start us, length us, event | category | flops | bytes accessed | tf_op | source)
XLA Modules:
  0.0 99.1 jit_solution(3790635070833739764)
XLA Ops:
  0.6 0.0 copy-start.3
  0.6 10.7 %shard_map.50 = (bf16[16,72,128]{2,1,0:T(8,128)(2,1)}, bf16[16,72,128]{2,1,0:T(8,128)(2,1)}) custom-call(bf16[64,9,2,512]{3,2,1,0:T(2,128)(2,1)} %alm_hbm.1, bf16[64,512,256]{2,1,0:T(8,128)(2,1)} %table_hbm.3), custom_call_target="tpu_custom_call" | custom-call | flops 301989888 | bytes 17956864 | tf_op jit(solution)/shard_map/pallas_call | solution.py:285
  11.4 3.0 %collective-permute-start = (bf16[16,72,128]{2,1,0:T(8,128)(2,1)}, bf16[16,72,128]{2,1,0:T(8,128)(2,1)S(1)}, u32[]{:S(2)}, u32[]{:S(2)}) collective-permute-start(bf16[16,72,128]{2,1,0:T(8,128)(2,1)} %get-tuple-element.7), channel_id=1, source_target_pairs={{0,1},{1,0},{2,3},{3,2},{4,5},{5,4},{6,7},{7,6},{8,9},{9,8},{10,11... | collective-permute-start | bytes 884744 | tf_op jit(solution)/shard_map/ppermute | solution.py:370
  14.4 7.2 %collective-permute-done = bf16[16,72,128]{2,1,0:T(8,128)(2,1)S(1)} collective-permute-done((bf16[16,72,128]{2,1,0:T(8,128)(2,1)}, bf16[16,72,128]{2,1,0:T(8,128)(2,1)S(1)}, u32[]{:S(2)}, u32[]{:S(2)}) %collective-permute-start) | collective-permute-done | bytes 294944 | tf_op jit(solution)/shard_map/ppermute | solution.py:370
  21.6 1.8 %add_convert_fusion = bf16[16,72,128]{2,1,0:T(8,128)(2,1)} fusion(bf16[16,72,128]{2,1,0:T(8,128)(2,1)S(1)} %collective-permute-done, bf16[16,72,128]{2,1,0:T(8,128)(2,1)} %get-tuple-element.6), kind=kLoop, calls=%fused_computation | loop fusion | flops 589824 | bytes 884736 | tf_op jit(solution)/shard_map/convert_element_type | solution.py:399
  23.4 6.1 %all-to-all-start = ((bf16[16,72,128]{2,1,0:T(8,128)(2,1)}), bf16[16,72,128]{2,1,0:T(8,128)(2,1)S(1)}, u32[]{:S(2)}, u32[]{:S(2)}) async-start(bf16[16,72,128]{2,1,0:T(8,128)(2,1)} %add_convert_fusion), calls=%async_computation | async-start | bytes 589824 | tf_op jit(solution)/shard_map/all_to_all | solution.py:399
  29.6 0.0 copy-done.3
  29.6 0.2 broadcast_in_dim.8
  29.8 0.2 convert_element_type.39.order_ref
  30.0 0.2 broadcast_in_dim.7
  30.2 0.3 reshape.82
  30.5 10.1 %shard_map.51.basis_hbm = bf16[8,2048,256]{2,1,0:T(8,128)(2,1)S(1)} custom-call(f32[2048,1]{1,0:T(8,128)S(1)} %convert_element_type.39.order_ref), custom_call_target="tpu_custom_call" | custom-call | flops 33554432 | bytes 8388608 | tf_op jit(solution)/shard_map/pallas_call | solution.py:71
  40.6 0.0 copy-start.1
  40.6 3.2 %copy-done.1 = bf16[8,2048,256]{2,1,0:T(8,128)(2,1)} copy-done((bf16[8,2048,256]{2,1,0:T(8,128)(2,1)}, bf16[8,2048,256]{2,1,0:T(8,128)(2,1)S(1)}, u32[]{:S(2)}) %copy-start.1) | copy-done | bytes 8388632
  43.9 0.0 all-to-all-done.modes_ref
  43.9 0.0 copy-start.2
  43.9 3.4 %copy-done.2 = bf16[8,2048,256]{2,1,0:T(8,128)(2,1)S(1)} copy-done((bf16[8,2048,256]{2,1,0:T(8,128)(2,1)S(1)}, bf16[8,2048,256]{2,1,0:T(8,128)(2,1)}, u32[]{:S(2)}) %copy-start.2) | copy-done | bytes 8388632
  47.3 17.6 %shard_map.52 = (f32[32,8,128]{2,1,0:T(8,128)S(1)}, bf16[16,8,128]{2,1,0:T(8,128)(2,1)}) custom-call(bf16[16,72,128]{2,1,0:T(8,128)(2,1)S(1)} %all-to-all-done.modes_ref, f32[1,2048]{1,0:T(1,128)S(1)} %fusion.2.odd_ref, bf16[8,2048,256]{2,1,0:T(8,128)(2,1)S(1)} %copy-done.2), custom_call_target="tpu_custom_call" | custom-call | flops 1342177280 | bytes 8388608 | tf_op jit(solution)/shard_map/pallas_call | solution.py:196
  64.9 0.2 copy.6
  65.1 0.3 reshape.83
  65.4 0.1 constant_dynamic-slice_fusion
  65.6 1.6 %collective-permute-start.1 = (f32[8,2048]{1,0:T(8,128)S(1)}, f32[8,2048]{1,0:T(8,128)S(1)}, u32[]{:S(2)}, u32[]{:S(2)}) collective-permute-start(f32[8,2048]{1,0:T(8,128)S(1)} %bitcast.12), channel_id=1, source_target_pairs={{0,1},{1,0},{2,3},{3,2},{4,5},{5,4},{6,7},{7,6},{8,9},{9,8},{10,11... | collective-permute-start | bytes 196616 | tf_op jit(solution)/shard_map/ppermute | solution.py:370
  67.2 6.0 %all-to-all-start.1 = ((bf16[16,8,128]{2,1,0:T(8,128)(2,1)}), bf16[16,8,128]{2,1,0:T(8,128)(2,1)S(1)}, u32[]{:S(2)}, u32[]{:S(2)}) async-start(bf16[16,8,128]{2,1,0:T(8,128)(2,1)} %get-tuple-element.9), calls=%async_computation.1 | async-start | bytes 65536 | tf_op jit(solution)/shard_map/all_to_all | solution.py:417
  73.2 6.6 %all-to-all-done.1.refs_0_ = bf16[16,8,128]{2,1,0:T(8,128)(2,1)S(1)} async-done(((bf16[16,8,128]{2,1,0:T(8,128)(2,1)}), bf16[16,8,128]{2,1,0:T(8,128)(2,1)S(1)}, u32[]{:S(2)}, u32[]{:S(2)}) %all-to-all-start.1) | async-done | bytes 32800 | tf_op jit(solution)/shard_map/all_to_all | solution.py:417
  79.8 0.5 collective-permute-start.2
  80.3 0.0 collective-permute-done.1
  80.3 0.7 maximum_bitcast_fusion
  81.0 2.7 %collective-permute-done.2.refs_1_ = bf16[16,8,128]{2,1,0:T(8,128)(2,1)S(1)} collective-permute-done((bf16[16,8,128]{2,1,0:T(8,128)(2,1)S(1)}, bf16[16,8,128]{2,1,0:T(8,128)(2,1)S(1)}, u32[]{:S(2)}, u32[]{:S(2)}) %collective-permute-start.2) | collective-permute-done | bytes 32800 | tf_op jit(solution)/shard_map/ppermute | solution.py:370
  83.7 0.0 copy-start
  83.7 5.8 %copy-done = bf16[64,512,256]{2,1,0:T(8,128)(2,1)S(1)} copy-done((bf16[64,512,256]{2,1,0:T(8,128)(2,1)S(1)}, bf16[64,512,256]{2,1,0:T(8,128)(2,1)}, u32[]{:S(2)}) %copy-start) | copy-done | bytes 16777240
  89.5 9.7 %shard_map.53 = f32[64,2,512]{2,1,0:T(2,128)} custom-call(bf16[64,512,256]{2,1,0:T(8,128)(2,1)S(1)} %copy-done, bf16[16,8,128]{2,1,0:T(8,128)(2,1)S(1)} %all-to-all-done.1.refs_0_, bf16[16,8,128]{2,1,0:T(8,128)(2,1)S(1)} %collective-permute-done.2.refs_1_), custom_call_target="tpu_custom_call" | custom-call | flops 2147483648 | bytes 16777216 | tf_op jit(solution)/shard_map/pallas_call | solution.py:345
  (5 shorter events, 0.1 us)
Async XLA Ops:
  0.6 28.9 %copy-start.3 = (s32[1024]{0:T(1024)S(1)}, s32[1024]{0:T(1024)}, u32[]{:S(2)}) copy-start(s32[1024]{0:T(1024)} %param.5) | copy-start | bytes 12292
  11.4 10.2 %collective-permute-start = (bf16[16,72,128]{2,1,0:T(8,128)(2,1)}, bf16[16,72,128]{2,1,0:T(8,128)(2,1)S(1)}, u32[]{:S(2)}, u32[]{:S(2)}) collective-permute-start(bf16[16,72,128]{2,1,0:T(8,128)(2,1)} %get-tuple-element.7), channel_id=1, source_target_pairs={{0,1},{1,0},{2,3},{3,2},{4,5},{5,4},{6,7},{7,6},{8,9},{9,8},{10,11... | collective-permute-start | bytes 884744 | tf_op jit(solution)/shard_map/ppermute | solution.py:370
  23.4 20.5 %all-to-all-start = ((bf16[16,72,128]{2,1,0:T(8,128)(2,1)}), bf16[16,72,128]{2,1,0:T(8,128)(2,1)S(1)}, u32[]{:S(2)}, u32[]{:S(2)}) async-start(bf16[16,72,128]{2,1,0:T(8,128)(2,1)} %add_convert_fusion), calls=%async_computation | async-start | bytes 589824 | tf_op jit(solution)/shard_map/all_to_all | solution.py:399
  40.6 3.2 %copy-start.1 = (bf16[8,2048,256]{2,1,0:T(8,128)(2,1)}, bf16[8,2048,256]{2,1,0:T(8,128)(2,1)S(1)}, u32[]{:S(2)}) copy-start(bf16[8,2048,256]{2,1,0:T(8,128)(2,1)S(1)} %shard_map.51.basis_hbm) | copy-start | bytes 25165828
  43.9 3.4 %copy-start.2 = (bf16[8,2048,256]{2,1,0:T(8,128)(2,1)S(1)}, bf16[8,2048,256]{2,1,0:T(8,128)(2,1)}, u32[]{:S(2)}) copy-start(bf16[8,2048,256]{2,1,0:T(8,128)(2,1)} %copy-done.1) | copy-start | bytes 25165828
  65.6 14.7 %collective-permute-start.1 = (f32[8,2048]{1,0:T(8,128)S(1)}, f32[8,2048]{1,0:T(8,128)S(1)}, u32[]{:S(2)}, u32[]{:S(2)}) collective-permute-start(f32[8,2048]{1,0:T(8,128)S(1)} %bitcast.12), channel_id=1, source_target_pairs={{0,1},{1,0},{2,3},{3,2},{4,5},{5,4},{6,7},{7,6},{8,9},{9,8},{10,11... | collective-permute-start | bytes 196616 | tf_op jit(solution)/shard_map/ppermute | solution.py:370
  67.2 12.6 %all-to-all-start.1 = ((bf16[16,8,128]{2,1,0:T(8,128)(2,1)}), bf16[16,8,128]{2,1,0:T(8,128)(2,1)S(1)}, u32[]{:S(2)}, u32[]{:S(2)}) async-start(bf16[16,8,128]{2,1,0:T(8,128)(2,1)} %get-tuple-element.9), calls=%async_computation.1 | async-start | bytes 65536 | tf_op jit(solution)/shard_map/all_to_all | solution.py:417
  79.8 3.9 %collective-permute-start.2 = (bf16[16,8,128]{2,1,0:T(8,128)(2,1)S(1)}, bf16[16,8,128]{2,1,0:T(8,128)(2,1)S(1)}, u32[]{:S(2)}, u32[]{:S(2)}) collective-permute-start(bf16[16,8,128]{2,1,0:T(8,128)(2,1)S(1)} %all-to-all-done.1.refs_0_), channel_id=1, source_target_pairs={{0,1},{1,0},{2,3},{3,2},{4,5},{5,4},{6,7},{7,6},{8,9},{9,8},{10,11... | collective-permute-start | bytes 98312 | tf_op jit(solution)/shard_map/ppermute | solution.py:370
  83.7 5.8 %copy-start = (bf16[64,512,256]{2,1,0:T(8,128)(2,1)S(1)}, bf16[64,512,256]{2,1,0:T(8,128)(2,1)}, u32[]{:S(2)}) copy-start(bf16[64,512,256]{2,1,0:T(8,128)(2,1)} %table_hbm.3) | copy-start | bytes 50331652

commit v3 on v2

v3 whole, which is shorter than its diff:
```python
import functools
import math

import jax
import jax.numpy as jnp
from jax import lax
from jax.experimental import pallas as pl
from jax.experimental.pallas import tpu as pltpu
from jax.sharding import PartitionSpec as P

C = 9
L = 1024
NLON = 4096
HALO = 32

RIDGE = 0.1
EPSILON = 1e-06

WINDOW = 2 * HALO + 1
LANES = NLON // HALO
HALF = LANES // 2
PAIRS = [(a_at, b_at) for a_at in range(C) for b_at in range(a_at, C)]
VMEM_LIMIT = 60 * 1024 * 1024


def round_up(value, multiple):
    return (value + multiple - 1) // multiple * multiple


def cos_turns(turns):
    nearest = (turns + 12582912.0) - 12582912.0
    quarter = 1.0 - 4.0 * jnp.abs(turns - nearest)
    square = quarter * quarter
    tail = square * (1.6044118478736e-04 - square * 3.598843235e-06)
    tail = square * (-4.68175413531868e-03 + tail)
    tail = square * (7.96926262461670e-02 + tail)
    tail = square * (-6.45964097506246e-01 + tail)
    return quarter * (1.57079632679490 + tail)


def basis_kernel(slots, order_ref, basis_ref):
    rows = 64
    begin = pl.program_id(0) * order_ref.shape[0]
    row = lax.broadcasted_iota(jnp.int32, (rows, LANES), 0)
    lane = lax.broadcasted_iota(jnp.int32, (rows, LANES), 1)
    cell = (HALO * (lane % HALF) + lane // HALF).astype(jnp.float32) / NLON
    scaling = 1.0 / math.sqrt(L)
    for first in range(0, order_ref.shape[0], rows):
        span = slice(first, first + rows)
        part = (row + (begin + first)) // slots % 2
        order = jnp.broadcast_to(order_ref[span, :], (rows, LANES))
        turns = order * cell + part.astype(jnp.float32) * 0.25
        step = order * (2.0 / NLON)
        before = cos_turns(turns) * scaling
        now = cos_turns(turns + step) * scaling
        twice = 2.0 * cos_turns(step)
        for column in range(HALO // 2):
            lanes = slice(column % 2 * LANES, (column % 2 + 1) * LANES)
            basis_ref[column // 2, span, lanes] = before.astype(jnp.bfloat16)
            if column < HALO // 2 - 1:
                before, now = now, twice * now - before


def make_basis(order_rows, slots):
    rows = order_rows.shape[0]
    block = 256
    chunks = HALO // 4
    return pl.pallas_call(
        functools.partial(basis_kernel, slots),
        grid=(rows // block,),
        in_specs=[pl.BlockSpec((block, 1), lambda at: (at, 0))],
        out_specs=pl.BlockSpec((chunks, block, 2 * LANES), lambda at: (0, at, 0)),
        out_shape=jax.ShapeDtypeStruct((chunks, rows, 2 * LANES), jnp.bfloat16),
        cost_estimate=pl.CostEstimate(
            flops=rows * chunks * 2 * LANES * 8, bytes_accessed=rows * chunks * 4 * LANES, transcendentals=0
        ),
        compiler_params=pltpu.CompilerParams(vmem_limit_bytes=VMEM_LIMIT),
    )(order_rows)


def reciprocal(value):
    guess = pl.reciprocal(value, approx=True)
    return guess * (2.0 - value * guess)


def combine(entries, maps):
    entries = dict(entries)
    trace = entries[0, 0]
    for at in range(1, C):
        trace = trace + entries[at, at]
    ridge = RIDGE * (trace * (1.0 / C) + WINDOW * EPSILON)
    for at in range(C):
        entries[at, at] = entries[at, at] + ridge
    ones = [None] * C
    maps = list(maps)
    top = bottom = None
    for at in range(C):
        inverse = reciprocal(entries[at, at])
        scaled = inverse if at == 0 else inverse * ones[at]
        term = scaled * maps[at]
        top = term if top is None else top + term
        term = scaled if at == 0 else scaled * ones[at]
        bottom = term if bottom is None else bottom + term
        for row in range(at + 1, C):
            ratio = entries[at, row] * inverse
            ones[row] = 1.0 - ratio if at == 0 else ones[row] - ratio * ones[at]
            maps[row] = maps[row] - ratio * maps[at]
            for col in range(row, C):
                entries[row, col] = entries[row, col] - ratio * entries[at, col]
    return top * reciprocal(bottom)


def ilc_kernel(modes_ref, odd_ref, basis_hbm, ilc_ref, spectra_ref, basis_ref, lhs_ref, maps_ref, sums_ref, low_ref, found_ref, sems):
    groups, shares, rows, width = modes_ref.shape
    chunks = basis_ref.shape[0]
    cycles = rows // C
    second = round_up(rows, 16)
    for chunk in range(chunks):
        pltpu.make_async_copy(basis_hbm.at[chunk], basis_ref.at[chunk], sems.at[chunk]).start()
    for group in range(groups):
        span = slice(group * width, (group + 1) * width)
        odd = odd_ref[:, span]
        values = modes_ref[group, 0].astype(jnp.float32)
        for share in range(1, shares):
            values = values + modes_ref[group, share].astype(jnp.float32)
        lhs_ref[0:rows, span] = (values * (1.0 - odd)).astype(jnp.bfloat16)
        lhs_ref[second : second + rows, span] = (values * odd).astype(jnp.bfloat16)
    low_half = lax.broadcasted_iota(jnp.int32, (cycles, LANES), 1) < HALF
    for chunk in range(chunks):
        pltpu.make_async_copy(basis_hbm.at[chunk], basis_ref.at[chunk], sems.at[chunk]).wait()
        result = jnp.dot(lhs_ref[...], basis_ref[chunk], preferred_element_type=jnp.float32)
        for part in range(2):
            at = 4 * chunk + 2 * part
            even_part = result[0:rows, part * LANES : (part + 1) * LANES]
            odd_part = result[second : second + rows, part * LANES : (part + 1) * LANES]
            near = even_part + odd_part
            far = even_part - odd_part
            wide = jnp.concatenate([low_half] * C, axis=0)
            maps_ref[at] = jnp.where(wide, near, pltpu.roll(far, HALF, 1))
            maps_ref[at + 1] = jnp.where(wide, pltpu.roll(near, HALF, 1), far)

    def maps_at(at):
        return [maps_ref[at, chan * cycles : (chan + 1) * cycles, :] for chan in range(C)]

    for first in range(0, len(PAIRS), 15):
        some = PAIRS[first : first + 15]

        def add(at, totals, some=some):
            values = maps_at(at)
            return tuple(total + values[a_at] * values[b_at] for total, (a_at, b_at) in zip(totals, some))

        zero = jnp.zeros((cycles, LANES), jnp.float32)
        totals = lax.fori_loop(0, HALO, add, (zero,) * len(some))
        for pair, total in enumerate(totals):
            sums_ref[first + pair] = total + pltpu.roll(total, 1, 1)

    def smooth(at, leaves):
        ahead = [pltpu.roll(value, LANES - 1, 1) for value in maps_at(at)]
        behind = [pltpu.roll(value, 1, 1) for value in maps_at(jnp.maximum(at - 1, 0))]
        behind = [value * leaves for value in behind]
        entries = {}
        for pair, (a_at, b_at) in enumerate(PAIRS):
            total = sums_ref[pair] + (ahead[a_at] * ahead[b_at] - behind[a_at] * behind[b_at])
            sums_ref[pair] = total
            entries[a_at, b_at] = total
        return entries

    def two_vectors(at, first):
        found = []
        for part in range(2):
            leaves = jnp.where(at == 0, 0.0, 1.0) if first and part == 0 else 1.0
            value = combine(smooth(at + part, leaves), maps_at(at + part))
            ilc_ref[at + part] = value
            found.append(value)
        near = jnp.where(low_half, found[0], pltpu.roll(found[1], HALF, 1))
        far = jnp.where(low_half, pltpu.roll(found[0], HALF, 1), found[1])
        return jnp.concatenate([near, far], axis=0).astype(jnp.bfloat16)

    def spectra_of(chunk):
        return lax.dot_general(
            low_ref[chunk], basis_ref[chunk], (((1,), (1,)), ((), ())), preferred_element_type=jnp.float32
        )

    found_ref[...] = jnp.zeros_like(found_ref)
    low_ref[...] = jnp.zeros_like(low_ref)

    def solve_chunk(chunk, carry):
        found_ref[...] += spectra_of(jnp.maximum(chunk - 1, 0))
        low_ref[chunk, :, 0:LANES] = two_vectors(4 * chunk, True)
        low_ref[chunk, :, LANES : 2 * LANES] = two_vectors(4 * chunk + 2, False)
        return carry

    lax.fori_loop(0, chunks, solve_chunk, 0)
    found_ref[...] += spectra_of(chunks - 1)
    for group in range(groups):
        span = slice(group * width, (group + 1) * width)
        sign = 1.0 - 2.0 * odd_ref[:, span]
        value = (found_ref[0:cycles, span] + sign * found_ref[cycles:, span]).astype(jnp.bfloat16)
        for share in range(shares):
            spectra_ref[group, share] = value


def run_ilc(modes, odd, basis):
    groups, shares, rows, width = modes.shape
    chunks, depth, columns = basis.shape
    cycles = rows // C
    vmem = pl.BlockSpec(memory_space=pltpu.VMEM)
    return pl.pallas_call(
        ilc_kernel,
        in_specs=[vmem, vmem, pl.BlockSpec(memory_space=pl.ANY)],
        out_specs=[vmem, vmem],
        out_shape=[
            jax.ShapeDtypeStruct((HALO, cycles, LANES), jnp.float32),
            jax.ShapeDtypeStruct((groups, shares, cycles, width), jnp.bfloat16),
        ],
        scratch_shapes=[
            pltpu.VMEM((chunks, depth, columns), jnp.bfloat16),
            pltpu.VMEM((2 * round_up(rows, 16), depth), jnp.bfloat16),
            pltpu.VMEM((HALO, rows, LANES), jnp.float32),
            pltpu.VMEM((len(PAIRS), cycles, LANES), jnp.float32),
            pltpu.VMEM((chunks, 2 * cycles, columns), jnp.bfloat16),
            pltpu.VMEM((2 * cycles, depth), jnp.float32),
            pltpu.SemaphoreType.DMA((chunks,)),
        ],
        cost_estimate=pl.CostEstimate(
            flops=2 * chunks * depth * columns * (2 * rows + 2 * cycles),
            bytes_accessed=chunks * depth * columns * 2,
            transcendentals=0,
        ),
        compiler_params=pltpu.CompilerParams(vmem_limit_bytes=VMEM_LIMIT),
    )(modes, odd, basis)


def start_table(table_hbm, table_ref, sems):
    parts = sems.shape[0]
    slots = table_ref.shape[0] // parts
    for part in range(parts):
        span = slice(part * slots, (part + 1) * slots)
        pltpu.make_async_copy(table_hbm.at[span], table_ref.at[span], sems.at[part]).start()


def wait_table(table_hbm, table_ref, sems, part):
    slots = table_ref.shape[0] // sems.shape[0]
    span = pl.ds(part * slots, slots)
    pltpu.make_async_copy(table_hbm.at[span], table_ref.at[span], sems.at[part]).wait()


def modes_kernel(alm_hbm, table_hbm, out_ref, alm_ref, table_ref, lhs_ref, held_ref, turned_ref, alm_sem, sems):
    parts = sems.shape[0]
    total_slots = table_ref.shape[0]
    slots = total_slots // parts
    targets, rows = out_ref.shape[:2]
    cycles = rows // C
    height = held_ref.shape[1] // total_slots
    alm_copy = pltpu.make_async_copy(alm_hbm, alm_ref, alm_sem)
    alm_copy.start()
    start_table(table_hbm, table_ref, sems)
    alm_copy.wait()

    def some_slots(part, carry):
        wait_table(table_hbm, table_ref, sems, part)
        for slot in range(slots):
            at = part * slots + slot
            for chan in range(C):
                lhs_ref[slot, 2 * chan : 2 * chan + 2, :] = alm_ref[at, chan].astype(jnp.float32)
            result = jnp.dot(
                lhs_ref[slot].astype(jnp.bfloat16), table_ref[at], preferred_element_type=jnp.float32
            )
            for lanes in range(held_ref.shape[0]):
                piece = result[:, lanes * LANES : (lanes + 1) * LANES]
                held_ref[lanes, pl.ds(pl.multiple_of(at * height, 8), height), :] = piece
        return carry

    lax.fori_loop(0, parts, some_slots, 0)
    for chan in range(C):
        for lanes in range(held_ref.shape[0]):
            both = [held_ref[lanes, pl.ds(2 * chan + part, total_slots, stride=height), :] for part in range(2)]
            turned_ref[chan, lanes * LANES : (lanes + 1) * LANES, :] = jnp.concatenate(both, axis=0).T
    for target in range(targets):
        span = slice(target * cycles, (target + 1) * cycles)
        block = jnp.concatenate([turned_ref[chan, span, :] for chan in range(C)], axis=0)
        out_ref[target] = block.astype(jnp.bfloat16)


def make_modes(alm, legendre, targets):
    slot_count, degrees, total = legendre.shape
    slots = 8
    parts = slot_count // slots
    width = 2 * slot_count
    height = round_up(2 * C, 8)
    return pl.pallas_call(
        modes_kernel,
        in_specs=[pl.BlockSpec(memory_space=pl.ANY)] * 2,
        out_specs=pl.BlockSpec(memory_space=pltpu.VMEM),
        out_shape=jax.ShapeDtypeStruct((targets, C * (total // targets), width), jnp.bfloat16),
        scratch_shapes=[
            pltpu.VMEM(alm.shape, jnp.bfloat16),
            pltpu.VMEM(legendre.shape, jnp.bfloat16),
            pltpu.VMEM((slots, height, degrees), jnp.float32),
            pltpu.VMEM((total // LANES, slot_count * height, LANES), jnp.float32),
            pltpu.VMEM((C, total, width), jnp.float32),
            pltpu.SemaphoreType.DMA,
            pltpu.SemaphoreType.DMA((parts,)),
        ],
        cost_estimate=pl.CostEstimate(
            flops=2 * slot_count * degrees * total * 2 * C,
            bytes_accessed=slot_count * degrees * (total + 2 * C) * 2,
            transcendentals=0,
        ),
        compiler_params=pltpu.CompilerParams(vmem_limit_bytes=62 * 1024 * 1024),
    )(alm, legendre)


def analysis_kernel(table_hbm, spectra_ref, out_ref, table_ref, total_ref, turned_ref, sems):
    parts = sems.shape[0]
    total_slots = table_ref.shape[0]
    slots = total_slots // parts
    start_table(table_hbm, table_ref, sems)
    spectra = spectra_ref[...]
    lane = lax.broadcasted_iota(jnp.int32, (1, spectra.shape[1]), 1) % total_slots
    total_ref[...] = jnp.zeros_like(total_ref)

    def some_slots(part, carry):
        masks = [(lane == part * slots + slot).astype(jnp.float32).astype(jnp.bfloat16) for slot in range(slots)]
        rhs = jnp.concatenate([spectra_ref[...] * mask for mask in masks], axis=0)
        wait_table(table_hbm, table_ref, sems, part)
        lhs = jnp.concatenate([table_ref[part * slots + slot] for slot in range(slots)], axis=1)
        total_ref[...] += jnp.dot(lhs, rhs, preferred_element_type=jnp.float32)
        return carry

    lax.fori_loop(0, parts, some_slots, 0)
    for lanes in range(turned_ref.shape[0]):
        span = slice(lanes * LANES, (lanes + 1) * LANES)
        turned_ref[lanes] = total_ref[span, :].T
        for slot in range(total_slots):
            out_ref[slot, :, span] = turned_ref[lanes, pl.ds(slot, 2, stride=total_slots), :]


def analyse(legendre, spectra):
    slot_count, degrees, total = legendre.shape
    slots = 8
    width = 2 * slot_count
    vmem = pl.BlockSpec(memory_space=pltpu.VMEM)
    return pl.pallas_call(
        analysis_kernel,
        in_specs=[pl.BlockSpec(memory_space=pl.ANY), vmem],
        out_specs=vmem,
        out_shape=jax.ShapeDtypeStruct((slot_count, 2, degrees), jnp.float32),
        scratch_shapes=[
            pltpu.VMEM(legendre.shape, jnp.bfloat16),
            pltpu.VMEM((degrees, width), jnp.float32),
            pltpu.VMEM((degrees // LANES, width, LANES), jnp.float32),
            pltpu.SemaphoreType.DMA((slot_count // slots,)),
        ],
        cost_estimate=pl.CostEstimate(
            flops=2 * slot_count * degrees * total * width,
            bytes_accessed=slot_count * degrees * total * 2,
            transcendentals=0,
        ),
        compiler_params=pltpu.CompilerParams(vmem_limit_bytes=62 * 1024 * 1024),
    )(legendre, spectra)


def from_other_tiles(sends):
    count = len(sends)
    got = [sends[0]]
    for hop in range(1, count):
        got.append(lax.ppermute(sends[hop], "tile", [(at, (at + hop) % count) for at in range(count)]))
    return got


def in_tile_order(got):
    count = len(got)
    tile_at = lax.axis_index("tile")
    stacked = jnp.stack(got)
    return jnp.stack(
        [lax.dynamic_index_in_dim(stacked, (tile_at - at) % count, 0, keepdims=False) for at in range(count)]
    )


def body(alm, legendre, order_of_slot):
    tile_count = lax.axis_size("tile")
    band_count = lax.axis_size("band")
    tile_at = lax.axis_index("tile")
    slot_count = alm.shape[0]
    targets = band_count * tile_count
    cycles = legendre.shape[2] // targets
    padded = round_up(cycles, 8)
    depth = 2 * L
    width = 2 * slot_count
    group_width = math.lcm(width, LANES)
    groups = depth // group_width
    plain = group_width == width and padded == cycles
    axes = ("band", "tile")

    partial = make_modes(alm, legendre, targets)
    partial = lax.all_to_all(partial, axes, split_axis=0, concat_axis=0, tiled=True)
    modes = partial.reshape(band_count, tile_count, C * cycles, width)
    if not plain:
        modes = jnp.sum(modes.astype(jnp.float32), axis=1).astype(jnp.bfloat16)
        modes = modes.reshape(groups, group_width // width, C, cycles, width)
        modes = modes.transpose(0, 2, 3, 1, 4).reshape(groups, C, cycles, group_width)
        modes = jnp.pad(modes, ((0, 0), (0, 0), (0, padded - cycles), (0, 0)))
        modes = modes.reshape(groups, 1, C * padded, group_width)

    order_rows = jnp.broadcast_to(order_of_slot.reshape(band_count, 1, slot_count), (band_count, 2, slot_count))
    order_rows = order_rows.reshape(depth)
    basis = make_basis(order_rows.astype(jnp.float32)[:, None], slot_count)
    odd = (order_rows % 2).astype(jnp.float32)[None, :]
    vectors, spectra = run_ilc(modes, odd, basis)

    if not plain:
        spectra = spectra[:, 0, :cycles].reshape(groups, cycles, group_width // width, width)
        spectra = spectra.transpose(0, 2, 1, 3).reshape(band_count, 1, cycles, width)
        spectra = jnp.broadcast_to(spectra, (band_count, tile_count, cycles, width))
    spectra = spectra.reshape(targets, cycles, width)
    routed = lax.all_to_all(spectra, axes, split_axis=0, concat_axis=0, tiled=True)
    vectors, routed = lax.optimization_barrier((vectors, routed))
    ilc_alm = analyse(legendre, routed.reshape(targets * cycles, width))

    own = vectors[:, :cycles].transpose(1, 2, 0).reshape(cycles, tile_count, NLON // tile_count)
    own = own.transpose(1, 0, 2)
    sends = [
        lax.dynamic_index_in_dim(own, (tile_at + hop) % tile_count, 0, keepdims=False) for hop in range(tile_count)
    ]
    ilc_map = in_tile_order(from_other_tiles(sends))
    return (ilc_map.reshape(tile_count * cycles, NLON // tile_count), ilc_alm)


def solution(mesh):
    placed = (P("band", None, None, "tile"), P("band", "tile", None), P())
    return jax.shard_map(
        body,
        mesh=mesh,
        in_specs=placed,
        out_specs=(P("band", "tile"), P("band", None, "tile")),
        check_vma=False,
    )
```

time: 99.5 us -> 73.9 us (0.74)
  local copies, waits for them, and re-layouts: 14 us -> 4.73 us
  starting transfers between devices: 17.2 us -> 11.4 us
  Pallas kernels: 48.1 us -> 42.8 us
  waiting for transfers between devices: 16.5 us -> 12.4 us
  other arithmetic: 2.51 us -> 1.34 us
    unnamed x10 -> x8, local copies, waits for them, and re-layouts: 12.4 us -> 0.91 us
    ppermute x3 -> x1, waiting for transfers between devices: 9.92 us -> 0.01 us  [from_other_tiles(): lax.ppermute(sends[hop], 'tile', [(at, (at + hop) % count) for at in rang...]
    all_to_all x2, waiting for transfers between devices: 6.58 us -> 12.4 us  [the longest x1 7.56 us: body(): lax.all_to_all(spectra, axes, split_axis=0, concat_axis=0, tiled=True)]
    ppermute x3 -> x1, starting transfers between devices: 5.15 us -> 0.49 us  [from_other_tiles(): lax.ppermute(sends[hop], 'tile', [(at, (at + hop) % count) for at in rang...]
    pallas_call x1, Pallas kernels: 17.6 us -> 14 us  [run_ilc(): pl.pallas_call(ilc_kernel, in_specs=[vmem, vmem, pl.BlockSpec(memory_spac...]
    convert_element_type x1, local copies, waits for them, and re-layouts: 0.21 us -> 2.09 us  [body(): basis = make_basis(order_rows.astype(jnp.float32)[:, None], slot_count)]
    convert_element_type x2 -> x1, other arithmetic: 1.78 us -> 0.01 us  [body(): basis = make_basis(order_rows.astype(jnp.float32)[:, None], slot_count)]
    pallas_call x1, Pallas kernels: 10.1 us -> 8.69 us  [make_basis(): pl.pallas_call(functools.partial(basis_kernel, slots), grid=(rows // bloc...]
  transfers between devices with their start and end apart: 5 -> 3, of which waited for: 3 -> 2; matrix products, arithmetic and copies ran while one was open for 2% -> 4% of each run, Pallas kernels for 10% -> 25%
where the time goes in v3:
time: 73.9 us; the launch traced here: 73.4 us
  Pallas kernels  42.8 us (58%)
  waiting for transfers between devices  12.4 us (17%)
  starting transfers between devices  11.4 us (15%)
  local copies, waits for them, and re-layouts  4.73 us (6%)
  other arithmetic  1.34 us (2%)
  between operations  0.79 us (1%)
    pallas_call x1, Pallas kernels, run_ilc(): pl.pallas_call(ilc_kernel, in_specs=[vmem, vmem, pl.BlockSpec(memory_spac...  14 us
    pallas_call x1, Pallas kernels, make_modes(): pl.pallas_call(modes_kernel, in_specs=[pl.BlockSpec(memory_space=pl.ANY)]...  10.5 us
    pallas_call x1, Pallas kernels, analyse(): pl.pallas_call(analysis_kernel, in_specs=[pl.BlockSpec(memory_space=pl.AN...  9.63 us
    pallas_call x1, Pallas kernels, make_basis(): pl.pallas_call(functools.partial(basis_kernel, slots), grid=(rows // bloc...  8.69 us
    all_to_all x1, waiting for transfers between devices, body(): lax.all_to_all(spectra, axes, split_axis=0, concat_axis=0, tiled=True)  7.56 us
    all_to_all x1, starting transfers between devices, body(): lax.all_to_all(partial, axes, split_axis=0, concat_axis=0, tiled=True)  7.3 us
    all_to_all x1, waiting for transfers between devices, body(): lax.all_to_all(partial, axes, split_axis=0, concat_axis=0, tiled=True)  4.8 us
    all_to_all x1, starting transfers between devices, body(): lax.all_to_all(spectra, axes, split_axis=0, concat_axis=0, tiled=True)  3.62 us
  transfers between devices with their start and end apart: 3, of which 2 were waited for; matrix products, arithmetic and copies ran while one was open for 4% of the time, Pallas kernels for 25%

profile of v3, /device:TPU:0, one launch (start us, length us, event | category | flops | bytes accessed | tf_op | source)
XLA Modules:
  0.0 73.4 jit_solution(11447987300599337384)
XLA Ops:
  0.6 0.0 copy-start.2
  0.6 10.5 %shard_map.50 = bf16[32,72,128]{2,1,0:T(8,128)(2,1)} custom-call(bf16[64,9,2,512]{3,2,1,0:T(2,128)(2,1)} %alm_hbm.1, bf16[64,512,256]{2,1,0:T(8,128)(2,1)} %table_hbm.3), custom_call_target="tpu_custom_call" | custom-call | flops 301989888 | bytes 17956864 | tf_op jit(solution)/shard_map/pallas_call | solution.py:291
  11.1 7.3 %all-to-all-start = ((bf16[32,72,128]{2,1,0:T(8,128)(2,1)}), bf16[32,72,128]{2,1,0:T(8,128)(2,1)S(1)}, u32[]{:S(2)}, u32[]{:S(2)}) async-start(bf16[32,72,128]{2,1,0:T(8,128)(2,1)} %shard_map.50), calls=%async_computation | async-start | bytes 1179648 | tf_op jit(solution)/shard_map/all_to_all | solution.py:397
  18.4 0.0 copy-done.2
  18.4 0.1 broadcast_in_dim.11
  18.5 2.1 %convert_element_type.27.order_ref = f32[2048,1]{1,0:T(8,128)} reshape(f32[16,2,64]{2,1,0:T(2,128)S(1)} %broadcast_in_dim.13) | data formatting | bytes 16384 | tf_op jit(solution)/shard_map/convert_element_type | solution.py:408
  20.6 0.1 reshape.94
  20.7 8.7 %shard_map.51.basis_hbm = bf16[8,2048,256]{2,1,0:T(8,128)(2,1)} custom-call(f32[2048,1]{1,0:T(8,128)} %convert_element_type.27.order_ref), custom_call_target="tpu_custom_call" | custom-call | flops 33554432 | bytes 8388608 | tf_op jit(solution)/shard_map/pallas_call | solution.py:68
  29.4 0.6 fusion.2.odd_ref
  30.0 4.8 %all-to-all-done = bf16[32,72,128]{2,1,0:T(8,128)(2,1)S(1)} async-done(((bf16[32,72,128]{2,1,0:T(8,128)(2,1)}), bf16[32,72,128]{2,1,0:T(8,128)(2,1)S(1)}, u32[]{:S(2)}, u32[]{:S(2)}) %all-to-all-start) | async-done | bytes 589856 | tf_op jit(solution)/shard_map/all_to_all | solution.py:397
  34.8 0.0 copy-start
  34.8 0.8 %copy-done = bf16[32,72,128]{2,1,0:T(8,128)(2,1)} copy-done((bf16[32,72,128]{2,1,0:T(8,128)(2,1)}, bf16[32,72,128]{2,1,0:T(8,128)(2,1)S(1)}, u32[]{:S(2)}) %copy-start) | copy-done | bytes 589848
  35.7 14.0 %shard_map.52 = (f32[32,8,128]{2,1,0:T(8,128)}, bf16[16,2,8,128]{3,2,1,0:T(8,128)(2,1)}) custom-call(bf16[16,2,72,128]{3,2,1,0:T(8,128)(2,1)} %bitcast.13, f32[1,2048]{1,0:T(1,128)} %fusion.2.odd_ref, bf16[8,2048,256]{2,1,0:T(8,128)(2,1)} %shard_map.51.basis_hbm), custom_call_target="tpu_custom_call" | custom-call | flops 1342177280 | bytes 8388608 | tf_op jit(solution)/shard_map/pallas_call | solution.py:208
  49.7 3.6 %all-to-all-start.1 = ((bf16[32,8,128]{2,1,0:T(8,128)(2,1)}), bf16[32,8,128]{2,1,0:T(8,128)(2,1)S(1)}, u32[]{:S(2)}, u32[]{:S(2)}) async-start(bf16[32,8,128]{2,1,0:T(8,128)(2,1)} %bitcast.17), calls=%async_computation.1 | async-start | bytes 131072 | tf_op jit(solution)/shard_map/all_to_all | solution.py:417
  53.4 7.6 %all-to-all-done.1 = bf16[32,8,128]{2,1,0:T(8,128)(2,1)S(1)} async-done(((bf16[32,8,128]{2,1,0:T(8,128)(2,1)}), bf16[32,8,128]{2,1,0:T(8,128)(2,1)S(1)}, u32[]{:S(2)}, u32[]{:S(2)}) %all-to-all-start.1) | async-done | bytes 65568 | tf_op jit(solution)/shard_map/all_to_all | solution.py:417
  60.9 0.0 copy-start.1
  61.0 1.1 %copy.6 = f32[8,128,32]{2,1,0:T(8,128)S(1)} copy(f32[8,128,32]{1,0,2:T(8,128)} %bitcast.16) | data formatting | bytes 262144 | tf_op jit(solution)/shard_map/transpose | solution.py:421
  62.1 0.3 reshape.96
  62.4 0.1 constant_dynamic-slice_fusion
  62.6 0.5 collective-permute-start
  63.0 0.0 copy-done.1
  63.0 9.6 %shard_map.53 = f32[64,2,512]{2,1,0:T(2,128)} custom-call(bf16[64,512,256]{2,1,0:T(8,128)(2,1)} %table_hbm.3, bf16[256,128]{1,0:T(8,128)(2,1)} %bitcast.14), custom_call_target="tpu_custom_call" | custom-call | flops 2147483648 | bytes 16777216 | tf_op jit(solution)/shard_map/pallas_call | solution.py:344
  72.7 0.0 collective-permute-done
  72.8 0.7 maximum_bitcast_fusion
  (6 shorter events, 0.1 us)
Async XLA Ops:
  0.6 17.8 %copy-start.2 = (s32[1024]{0:T(1024)S(1)}, s32[1024]{0:T(1024)}, u32[]{:S(2)}) copy-start(s32[1024]{0:T(1024)} %param.5) | copy-start | bytes 12292
  11.1 23.7 %all-to-all-start = ((bf16[32,72,128]{2,1,0:T(8,128)(2,1)}), bf16[32,72,128]{2,1,0:T(8,128)(2,1)S(1)}, u32[]{:S(2)}, u32[]{:S(2)}) async-start(bf16[32,72,128]{2,1,0:T(8,128)(2,1)} %shard_map.50), calls=%async_computation | async-start | bytes 1179648 | tf_op jit(solution)/shard_map/all_to_all | solution.py:397
  34.8 0.8 %copy-start = (bf16[32,72,128]{2,1,0:T(8,128)(2,1)}, bf16[32,72,128]{2,1,0:T(8,128)(2,1)S(1)}, u32[]{:S(2)}) copy-start(bf16[32,72,128]{2,1,0:T(8,128)(2,1)S(1)} %all-to-all-done) | copy-start | bytes 1769476
  49.7 11.2 %all-to-all-start.1 = ((bf16[32,8,128]{2,1,0:T(8,128)(2,1)}), bf16[32,8,128]{2,1,0:T(8,128)(2,1)S(1)}, u32[]{:S(2)}, u32[]{:S(2)}) async-start(bf16[32,8,128]{2,1,0:T(8,128)(2,1)} %bitcast.17), calls=%async_computation.1 | async-start | bytes 131072 | tf_op jit(solution)/shard_map/all_to_all | solution.py:417
  60.9 2.1 %copy-start.1 = (bf16[32,8,128]{2,1,0:T(8,128)(2,1)}, bf16[32,8,128]{2,1,0:T(8,128)(2,1)S(1)}, u32[]{:S(2)}) copy-start(bf16[32,8,128]{2,1,0:T(8,128)(2,1)S(1)} %all-to-all-done.1) | copy-start | bytes 196612
  62.6 10.2 %collective-permute-start = (f32[8,2048]{1,0:T(8,128)S(1)}, f32[8,2048]{1,0:T(8,128)S(1)}, u32[]{:S(2)}, u32[]{:S(2)}) collective-permute-start(f32[8,2048]{1,0:T(8,128)S(1)} %bitcast.18), channel_id=1, source_target_pairs={{0,1},{1,0},{2,3},{3,2},{4,5},{5,4},{6,7},{7,6},{8,9},{9,8},{10,11... | collective-permute-start | bytes 196616 | tf_op jit(solution)/shard_map/ppermute | solution.py:368

commit v4 on v3

--- a/solution.py
+++ b/solution.py
@@ -20,7 +20,8 @@
 LANES = NLON // HALO
 HALF = LANES // 2
 PAIRS = [(a_at, b_at) for a_at in range(C) for b_at in range(a_at, C)]
-VMEM_LIMIT = 60 * 1024 * 1024
+VMEM_LIMIT = 56 * 1024 * 1024
+IN_FLIGHT = 4
 
 
 def round_up(value, multiple):
@@ -78,35 +79,62 @@
     )(order_rows)
 
 
+def part_copy(source, target, sems, part):
+    count = source.shape[0] // sems.shape[0]
+    span = pl.ds(part * count, count)
+    return pltpu.make_async_copy(source.at[span], target.at[span], sems.at[part])
+
+
+def start_some(source, target, sems):
+    for part in range(min(IN_FLIGHT, sems.shape[0])):
+        part_copy(source, target, sems, part).start()
+
+
+def next_part(source, target, sems, part):
+    part_copy(source, target, sems, part).wait()
+
+    @pl.when(part + IN_FLIGHT < sems.shape[0])
+    def _():
+        part_copy(source, target, sems, part + IN_FLIGHT).start()
+
+
 def reciprocal(value):
     guess = pl.reciprocal(value, approx=True)
     return guess * (2.0 - value * guess)
 
 
-def combine(entries, maps):
-    entries = dict(entries)
-    trace = entries[0, 0]
+def combine(entry, map_of):
+    diagonal = [entry(at, at) for at in range(C)]
+    trace = diagonal[0]
     for at in range(1, C):
-        trace = trace + entries[at, at]
+        trace = trace + diagonal[at]
     ridge = RIDGE * (trace * (1.0 / C) + WINDOW * EPSILON)
-    for at in range(C):
-        entries[at, at] = entries[at, at] + ridge
-    ones = [None] * C
-    maps = list(maps)
+    upper, inverses, ones, maps = {}, [], [], []
     top = bottom = None
-    for at in range(C):
-        inverse = reciprocal(entries[at, at])
-        scaled = inverse if at == 0 else inverse * ones[at]
-        term = scaled * maps[at]
+    for row in range(C):
+        ratios = [upper[at, row] * inverses[at] for at in range(row)]
+        pivot = diagonal[row] + ridge
+        for at in range(row):
+            pivot = pivot - ratios[at] * upper[at, row]
+        inverse = reciprocal(pivot)
+        for col in range(row + 1, C):
+            value = entry(row, col)
+            for at in range(row):
+                value = value - ratios[at] * upper[at, col]
+            upper[row, col] = value
+        one = 1.0
+        own = map_of(row)
+        for at in range(row):
+            one = one - (ratios[at] if at == 0 else ratios[at] * ones[at])
+            own = own - ratios[at] * maps[at]
+        scaled = inverse if row == 0 else inverse * one
+        term = scaled * own
         top = term if top is None else top + term
-        term = scaled if at == 0 else scaled * ones[at]
+        term = scaled if row == 0 else scaled * one
         bottom = term if bottom is None else bottom + term
-        for row in range(at + 1, C):
-            ratio = entries[at, row] * inverse
-            ones[row] = 1.0 - ratio if at == 0 else ones[row] - ratio * ones[at]
-            maps[row] = maps[row] - ratio * maps[at]
-            for col in range(row, C):
-                entries[row, col] = entries[row, col] - ratio * entries[at, col]
+        inverses.append(inverse)
+        ones.append(one)
+        maps.append(own)
     return top * reciprocal(bottom)
 
 
@@ -115,8 +143,7 @@
     chunks = basis_ref.shape[0]
     cycles = rows // C
     second = round_up(rows, 16)
-    for chunk in range(chunks):
-        pltpu.make_async_copy(basis_hbm.at[chunk], basis_ref.at[chunk], sems.at[chunk]).start()
+    start_some(basis_hbm, basis_ref, sems)
     for group in range(groups):
         span = slice(group * width, (group + 1) * width)
         odd = odd_ref[:, span]
@@ -126,52 +153,59 @@
         lhs_ref[0:rows, span] = (values * (1.0 - odd)).astype(jnp.bfloat16)
         lhs_ref[second : second + rows, span] = (values * odd).astype(jnp.bfloat16)
     low_half = lax.broadcasted_iota(jnp.int32, (cycles, LANES), 1) < HALF
-    for chunk in range(chunks):
-        pltpu.make_async_copy(basis_hbm.at[chunk], basis_ref.at[chunk], sems.at[chunk]).wait()
+    sums_ref[...] = jnp.zeros_like(sums_ref)
+
+    def map_of(at, chan):
+        return maps_ref[at, chan * cycles : (chan + 1) * cycles, :]
+
+    def maps_of_chunk(chunk):
+        next_part(basis_hbm, basis_ref, sems, chunk)
         result = jnp.dot(lhs_ref[...], basis_ref[chunk], preferred_element_type=jnp.float32)
         for part in range(2):
             at = 4 * chunk + 2 * part
-            even_part = result[0:rows, part * LANES : (part + 1) * LANES]
-            odd_part = result[second : second + rows, part * LANES : (part + 1) * LANES]
-            near = even_part + odd_part
-            far = even_part - odd_part
-            wide = jnp.concatenate([low_half] * C, axis=0)
-            maps_ref[at] = jnp.where(wide, near, pltpu.roll(far, HALF, 1))
-            maps_ref[at + 1] = jnp.where(wide, pltpu.roll(near, HALF, 1), far)
-
-    def maps_at(at):
-        return [maps_ref[at, chan * cycles : (chan + 1) * cycles, :] for chan in range(C)]
-
-    for first in range(0, len(PAIRS), 15):
-        some = PAIRS[first : first + 15]
-
-        def add(at, totals, some=some):
-            values = maps_at(at)
-            return tuple(total + values[a_at] * values[b_at] for total, (a_at, b_at) in zip(totals, some))
-
-        zero = jnp.zeros((cycles, LANES), jnp.float32)
-        totals = lax.fori_loop(0, HALO, add, (zero,) * len(some))
-        for pair, total in enumerate(totals):
-            sums_ref[first + pair] = total + pltpu.roll(total, 1, 1)
-
-    def smooth(at, leaves):
-        ahead = [pltpu.roll(value, LANES - 1, 1) for value in maps_at(at)]
-        behind = [pltpu.roll(value, 1, 1) for value in maps_at(jnp.maximum(at - 1, 0))]
-        behind = [value * leaves for value in behind]
-        entries = {}
+            for chan in range(C):
+                span = slice(chan * cycles, (chan + 1) * cycles)
+                even_part = result[span, part * LANES : (part + 1) * LANES]
+                odd_part = result[second + chan * cycles : second + (chan + 1) * cycles, part * LANES : (part + 1) * LANES]
+                near = even_part + odd_part
+                far = even_part - odd_part
+                maps_ref[at, span, :] = jnp.where(low_half, near, pltpu.roll(far, HALF, 1))
+                maps_ref[at + 1, span, :] = jnp.where(low_half, pltpu.roll(near, HALF, 1), far)
+
+    def add_totals(chunk):
         for pair, (a_at, b_at) in enumerate(PAIRS):
+            total = sums_ref[pair]
+            for part in range(4):
+                total = total + map_of(4 * chunk + part, a_at) * map_of(4 * chunk + part, b_at)
+            sums_ref[pair] = total
+
+    maps_of_chunk(0)
+    for chunk in range(1, chunks):
+        maps_of_chunk(chunk)
+        add_totals(chunk - 1)
+    add_totals(chunks - 1)
+    for pair in range(len(PAIRS)):
+        total = sums_ref[pair]
+        sums_ref[pair] = total + pltpu.roll(total, 1, 1)
+
+    def solve(at, leaves):
+        ahead = [pltpu.roll(map_of(at, chan), LANES - 1, 1) for chan in range(C)]
+        before = jnp.maximum(at - 1, 0)
+        behind = [pltpu.roll(map_of(before, chan), 1, 1) * leaves for chan in range(C)]
+
+        def entry(a_at, b_at):
+            pair = PAIRS.index((a_at, b_at))
             total = sums_ref[pair] + (ahead[a_at] * ahead[b_at] - behind[a_at] * behind[b_at])
             sums_ref[pair] = total
-            entries[a_at, b_at] = total
-        return entries
+            return total
+
+        value = combine(entry, lambda chan: map_of(at, chan))
+        ilc_ref[at] = value
+        return value
 
     def two_vectors(at, first):
-        found = []
-        for part in range(2):
-            leaves = jnp.where(at == 0, 0.0, 1.0) if first and part == 0 else 1.0
-            value = combine(smooth(at + part, leaves), maps_at(at + part))
-            ilc_ref[at + part] = value
-            found.append(value)
+        leaves = jnp.where(at == 0, 0.0, 1.0) if first else 1.0
+        found = [solve(at, leaves), solve(at + 1, 1.0)]
         near = jnp.where(low_half, found[0], pltpu.roll(found[1], HALF, 1))
         far = jnp.where(low_half, pltpu.roll(found[0], HALF, 1), found[1])
         return jnp.concatenate([near, far], axis=0).astype(jnp.bfloat16)
@@ -231,21 +265,7 @@
     )(modes, odd, basis)
 
 
-def start_table(table_hbm, table_ref, sems):
-    parts = sems.shape[0]
-    slots = table_ref.shape[0] // parts
-    for part in range(parts):
-        span = slice(part * slots, (part + 1) * slots)
-        pltpu.make_async_copy(table_hbm.at[span], table_ref.at[span], sems.at[part]).start()
-
-
-def wait_table(table_hbm, table_ref, sems, part):
-    slots = table_ref.shape[0] // sems.shape[0]
-    span = pl.ds(part * slots, slots)
-    pltpu.make_async_copy(table_hbm.at[span], table_ref.at[span], sems.at[part]).wait()
-
-
-def modes_kernel(alm_hbm, table_hbm, out_ref, alm_ref, table_ref, lhs_ref, held_ref, turned_ref, alm_sem, sems):
+def modes_kernel(alm_hbm, table_hbm, out_ref, alm_ref, table_ref, lhs_ref, low_ref, held_ref, turned_ref, alm_sem, sems):
     parts = sems.shape[0]
     total_slots = table_ref.shape[0]
     slots = total_slots // parts
@@ -254,20 +274,27 @@
     height = held_ref.shape[1] // total_slots
     alm_copy = pltpu.make_async_copy(alm_hbm, alm_ref, alm_sem)
     alm_copy.start()
-    start_table(table_hbm, table_ref, sems)
+    start_some(table_hbm, table_ref, sems)
+    lhs_ref[...] = jnp.zeros_like(lhs_ref)
     alm_copy.wait()
 
-    def some_slots(part, carry):
-        wait_table(table_hbm, table_ref, sems, part)
+    def stack_rows(part, carry):
         for slot in range(slots):
             at = part * slots + slot
             for chan in range(C):
                 lhs_ref[slot, 2 * chan : 2 * chan + 2, :] = alm_ref[at, chan].astype(jnp.float32)
-            result = jnp.dot(
-                lhs_ref[slot].astype(jnp.bfloat16), table_ref[at], preferred_element_type=jnp.float32
-            )
+            low_ref[at] = lhs_ref[slot].astype(jnp.bfloat16)
+        return carry
+
+    lax.fori_loop(0, parts, stack_rows, 0)
+
+    def some_slots(part, carry):
+        next_part(table_hbm, table_ref, sems, part)
+        for slot in range(slots):
+            at = part * slots + slot
+            result = jnp.dot(low_ref[at], table_ref[at], preferred_element_type=jnp.float32)
             for lanes in range(held_ref.shape[0]):
-                piece = result[:, lanes * LANES : (lanes + 1) * LANES]
+                piece = result[0:height, lanes * LANES : (lanes + 1) * LANES]
                 held_ref[lanes, pl.ds(pl.multiple_of(at * height, 8), height), :] = piece
         return carry
 
@@ -284,7 +311,7 @@
 
 def make_modes(alm, legendre, targets):
     slot_count, degrees, total = legendre.shape
-    slots = 8
+    slots = 4
     parts = slot_count // slots
     width = 2 * slot_count
     height = round_up(2 * C, 8)
@@ -296,7 +323,8 @@
         scratch_shapes=[
             pltpu.VMEM(alm.shape, jnp.bfloat16),
             pltpu.VMEM(legendre.shape, jnp.bfloat16),
-            pltpu.VMEM((slots, height, degrees), jnp.float32),
+            pltpu.VMEM((slots, round_up(2 * C, 16), degrees), jnp.float32),
+            pltpu.VMEM((slot_count, round_up(2 * C, 16), degrees), jnp.bfloat16),
             pltpu.VMEM((total // LANES, slot_count * height, LANES), jnp.float32),
             pltpu.VMEM((C, total, width), jnp.float32),
             pltpu.SemaphoreType.DMA,
@@ -315,7 +343,7 @@
     parts = sems.shape[0]
     total_slots = table_ref.shape[0]
     slots = total_slots // parts
-    start_table(table_hbm, table_ref, sems)
+    start_some(table_hbm, table_ref, sems)
     spectra = spectra_ref[...]
     lane = lax.broadcasted_iota(jnp.int32, (1, spectra.shape[1]), 1) % total_slots
     total_ref[...] = jnp.zeros_like(total_ref)
@@ -323,7 +351,7 @@
     def some_slots(part, carry):
         masks = [(lane == part * slots + slot).astype(jnp.float32).astype(jnp.bfloat16) for slot in range(slots)]
         rhs = jnp.concatenate([spectra_ref[...] * mask for mask in masks], axis=0)
-        wait_table(table_hbm, table_ref, sems, part)
+        next_part(table_hbm, table_ref, sems, part)
         lhs = jnp.concatenate([table_ref[part * slots + slot] for slot in range(slots)], axis=1)
         total_ref[...] += jnp.dot(lhs, rhs, preferred_element_type=jnp.float32)
         return carry
@@ -338,7 +366,7 @@
 
 def analyse(legendre, spectra):
     slot_count, degrees, total = legendre.shape
-    slots = 8
+    slots = 4
     width = 2 * slot_count
     vmem = pl.BlockSpec(memory_space=pltpu.VMEM)
     return pl.pallas_call(

time: 73.9 us -> 73.4 us (level)
    pallas_call x1, Pallas kernels: 14 us -> 12.8 us  [run_ilc(): pl.pallas_call(ilc_kernel, in_specs=[vmem, vmem, pl.BlockSpec(memory_spac...]
    pallas_call x1, Pallas kernels: 9.63 us -> 10.7 us  [analyse(): pl.pallas_call(analysis_kernel, in_specs=[pl.BlockSpec(memory_space=pl.AN...]
  transfers between devices with their start and end apart: 3 -> 3, of which waited for: 2 -> 2; matrix products, arithmetic and copies ran while one was open for 4% -> 4% of each run, Pallas kernels for 25% -> 27%
where the time goes in v4:
time: 73.4 us; the launch traced here: 72.9 us
  Pallas kernels  42.2 us (57%)
  waiting for transfers between devices  12.4 us (17%)
  starting transfers between devices  11.4 us (16%)
  local copies, waits for them, and re-layouts  4.73 us (6%)
  other arithmetic  1.34 us (2%)
  between operations  0.79 us (1%)
    pallas_call x1, Pallas kernels, run_ilc(): pl.pallas_call(ilc_kernel, in_specs=[vmem, vmem, pl.BlockSpec(memory_spac...  12.8 us
    pallas_call x1, Pallas kernels, analyse(): pl.pallas_call(analysis_kernel, in_specs=[pl.BlockSpec(memory_space=pl.AN...  10.7 us
    pallas_call x1, Pallas kernels, make_modes(): pl.pallas_call(modes_kernel, in_specs=[pl.BlockSpec(memory_space=pl.ANY)]...  10 us
    pallas_call x1, Pallas kernels, make_basis(): pl.pallas_call(functools.partial(basis_kernel, slots), grid=(rows // bloc...  8.69 us
    all_to_all x1, waiting for transfers between devices, body(): lax.all_to_all(spectra, axes, split_axis=0, concat_axis=0, tiled=True)  7.56 us
    all_to_all x1, starting transfers between devices, body(): lax.all_to_all(partial, axes, split_axis=0, concat_axis=0, tiled=True)  7.3 us
    all_to_all x1, waiting for transfers between devices, body(): lax.all_to_all(partial, axes, split_axis=0, concat_axis=0, tiled=True)  4.8 us
    all_to_all x1, starting transfers between devices, body(): lax.all_to_all(spectra, axes, split_axis=0, concat_axis=0, tiled=True)  3.63 us
  transfers between devices with their start and end apart: 3, of which 2 were waited for; matrix products, arithmetic and copies ran while one was open for 4% of the time, Pallas kernels for 27%

profile of v4, /device:TPU:0, one launch (start us, length us, event | category | flops | bytes accessed | tf_op | source)
XLA Modules:
  0.0 72.9 jit_solution(11143825509498324549)
XLA Ops:
  0.6 0.0 copy-start.2
  0.6 10.0 %shard_map.50 = bf16[32,72,128]{2,1,0:T(8,128)(2,1)} custom-call(bf16[64,9,2,512]{3,2,1,0:T(2,128)(2,1)} %alm_hbm.1, bf16[64,512,256]{2,1,0:T(8,128)(2,1)} %table_hbm.3), custom_call_target="tpu_custom_call" | custom-call | flops 301989888 | bytes 17956864 | tf_op jit(solution)/shard_map/pallas_call | solution.py:318
  10.6 7.3 %all-to-all-start = ((bf16[32,72,128]{2,1,0:T(8,128)(2,1)}), bf16[32,72,128]{2,1,0:T(8,128)(2,1)S(1)}, u32[]{:S(2)}, u32[]{:S(2)}) async-start(bf16[32,72,128]{2,1,0:T(8,128)(2,1)} %shard_map.50), calls=%async_computation | async-start | bytes 1179648 | tf_op jit(solution)/shard_map/all_to_all | solution.py:425
  18.0 0.0 copy-done.2
  18.0 0.1 broadcast_in_dim.11
  18.1 2.1 %convert_element_type.27.order_ref = f32[2048,1]{1,0:T(8,128)} reshape(f32[16,2,64]{2,1,0:T(2,128)S(1)} %broadcast_in_dim.13) | data formatting | bytes 16384 | tf_op jit(solution)/shard_map/convert_element_type | solution.py:436
  20.2 0.1 reshape.94
  20.2 8.7 %shard_map.51.basis_hbm = bf16[8,2048,256]{2,1,0:T(8,128)(2,1)} custom-call(f32[2048,1]{1,0:T(8,128)} %convert_element_type.27.order_ref), custom_call_target="tpu_custom_call" | custom-call | flops 33554432 | bytes 8388608 | tf_op jit(solution)/shard_map/pallas_call | solution.py:69
  28.9 0.6 fusion.2.odd_ref
  29.6 4.8 %all-to-all-done = bf16[32,72,128]{2,1,0:T(8,128)(2,1)S(1)} async-done(((bf16[32,72,128]{2,1,0:T(8,128)(2,1)}), bf16[32,72,128]{2,1,0:T(8,128)(2,1)S(1)}, u32[]{:S(2)}, u32[]{:S(2)}) %all-to-all-start) | async-done | bytes 589856 | tf_op jit(solution)/shard_map/all_to_all | solution.py:425
  34.4 0.0 copy-start
  34.4 0.8 %copy-done = bf16[32,72,128]{2,1,0:T(8,128)(2,1)} copy-done((bf16[32,72,128]{2,1,0:T(8,128)(2,1)}, bf16[32,72,128]{2,1,0:T(8,128)(2,1)S(1)}, u32[]{:S(2)}) %copy-start) | copy-done | bytes 589848
  35.2 12.8 %shard_map.52 = (f32[32,8,128]{2,1,0:T(8,128)}, bf16[16,2,8,128]{3,2,1,0:T(8,128)(2,1)}) custom-call(bf16[16,2,72,128]{3,2,1,0:T(8,128)(2,1)} %bitcast.13, f32[1,2048]{1,0:T(1,128)} %fusion.2.odd_ref, bf16[8,2048,256]{2,1,0:T(8,128)(2,1)} %shard_map.51.basis_hbm), custom_call_target="tpu_custom_call" | custom-call | flops 1342177280 | bytes 8388608 | tf_op jit(solution)/shard_map/pallas_call | solution.py:242
  48.0 3.6 %all-to-all-start.1 = ((bf16[32,8,128]{2,1,0:T(8,128)(2,1)}), bf16[32,8,128]{2,1,0:T(8,128)(2,1)S(1)}, u32[]{:S(2)}, u32[]{:S(2)}) async-start(bf16[32,8,128]{2,1,0:T(8,128)(2,1)} %bitcast.17), calls=%async_computation.1 | async-start | bytes 131072 | tf_op jit(solution)/shard_map/all_to_all | solution.py:445
  51.7 7.6 %all-to-all-done.1 = bf16[32,8,128]{2,1,0:T(8,128)(2,1)S(1)} async-done(((bf16[32,8,128]{2,1,0:T(8,128)(2,1)}), bf16[32,8,128]{2,1,0:T(8,128)(2,1)S(1)}, u32[]{:S(2)}, u32[]{:S(2)}) %all-to-all-start.1) | async-done | bytes 65568 | tf_op jit(solution)/shard_map/all_to_all | solution.py:445
  59.3 0.0 copy-start.1
  59.3 1.1 %copy.6 = f32[8,128,32]{2,1,0:T(8,128)S(1)} copy(f32[8,128,32]{1,0,2:T(8,128)} %bitcast.16) | data formatting | bytes 262144 | tf_op jit(solution)/shard_map/transpose | solution.py:449
  60.4 0.3 reshape.96
  60.7 0.1 constant_dynamic-slice_fusion
  60.9 0.5 collective-permute-start
  61.4 0.0 copy-done.1
  61.4 10.7 %shard_map.53 = f32[64,2,512]{2,1,0:T(2,128)} custom-call(bf16[64,512,256]{2,1,0:T(8,128)(2,1)} %table_hbm.3, bf16[256,128]{1,0:T(8,128)(2,1)} %bitcast.14), custom_call_target="tpu_custom_call" | custom-call | flops 2147483648 | bytes 16777216 | tf_op jit(solution)/shard_map/pallas_call | solution.py:372
  72.2 0.0 collective-permute-done
  72.2 0.7 maximum_bitcast_fusion
  (6 shorter events, 0.1 us)
Async XLA Ops:
  0.6 17.3 %copy-start.2 = (s32[1024]{0:T(1024)S(1)}, s32[1024]{0:T(1024)}, u32[]{:S(2)}) copy-start(s32[1024]{0:T(1024)} %param.5) | copy-start | bytes 12292
  10.6 23.7 %all-to-all-start = ((bf16[32,72,128]{2,1,0:T(8,128)(2,1)}), bf16[32,72,128]{2,1,0:T(8,128)(2,1)S(1)}, u32[]{:S(2)}, u32[]{:S(2)}) async-start(bf16[32,72,128]{2,1,0:T(8,128)(2,1)} %shard_map.50), calls=%async_computation | async-start | bytes 1179648 | tf_op jit(solution)/shard_map/all_to_all | solution.py:425
  34.4 0.8 %copy-start = (bf16[32,72,128]{2,1,0:T(8,128)(2,1)}, bf16[32,72,128]{2,1,0:T(8,128)(2,1)S(1)}, u32[]{:S(2)}) copy-start(bf16[32,72,128]{2,1,0:T(8,128)(2,1)S(1)} %all-to-all-done) | copy-start | bytes 1769476
  48.0 11.2 %all-to-all-start.1 = ((bf16[32,8,128]{2,1,0:T(8,128)(2,1)}), bf16[32,8,128]{2,1,0:T(8,128)(2,1)S(1)}, u32[]{:S(2)}, u32[]{:S(2)}) async-start(bf16[32,8,128]{2,1,0:T(8,128)(2,1)} %bitcast.17), calls=%async_computation.1 | async-start | bytes 131072 | tf_op jit(solution)/shard_map/all_to_all | solution.py:445
  59.3 2.1 %copy-start.1 = (bf16[32,8,128]{2,1,0:T(8,128)(2,1)}, bf16[32,8,128]{2,1,0:T(8,128)(2,1)S(1)}, u32[]{:S(2)}) copy-start(bf16[32,8,128]{2,1,0:T(8,128)(2,1)S(1)} %all-to-all-done.1) | copy-start | bytes 196612
  60.9 11.3 %collective-permute-start = (f32[8,2048]{1,0:T(8,128)S(1)}, f32[8,2048]{1,0:T(8,128)S(1)}, u32[]{:S(2)}, u32[]{:S(2)}) collective-permute-start(f32[8,2048]{1,0:T(8,128)S(1)} %bitcast.18), channel_id=1, source_target_pairs={{0,1},{1,0},{2,3},{3,2},{4,5},{5,4},{6,7},{7,6},{8,9},{9,8},{10,11... | collective-permute-start | bytes 196616 | tf_op jit(solution)/shard_map/ppermute | solution.py:396

commit v5 on v4

--- a/solution.py
+++ b/solution.py
@@ -20,7 +20,8 @@
 LANES = NLON // HALO
 HALF = LANES // 2
 PAIRS = [(a_at, b_at) for a_at in range(C) for b_at in range(a_at, C)]
-VMEM_LIMIT = 56 * 1024 * 1024
+VMEM_LIMIT = 48 * 1024 * 1024
+CHUNK = 8
 IN_FLIGHT = 4
 
 
@@ -56,8 +57,8 @@
         now = cos_turns(turns + step) * scaling
         twice = 2.0 * cos_turns(step)
         for column in range(HALO // 2):
-            lanes = slice(column % 2 * LANES, (column % 2 + 1) * LANES)
-            basis_ref[column // 2, span, lanes] = before.astype(jnp.bfloat16)
+            at = column % (CHUNK // 2) * LANES
+            basis_ref[column // (CHUNK // 2), span, at : at + LANES] = before.astype(jnp.bfloat16)
             if column < HALO // 2 - 1:
                 before, now = now, twice * now - before
 
@@ -65,15 +66,16 @@
 def make_basis(order_rows, slots):
     rows = order_rows.shape[0]
     block = 256
-    chunks = HALO // 4
+    chunks = HALO // CHUNK
+    columns = CHUNK // 2 * LANES
     return pl.pallas_call(
         functools.partial(basis_kernel, slots),
         grid=(rows // block,),
         in_specs=[pl.BlockSpec((block, 1), lambda at: (at, 0))],
-        out_specs=pl.BlockSpec((chunks, block, 2 * LANES), lambda at: (0, at, 0)),
-        out_shape=jax.ShapeDtypeStruct((chunks, rows, 2 * LANES), jnp.bfloat16),
+        out_specs=pl.BlockSpec((chunks, block, columns), lambda at: (0, at, 0)),
+        out_shape=jax.ShapeDtypeStruct((chunks, rows, columns), jnp.bfloat16),
         cost_estimate=pl.CostEstimate(
-            flops=rows * chunks * 2 * LANES * 8, bytes_accessed=rows * chunks * 4 * LANES, transcendentals=0
+            flops=rows * chunks * columns * 8, bytes_accessed=rows * chunks * columns * 2, transcendentals=0
         ),
         compiler_params=pltpu.CompilerParams(vmem_limit_bytes=VMEM_LIMIT),
     )(order_rows)
@@ -161,8 +163,8 @@
     def maps_of_chunk(chunk):
         next_part(basis_hbm, basis_ref, sems, chunk)
         result = jnp.dot(lhs_ref[...], basis_ref[chunk], preferred_element_type=jnp.float32)
-        for part in range(2):
-            at = 4 * chunk + 2 * part
+        for part in range(CHUNK // 2):
+            at = CHUNK * chunk + 2 * part
             for chan in range(C):
                 span = slice(chan * cycles, (chan + 1) * cycles)
                 even_part = result[span, part * LANES : (part + 1) * LANES]
@@ -175,8 +177,8 @@
     def add_totals(chunk):
         for pair, (a_at, b_at) in enumerate(PAIRS):
             total = sums_ref[pair]
-            for part in range(4):
-                total = total + map_of(4 * chunk + part, a_at) * map_of(4 * chunk + part, b_at)
+            for at in range(CHUNK * chunk, CHUNK * (chunk + 1)):
+                total = total + map_of(at, a_at) * map_of(at, b_at)
             sums_ref[pair] = total
 
     maps_of_chunk(0)
@@ -220,8 +222,8 @@
 
     def solve_chunk(chunk, carry):
         found_ref[...] += spectra_of(jnp.maximum(chunk - 1, 0))
-        low_ref[chunk, :, 0:LANES] = two_vectors(4 * chunk, True)
-        low_ref[chunk, :, LANES : 2 * LANES] = two_vectors(4 * chunk + 2, False)
+        for part in range(CHUNK // 2):
+            low_ref[chunk, :, part * LANES : (part + 1) * LANES] = two_vectors(CHUNK * chunk + 2 * part, part == 0)
         return carry
 
     lax.fori_loop(0, chunks, solve_chunk, 0)
@@ -272,6 +274,7 @@
     targets, rows = out_ref.shape[:2]
     cycles = rows // C
     height = held_ref.shape[1] // total_slots
+    total = table_ref.shape[2]
     alm_copy = pltpu.make_async_copy(alm_hbm, alm_ref, alm_sem)
     alm_copy.start()
     start_some(table_hbm, table_ref, sems)
@@ -280,22 +283,27 @@
 
     def stack_rows(part, carry):
         for slot in range(slots):
-            at = part * slots + slot
+            first = slot % 2 * height
             for chan in range(C):
-                lhs_ref[slot, 2 * chan : 2 * chan + 2, :] = alm_ref[at, chan].astype(jnp.float32)
-            low_ref[at] = lhs_ref[slot].astype(jnp.bfloat16)
+                span = slice(first + 2 * chan, first + 2 * chan + 2)
+                lhs_ref[slot // 2, span, :] = alm_ref[part * slots + slot, chan].astype(jnp.float32)
+        for pair in range(slots // 2):
+            low_ref[part * (slots // 2) + pair] = lhs_ref[pair].astype(jnp.bfloat16)
         return carry
 
     lax.fori_loop(0, parts, stack_rows, 0)
 
     def some_slots(part, carry):
         next_part(table_hbm, table_ref, sems, part)
-        for slot in range(slots):
-            at = part * slots + slot
-            result = jnp.dot(low_ref[at], table_ref[at], preferred_element_type=jnp.float32)
-            for lanes in range(held_ref.shape[0]):
-                piece = result[0:height, lanes * LANES : (lanes + 1) * LANES]
-                held_ref[lanes, pl.ds(pl.multiple_of(at * height, 8), height), :] = piece
+        for pair in range(slots // 2):
+            at = part * slots + 2 * pair
+            both = jnp.concatenate([table_ref[at], table_ref[at + 1]], axis=1)
+            result = jnp.dot(low_ref[part * (slots // 2) + pair], both, preferred_element_type=jnp.float32)
+            for slot in range(2):
+                rows = pl.ds(pl.multiple_of((at + slot) * height, 8), height)
+                own = result[slot * height : (slot + 1) * height, slot * total : (slot + 1) * total]
+                for lanes in range(held_ref.shape[0]):
+                    held_ref[lanes, rows, :] = own[:, lanes * LANES : (lanes + 1) * LANES]
         return carry
 
     lax.fori_loop(0, parts, some_slots, 0)
@@ -323,8 +331,8 @@
         scratch_shapes=[
             pltpu.VMEM(alm.shape, jnp.bfloat16),
             pltpu.VMEM(legendre.shape, jnp.bfloat16),
-            pltpu.VMEM((slots, round_up(2 * C, 16), degrees), jnp.float32),
-            pltpu.VMEM((slot_count, round_up(2 * C, 16), degrees), jnp.bfloat16),
+            pltpu.VMEM((slots // 2, 2 * height, degrees), jnp.float32),
+            pltpu.VMEM((slot_count // 2, 2 * height, degrees), jnp.bfloat16),
             pltpu.VMEM((total // LANES, slot_count * height, LANES), jnp.float32),
             pltpu.VMEM((C, total, width), jnp.float32),
             pltpu.SemaphoreType.DMA,
@@ -339,34 +347,32 @@
     )(alm, legendre)
 
 
-def analysis_kernel(table_hbm, spectra_ref, out_ref, table_ref, total_ref, turned_ref, sems):
+def analysis_kernel(table_hbm, spectra_ref, out_ref, table_ref, turned_ref, sems):
     parts = sems.shape[0]
-    total_slots = table_ref.shape[0]
+    total_slots, degrees, total = table_ref.shape
     slots = total_slots // parts
     start_some(table_hbm, table_ref, sems)
-    spectra = spectra_ref[...]
-    lane = lax.broadcasted_iota(jnp.int32, (1, spectra.shape[1]), 1) % total_slots
-    total_ref[...] = jnp.zeros_like(total_ref)
+    turned_ref[...] = spectra_ref[...].astype(jnp.float32).T
 
     def some_slots(part, carry):
-        masks = [(lane == part * slots + slot).astype(jnp.float32).astype(jnp.bfloat16) for slot in range(slots)]
-        rhs = jnp.concatenate([spectra_ref[...] * mask for mask in masks], axis=0)
+        first = pl.multiple_of(part * slots, slots)
+        rows = [turned_ref[pl.ds(first + share * total_slots, slots), :] for share in range(2)]
+        lhs = jnp.concatenate(rows, axis=0).astype(jnp.bfloat16)
         next_part(table_hbm, table_ref, sems, part)
-        lhs = jnp.concatenate([table_ref[part * slots + slot] for slot in range(slots)], axis=1)
-        total_ref[...] += jnp.dot(lhs, rhs, preferred_element_type=jnp.float32)
+        table = table_ref[pl.ds(first, slots)].reshape(slots * degrees, total)
+        result = lax.dot_general(lhs, table, (((1,), (1,)), ((), ())), preferred_element_type=jnp.float32)
+        for slot in range(slots):
+            span = slice(slot * degrees, (slot + 1) * degrees)
+            out_ref[part * slots + slot, 0:1, :] = result[slot : slot + 1, span]
+            out_ref[part * slots + slot, 1:2, :] = result[slots + slot : slots + slot + 1, span]
         return carry
 
     lax.fori_loop(0, parts, some_slots, 0)
-    for lanes in range(turned_ref.shape[0]):
-        span = slice(lanes * LANES, (lanes + 1) * LANES)
-        turned_ref[lanes] = total_ref[span, :].T
-        for slot in range(total_slots):
-            out_ref[slot, :, span] = turned_ref[lanes, pl.ds(slot, 2, stride=total_slots), :]
 
 
 def analyse(legendre, spectra):
     slot_count, degrees, total = legendre.shape
-    slots = 4
+    slots = 8
     width = 2 * slot_count
     vmem = pl.BlockSpec(memory_space=pltpu.VMEM)
     return pl.pallas_call(
@@ -376,16 +382,15 @@
         out_shape=jax.ShapeDtypeStruct((slot_count, 2, degrees), jnp.float32),
         scratch_shapes=[
             pltpu.VMEM(legendre.shape, jnp.bfloat16),
-            pltpu.VMEM((degrees, width), jnp.float32),
-            pltpu.VMEM((degrees // LANES, width, LANES), jnp.float32),
+            pltpu.VMEM((width, total), jnp.float32),
             pltpu.SemaphoreType.DMA((slot_count // slots,)),
         ],
         cost_estimate=pl.CostEstimate(
-            flops=2 * slot_count * degrees * total * width,
+            flops=2 * slot_count * degrees * total * 2 * slots,
             bytes_accessed=slot_count * degrees * total * 2,
             transcendentals=0,
         ),
-        compiler_params=pltpu.CompilerParams(vmem_limit_bytes=62 * 1024 * 1024),
+        compiler_params=pltpu.CompilerParams(vmem_limit_bytes=50 * 1024 * 1024),
     )(legendre, spectra)
 
 

time: 73.4 us -> 65.8 us (0.90)
  Pallas kernels: 42.2 us -> 35.1 us
  waiting for transfers between devices: 12.4 us -> 15.6 us
  local copies, waits for them, and re-layouts: 4.73 us -> 1.88 us
    all_to_all x1, waiting for transfers between devices: 4.8 us -> 8.01 us  [body(): lax.all_to_all(partial, axes, split_axis=0, concat_axis=0, tiled=True)]
    pallas_call x1, Pallas kernels: 10.7 us -> 7.74 us  [analyse(): pl.pallas_call(analysis_kernel, in_specs=[pl.BlockSpec(memory_space=pl.AN...]
    pallas_call x1, Pallas kernels: 12.8 us -> 10.4 us  [run_ilc(): pl.pallas_call(ilc_kernel, in_specs=[vmem, vmem, pl.BlockSpec(memory_spac...]
    pallas_call x1, Pallas kernels: 8.69 us -> 7.14 us  [make_basis(): pl.pallas_call(functools.partial(basis_kernel, slots), grid=(rows // bloc...]
    convert_element_type x1, local copies, waits for them, and re-layouts: 2.09 us -> 1.01 us  [body(): basis = make_basis(order_rows.astype(jnp.float32)[:, None], slot_count)]
    transpose x1, local copies, waits for them, and re-layouts: 1.13 us -> 0.21 us  [body(): vectors[:, :cycles].transpose(1, 2, 0)]
    unnamed x8 -> x4, local copies, waits for them, and re-layouts: 0.91 us -> 0.05 us
  transfers between devices with their start and end apart: 3 -> 3, of which waited for: 2 -> 2; matrix products, arithmetic and copies ran while one was open for 4% -> 2% of each run, Pallas kernels for 27% -> 23%
where the time goes in v5:
time: 65.8 us; the launch traced here: 65.5 us
  Pallas kernels  35.1 us (53%)
  waiting for transfers between devices  15.6 us (24%)
  starting transfers between devices  11.4 us (17%)
  local copies, waits for them, and re-layouts  1.88 us (3%)
  between operations  0.78 us (1%)
  other arithmetic  0.75 us (1%)
    pallas_call x1, Pallas kernels, run_ilc(): pl.pallas_call(ilc_kernel, in_specs=[vmem, vmem, pl.BlockSpec(memory_spac...  10.4 us
    pallas_call x1, Pallas kernels, make_modes(): pl.pallas_call(modes_kernel, in_specs=[pl.BlockSpec(memory_space=pl.ANY)]...  9.86 us
    all_to_all x1, waiting for transfers between devices, body(): lax.all_to_all(partial, axes, split_axis=0, concat_axis=0, tiled=True)  8.01 us
    pallas_call x1, Pallas kernels, analyse(): pl.pallas_call(analysis_kernel, in_specs=[pl.BlockSpec(memory_space=pl.AN...  7.74 us
    all_to_all x1, waiting for transfers between devices, body(): lax.all_to_all(spectra, axes, split_axis=0, concat_axis=0, tiled=True)  7.58 us
    all_to_all x1, starting transfers between devices, body(): lax.all_to_all(partial, axes, split_axis=0, concat_axis=0, tiled=True)  7.3 us
    pallas_call x1, Pallas kernels, make_basis(): pl.pallas_call(functools.partial(basis_kernel, slots), grid=(rows // bloc...  7.14 us
    all_to_all x1, starting transfers between devices, body(): lax.all_to_all(spectra, axes, split_axis=0, concat_axis=0, tiled=True)  3.62 us
  transfers between devices with their start and end apart: 3, of which 2 were waited for; matrix products, arithmetic and copies ran while one was open for 2% of the time, Pallas kernels for 23%

profile of v5, /device:TPU:0, one launch (start us, length us, event | category | flops | bytes accessed | tf_op | source)
XLA Modules:
  0.0 65.5 jit_solution(18418040468930561406)
XLA Ops:
  0.6 0.0 copy-start
  0.6 9.9 %shard_map.50 = bf16[32,72,128]{2,1,0:T(8,128)(2,1)} custom-call(bf16[64,9,2,512]{3,2,1,0:T(2,128)(2,1)} %alm_hbm.1, bf16[64,512,256]{2,1,0:T(8,128)(2,1)} %table_hbm.3), custom_call_target="tpu_custom_call" | custom-call | flops 301989888 | bytes 17956864 | tf_op jit(solution)/shard_map/pallas_call | solution.py:326
  10.5 7.3 %all-to-all-start = ((bf16[32,72,128]{2,1,0:T(8,128)(2,1)}), bf16[32,72,128]{2,1,0:T(8,128)(2,1)S(1)}, u32[]{:S(2)}, u32[]{:S(2)}) async-start(bf16[32,72,128]{2,1,0:T(8,128)(2,1)} %shard_map.50), calls=%async_computation | async-start | bytes 1179648 | tf_op jit(solution)/shard_map/all_to_all | solution.py:430
  17.8 0.0 copy-done
  17.8 0.1 broadcast_in_dim.11
  17.9 1.0 %convert_element_type.27.order_ref = f32[2048,1]{1,0:T(8,128)S(1)} reshape(f32[16,2,64]{2,1,0:T(2,128)S(1)} %broadcast_in_dim.13) | data formatting | bytes 16384 | tf_op jit(solution)/shard_map/convert_element_type | solution.py:441
  19.0 0.1 reshape.94
  19.0 7.1 %shard_map.51.basis_hbm = bf16[4,2048,512]{2,1,0:T(8,128)(2,1)} custom-call(f32[2048,1]{1,0:T(8,128)S(1)} %convert_element_type.27.order_ref), custom_call_target="tpu_custom_call" | custom-call | flops 33554432 | bytes 8388608 | tf_op jit(solution)/shard_map/pallas_call | solution.py:71
  26.2 8.0 %all-to-all-done = bf16[32,72,128]{2,1,0:T(8,128)(2,1)S(1)} async-done(((bf16[32,72,128]{2,1,0:T(8,128)(2,1)}), bf16[32,72,128]{2,1,0:T(8,128)(2,1)S(1)}, u32[]{:S(2)}, u32[]{:S(2)}) %all-to-all-start) | async-done | bytes 589856 | tf_op jit(solution)/shard_map/all_to_all | solution.py:430
  34.2 10.4 %shard_map.52 = (f32[32,8,128]{2,1,0:T(8,128)S(1)}, bf16[16,2,8,128]{3,2,1,0:T(8,128)(2,1)}) custom-call(bf16[16,2,72,128]{3,2,1,0:T(8,128)(2,1)S(1)} %bitcast.13, f32[1,2048]{1,0:T(1,128)S(1)} %fusion.2.odd_ref, bf16[4,2048,512]{2,1,0:T(8,128)(2,1)} %shard_map.51.basis_hbm), custom_call_target="tpu_custom_call" | custom-call | flops 1342177280 | bytes 8388608 | tf_op jit(solution)/shard_map/pallas_call | solution.py:244
  44.6 3.6 %all-to-all-start.1 = ((bf16[32,8,128]{2,1,0:T(8,128)(2,1)}), bf16[32,8,128]{2,1,0:T(8,128)(2,1)S(1)}, u32[]{:S(2)}, u32[]{:S(2)}) async-start(bf16[32,8,128]{2,1,0:T(8,128)(2,1)} %bitcast.1), calls=%async_computation.1 | async-start | bytes 131072 | tf_op jit(solution)/shard_map/all_to_all | solution.py:450
  48.3 7.6 %all-to-all-done.1 = bf16[32,8,128]{2,1,0:T(8,128)(2,1)S(1)} async-done(((bf16[32,8,128]{2,1,0:T(8,128)(2,1)}), bf16[32,8,128]{2,1,0:T(8,128)(2,1)S(1)}, u32[]{:S(2)}, u32[]{:S(2)}) %all-to-all-start.1) | async-done | bytes 65568 | tf_op jit(solution)/shard_map/all_to_all | solution.py:450
  55.8 0.2 copy.6
  56.0 0.3 reshape.96
  56.4 0.1 constant_dynamic-slice_fusion
  56.5 0.5 collective-permute-start
  57.0 7.7 %shard_map.53 = f32[64,2,512]{2,1,0:T(2,128)} custom-call(bf16[64,512,256]{2,1,0:T(8,128)(2,1)} %table_hbm.3, bf16[256,128]{1,0:T(8,128)(2,1)S(1)} %bitcast.14), custom_call_target="tpu_custom_call" | custom-call | flops 268435456 | bytes 16777216 | tf_op jit(solution)/shard_map/pallas_call | solution.py:378
  64.8 0.0 collective-permute-done
  64.8 0.7 %maximum_bitcast_fusion = f32[16,2048]{1,0:T(8,128)} fusion(f32[1,8,2048]{2,1,0:T(8,128)S(1)} %get-tuple-element.11, f32[1,8,2048]{2,1,0:T(8,128)S(1)} %get-tuple-element.10), kind=kLoop, calls=%fused_computation.4 | loop fusion | flops 32768 | bytes 262144 | tf_op jit(solution)/shard_map/reshape | solution.py:460
  (7 shorter events, 0.1 us)
Async XLA Ops:
  0.6 17.2 %copy-start = (s32[1024]{0:T(1024)S(1)}, s32[1024]{0:T(1024)}, u32[]{:S(2)}) copy-start(s32[1024]{0:T(1024)} %param.5) | copy-start | bytes 12292
  10.5 23.7 %all-to-all-start = ((bf16[32,72,128]{2,1,0:T(8,128)(2,1)}), bf16[32,72,128]{2,1,0:T(8,128)(2,1)S(1)}, u32[]{:S(2)}, u32[]{:S(2)}) async-start(bf16[32,72,128]{2,1,0:T(8,128)(2,1)} %shard_map.50), calls=%async_computation | async-start | bytes 1179648 | tf_op jit(solution)/shard_map/all_to_all | solution.py:430
  44.6 11.2 %all-to-all-start.1 = ((bf16[32,8,128]{2,1,0:T(8,128)(2,1)}), bf16[32,8,128]{2,1,0:T(8,128)(2,1)S(1)}, u32[]{:S(2)}, u32[]{:S(2)}) async-start(bf16[32,8,128]{2,1,0:T(8,128)(2,1)} %bitcast.1), calls=%async_computation.1 | async-start | bytes 131072 | tf_op jit(solution)/shard_map/all_to_all | solution.py:450
  56.5 8.3 %collective-permute-start = (f32[8,2048]{1,0:T(8,128)S(1)}, f32[8,2048]{1,0:T(8,128)S(1)}, u32[]{:S(2)}, u32[]{:S(2)}) collective-permute-start(f32[8,2048]{1,0:T(8,128)S(1)} %bitcast.17), channel_id=1, source_target_pairs={{0,1},{1,0},{2,3},{3,2},{4,5},{5,4},{6,7},{7,6},{8,9},{9,8},{10,11... | collective-permute-start | bytes 196616 | tf_op jit(solution)/shard_map/ppermute | solution.py:401

commit v6 on v5

--- a/solution.py
+++ b/solution.py
@@ -19,10 +19,12 @@
 WINDOW = 2 * HALO + 1
 LANES = NLON // HALO
 HALF = LANES // 2
-PAIRS = [(a_at, b_at) for a_at in range(C) for b_at in range(a_at, C)]
+REST = C - 1
+PAIRS = [(a_at, b_at) for a_at in range(REST) for b_at in range(a_at, REST)] + [(a_at, REST) for a_at in range(REST)]
+SUMS = len(PAIRS) + 1
 VMEM_LIMIT = 48 * 1024 * 1024
 CHUNK = 8
-IN_FLIGHT = 4
+IN_FLIGHT = 3
 
 
 def round_up(value, multiple):
@@ -105,44 +107,39 @@
     return guess * (2.0 - value * guess)
 
 
-def combine(entry, map_of):
-    diagonal = [entry(at, at) for at in range(C)]
-    trace = diagonal[0]
-    for at in range(1, C):
-        trace = trace + diagonal[at]
-    ridge = RIDGE * (trace * (1.0 / C) + WINDOW * EPSILON)
-    upper, inverses, ones, maps = {}, [], [], []
-    top = bottom = None
-    for row in range(C):
+def combine(sum_of, map_of):
+    ridge = RIDGE * (sum_of(SUMS - 1) * (1.0 / C) + WINDOW * EPSILON)
+    upper, inverses, rights, maps = {}, [], [], []
+    value = map_of(REST)
+    for row in range(REST):
         ratios = [upper[at, row] * inverses[at] for at in range(row)]
-        pivot = diagonal[row] + ridge
+        pivot = sum_of(PAIRS.index((row, row))) + (ridge + ridge)
         for at in range(row):
             pivot = pivot - ratios[at] * upper[at, row]
         inverse = reciprocal(pivot)
-        for col in range(row + 1, C):
-            value = entry(row, col)
-            for at in range(row):
-                value = value - ratios[at] * upper[at, col]
-            upper[row, col] = value
-        one = 1.0
+        right = ridge - sum_of(PAIRS.index((row, REST)))
         own = map_of(row)
         for at in range(row):
-            one = one - (ratios[at] if at == 0 else ratios[at] * ones[at])
+            right = right - ratios[at] * rights[at]
             own = own - ratios[at] * maps[at]
-        scaled = inverse if row == 0 else inverse * one
-        term = scaled * own
-        top = term if top is None else top + term
-        term = scaled if row == 0 else scaled * one
-        bottom = term if bottom is None else bottom + term
+        for col in range(row + 1, REST):
+            entry = sum_of(PAIRS.index((row, col))) + ridge
+            for at in range(row):
+                entry = entry - ratios[at] * upper[at, col]
+            upper[row, col] = entry
+        value = value + (right * inverse) * own
         inverses.append(inverse)
-        ones.append(one)
+        rights.append(right)
         maps.append(own)
-    return top * reciprocal(bottom)
+    return value
 
 
 def ilc_kernel(modes_ref, odd_ref, basis_hbm, ilc_ref, spectra_ref, basis_ref, lhs_ref, maps_ref, sums_ref, low_ref, found_ref, sems):
     groups, shares, rows, width = modes_ref.shape
-    chunks = basis_ref.shape[0]
+    columns = basis_ref.shape[2]
+    depth = lhs_ref.shape[1]
+    pieces = depth // basis_ref.shape[1]
+    chunks = basis_ref.shape[0] // pieces
     cycles = rows // C
     second = round_up(rows, 16)
     start_some(basis_hbm, basis_ref, sems)
@@ -157,28 +154,44 @@
     low_half = lax.broadcasted_iota(jnp.int32, (cycles, LANES), 1) < HALF
     sums_ref[...] = jnp.zeros_like(sums_ref)
 
-    def map_of(at, chan):
-        return maps_ref[at, chan * cycles : (chan + 1) * cycles, :]
+    def store_maps(at, maps):
+        squares = maps[0] * maps[0]
+        for chan in range(1, C):
+            squares = squares + maps[chan] * maps[chan]
+            maps_ref[at, chan - 1] = maps[chan] - maps[0]
+        maps_ref[at, REST] = maps[0]
+        maps_ref[at, C] = squares
 
     def maps_of_chunk(chunk):
-        next_part(basis_hbm, basis_ref, sems, chunk)
-        result = jnp.dot(lhs_ref[...], basis_ref[chunk], preferred_element_type=jnp.float32)
+        for piece in range(pieces):
+            next_part(basis_hbm, basis_ref, sems, chunk * pieces + piece)
+        basis = basis_ref[chunk * pieces : (chunk + 1) * pieces].reshape(depth, columns)
+        result = jnp.dot(lhs_ref[...], basis, preferred_element_type=jnp.float32)
         for part in range(CHUNK // 2):
             at = CHUNK * chunk + 2 * part
+            lanes = slice(part * LANES, (part + 1) * LANES)
+            left, right = [], []
             for chan in range(C):
-                span = slice(chan * cycles, (chan + 1) * cycles)
-                even_part = result[span, part * LANES : (part + 1) * LANES]
-                odd_part = result[second + chan * cycles : second + (chan + 1) * cycles, part * LANES : (part + 1) * LANES]
+                even_part = result[chan * cycles : (chan + 1) * cycles, lanes]
+                odd_part = result[second + chan * cycles : second + (chan + 1) * cycles, lanes]
                 near = even_part + odd_part
                 far = even_part - odd_part
-                maps_ref[at, span, :] = jnp.where(low_half, near, pltpu.roll(far, HALF, 1))
-                maps_ref[at + 1, span, :] = jnp.where(low_half, pltpu.roll(near, HALF, 1), far)
+                left.append(jnp.where(low_half, near, pltpu.roll(far, HALF, 1)))
+                right.append(jnp.where(low_half, pltpu.roll(near, HALF, 1), far))
+            store_maps(at, left)
+            store_maps(at + 1, right)
+
+    def product(at, pair):
+        if pair == SUMS - 1:
+            return maps_ref[at, C]
+        a_at, b_at = PAIRS[pair]
+        return maps_ref[at, a_at] * maps_ref[at, b_at]
 
     def add_totals(chunk):
-        for pair, (a_at, b_at) in enumerate(PAIRS):
+        for pair in range(SUMS):
             total = sums_ref[pair]
             for at in range(CHUNK * chunk, CHUNK * (chunk + 1)):
-                total = total + map_of(at, a_at) * map_of(at, b_at)
+                total = total + product(at, pair)
             sums_ref[pair] = total
 
     maps_of_chunk(0)
@@ -186,35 +199,32 @@
         maps_of_chunk(chunk)
         add_totals(chunk - 1)
     add_totals(chunks - 1)
-    for pair in range(len(PAIRS)):
+    for pair in range(SUMS):
         total = sums_ref[pair]
-        sums_ref[pair] = total + pltpu.roll(total, 1, 1)
-
-    def solve(at, leaves):
-        ahead = [pltpu.roll(map_of(at, chan), LANES - 1, 1) for chan in range(C)]
-        before = jnp.maximum(at - 1, 0)
-        behind = [pltpu.roll(map_of(before, chan), 1, 1) * leaves for chan in range(C)]
-
-        def entry(a_at, b_at):
-            pair = PAIRS.index((a_at, b_at))
-            total = sums_ref[pair] + (ahead[a_at] * ahead[b_at] - behind[a_at] * behind[b_at])
-            sums_ref[pair] = total
+        sums_ref[pair] = pltpu.roll(total, 1, 1) + pltpu.roll(total, 2, 1)
+
+    def solve(at):
+        def sum_of(pair):
+            own = product(at, pair)
+            total = sums_ref[pair] + own
+            sums_ref[pair] = total - pltpu.roll(own, 2, 1)
             return total
 
-        value = combine(entry, lambda chan: map_of(at, chan))
+        value = combine(sum_of, lambda chan: pltpu.roll(maps_ref[at, chan], 1, 1))
+        value = pltpu.roll(value, LANES - 1, 1)
         ilc_ref[at] = value
         return value
 
-    def two_vectors(at, first):
-        leaves = jnp.where(at == 0, 0.0, 1.0) if first else 1.0
-        found = [solve(at, leaves), solve(at + 1, 1.0)]
+    def two_vectors(at):
+        found = [solve(at), solve(at + 1)]
         near = jnp.where(low_half, found[0], pltpu.roll(found[1], HALF, 1))
         far = jnp.where(low_half, pltpu.roll(found[0], HALF, 1), found[1])
         return jnp.concatenate([near, far], axis=0).astype(jnp.bfloat16)
 
     def spectra_of(chunk):
+        basis = basis_ref[pl.ds(chunk * pieces, pieces)].reshape(depth, columns)
         return lax.dot_general(
-            low_ref[chunk], basis_ref[chunk], (((1,), (1,)), ((), ())), preferred_element_type=jnp.float32
+            low_ref[chunk], basis, (((1,), (1,)), ((), ())), preferred_element_type=jnp.float32
         )
 
     found_ref[...] = jnp.zeros_like(found_ref)
@@ -223,7 +233,7 @@
     def solve_chunk(chunk, carry):
         found_ref[...] += spectra_of(jnp.maximum(chunk - 1, 0))
         for part in range(CHUNK // 2):
-            low_ref[chunk, :, part * LANES : (part + 1) * LANES] = two_vectors(CHUNK * chunk + 2 * part, part == 0)
+            low_ref[chunk, :, part * LANES : (part + 1) * LANES] = two_vectors(CHUNK * chunk + 2 * part)
         return carry
 
     lax.fori_loop(0, chunks, solve_chunk, 0)
@@ -239,6 +249,8 @@
 def run_ilc(modes, odd, basis):
     groups, shares, rows, width = modes.shape
     chunks, depth, columns = basis.shape
+    pieces = 2
+    basis = basis.reshape(chunks * pieces, depth // pieces, columns)
     cycles = rows // C
     vmem = pl.BlockSpec(memory_space=pltpu.VMEM)
     return pl.pallas_call(
@@ -250,13 +262,13 @@
             jax.ShapeDtypeStruct((groups, shares, cycles, width), jnp.bfloat16),
         ],
         scratch_shapes=[
-            pltpu.VMEM((chunks, depth, columns), jnp.bfloat16),
+            pltpu.VMEM(basis.shape, jnp.bfloat16),
             pltpu.VMEM((2 * round_up(rows, 16), depth), jnp.bfloat16),
-            pltpu.VMEM((HALO, rows, LANES), jnp.float32),
-            pltpu.VMEM((len(PAIRS), cycles, LANES), jnp.float32),
+            pltpu.VMEM((HALO, C + 1, cycles, LANES), jnp.float32),
+            pltpu.VMEM((SUMS, cycles, LANES), jnp.float32),
             pltpu.VMEM((chunks, 2 * cycles, columns), jnp.bfloat16),
             pltpu.VMEM((2 * cycles, depth), jnp.float32),
-            pltpu.SemaphoreType.DMA((chunks,)),
+            pltpu.SemaphoreType.DMA((chunks * pieces,)),
         ],
         cost_estimate=pl.CostEstimate(
             flops=2 * chunks * depth * columns * (2 * rows + 2 * cycles),
@@ -267,7 +279,7 @@
     )(modes, odd, basis)
 
 
-def modes_kernel(alm_hbm, table_hbm, out_ref, alm_ref, table_ref, lhs_ref, low_ref, held_ref, turned_ref, alm_sem, sems):
+def modes_kernel(alm_hbm, table_hbm, out_ref, alm_ref, table_ref, lhs_ref, held_ref, turned_ref, alm_sem, sems):
     parts = sems.shape[0]
     total_slots = table_ref.shape[0]
     slots = total_slots // parts
@@ -281,29 +293,29 @@
     lhs_ref[...] = jnp.zeros_like(lhs_ref)
     alm_copy.wait()
 
-    def stack_rows(part, carry):
+    def stack_rows(part):
         for slot in range(slots):
             first = slot % 2 * height
             for chan in range(C):
                 span = slice(first + 2 * chan, first + 2 * chan + 2)
-                lhs_ref[slot // 2, span, :] = alm_ref[part * slots + slot, chan].astype(jnp.float32)
-        for pair in range(slots // 2):
-            low_ref[part * (slots // 2) + pair] = lhs_ref[pair].astype(jnp.bfloat16)
-        return carry
-
-    lax.fori_loop(0, parts, stack_rows, 0)
+                lhs_ref[part % 2, slot // 2, span, :] = alm_ref[part * slots + slot, chan].astype(jnp.float32)
+
+    stack_rows(0)
 
     def some_slots(part, carry):
         next_part(table_hbm, table_ref, sems, part)
         for pair in range(slots // 2):
             at = part * slots + 2 * pair
             both = jnp.concatenate([table_ref[at], table_ref[at + 1]], axis=1)
-            result = jnp.dot(low_ref[part * (slots // 2) + pair], both, preferred_element_type=jnp.float32)
+            lhs = lhs_ref[part % 2, pair].astype(jnp.bfloat16)
+            result = jnp.dot(lhs, both, preferred_element_type=jnp.float32)
             for slot in range(2):
                 rows = pl.ds(pl.multiple_of((at + slot) * height, 8), height)
                 own = result[slot * height : (slot + 1) * height, slot * total : (slot + 1) * total]
                 for lanes in range(held_ref.shape[0]):
                     held_ref[lanes, rows, :] = own[:, lanes * LANES : (lanes + 1) * LANES]
+
+        stack_rows(jnp.minimum(part + 1, parts - 1))
         return carry
 
     lax.fori_loop(0, parts, some_slots, 0)
@@ -331,8 +343,7 @@
         scratch_shapes=[
             pltpu.VMEM(alm.shape, jnp.bfloat16),
             pltpu.VMEM(legendre.shape, jnp.bfloat16),
-            pltpu.VMEM((slots // 2, 2 * height, degrees), jnp.float32),
-            pltpu.VMEM((slot_count // 2, 2 * height, degrees), jnp.bfloat16),
+            pltpu.VMEM((2, slots // 2, 2 * height, degrees), jnp.float32),
             pltpu.VMEM((total // LANES, slot_count * height, LANES), jnp.float32),
             pltpu.VMEM((C, total, width), jnp.float32),
             pltpu.SemaphoreType.DMA,
@@ -348,9 +359,10 @@
 
 
 def analysis_kernel(table_hbm, spectra_ref, out_ref, table_ref, turned_ref, sems):
-    parts = sems.shape[0]
     total_slots, degrees, total = table_ref.shape
-    slots = total_slots // parts
+    slots = 8
+    pieces = sems.shape[0] * slots // total_slots
+    few = slots // pieces
     start_some(table_hbm, table_ref, sems)
     turned_ref[...] = spectra_ref[...].astype(jnp.float32).T
 
@@ -358,16 +370,18 @@
         first = pl.multiple_of(part * slots, slots)
         rows = [turned_ref[pl.ds(first + share * total_slots, slots), :] for share in range(2)]
         lhs = jnp.concatenate(rows, axis=0).astype(jnp.bfloat16)
-        next_part(table_hbm, table_ref, sems, part)
-        table = table_ref[pl.ds(first, slots)].reshape(slots * degrees, total)
-        result = lax.dot_general(lhs, table, (((1,), (1,)), ((), ())), preferred_element_type=jnp.float32)
-        for slot in range(slots):
-            span = slice(slot * degrees, (slot + 1) * degrees)
-            out_ref[part * slots + slot, 0:1, :] = result[slot : slot + 1, span]
-            out_ref[part * slots + slot, 1:2, :] = result[slots + slot : slots + slot + 1, span]
+        for piece in range(pieces):
+            next_part(table_hbm, table_ref, sems, part * pieces + piece)
+            table = table_ref[pl.ds(first + piece * few, few)].reshape(few * degrees, total)
+            result = lax.dot_general(lhs, table, (((1,), (1,)), ((), ())), preferred_element_type=jnp.float32)
+            for at in range(few):
+                slot = piece * few + at
+                span = slice(at * degrees, (at + 1) * degrees)
+                out_ref[first + slot, 0:1, :] = result[slot : slot + 1, span]
+                out_ref[first + slot, 1:2, :] = result[slots + slot : slots + slot + 1, span]
         return carry
 
-    lax.fori_loop(0, parts, some_slots, 0)
+    lax.fori_loop(0, total_slots // slots, some_slots, 0)
 
 
 def analyse(legendre, spectra):
@@ -383,7 +397,7 @@
         scratch_shapes=[
             pltpu.VMEM(legendre.shape, jnp.bfloat16),
             pltpu.VMEM((width, total), jnp.float32),
-            pltpu.SemaphoreType.DMA((slot_count // slots,)),
+            pltpu.SemaphoreType.DMA((slot_count // 4,)),
         ],
         cost_estimate=pl.CostEstimate(
             flops=2 * slot_count * degrees * total * 2 * slots,
@@ -448,16 +462,13 @@
         spectra = jnp.broadcast_to(spectra, (band_count, tile_count, cycles, width))
     spectra = spectra.reshape(targets, cycles, width)
     routed = lax.all_to_all(spectra, axes, split_axis=0, concat_axis=0, tiled=True)
-    vectors, routed = lax.optimization_barrier((vectors, routed))
+    found = in_tile_order(from_other_tiles([vectors[:, :cycles]] * tile_count))
+    lanes = LANES // tile_count
+    found = lax.dynamic_slice_in_dim(found, tile_at * lanes, lanes, axis=3)
+    ilc_map = found.transpose(0, 2, 3, 1).reshape(tile_count * cycles, NLON // tile_count)
+    routed, ilc_map = lax.optimization_barrier((routed, ilc_map))
     ilc_alm = analyse(legendre, routed.reshape(targets * cycles, width))
-
-    own = vectors[:, :cycles].transpose(1, 2, 0).reshape(cycles, tile_count, NLON // tile_count)
-    own = own.transpose(1, 0, 2)
-    sends = [
-        lax.dynamic_index_in_dim(own, (tile_at + hop) % tile_count, 0, keepdims=False) for hop in range(tile_count)
-    ]
-    ilc_map = in_tile_order(from_other_tiles(sends))
-    return (ilc_map.reshape(tile_count * cycles, NLON // tile_count), ilc_alm)
+    return (ilc_map, ilc_alm)
 
 
 def solution(mesh):

time: 65.8 us -> 67.4 us (1.024)
  Pallas kernels: 35.1 us -> 37.9 us
  waiting for transfers between devices: 15.6 us -> 14.3 us
    all_to_all x1, waiting for transfers between devices: 7.58 us -> 4.18 us  [body(): lax.all_to_all(spectra, axes, split_axis=0, concat_axis=0, tiled=True)]
    ppermute x1, waiting for transfers between devices: 0.01 us -> 2.11 us  [from_other_tiles(): lax.ppermute(sends[hop], 'tile', [(at, (at + hop) % count) for at in rang...]
    pallas_call x1, Pallas kernels: 7.74 us -> 9.37 us  [analyse(): pl.pallas_call(analysis_kernel, in_specs=[pl.BlockSpec(memory_space=pl.AN...]
    ppermute x1, starting transfers between devices: 0.49 us -> 1.72 us  [from_other_tiles(): lax.ppermute(sends[hop], 'tile', [(at, (at + hop) % count) for at in rang...]
    all_to_all x1, starting transfers between devices: 3.62 us -> 2.57 us  [body(): lax.all_to_all(spectra, axes, split_axis=0, concat_axis=0, tiled=True)]
    pallas_call x1, Pallas kernels: 10.4 us -> 11.1 us  [run_ilc(): pl.pallas_call(ilc_kernel, in_specs=[vmem, vmem, pl.BlockSpec(memory_spac...]
  transfers between devices with their start and end apart: 3 -> 3, of which waited for: 2 -> 3; matrix products, arithmetic and copies ran while one was open for 2% -> 4% of each run, Pallas kernels for 23% -> 11%
where the time goes in v6:
time: 67.4 us; the launch traced here: 67.1 us
  Pallas kernels  37.9 us (56%)
  waiting for transfers between devices  14.3 us (21%)
  starting transfers between devices  11.6 us (17%)
  local copies, waits for them, and re-layouts  2.31 us (3%)
  between operations  0.72 us (1%)
    pallas_call x1, Pallas kernels, run_ilc(): pl.pallas_call(ilc_kernel, in_specs=[vmem, vmem, pl.BlockSpec(memory_spac...  11.1 us
    pallas_call x1, Pallas kernels, make_modes(): pl.pallas_call(modes_kernel, in_specs=[pl.BlockSpec(memory_space=pl.ANY)]...  10.4 us
    pallas_call x1, Pallas kernels, analyse(): pl.pallas_call(analysis_kernel, in_specs=[pl.BlockSpec(memory_space=pl.AN...  9.37 us
    all_to_all x1, waiting for transfers between devices, body(): lax.all_to_all(partial, axes, split_axis=0, concat_axis=0, tiled=True)  8 us
    all_to_all x1, starting transfers between devices, body(): lax.all_to_all(partial, axes, split_axis=0, concat_axis=0, tiled=True)  7.3 us
    pallas_call x1, Pallas kernels, make_basis(): pl.pallas_call(functools.partial(basis_kernel, slots), grid=(rows // bloc...  7.15 us
    all_to_all x1, waiting for transfers between devices, body(): lax.all_to_all(spectra, axes, split_axis=0, concat_axis=0, tiled=True)  4.18 us
    all_to_all x1, starting transfers between devices, body(): lax.all_to_all(spectra, axes, split_axis=0, concat_axis=0, tiled=True)  2.57 us
  transfers between devices with their start and end apart: 3, of which 3 were waited for; matrix products, arithmetic and copies ran while one was open for 4% of the time, Pallas kernels for 11%

profile of v6, /device:TPU:0, one launch (start us, length us, event | category | flops | bytes accessed | tf_op | source)
XLA Modules:
  0.0 67.1 jit_solution(9980118102221237150)
XLA Ops:
  0.6 0.0 copy-start
  0.6 10.4 %shard_map.50 = bf16[32,72,128]{2,1,0:T(8,128)(2,1)} custom-call(bf16[64,9,2,512]{3,2,1,0:T(2,128)(2,1)} %alm_hbm.1, bf16[64,512,256]{2,1,0:T(8,128)(2,1)} %table_hbm.3), custom_call_target="tpu_custom_call" | custom-call | flops 301989888 | bytes 17956864 | tf_op jit(solution)/shard_map/pallas_call | solution.py:338
  11.0 7.3 %all-to-all-start = ((bf16[32,72,128]{2,1,0:T(8,128)(2,1)}), bf16[32,72,128]{2,1,0:T(8,128)(2,1)S(1)}, u32[]{:S(2)}, u32[]{:S(2)}) async-start(bf16[32,72,128]{2,1,0:T(8,128)(2,1)} %shard_map.50), calls=%async_computation | async-start | bytes 1179648 | tf_op jit(solution)/shard_map/all_to_all | solution.py:444
  18.3 0.0 copy-done
  18.3 0.1 broadcast_in_dim.11
  18.4 1.0 %convert_element_type.27.order_ref = f32[2048,1]{1,0:T(8,128)S(1)} reshape(f32[16,2,64]{2,1,0:T(2,128)S(1)} %broadcast_in_dim.13) | data formatting | bytes 16384 | tf_op jit(solution)/shard_map/convert_element_type | solution.py:455
  19.4 0.1 reshape.91
  19.5 7.2 %shard_map.51 = bf16[4,2048,512]{2,1,0:T(8,128)(2,1)} custom-call(f32[2048,1]{1,0:T(8,128)S(1)} %convert_element_type.27.order_ref), custom_call_target="tpu_custom_call" | custom-call | flops 33554432 | bytes 8388608 | tf_op jit(solution)/shard_map/pallas_call | solution.py:73
  26.7 8.0 %all-to-all-done = bf16[32,72,128]{2,1,0:T(8,128)(2,1)S(1)} async-done(((bf16[32,72,128]{2,1,0:T(8,128)(2,1)}), bf16[32,72,128]{2,1,0:T(8,128)(2,1)S(1)}, u32[]{:S(2)}, u32[]{:S(2)}) %all-to-all-start) | async-done | bytes 589856 | tf_op jit(solution)/shard_map/all_to_all | solution.py:444
  34.7 11.1 %shard_map.52 = (f32[32,8,128]{2,1,0:T(8,128)S(1)}, bf16[16,2,8,128]{3,2,1,0:T(8,128)(2,1)}) custom-call(bf16[16,2,72,128]{3,2,1,0:T(8,128)(2,1)S(1)} %bitcast.10, f32[1,2048]{1,0:T(1,128)S(1)} %fusion.3.odd_ref, bf16[8,1024,512]{2,1,0:T(8,128)(2,1)} %bitcast.13), custom_call_target="tpu_custom_call" | custom-call | flops 1342177280 | bytes 8388608 | tf_op jit(solution)/shard_map/pallas_call | solution.py:256
  45.8 1.7 %collective-permute-start = (f32[32,8,128]{2,1,0:T(8,128)S(1)}, f32[32,8,128]{2,1,0:T(8,128)S(1)}, u32[]{:S(2)}, u32[]{:S(2)}) collective-permute-start(f32[32,8,128]{2,1,0:T(8,128)S(1)} %get-tuple-element.7), channel_id=1, source_target_pairs={{0,1},{1,0},{2,3},{3,2},{4,5},{5,4},{6,7},{7,6},{8,9},{9,8},{10,11... | collective-permute-start | bytes 393224 | tf_op jit(solution)/shard_map/ppermute | solution.py:415
  47.5 2.6 %all-to-all-start.1 = ((bf16[32,8,128]{2,1,0:T(8,128)(2,1)}), bf16[32,8,128]{2,1,0:T(8,128)(2,1)S(1)}, u32[]{:S(2)}, u32[]{:S(2)}) async-start(bf16[32,8,128]{2,1,0:T(8,128)(2,1)} %bitcast.2), calls=%async_computation.1 | async-start | bytes 131072 | tf_op jit(solution)/shard_map/all_to_all | solution.py:464
  50.1 2.1 %collective-permute-done = f32[32,8,128]{2,1,0:T(8,128)S(1)} collective-permute-done((f32[32,8,128]{2,1,0:T(8,128)S(1)}, f32[32,8,128]{2,1,0:T(8,128)S(1)}, u32[]{:S(2)}, u32[]{:S(2)}) %collective-permute-start) | collective-permute-done | bytes 131104 | tf_op jit(solution)/shard_map/ppermute | solution.py:415
  52.2 0.1 fusion.2
  52.2 0.1 fusion
  52.4 0.2 copy.6
  52.6 0.9 %reshape.94 = f32[16,2048]{1,0:T(8,128)} reshape(f32[2,8,64,32]{3,2,1,0:T(8,128)S(1)} %copy.6) | data formatting | bytes 262144 | tf_op jit(solution)/shard_map/reshape | solution.py:468
  53.5 4.2 %all-to-all-done.1 = bf16[32,8,128]{2,1,0:T(8,128)(2,1)S(1)} async-done(((bf16[32,8,128]{2,1,0:T(8,128)(2,1)}), bf16[32,8,128]{2,1,0:T(8,128)(2,1)S(1)}, u32[]{:S(2)}, u32[]{:S(2)}) %all-to-all-start.1) | async-done | bytes 65568 | tf_op jit(solution)/shard_map/all_to_all | solution.py:464
  57.7 9.4 %shard_map.53 = f32[64,2,512]{2,1,0:T(2,128)} custom-call(bf16[64,512,256]{2,1,0:T(8,128)(2,1)} %table_hbm.3, bf16[256,128]{1,0:T(8,128)(2,1)S(1)} %bitcast.11), custom_call_target="tpu_custom_call" | custom-call | flops 268435456 | bytes 16777216 | tf_op jit(solution)/shard_map/pallas_call | solution.py:392
  (4 shorter events, 0.1 us)
Async XLA Ops:
  0.6 17.7 %copy-start = (s32[1024]{0:T(1024)S(1)}, s32[1024]{0:T(1024)}, u32[]{:S(2)}) copy-start(s32[1024]{0:T(1024)} %param.5) | copy-start | bytes 12292
  11.0 23.7 %all-to-all-start = ((bf16[32,72,128]{2,1,0:T(8,128)(2,1)}), bf16[32,72,128]{2,1,0:T(8,128)(2,1)S(1)}, u32[]{:S(2)}, u32[]{:S(2)}) async-start(bf16[32,72,128]{2,1,0:T(8,128)(2,1)} %shard_map.50), calls=%async_computation | async-start | bytes 1179648 | tf_op jit(solution)/shard_map/all_to_all | solution.py:444
  45.8 6.4 %collective-permute-start = (f32[32,8,128]{2,1,0:T(8,128)S(1)}, f32[32,8,128]{2,1,0:T(8,128)S(1)}, u32[]{:S(2)}, u32[]{:S(2)}) collective-permute-start(f32[32,8,128]{2,1,0:T(8,128)S(1)} %get-tuple-element.7), channel_id=1, source_target_pairs={{0,1},{1,0},{2,3},{3,2},{4,5},{5,4},{6,7},{7,6},{8,9},{9,8},{10,11... | collective-permute-start | bytes 393224 | tf_op jit(solution)/shard_map/ppermute | solution.py:415
  47.5 10.2 %all-to-all-start.1 = ((bf16[32,8,128]{2,1,0:T(8,128)(2,1)}), bf16[32,8,128]{2,1,0:T(8,128)(2,1)S(1)}, u32[]{:S(2)}, u32[]{:S(2)}) async-start(bf16[32,8,128]{2,1,0:T(8,128)(2,1)} %bitcast.2), calls=%async_computation.1 | async-start | bytes 131072 | tf_op jit(solution)/shard_map/all_to_all | solution.py:464

commit v7 on v6

--- a/solution.py
+++ b/solution.py
@@ -24,7 +24,6 @@
 SUMS = len(PAIRS) + 1
 VMEM_LIMIT = 48 * 1024 * 1024
 CHUNK = 8
-IN_FLIGHT = 3
 
 
 def round_up(value, multiple):
@@ -89,17 +88,9 @@
     return pltpu.make_async_copy(source.at[span], target.at[span], sems.at[part])
 
 
-def start_some(source, target, sems):
-    for part in range(min(IN_FLIGHT, sems.shape[0])):
+def start_parts(source, target, sems):
+    for part in range(sems.shape[0]):
         part_copy(source, target, sems, part).start()
-
-
-def next_part(source, target, sems, part):
-    part_copy(source, target, sems, part).wait()
-
-    @pl.when(part + IN_FLIGHT < sems.shape[0])
-    def _():
-        part_copy(source, target, sems, part + IN_FLIGHT).start()
 
 
 def reciprocal(value):
@@ -142,7 +133,7 @@
     chunks = basis_ref.shape[0] // pieces
     cycles = rows // C
     second = round_up(rows, 16)
-    start_some(basis_hbm, basis_ref, sems)
+    start_parts(basis_hbm, basis_ref, sems)
     for group in range(groups):
         span = slice(group * width, (group + 1) * width)
         odd = odd_ref[:, span]
@@ -164,7 +155,7 @@
 
     def maps_of_chunk(chunk):
         for piece in range(pieces):
-            next_part(basis_hbm, basis_ref, sems, chunk * pieces + piece)
+            part_copy(basis_hbm, basis_ref, sems, chunk * pieces + piece).wait()
         basis = basis_ref[chunk * pieces : (chunk + 1) * pieces].reshape(depth, columns)
         result = jnp.dot(lhs_ref[...], basis, preferred_element_type=jnp.float32)
         for part in range(CHUNK // 2):
@@ -289,7 +280,7 @@
     total = table_ref.shape[2]
     alm_copy = pltpu.make_async_copy(alm_hbm, alm_ref, alm_sem)
     alm_copy.start()
-    start_some(table_hbm, table_ref, sems)
+    start_parts(table_hbm, table_ref, sems)
     lhs_ref[...] = jnp.zeros_like(lhs_ref)
     alm_copy.wait()
 
@@ -303,7 +294,7 @@
     stack_rows(0)
 
     def some_slots(part, carry):
-        next_part(table_hbm, table_ref, sems, part)
+        part_copy(table_hbm, table_ref, sems, part).wait()
         for pair in range(slots // 2):
             at = part * slots + 2 * pair
             both = jnp.concatenate([table_ref[at], table_ref[at + 1]], axis=1)
@@ -363,7 +354,7 @@
     slots = 8
     pieces = sems.shape[0] * slots // total_slots
     few = slots // pieces
-    start_some(table_hbm, table_ref, sems)
+    start_parts(table_hbm, table_ref, sems)
     turned_ref[...] = spectra_ref[...].astype(jnp.float32).T
 
     def some_slots(part, carry):
@@ -371,7 +362,7 @@
         rows = [turned_ref[pl.ds(first + share * total_slots, slots), :] for share in range(2)]
         lhs = jnp.concatenate(rows, axis=0).astype(jnp.bfloat16)
         for piece in range(pieces):
-            next_part(table_hbm, table_ref, sems, part * pieces + piece)
+            part_copy(table_hbm, table_ref, sems, part * pieces + piece).wait()
             table = table_ref[pl.ds(first + piece * few, few)].reshape(few * degrees, total)
             result = lax.dot_general(lhs, table, (((1,), (1,)), ((), ())), preferred_element_type=jnp.float32)
             for at in range(few):

time: 67.4 us -> 67.5 us (level)
    pallas_call x1, Pallas kernels: 10.4 us -> 12.6 us  [make_modes(): pl.pallas_call(modes_kernel, in_specs=[pl.BlockSpec(memory_space=pl.ANY)]...]
    pallas_call x1, Pallas kernels: 11.1 us -> 9.98 us  [run_ilc(): pl.pallas_call(ilc_kernel, in_specs=[vmem, vmem, pl.BlockSpec(memory_spac...]
    pallas_call x1, Pallas kernels: 9.37 us -> 8.39 us  [analyse(): pl.pallas_call(analysis_kernel, in_specs=[pl.BlockSpec(memory_space=pl.AN...]
where the time goes in v7:
time: 67.5 us; the launch traced here: 67.2 us
  Pallas kernels  38.1 us (56%)
  waiting for transfers between devices  14.3 us (21%)
  starting transfers between devices  11.6 us (17%)
  local copies, waits for them, and re-layouts  2.31 us (3%)
  between operations  0.72 us (1%)
    pallas_call x1, Pallas kernels, make_modes(): pl.pallas_call(modes_kernel, in_specs=[pl.BlockSpec(memory_space=pl.ANY)]...  12.6 us
    pallas_call x1, Pallas kernels, run_ilc(): pl.pallas_call(ilc_kernel, in_specs=[vmem, vmem, pl.BlockSpec(memory_spac...  9.98 us
    pallas_call x1, Pallas kernels, analyse(): pl.pallas_call(analysis_kernel, in_specs=[pl.BlockSpec(memory_space=pl.AN...  8.39 us
    all_to_all x1, waiting for transfers between devices, body(): lax.all_to_all(partial, axes, split_axis=0, concat_axis=0, tiled=True)  8 us
    all_to_all x1, starting transfers between devices, body(): lax.all_to_all(partial, axes, split_axis=0, concat_axis=0, tiled=True)  7.3 us
    pallas_call x1, Pallas kernels, make_basis(): pl.pallas_call(functools.partial(basis_kernel, slots), grid=(rows // bloc...  7.15 us
    all_to_all x1, waiting for transfers between devices, body(): lax.all_to_all(spectra, axes, split_axis=0, concat_axis=0, tiled=True)  4.18 us
    all_to_all x1, starting transfers between devices, body(): lax.all_to_all(spectra, axes, split_axis=0, concat_axis=0, tiled=True)  2.57 us
  transfers between devices with their start and end apart: 3, of which 3 were waited for; matrix products, arithmetic and copies ran while one was open for 4% of the time, Pallas kernels for 11%

profile of v7, /device:TPU:0, one launch (start us, length us, event | category | flops | bytes accessed | tf_op | source)
XLA Modules:
  0.0 67.2 jit_solution(5050855218520387400)
XLA Ops:
  0.6 0.0 copy-start
  0.6 12.6 %shard_map.50 = bf16[32,72,128]{2,1,0:T(8,128)(2,1)} custom-call(bf16[64,9,2,512]{3,2,1,0:T(2,128)(2,1)} %alm_hbm.1, bf16[64,512,256]{2,1,0:T(8,128)(2,1)} %table_hbm.3), custom_call_target="tpu_custom_call" | custom-call | flops 301989888 | bytes 17956864 | tf_op jit(solution)/shard_map/pallas_call | solution.py:329
  13.2 7.3 %all-to-all-start = ((bf16[32,72,128]{2,1,0:T(8,128)(2,1)}), bf16[32,72,128]{2,1,0:T(8,128)(2,1)S(1)}, u32[]{:S(2)}, u32[]{:S(2)}) async-start(bf16[32,72,128]{2,1,0:T(8,128)(2,1)} %shard_map.50), calls=%async_computation | async-start | bytes 1179648 | tf_op jit(solution)/shard_map/all_to_all | solution.py:435
  20.6 0.0 copy-done
  20.6 0.1 broadcast_in_dim.11
  20.7 1.0 %convert_element_type.27.order_ref = f32[2048,1]{1,0:T(8,128)S(1)} reshape(f32[16,2,64]{2,1,0:T(2,128)S(1)} %broadcast_in_dim.13) | data formatting | bytes 16384 | tf_op jit(solution)/shard_map/convert_element_type | solution.py:446
  21.7 0.1 reshape.91
  21.8 7.2 %shard_map.51 = bf16[4,2048,512]{2,1,0:T(8,128)(2,1)} custom-call(f32[2048,1]{1,0:T(8,128)S(1)} %convert_element_type.27.order_ref), custom_call_target="tpu_custom_call" | custom-call | flops 33554432 | bytes 8388608 | tf_op jit(solution)/shard_map/pallas_call | solution.py:72
  29.0 8.0 %all-to-all-done = bf16[32,72,128]{2,1,0:T(8,128)(2,1)S(1)} async-done(((bf16[32,72,128]{2,1,0:T(8,128)(2,1)}), bf16[32,72,128]{2,1,0:T(8,128)(2,1)S(1)}, u32[]{:S(2)}, u32[]{:S(2)}) %all-to-all-start) | async-done | bytes 589856 | tf_op jit(solution)/shard_map/all_to_all | solution.py:435
  37.0 10.0 %shard_map.52 = (f32[32,8,128]{2,1,0:T(8,128)S(1)}, bf16[16,2,8,128]{3,2,1,0:T(8,128)(2,1)}) custom-call(bf16[16,2,72,128]{3,2,1,0:T(8,128)(2,1)S(1)} %bitcast.10, f32[1,2048]{1,0:T(1,128)S(1)} %fusion.3.odd_ref, bf16[8,1024,512]{2,1,0:T(8,128)(2,1)} %bitcast.13), custom_call_target="tpu_custom_call" | custom-call | flops 1342177280 | bytes 8388608 | tf_op jit(solution)/shard_map/pallas_call | solution.py:247
  46.9 1.7 %collective-permute-start = (f32[32,8,128]{2,1,0:T(8,128)S(1)}, f32[32,8,128]{2,1,0:T(8,128)S(1)}, u32[]{:S(2)}, u32[]{:S(2)}) collective-permute-start(f32[32,8,128]{2,1,0:T(8,128)S(1)} %get-tuple-element.7), channel_id=1, source_target_pairs={{0,1},{1,0},{2,3},{3,2},{4,5},{5,4},{6,7},{7,6},{8,9},{9,8},{10,11... | collective-permute-start | bytes 393224 | tf_op jit(solution)/shard_map/ppermute | solution.py:406
  48.7 2.6 %all-to-all-start.1 = ((bf16[32,8,128]{2,1,0:T(8,128)(2,1)}), bf16[32,8,128]{2,1,0:T(8,128)(2,1)S(1)}, u32[]{:S(2)}, u32[]{:S(2)}) async-start(bf16[32,8,128]{2,1,0:T(8,128)(2,1)} %bitcast.2), calls=%async_computation.1 | async-start | bytes 131072 | tf_op jit(solution)/shard_map/all_to_all | solution.py:455
  51.2 2.1 %collective-permute-done = f32[32,8,128]{2,1,0:T(8,128)S(1)} collective-permute-done((f32[32,8,128]{2,1,0:T(8,128)S(1)}, f32[32,8,128]{2,1,0:T(8,128)S(1)}, u32[]{:S(2)}, u32[]{:S(2)}) %collective-permute-start) | collective-permute-done | bytes 131104 | tf_op jit(solution)/shard_map/ppermute | solution.py:406
  53.3 0.1 fusion.2
  53.4 0.1 fusion
  53.5 0.2 copy.6
  53.8 0.9 %reshape.94 = f32[16,2048]{1,0:T(8,128)} reshape(f32[2,8,64,32]{3,2,1,0:T(8,128)S(1)} %copy.6) | data formatting | bytes 262144 | tf_op jit(solution)/shard_map/reshape | solution.py:459
  54.7 4.2 %all-to-all-done.1 = bf16[32,8,128]{2,1,0:T(8,128)(2,1)S(1)} async-done(((bf16[32,8,128]{2,1,0:T(8,128)(2,1)}), bf16[32,8,128]{2,1,0:T(8,128)(2,1)S(1)}, u32[]{:S(2)}, u32[]{:S(2)}) %all-to-all-start.1) | async-done | bytes 65568 | tf_op jit(solution)/shard_map/all_to_all | solution.py:455
  58.8 8.4 %shard_map.53 = f32[64,2,512]{2,1,0:T(2,128)} custom-call(bf16[64,512,256]{2,1,0:T(8,128)(2,1)} %table_hbm.3, bf16[256,128]{1,0:T(8,128)(2,1)S(1)} %bitcast.11), custom_call_target="tpu_custom_call" | custom-call | flops 268435456 | bytes 16777216 | tf_op jit(solution)/shard_map/pallas_call | solution.py:383
  (4 shorter events, 0.1 us)
Async XLA Ops:
  0.6 19.9 %copy-start = (s32[1024]{0:T(1024)S(1)}, s32[1024]{0:T(1024)}, u32[]{:S(2)}) copy-start(s32[1024]{0:T(1024)} %param.5) | copy-start | bytes 12292
  13.2 23.7 %all-to-all-start = ((bf16[32,72,128]{2,1,0:T(8,128)(2,1)}), bf16[32,72,128]{2,1,0:T(8,128)(2,1)S(1)}, u32[]{:S(2)}, u32[]{:S(2)}) async-start(bf16[32,72,128]{2,1,0:T(8,128)(2,1)} %shard_map.50), calls=%async_computation | async-start | bytes 1179648 | tf_op jit(solution)/shard_map/all_to_all | solution.py:435
  46.9 6.4 %collective-permute-start = (f32[32,8,128]{2,1,0:T(8,128)S(1)}, f32[32,8,128]{2,1,0:T(8,128)S(1)}, u32[]{:S(2)}, u32[]{:S(2)}) collective-permute-start(f32[32,8,128]{2,1,0:T(8,128)S(1)} %get-tuple-element.7), channel_id=1, source_target_pairs={{0,1},{1,0},{2,3},{3,2},{4,5},{5,4},{6,7},{7,6},{8,9},{9,8},{10,11... | collective-permute-start | bytes 393224 | tf_op jit(solution)/shard_map/ppermute | solution.py:406
  48.7 10.2 %all-to-all-start.1 = ((bf16[32,8,128]{2,1,0:T(8,128)(2,1)}), bf16[32,8,128]{2,1,0:T(8,128)(2,1)S(1)}, u32[]{:S(2)}, u32[]{:S(2)}) async-start(bf16[32,8,128]{2,1,0:T(8,128)(2,1)} %bitcast.2), calls=%async_computation.1 | async-start | bytes 131072 | tf_op jit(solution)/shard_map/all_to_all | solution.py:455

commit v8 on v6

--- a/solution.py
+++ b/solution.py
@@ -23,8 +23,9 @@
 PAIRS = [(a_at, b_at) for a_at in range(REST) for b_at in range(a_at, REST)] + [(a_at, REST) for a_at in range(REST)]
 SUMS = len(PAIRS) + 1
 VMEM_LIMIT = 48 * 1024 * 1024
+IN_FLIGHT = 6
+HALVES = 2
 CHUNK = 8
-IN_FLIGHT = 3
 
 
 def round_up(value, multiple):
@@ -51,7 +52,7 @@
     scaling = 1.0 / math.sqrt(L)
     for first in range(0, order_ref.shape[0], rows):
         span = slice(first, first + rows)
-        part = (row + (begin + first)) // slots % 2
+        part = (row + (begin + first)) // (slots // HALVES) % 2
         order = jnp.broadcast_to(order_ref[span, :], (rows, LANES))
         turns = order * cell + part.astype(jnp.float32) * 0.25
         step = order * (2.0 / NLON)
@@ -89,16 +90,14 @@
     return pltpu.make_async_copy(source.at[span], target.at[span], sems.at[part])
 
 
-def start_some(source, target, sems):
-    for part in range(min(IN_FLIGHT, sems.shape[0])):
+def start_parts(source, target, sems, count):
+    for part in range(min(count, sems.shape[0])):
         part_copy(source, target, sems, part).start()
 
 
 def next_part(source, target, sems, part):
     part_copy(source, target, sems, part).wait()
-
-    @pl.when(part + IN_FLIGHT < sems.shape[0])
-    def _():
+    if part + IN_FLIGHT < sems.shape[0]:
         part_copy(source, target, sems, part + IN_FLIGHT).start()
 
 
@@ -142,7 +141,7 @@
     chunks = basis_ref.shape[0] // pieces
     cycles = rows // C
     second = round_up(rows, 16)
-    start_some(basis_hbm, basis_ref, sems)
+    start_parts(basis_hbm, basis_ref, sems, IN_FLIGHT)
     for group in range(groups):
         span = slice(group * width, (group + 1) * width)
         odd = odd_ref[:, span]
@@ -279,30 +278,26 @@
     )(modes, odd, basis)
 
 
-def modes_kernel(alm_hbm, table_hbm, out_ref, alm_ref, table_ref, lhs_ref, held_ref, turned_ref, alm_sem, sems):
+def modes_kernel(alm_hbm, table_hbm, out_ref, alm_ref, table_ref, lhs_ref, held_ref, turned_ref, alm_sems, sems):
     parts = sems.shape[0]
-    total_slots = table_ref.shape[0]
+    total_slots, _, total = table_ref.shape
     slots = total_slots // parts
     targets, rows = out_ref.shape[:2]
     cycles = rows // C
     height = held_ref.shape[1] // total_slots
-    total = table_ref.shape[2]
-    alm_copy = pltpu.make_async_copy(alm_hbm, alm_ref, alm_sem)
-    alm_copy.start()
-    start_some(table_hbm, table_ref, sems)
+    start_parts(alm_hbm, alm_ref, alm_sems, parts)
+    start_parts(table_hbm, table_ref, sems, IN_FLIGHT)
     lhs_ref[...] = jnp.zeros_like(lhs_ref)
-    alm_copy.wait()
 
     def stack_rows(part):
+        part_copy(alm_hbm, alm_ref, alm_sems, part).wait()
         for slot in range(slots):
             first = slot % 2 * height
             for chan in range(C):
                 span = slice(first + 2 * chan, first + 2 * chan + 2)
                 lhs_ref[part % 2, slot // 2, span, :] = alm_ref[part * slots + slot, chan].astype(jnp.float32)
 
-    stack_rows(0)
-
-    def some_slots(part, carry):
+    def some_slots(part):
         next_part(table_hbm, table_ref, sems, part)
         for pair in range(slots // 2):
             at = part * slots + 2 * pair
@@ -310,19 +305,27 @@
             lhs = lhs_ref[part % 2, pair].astype(jnp.bfloat16)
             result = jnp.dot(lhs, both, preferred_element_type=jnp.float32)
             for slot in range(2):
-                rows = pl.ds(pl.multiple_of((at + slot) * height, 8), height)
+                rows = slice((at + slot) * height, (at + slot + 1) * height)
                 own = result[slot * height : (slot + 1) * height, slot * total : (slot + 1) * total]
                 for lanes in range(held_ref.shape[0]):
                     held_ref[lanes, rows, :] = own[:, lanes * LANES : (lanes + 1) * LANES]
 
-        stack_rows(jnp.minimum(part + 1, parts - 1))
-        return carry
-
-    lax.fori_loop(0, parts, some_slots, 0)
-    for chan in range(C):
-        for lanes in range(held_ref.shape[0]):
-            both = [held_ref[lanes, pl.ds(2 * chan + part, total_slots, stride=height), :] for part in range(2)]
-            turned_ref[chan, lanes * LANES : (lanes + 1) * LANES, :] = jnp.concatenate(both, axis=0).T
+    def turn(half):
+        count = total_slots // HALVES
+        first = half * count * height
+        for chan in range(C):
+            for lanes in range(held_ref.shape[0]):
+                both = [held_ref[lanes, pl.ds(first + 2 * chan + part, count, stride=height), :] for part in range(2)]
+                span = slice(half * 2 * count, (half + 1) * 2 * count)
+                turned_ref[chan, lanes * LANES : (lanes + 1) * LANES, span] = jnp.concatenate(both, axis=0).T
+
+    stack_rows(0)
+    for part in range(parts):
+        if part + 1 < parts:
+            stack_rows(part + 1)
+        some_slots(part)
+        if (part + 1) * HALVES % parts == 0:
+            turn((part + 1) * HALVES // parts - 1)
     for target in range(targets):
         span = slice(target * cycles, (target + 1) * cycles)
         block = jnp.concatenate([turned_ref[chan, span, :] for chan in range(C)], axis=0)
@@ -346,7 +349,7 @@
             pltpu.VMEM((2, slots // 2, 2 * height, degrees), jnp.float32),
             pltpu.VMEM((total // LANES, slot_count * height, LANES), jnp.float32),
             pltpu.VMEM((C, total, width), jnp.float32),
-            pltpu.SemaphoreType.DMA,
+            pltpu.SemaphoreType.DMA((parts,)),
             pltpu.SemaphoreType.DMA((parts,)),
         ],
         cost_estimate=pl.CostEstimate(
@@ -362,26 +365,21 @@
     total_slots, degrees, total = table_ref.shape
     slots = 8
     pieces = sems.shape[0] * slots // total_slots
-    few = slots // pieces
-    start_some(table_hbm, table_ref, sems)
+    start_parts(table_hbm, table_ref, sems, IN_FLIGHT)
     turned_ref[...] = spectra_ref[...].astype(jnp.float32).T
-
-    def some_slots(part, carry):
-        first = pl.multiple_of(part * slots, slots)
-        rows = [turned_ref[pl.ds(first + share * total_slots, slots), :] for share in range(2)]
+    count = total_slots // HALVES
+    for first in range(0, total_slots, slots):
+        row = first // count * 2 * count + first % count
+        rows = [turned_ref[row + share * count : row + share * count + slots, :] for share in range(2)]
         lhs = jnp.concatenate(rows, axis=0).astype(jnp.bfloat16)
         for piece in range(pieces):
-            next_part(table_hbm, table_ref, sems, part * pieces + piece)
-            table = table_ref[pl.ds(first + piece * few, few)].reshape(few * degrees, total)
-            result = lax.dot_general(lhs, table, (((1,), (1,)), ((), ())), preferred_element_type=jnp.float32)
-            for at in range(few):
-                slot = piece * few + at
-                span = slice(at * degrees, (at + 1) * degrees)
-                out_ref[first + slot, 0:1, :] = result[slot : slot + 1, span]
-                out_ref[first + slot, 1:2, :] = result[slots + slot : slots + slot + 1, span]
-        return carry
-
-    lax.fori_loop(0, total_slots // slots, some_slots, 0)
+            next_part(table_hbm, table_ref, sems, first // slots * pieces + piece)
+        table = table_ref[first : first + slots].reshape(slots * degrees, total)
+        result = lax.dot_general(lhs, table, (((1,), (1,)), ((), ())), preferred_element_type=jnp.float32)
+        for slot in range(slots):
+            span = slice(slot * degrees, (slot + 1) * degrees)
+            out_ref[first + slot, 0:1, :] = result[slot : slot + 1, span]
+            out_ref[first + slot, 1:2, :] = result[slots + slot : slots + slot + 1, span]
 
 
 def analyse(legendre, spectra):
@@ -450,8 +448,8 @@
         modes = jnp.pad(modes, ((0, 0), (0, 0), (0, padded - cycles), (0, 0)))
         modes = modes.reshape(groups, 1, C * padded, group_width)
 
-    order_rows = jnp.broadcast_to(order_of_slot.reshape(band_count, 1, slot_count), (band_count, 2, slot_count))
-    order_rows = order_rows.reshape(depth)
+    order_rows = order_of_slot.reshape(band_count * HALVES, 1, slot_count // HALVES)
+    order_rows = jnp.broadcast_to(order_rows, (band_count * HALVES, 2, slot_count // HALVES)).reshape(depth)
     basis = make_basis(order_rows.astype(jnp.float32)[:, None], slot_count)
     odd = (order_rows % 2).astype(jnp.float32)[None, :]
     vectors, spectra = run_ilc(modes, odd, basis)

time: 67.4 us -> 63.9 us (0.948)
  Pallas kernels: 37.9 us -> 34.4 us
    pallas_call x1, Pallas kernels: 9.37 us -> 7.82 us  [analyse(): pl.pallas_call(analysis_kernel, in_specs=[pl.BlockSpec(memory_space=pl.AN...]
    pallas_call x1, Pallas kernels: 11.1 us -> 10 us  [run_ilc(): pl.pallas_call(ilc_kernel, in_specs=[vmem, vmem, pl.BlockSpec(memory_spac...]
    pallas_call x1, Pallas kernels: 10.4 us -> 9.38 us  [make_modes(): pl.pallas_call(modes_kernel, in_specs=[pl.BlockSpec(memory_space=pl.ANY)]...]
where the time goes in v8:
time: 63.9 us; the launch traced here: 63.6 us
  Pallas kernels  34.4 us (54%)
  waiting for transfers between devices  14 us (22%)
  starting transfers between devices  11.8 us (18%)
  local copies, waits for them, and re-layouts  2.42 us (4%)
  between operations  0.88 us (1%)
    pallas_call x1, Pallas kernels, run_ilc(): pl.pallas_call(ilc_kernel, in_specs=[vmem, vmem, pl.BlockSpec(memory_spac...  10 us
    pallas_call x1, Pallas kernels, make_modes(): pl.pallas_call(modes_kernel, in_specs=[pl.BlockSpec(memory_space=pl.ANY)]...  9.38 us
    all_to_all x1, waiting for transfers between devices, body(): lax.all_to_all(partial, axes, split_axis=0, concat_axis=0, tiled=True)  7.87 us
    pallas_call x1, Pallas kernels, analyse(): pl.pallas_call(analysis_kernel, in_specs=[pl.BlockSpec(memory_space=pl.AN...  7.82 us
    all_to_all x1, starting transfers between devices, body(): lax.all_to_all(partial, axes, split_axis=0, concat_axis=0, tiled=True)  7.3 us
    pallas_call x1, Pallas kernels, make_basis(): pl.pallas_call(functools.partial(basis_kernel, slots), grid=(rows // bloc...  7.17 us
    all_to_all x1, waiting for transfers between devices, body(): lax.all_to_all(spectra, axes, split_axis=0, concat_axis=0, tiled=True)  4.18 us
    all_to_all x1, starting transfers between devices, body(): lax.all_to_all(spectra, axes, split_axis=0, concat_axis=0, tiled=True)  2.75 us
  transfers between devices with their start and end apart: 3, of which 3 were waited for; matrix products, arithmetic and copies ran while one was open for 4% of the time, Pallas kernels for 11%

profile of v8, /device:TPU:0, one launch (start us, length us, event | category | flops | bytes accessed | tf_op | source)
XLA Modules:
  0.0 63.6 jit_solution(17197704286954030470)
XLA Ops:
  0.6 0.0 copy-start
  0.6 9.4 %shard_map.50 = bf16[32,72,128]{2,1,0:T(8,128)(2,1)} custom-call(bf16[64,9,2,512]{3,2,1,0:T(2,128)(2,1)} %alm_hbm.1, bf16[64,512,256]{2,1,0:T(8,128)(2,1)} %table_hbm.3), custom_call_target="tpu_custom_call" | custom-call | flops 301989888 | bytes 17956864 | tf_op jit(solution)/shard_map/pallas_call | solution.py:341
  10.0 7.3 %all-to-all-start = ((bf16[32,72,128]{2,1,0:T(8,128)(2,1)}), bf16[32,72,128]{2,1,0:T(8,128)(2,1)S(1)}, u32[]{:S(2)}, u32[]{:S(2)}) async-start(bf16[32,72,128]{2,1,0:T(8,128)(2,1)} %shard_map.50), calls=%async_computation | async-start | bytes 1179648 | tf_op jit(solution)/shard_map/all_to_all | solution.py:442
  17.3 0.0 copy-done
  17.3 0.1 broadcast_in_dim.11
  17.4 1.1 %convert_element_type.27.order_ref = f32[2048,1]{1,0:T(8,128)S(1)} reshape(f32[32,2,32]{2,1,0:T(2,128)S(1)} %broadcast_in_dim.13) | data formatting | bytes 16384 | tf_op jit(solution)/shard_map/convert_element_type | solution.py:453
  18.6 0.1 reshape.91
  18.7 7.2 %shard_map.51 = bf16[4,2048,512]{2,1,0:T(8,128)(2,1)} custom-call(f32[2048,1]{1,0:T(8,128)S(1)} %convert_element_type.27.order_ref), custom_call_target="tpu_custom_call" | custom-call | flops 33554432 | bytes 8388608 | tf_op jit(solution)/shard_map/pallas_call | solution.py:74
  25.9 7.9 %all-to-all-done = bf16[32,72,128]{2,1,0:T(8,128)(2,1)S(1)} async-done(((bf16[32,72,128]{2,1,0:T(8,128)(2,1)}), bf16[32,72,128]{2,1,0:T(8,128)(2,1)S(1)}, u32[]{:S(2)}, u32[]{:S(2)}) %all-to-all-start) | async-done | bytes 589856 | tf_op jit(solution)/shard_map/all_to_all | solution.py:442
  33.7 10.0 %shard_map.52 = (f32[32,8,128]{2,1,0:T(8,128)S(1)}, bf16[16,2,8,128]{3,2,1,0:T(8,128)(2,1)}) custom-call(bf16[16,2,72,128]{3,2,1,0:T(8,128)(2,1)S(1)} %bitcast.10, f32[1,2048]{1,0:T(1,128)S(1)} %fusion.3.odd_ref, bf16[8,1024,512]{2,1,0:T(8,128)(2,1)} %bitcast.13), custom_call_target="tpu_custom_call" | custom-call | flops 1342177280 | bytes 8388608 | tf_op jit(solution)/shard_map/pallas_call | solution.py:255
  43.8 1.7 %collective-permute-start = (f32[32,8,128]{2,1,0:T(8,128)S(1)}, f32[32,8,128]{2,1,0:T(8,128)S(1)}, u32[]{:S(2)}, u32[]{:S(2)}) collective-permute-start(f32[32,8,128]{2,1,0:T(8,128)S(1)} %get-tuple-element.7), channel_id=1, source_target_pairs={{0,1},{1,0},{2,3},{3,2},{4,5},{5,4},{6,7},{7,6},{8,9},{9,8},{10,11... | collective-permute-start | bytes 393224 | tf_op jit(solution)/shard_map/ppermute | solution.py:413
  45.5 2.8 %all-to-all-start.1 = ((bf16[32,8,128]{2,1,0:T(8,128)(2,1)}), bf16[32,8,128]{2,1,0:T(8,128)(2,1)S(1)}, u32[]{:S(2)}, u32[]{:S(2)}) async-start(bf16[32,8,128]{2,1,0:T(8,128)(2,1)} %bitcast.2), calls=%async_computation.1 | async-start | bytes 131072 | tf_op jit(solution)/shard_map/all_to_all | solution.py:462
  48.2 1.9 %collective-permute-done = f32[32,8,128]{2,1,0:T(8,128)S(1)} collective-permute-done((f32[32,8,128]{2,1,0:T(8,128)S(1)}, f32[32,8,128]{2,1,0:T(8,128)S(1)}, u32[]{:S(2)}, u32[]{:S(2)}) %collective-permute-start) | collective-permute-done | bytes 131104 | tf_op jit(solution)/shard_map/ppermute | solution.py:413
  50.2 0.1 fusion.2
  50.2 0.1 fusion
  50.4 0.2 copy.6
  50.6 0.9 %reshape.94 = f32[16,2048]{1,0:T(8,128)} reshape(f32[2,8,64,32]{3,2,1,0:T(8,128)S(1)} %copy.6) | data formatting | bytes 262144 | tf_op jit(solution)/shard_map/reshape | solution.py:466
  51.5 4.2 %all-to-all-done.1 = bf16[32,8,128]{2,1,0:T(8,128)(2,1)S(1)} async-done(((bf16[32,8,128]{2,1,0:T(8,128)(2,1)}), bf16[32,8,128]{2,1,0:T(8,128)(2,1)S(1)}, u32[]{:S(2)}, u32[]{:S(2)}) %all-to-all-start.1) | async-done | bytes 65568 | tf_op jit(solution)/shard_map/all_to_all | solution.py:462
  55.7 7.8 %shard_map.53 = f32[64,2,512]{2,1,0:T(2,128)} custom-call(bf16[64,512,256]{2,1,0:T(8,128)(2,1)} %table_hbm.3, bf16[256,128]{1,0:T(8,128)(2,1)S(1)} %bitcast.11), custom_call_target="tpu_custom_call" | custom-call | flops 268435456 | bytes 16777216 | tf_op jit(solution)/shard_map/pallas_call | solution.py:390
  (4 shorter events, 0.1 us)
Async XLA Ops:
  0.6 16.7 %copy-start = (s32[1024]{0:T(1024)S(1)}, s32[1024]{0:T(1024)}, u32[]{:S(2)}) copy-start(s32[1024]{0:T(1024)} %param.5) | copy-start | bytes 12292
  10.0 23.7 %all-to-all-start = ((bf16[32,72,128]{2,1,0:T(8,128)(2,1)}), bf16[32,72,128]{2,1,0:T(8,128)(2,1)S(1)}, u32[]{:S(2)}, u32[]{:S(2)}) async-start(bf16[32,72,128]{2,1,0:T(8,128)(2,1)} %shard_map.50), calls=%async_computation | async-start | bytes 1179648 | tf_op jit(solution)/shard_map/all_to_all | solution.py:442
  43.8 6.4 %collective-permute-start = (f32[32,8,128]{2,1,0:T(8,128)S(1)}, f32[32,8,128]{2,1,0:T(8,128)S(1)}, u32[]{:S(2)}, u32[]{:S(2)}) collective-permute-start(f32[32,8,128]{2,1,0:T(8,128)S(1)} %get-tuple-element.7), channel_id=1, source_target_pairs={{0,1},{1,0},{2,3},{3,2},{4,5},{5,4},{6,7},{7,6},{8,9},{9,8},{10,11... | collective-permute-start | bytes 393224 | tf_op jit(solution)/shard_map/ppermute | solution.py:413
  45.5 10.2 %all-to-all-start.1 = ((bf16[32,8,128]{2,1,0:T(8,128)(2,1)}), bf16[32,8,128]{2,1,0:T(8,128)(2,1)S(1)}, u32[]{:S(2)}, u32[]{:S(2)}) async-start(bf16[32,8,128]{2,1,0:T(8,128)(2,1)} %bitcast.2), calls=%async_computation.1 | async-start | bytes 131072 | tf_op jit(solution)/shard_map/all_to_all | solution.py:462

commit v9 on v8

--- a/solution.py
+++ b/solution.py
@@ -106,7 +106,7 @@
     return guess * (2.0 - value * guess)
 
 
-def combine(sum_of, map_of):
+def combine_steps(sum_of, map_of):
     ridge = RIDGE * (sum_of(SUMS - 1) * (1.0 / C) + WINDOW * EPSILON)
     upper, inverses, rights, maps = {}, [], [], []
     value = map_of(REST)
@@ -116,21 +116,30 @@
         for at in range(row):
             pivot = pivot - ratios[at] * upper[at, row]
         inverse = reciprocal(pivot)
+        yield None
         right = ridge - sum_of(PAIRS.index((row, REST)))
         own = map_of(row)
         for at in range(row):
             right = right - ratios[at] * rights[at]
             own = own - ratios[at] * maps[at]
+        yield None
         for col in range(row + 1, REST):
             entry = sum_of(PAIRS.index((row, col))) + ridge
             for at in range(row):
                 entry = entry - ratios[at] * upper[at, col]
             upper[row, col] = entry
+            yield None
         value = value + (right * inverse) * own
         inverses.append(inverse)
         rights.append(right)
         maps.append(own)
-    return value
+    yield value
+
+
+def in_step(generators):
+    for found in zip(*generators):
+        pass
+    return found
 
 
 def ilc_kernel(modes_ref, odd_ref, basis_hbm, ilc_ref, spectra_ref, basis_ref, lhs_ref, maps_ref, sums_ref, low_ref, found_ref, sems):
@@ -202,20 +211,19 @@
         total = sums_ref[pair]
         sums_ref[pair] = pltpu.roll(total, 1, 1) + pltpu.roll(total, 2, 1)
 
-    def solve(at):
+    def solve_steps(at):
         def sum_of(pair):
             own = product(at, pair)
             total = sums_ref[pair] + own
             sums_ref[pair] = total - pltpu.roll(own, 2, 1)
             return total
 
-        value = combine(sum_of, lambda chan: pltpu.roll(maps_ref[at, chan], 1, 1))
-        value = pltpu.roll(value, LANES - 1, 1)
-        ilc_ref[at] = value
-        return value
+        return combine_steps(sum_of, lambda chan: pltpu.roll(maps_ref[at, chan], 1, 1))
 
     def two_vectors(at):
-        found = [solve(at), solve(at + 1)]
+        found = [pltpu.roll(value, LANES - 1, 1) for value in in_step([solve_steps(at), solve_steps(at + 1)])]
+        ilc_ref[at] = found[0]
+        ilc_ref[at + 1] = found[1]
         near = jnp.where(low_half, found[0], pltpu.roll(found[1], HALF, 1))
         far = jnp.where(low_half, pltpu.roll(found[0], HALF, 1), found[1])
         return jnp.concatenate([near, far], axis=0).astype(jnp.bfloat16)
@@ -278,7 +286,9 @@
     )(modes, odd, basis)
 
 
-def modes_kernel(alm_hbm, table_hbm, out_ref, alm_ref, table_ref, lhs_ref, held_ref, turned_ref, alm_sems, sems):
+def modes_kernel(
+    alm_hbm, table_hbm, out_hbm, alm_ref, table_ref, lhs_ref, held_ref, turned_ref, out_ref, alm_sems, sems, out_sems
+):
     parts = sems.shape[0]
     total_slots, _, total = table_ref.shape
     slots = total_slots // parts
@@ -326,10 +336,15 @@
         some_slots(part)
         if (part + 1) * HALVES % parts == 0:
             turn((part + 1) * HALVES // parts - 1)
+    each = targets // out_sems.shape[0]
     for target in range(targets):
         span = slice(target * cycles, (target + 1) * cycles)
         block = jnp.concatenate([turned_ref[chan, span, :] for chan in range(C)], axis=0)
         out_ref[target] = block.astype(jnp.bfloat16)
+        if (target + 1) % each == 0:
+            part_copy(out_ref, out_hbm, out_sems, target // each).start()
+    for part in range(out_sems.shape[0]):
+        part_copy(out_ref, out_hbm, out_sems, part).wait()
 
 
 def make_modes(alm, legendre, targets):
@@ -338,19 +353,22 @@
     parts = slot_count // slots
     width = 2 * slot_count
     height = round_up(2 * C, 8)
+    out = jax.ShapeDtypeStruct((targets, C * (total // targets), width), jnp.bfloat16)
     return pl.pallas_call(
         modes_kernel,
         in_specs=[pl.BlockSpec(memory_space=pl.ANY)] * 2,
-        out_specs=pl.BlockSpec(memory_space=pltpu.VMEM),
-        out_shape=jax.ShapeDtypeStruct((targets, C * (total // targets), width), jnp.bfloat16),
+        out_specs=pl.BlockSpec(memory_space=pl.ANY),
+        out_shape=out,
         scratch_shapes=[
             pltpu.VMEM(alm.shape, jnp.bfloat16),
             pltpu.VMEM(legendre.shape, jnp.bfloat16),
             pltpu.VMEM((2, slots // 2, 2 * height, degrees), jnp.float32),
             pltpu.VMEM((total // LANES, slot_count * height, LANES), jnp.float32),
             pltpu.VMEM((C, total, width), jnp.float32),
+            pltpu.VMEM(out.shape, out.dtype),
             pltpu.SemaphoreType.DMA((parts,)),
             pltpu.SemaphoreType.DMA((parts,)),
+            pltpu.SemaphoreType.DMA((4,)),
         ],
         cost_estimate=pl.CostEstimate(
             flops=2 * slot_count * degrees * total * 2 * C,
@@ -361,25 +379,31 @@
     )(alm, legendre)
 
 
-def analysis_kernel(table_hbm, spectra_ref, out_ref, table_ref, turned_ref, sems):
+def analysis_kernel(table_hbm, spectra_ref, out_hbm, table_ref, turned_ref, out_ref, sems, out_sems):
     total_slots, degrees, total = table_ref.shape
     slots = 8
-    pieces = sems.shape[0] * slots // total_slots
+    few = total_slots // sems.shape[0]
     start_parts(table_hbm, table_ref, sems, IN_FLIGHT)
     turned_ref[...] = spectra_ref[...].astype(jnp.float32).T
     count = total_slots // HALVES
-    for first in range(0, total_slots, slots):
-        row = first // count * 2 * count + first % count
+    each = total_slots // out_sems.shape[0]
+    for first in range(0, total_slots, few):
+        group = first // slots * slots
+        row = group // count * 2 * count + group % count
         rows = [turned_ref[row + share * count : row + share * count + slots, :] for share in range(2)]
         lhs = jnp.concatenate(rows, axis=0).astype(jnp.bfloat16)
-        for piece in range(pieces):
-            next_part(table_hbm, table_ref, sems, first // slots * pieces + piece)
-        table = table_ref[first : first + slots].reshape(slots * degrees, total)
+        next_part(table_hbm, table_ref, sems, first // few)
+        table = table_ref[first : first + few].reshape(few * degrees, total)
         result = lax.dot_general(lhs, table, (((1,), (1,)), ((), ())), preferred_element_type=jnp.float32)
-        for slot in range(slots):
-            span = slice(slot * degrees, (slot + 1) * degrees)
-            out_ref[first + slot, 0:1, :] = result[slot : slot + 1, span]
-            out_ref[first + slot, 1:2, :] = result[slots + slot : slots + slot + 1, span]
+        for at in range(few):
+            slot = first - group + at
+            span = slice(at * degrees, (at + 1) * degrees)
+            out_ref[first + at, 0:1, :] = result[slot : slot + 1, span]
+            out_ref[first + at, 1:2, :] = result[slots + slot : slots + slot + 1, span]
+        if (first + few) % each == 0:
+            part_copy(out_ref, out_hbm, out_sems, first // each).start()
+    for part in range(out_sems.shape[0]):
+        part_copy(out_ref, out_hbm, out_sems, part).wait()
 
 
 def analyse(legendre, spectra):
@@ -390,12 +414,14 @@
     return pl.pallas_call(
         analysis_kernel,
         in_specs=[pl.BlockSpec(memory_space=pl.ANY), vmem],
-        out_specs=vmem,
+        out_specs=pl.BlockSpec(memory_space=pl.ANY),
         out_shape=jax.ShapeDtypeStruct((slot_count, 2, degrees), jnp.float32),
         scratch_shapes=[
             pltpu.VMEM(legendre.shape, jnp.bfloat16),
             pltpu.VMEM((width, total), jnp.float32),
+            pltpu.VMEM((slot_count, 2, degrees), jnp.float32),
             pltpu.SemaphoreType.DMA((slot_count // 4,)),
+            pltpu.SemaphoreType.DMA((4,)),
         ],
         cost_estimate=pl.CostEstimate(
             flops=2 * slot_count * degrees * total * 2 * slots,

time: 63.9 us -> 64.3 us (level)
  no operation moved by 1% of the time
where the time goes in v9:
time: 64.3 us; the launch traced here: 64.1 us
  Pallas kernels  34.8 us (54%)
  waiting for transfers between devices  14 us (22%)
  starting transfers between devices  11.8 us (18%)
  local copies, waits for them, and re-layouts  2.42 us (4%)
  between operations  0.88 us (1%)
    pallas_call x1, Pallas kernels, run_ilc(): pl.pallas_call(ilc_kernel, in_specs=[vmem, vmem, pl.BlockSpec(memory_spac...  9.96 us
    pallas_call x1, Pallas kernels, make_modes(): pl.pallas_call(modes_kernel, in_specs=[pl.BlockSpec(memory_space=pl.ANY)]...  9.34 us
    pallas_call x1, Pallas kernels, analyse(): pl.pallas_call(analysis_kernel, in_specs=[pl.BlockSpec(memory_space=pl.AN...  8.34 us
    all_to_all x1, waiting for transfers between devices, body(): lax.all_to_all(partial, axes, split_axis=0, concat_axis=0, tiled=True)  7.87 us
    all_to_all x1, starting transfers between devices, body(): lax.all_to_all(partial, axes, split_axis=0, concat_axis=0, tiled=True)  7.3 us
    pallas_call x1, Pallas kernels, make_basis(): pl.pallas_call(functools.partial(basis_kernel, slots), grid=(rows // bloc...  7.17 us
    all_to_all x1, waiting for transfers between devices, body(): lax.all_to_all(spectra, axes, split_axis=0, concat_axis=0, tiled=True)  4.18 us
    all_to_all x1, starting transfers between devices, body(): lax.all_to_all(spectra, axes, split_axis=0, concat_axis=0, tiled=True)  2.75 us
  transfers between devices with their start and end apart: 3, of which 3 were waited for; matrix products, arithmetic and copies ran while one was open for 4% of the time, Pallas kernels for 11%

profile of v9, /device:TPU:0, one launch (start us, length us, event | category | flops | bytes accessed | tf_op | source)
XLA Modules:
  0.0 64.1 jit_solution(8224946948834291086)
XLA Ops:
  0.6 0.0 copy-start
  0.6 9.3 %shard_map.50 = bf16[32,72,128]{2,1,0:T(8,128)(2,1)} custom-call(bf16[64,9,2,512]{3,2,1,0:T(2,128)(2,1)} %alm_hbm.1, bf16[64,512,256]{2,1,0:T(8,128)(2,1)} %table_hbm.3), custom_call_target="tpu_custom_call" | custom-call | flops 301989888 | bytes 17956864 | tf_op jit(solution)/shard_map/pallas_call | solution.py:357
  10.0 7.3 %all-to-all-start = ((bf16[32,72,128]{2,1,0:T(8,128)(2,1)}), bf16[32,72,128]{2,1,0:T(8,128)(2,1)S(1)}, u32[]{:S(2)}, u32[]{:S(2)}) async-start(bf16[32,72,128]{2,1,0:T(8,128)(2,1)} %shard_map.50), calls=%async_computation | async-start | bytes 1179648 | tf_op jit(solution)/shard_map/all_to_all | solution.py:468
  17.3 0.0 copy-done
  17.3 0.1 broadcast_in_dim.11
  17.4 1.1 %convert_element_type.27.order_ref = f32[2048,1]{1,0:T(8,128)S(1)} reshape(f32[32,2,32]{2,1,0:T(2,128)S(1)} %broadcast_in_dim.13) | data formatting | bytes 16384 | tf_op jit(solution)/shard_map/convert_element_type | solution.py:479
  18.5 0.1 reshape.91
  18.6 7.2 %shard_map.51 = bf16[4,2048,512]{2,1,0:T(8,128)(2,1)} custom-call(f32[2048,1]{1,0:T(8,128)S(1)} %convert_element_type.27.order_ref), custom_call_target="tpu_custom_call" | custom-call | flops 33554432 | bytes 8388608 | tf_op jit(solution)/shard_map/pallas_call | solution.py:74
  25.8 7.9 %all-to-all-done = bf16[32,72,128]{2,1,0:T(8,128)(2,1)S(1)} async-done(((bf16[32,72,128]{2,1,0:T(8,128)(2,1)}), bf16[32,72,128]{2,1,0:T(8,128)(2,1)S(1)}, u32[]{:S(2)}, u32[]{:S(2)}) %all-to-all-start) | async-done | bytes 589856 | tf_op jit(solution)/shard_map/all_to_all | solution.py:468
  33.7 10.0 %shard_map.52 = (f32[32,8,128]{2,1,0:T(8,128)S(1)}, bf16[16,2,8,128]{3,2,1,0:T(8,128)(2,1)}) custom-call(bf16[16,2,72,128]{3,2,1,0:T(8,128)(2,1)S(1)} %bitcast.10, f32[1,2048]{1,0:T(1,128)S(1)} %fusion.3.odd_ref, bf16[8,1024,512]{2,1,0:T(8,128)(2,1)} %bitcast.13), custom_call_target="tpu_custom_call" | custom-call | flops 1342177280 | bytes 8388608 | tf_op jit(solution)/shard_map/pallas_call | solution.py:263
  43.7 1.7 %collective-permute-start = (f32[32,8,128]{2,1,0:T(8,128)S(1)}, f32[32,8,128]{2,1,0:T(8,128)S(1)}, u32[]{:S(2)}, u32[]{:S(2)}) collective-permute-start(f32[32,8,128]{2,1,0:T(8,128)S(1)} %get-tuple-element.7), channel_id=1, source_target_pairs={{0,1},{1,0},{2,3},{3,2},{4,5},{5,4},{6,7},{7,6},{8,9},{9,8},{10,11... | collective-permute-start | bytes 393224 | tf_op jit(solution)/shard_map/ppermute | solution.py:439
  45.4 2.8 %all-to-all-start.1 = ((bf16[32,8,128]{2,1,0:T(8,128)(2,1)}), bf16[32,8,128]{2,1,0:T(8,128)(2,1)S(1)}, u32[]{:S(2)}, u32[]{:S(2)}) async-start(bf16[32,8,128]{2,1,0:T(8,128)(2,1)} %bitcast.2), calls=%async_computation.1 | async-start | bytes 131072 | tf_op jit(solution)/shard_map/all_to_all | solution.py:488
  48.1 1.9 %collective-permute-done = f32[32,8,128]{2,1,0:T(8,128)S(1)} collective-permute-done((f32[32,8,128]{2,1,0:T(8,128)S(1)}, f32[32,8,128]{2,1,0:T(8,128)S(1)}, u32[]{:S(2)}, u32[]{:S(2)}) %collective-permute-start) | collective-permute-done | bytes 131104 | tf_op jit(solution)/shard_map/ppermute | solution.py:439
  50.1 0.1 fusion.2
  50.1 0.1 fusion
  50.3 0.2 copy.6
  50.5 0.9 %reshape.94 = f32[16,2048]{1,0:T(8,128)} reshape(f32[2,8,64,32]{3,2,1,0:T(8,128)S(1)} %copy.6) | data formatting | bytes 262144 | tf_op jit(solution)/shard_map/reshape | solution.py:492
  51.4 4.2 %all-to-all-done.1 = bf16[32,8,128]{2,1,0:T(8,128)(2,1)S(1)} async-done(((bf16[32,8,128]{2,1,0:T(8,128)(2,1)}), bf16[32,8,128]{2,1,0:T(8,128)(2,1)S(1)}, u32[]{:S(2)}, u32[]{:S(2)}) %all-to-all-start.1) | async-done | bytes 65568 | tf_op jit(solution)/shard_map/all_to_all | solution.py:488
  55.6 8.3 %shard_map.53 = f32[64,2,512]{2,1,0:T(2,128)} custom-call(bf16[64,512,256]{2,1,0:T(8,128)(2,1)} %table_hbm.3, bf16[256,128]{1,0:T(8,128)(2,1)S(1)} %bitcast.11), custom_call_target="tpu_custom_call" | custom-call | flops 268435456 | bytes 16777216 | tf_op jit(solution)/shard_map/pallas_call | solution.py:414
  (4 shorter events, 0.1 us)
Async XLA Ops:
  0.6 16.7 %copy-start = (s32[1024]{0:T(1024)S(1)}, s32[1024]{0:T(1024)}, u32[]{:S(2)}) copy-start(s32[1024]{0:T(1024)} %param.5) | copy-start | bytes 12292
  10.0 23.7 %all-to-all-start = ((bf16[32,72,128]{2,1,0:T(8,128)(2,1)}), bf16[32,72,128]{2,1,0:T(8,128)(2,1)S(1)}, u32[]{:S(2)}, u32[]{:S(2)}) async-start(bf16[32,72,128]{2,1,0:T(8,128)(2,1)} %shard_map.50), calls=%async_computation | async-start | bytes 1179648 | tf_op jit(solution)/shard_map/all_to_all | solution.py:468
  43.7 6.4 %collective-permute-start = (f32[32,8,128]{2,1,0:T(8,128)S(1)}, f32[32,8,128]{2,1,0:T(8,128)S(1)}, u32[]{:S(2)}, u32[]{:S(2)}) collective-permute-start(f32[32,8,128]{2,1,0:T(8,128)S(1)} %get-tuple-element.7), channel_id=1, source_target_pairs={{0,1},{1,0},{2,3},{3,2},{4,5},{5,4},{6,7},{7,6},{8,9},{9,8},{10,11... | collective-permute-start | bytes 393224 | tf_op jit(solution)/shard_map/ppermute | solution.py:439
  45.4 10.2 %all-to-all-start.1 = ((bf16[32,8,128]{2,1,0:T(8,128)(2,1)}), bf16[32,8,128]{2,1,0:T(8,128)(2,1)S(1)}, u32[]{:S(2)}, u32[]{:S(2)}) async-start(bf16[32,8,128]{2,1,0:T(8,128)(2,1)} %bitcast.2), calls=%async_computation.1 | async-start | bytes 131072 | tf_op jit(solution)/shard_map/all_to_all | solution.py:488

commit v10 on v9

--- a/solution.py
+++ b/solution.py
@@ -220,31 +220,44 @@
 
         return combine_steps(sum_of, lambda chan: pltpu.roll(maps_ref[at, chan], 1, 1))
 
-    def two_vectors(at):
-        found = [pltpu.roll(value, LANES - 1, 1) for value in in_step([solve_steps(at), solve_steps(at + 1)])]
+    def two_vectors(at, beside):
+        found = in_step([solve_steps(at), solve_steps(at + 1), beside])[:2]
+        found = [pltpu.roll(value, LANES - 1, 1) for value in found]
         ilc_ref[at] = found[0]
         ilc_ref[at + 1] = found[1]
         near = jnp.where(low_half, found[0], pltpu.roll(found[1], HALF, 1))
         far = jnp.where(low_half, pltpu.roll(found[0], HALF, 1), found[1])
         return jnp.concatenate([near, far], axis=0).astype(jnp.bfloat16)
 
-    def spectra_of(chunk):
-        basis = basis_ref[pl.ds(chunk * pieces, pieces)].reshape(depth, columns)
-        return lax.dot_general(
+    share_rows = depth // (CHUNK // 2)
+    per_piece = depth // pieces // share_rows
+
+    def add_spectra(chunk, part):
+        first = part % per_piece * share_rows
+        basis = basis_ref[chunk * pieces + part // per_piece, first : first + share_rows, :]
+        found_ref[:, part * share_rows : (part + 1) * share_rows] += lax.dot_general(
             low_ref[chunk], basis, (((1,), (1,)), ((), ())), preferred_element_type=jnp.float32
         )
 
+    def spectra_steps(chunk, part):
+        for _ in range(8):
+            yield None
+        add_spectra(chunk, part)
+        while True:
+            yield None
+
     found_ref[...] = jnp.zeros_like(found_ref)
     low_ref[...] = jnp.zeros_like(low_ref)
 
     def solve_chunk(chunk, carry):
-        found_ref[...] += spectra_of(jnp.maximum(chunk - 1, 0))
-        for part in range(CHUNK // 2):
-            low_ref[chunk, :, part * LANES : (part + 1) * LANES] = two_vectors(CHUNK * chunk + 2 * part)
+        before = jnp.maximum(chunk - 1, 0)
+        found = [two_vectors(CHUNK * chunk + 2 * part, spectra_steps(before, part)) for part in range(CHUNK // 2)]
+        low_ref[chunk] = jnp.concatenate(found, axis=1)
         return carry
 
     lax.fori_loop(0, chunks, solve_chunk, 0)
-    found_ref[...] += spectra_of(chunks - 1)
+    for part in range(CHUNK // 2):
+        add_spectra(chunks - 1, part)
     for group in range(groups):
         span = slice(group * width, (group + 1) * width)
         sign = 1.0 - 2.0 * odd_ref[:, span]
@@ -299,26 +312,23 @@
     start_parts(table_hbm, table_ref, sems, IN_FLIGHT)
     lhs_ref[...] = jnp.zeros_like(lhs_ref)
 
-    def stack_rows(part):
-        part_copy(alm_hbm, alm_ref, alm_sems, part).wait()
-        for slot in range(slots):
-            first = slot % 2 * height
+    def stack_rows(part, pair):
+        for slot in range(2):
             for chan in range(C):
-                span = slice(first + 2 * chan, first + 2 * chan + 2)
-                lhs_ref[part % 2, slot // 2, span, :] = alm_ref[part * slots + slot, chan].astype(jnp.float32)
-
-    def some_slots(part):
-        next_part(table_hbm, table_ref, sems, part)
-        for pair in range(slots // 2):
-            at = part * slots + 2 * pair
-            both = jnp.concatenate([table_ref[at], table_ref[at + 1]], axis=1)
-            lhs = lhs_ref[part % 2, pair].astype(jnp.bfloat16)
-            result = jnp.dot(lhs, both, preferred_element_type=jnp.float32)
-            for slot in range(2):
-                rows = slice((at + slot) * height, (at + slot + 1) * height)
-                own = result[slot * height : (slot + 1) * height, slot * total : (slot + 1) * total]
-                for lanes in range(held_ref.shape[0]):
-                    held_ref[lanes, rows, :] = own[:, lanes * LANES : (lanes + 1) * LANES]
+                span = slice(slot * height + 2 * chan, slot * height + 2 * chan + 2)
+                own = alm_ref[part * slots + 2 * pair + slot, chan]
+                lhs_ref[part % 2, pair, span, :] = own.astype(jnp.float32)
+
+    def two_slots(part, pair):
+        at = part * slots + 2 * pair
+        both = jnp.concatenate([table_ref[at], table_ref[at + 1]], axis=1)
+        lhs = lhs_ref[part % 2, pair].astype(jnp.bfloat16)
+        result = jnp.dot(lhs, both, preferred_element_type=jnp.float32)
+        for slot in range(2):
+            rows = slice((at + slot) * height, (at + slot + 1) * height)
+            own = result[slot * height : (slot + 1) * height, slot * total : (slot + 1) * total]
+            for lanes in range(held_ref.shape[0]):
+                held_ref[lanes, rows, :] = own[:, lanes * LANES : (lanes + 1) * LANES]
 
     def turn(half):
         count = total_slots // HALVES
@@ -329,12 +339,17 @@
                 span = slice(half * 2 * count, (half + 1) * 2 * count)
                 turned_ref[chan, lanes * LANES : (lanes + 1) * LANES, span] = jnp.concatenate(both, axis=0).T
 
-    stack_rows(0)
-    for part in range(parts):
+    for part in range(-1, parts):
         if part + 1 < parts:
-            stack_rows(part + 1)
-        some_slots(part)
-        if (part + 1) * HALVES % parts == 0:
+            part_copy(alm_hbm, alm_ref, alm_sems, part + 1).wait()
+        if part >= 0:
+            next_part(table_hbm, table_ref, sems, part)
+        for pair in range(slots // 2):
+            if part >= 0:
+                two_slots(part, pair)
+            if part + 1 < parts:
+                stack_rows(part + 1, pair)
+        if (part + 1) * HALVES % parts == 0 and part >= 0:
             turn((part + 1) * HALVES // parts - 1)
     each = targets // out_sems.shape[0]
     for target in range(targets):
@@ -379,31 +394,25 @@
     )(alm, legendre)
 
 
-def analysis_kernel(table_hbm, spectra_ref, out_hbm, table_ref, turned_ref, out_ref, sems, out_sems):
+def analysis_kernel(table_hbm, spectra_ref, out_ref, table_ref, turned_ref, sems):
     total_slots, degrees, total = table_ref.shape
     slots = 8
-    few = total_slots // sems.shape[0]
+    pieces = sems.shape[0] * slots // total_slots
     start_parts(table_hbm, table_ref, sems, IN_FLIGHT)
     turned_ref[...] = spectra_ref[...].astype(jnp.float32).T
     count = total_slots // HALVES
-    each = total_slots // out_sems.shape[0]
-    for first in range(0, total_slots, few):
-        group = first // slots * slots
-        row = group // count * 2 * count + group % count
+    for first in range(0, total_slots, slots):
+        row = first // count * 2 * count + first % count
         rows = [turned_ref[row + share * count : row + share * count + slots, :] for share in range(2)]
         lhs = jnp.concatenate(rows, axis=0).astype(jnp.bfloat16)
-        next_part(table_hbm, table_ref, sems, first // few)
-        table = table_ref[first : first + few].reshape(few * degrees, total)
+        for piece in range(pieces):
+            next_part(table_hbm, table_ref, sems, first // slots * pieces + piece)
+        table = table_ref[first : first + slots].reshape(slots * degrees, total)
         result = lax.dot_general(lhs, table, (((1,), (1,)), ((), ())), preferred_element_type=jnp.float32)
-        for at in range(few):
-            slot = first - group + at
-            span = slice(at * degrees, (at + 1) * degrees)
-            out_ref[first + at, 0:1, :] = result[slot : slot + 1, span]
-            out_ref[first + at, 1:2, :] = result[slots + slot : slots + slot + 1, span]
-        if (first + few) % each == 0:
-            part_copy(out_ref, out_hbm, out_sems, first // each).start()
-    for part in range(out_sems.shape[0]):
-        part_copy(out_ref, out_hbm, out_sems, part).wait()
+        for slot in range(slots):
+            span = slice(slot * degrees, (slot + 1) * degrees)
+            out_ref[first + slot, 0:1, :] = result[slot : slot + 1, span]
+            out_ref[first + slot, 1:2, :] = result[slots + slot : slots + slot + 1, span]
 
 
 def analyse(legendre, spectra):
@@ -414,14 +423,12 @@
     return pl.pallas_call(
         analysis_kernel,
         in_specs=[pl.BlockSpec(memory_space=pl.ANY), vmem],
-        out_specs=pl.BlockSpec(memory_space=pl.ANY),
+        out_specs=vmem,
         out_shape=jax.ShapeDtypeStruct((slot_count, 2, degrees), jnp.float32),
         scratch_shapes=[
             pltpu.VMEM(legendre.shape, jnp.bfloat16),
             pltpu.VMEM((width, total), jnp.float32),
-            pltpu.VMEM((slot_count, 2, degrees), jnp.float32),
             pltpu.SemaphoreType.DMA((slot_count // 4,)),
-            pltpu.SemaphoreType.DMA((4,)),
         ],
         cost_estimate=pl.CostEstimate(
             flops=2 * slot_count * degrees * total * 2 * slots,

time: 64.3 us -> 63.7 us (level)
  no operation moved by 1% of the time
where the time goes in v10:
time: 63.7 us; the launch traced here: 63.4 us
  Pallas kernels  34.2 us (54%)
  waiting for transfers between devices  14 us (22%)
  starting transfers between devices  11.8 us (19%)
  local copies, waits for them, and re-layouts  2.42 us (4%)
  between operations  0.88 us (1%)
    pallas_call x1, Pallas kernels, run_ilc(): pl.pallas_call(ilc_kernel, in_specs=[vmem, vmem, pl.BlockSpec(memory_spac...  9.98 us
    pallas_call x1, Pallas kernels, make_modes(): pl.pallas_call(modes_kernel, in_specs=[pl.BlockSpec(memory_space=pl.ANY)]...  9.21 us
    all_to_all x1, waiting for transfers between devices, body(): lax.all_to_all(partial, axes, split_axis=0, concat_axis=0, tiled=True)  7.87 us
    pallas_call x1, Pallas kernels, analyse(): pl.pallas_call(analysis_kernel, in_specs=[pl.BlockSpec(memory_space=pl.AN...  7.82 us
    all_to_all x1, starting transfers between devices, body(): lax.all_to_all(partial, axes, split_axis=0, concat_axis=0, tiled=True)  7.3 us
    pallas_call x1, Pallas kernels, make_basis(): pl.pallas_call(functools.partial(basis_kernel, slots), grid=(rows // bloc...  7.17 us
    all_to_all x1, waiting for transfers between devices, body(): lax.all_to_all(spectra, axes, split_axis=0, concat_axis=0, tiled=True)  4.18 us
    all_to_all x1, starting transfers between devices, body(): lax.all_to_all(spectra, axes, split_axis=0, concat_axis=0, tiled=True)  2.75 us
  transfers between devices with their start and end apart: 3, of which 3 were waited for; matrix products, arithmetic and copies ran while one was open for 4% of the time, Pallas kernels for 11%

profile of v10, /device:TPU:0, one launch (start us, length us, event | category | flops | bytes accessed | tf_op | source)
XLA Modules:
  0.0 63.4 jit_solution(7096555017226506737)
XLA Ops:
  0.6 0.0 copy-start
  0.6 9.2 %shard_map.50 = bf16[32,72,128]{2,1,0:T(8,128)(2,1)} custom-call(bf16[64,9,2,512]{3,2,1,0:T(2,128)(2,1)} %alm_hbm.1, bf16[64,512,256]{2,1,0:T(8,128)(2,1)} %table_hbm.3), custom_call_target="tpu_custom_call" | custom-call | flops 301989888 | bytes 17956864 | tf_op jit(solution)/shard_map/pallas_call | solution.py:372
  9.9 7.3 %all-to-all-start = ((bf16[32,72,128]{2,1,0:T(8,128)(2,1)}), bf16[32,72,128]{2,1,0:T(8,128)(2,1)S(1)}, u32[]{:S(2)}, u32[]{:S(2)}) async-start(bf16[32,72,128]{2,1,0:T(8,128)(2,1)} %shard_map.50), calls=%async_computation | async-start | bytes 1179648 | tf_op jit(solution)/shard_map/all_to_all | solution.py:475
  17.2 0.0 copy-done
  17.2 0.1 broadcast_in_dim.11
  17.3 1.1 %convert_element_type.27.order_ref = f32[2048,1]{1,0:T(8,128)S(1)} reshape(f32[32,2,32]{2,1,0:T(2,128)S(1)} %broadcast_in_dim.13) | data formatting | bytes 16384 | tf_op jit(solution)/shard_map/convert_element_type | solution.py:486
  18.4 0.1 reshape.91
  18.5 7.2 %shard_map.51 = bf16[4,2048,512]{2,1,0:T(8,128)(2,1)} custom-call(f32[2048,1]{1,0:T(8,128)S(1)} %convert_element_type.27.order_ref), custom_call_target="tpu_custom_call" | custom-call | flops 33554432 | bytes 8388608 | tf_op jit(solution)/shard_map/pallas_call | solution.py:74
  25.7 7.9 %all-to-all-done = bf16[32,72,128]{2,1,0:T(8,128)(2,1)S(1)} async-done(((bf16[32,72,128]{2,1,0:T(8,128)(2,1)}), bf16[32,72,128]{2,1,0:T(8,128)(2,1)S(1)}, u32[]{:S(2)}, u32[]{:S(2)}) %all-to-all-start) | async-done | bytes 589856 | tf_op jit(solution)/shard_map/all_to_all | solution.py:475
  33.6 10.0 %shard_map.52 = (f32[32,8,128]{2,1,0:T(8,128)S(1)}, bf16[16,2,8,128]{3,2,1,0:T(8,128)(2,1)}) custom-call(bf16[16,2,72,128]{3,2,1,0:T(8,128)(2,1)S(1)} %bitcast.10, f32[1,2048]{1,0:T(1,128)S(1)} %fusion.3.odd_ref, bf16[8,1024,512]{2,1,0:T(8,128)(2,1)} %bitcast.13), custom_call_target="tpu_custom_call" | custom-call | flops 1342177280 | bytes 8388608 | tf_op jit(solution)/shard_map/pallas_call | solution.py:276
  43.6 1.7 %collective-permute-start = (f32[32,8,128]{2,1,0:T(8,128)S(1)}, f32[32,8,128]{2,1,0:T(8,128)S(1)}, u32[]{:S(2)}, u32[]{:S(2)}) collective-permute-start(f32[32,8,128]{2,1,0:T(8,128)S(1)} %get-tuple-element.7), channel_id=1, source_target_pairs={{0,1},{1,0},{2,3},{3,2},{4,5},{5,4},{6,7},{7,6},{8,9},{9,8},{10,11... | collective-permute-start | bytes 393224 | tf_op jit(solution)/shard_map/ppermute | solution.py:446
  45.3 2.8 %all-to-all-start.1 = ((bf16[32,8,128]{2,1,0:T(8,128)(2,1)}), bf16[32,8,128]{2,1,0:T(8,128)(2,1)S(1)}, u32[]{:S(2)}, u32[]{:S(2)}) async-start(bf16[32,8,128]{2,1,0:T(8,128)(2,1)} %bitcast.2), calls=%async_computation.1 | async-start | bytes 131072 | tf_op jit(solution)/shard_map/all_to_all | solution.py:495
  48.0 1.9 %collective-permute-done = f32[32,8,128]{2,1,0:T(8,128)S(1)} collective-permute-done((f32[32,8,128]{2,1,0:T(8,128)S(1)}, f32[32,8,128]{2,1,0:T(8,128)S(1)}, u32[]{:S(2)}, u32[]{:S(2)}) %collective-permute-start) | collective-permute-done | bytes 131104 | tf_op jit(solution)/shard_map/ppermute | solution.py:446
  50.0 0.1 fusion.2
  50.0 0.1 fusion
  50.2 0.2 copy.6
  50.4 0.9 %reshape.94 = f32[16,2048]{1,0:T(8,128)} reshape(f32[2,8,64,32]{3,2,1,0:T(8,128)S(1)} %copy.6) | data formatting | bytes 262144 | tf_op jit(solution)/shard_map/reshape | solution.py:499
  51.3 4.2 %all-to-all-done.1 = bf16[32,8,128]{2,1,0:T(8,128)(2,1)S(1)} async-done(((bf16[32,8,128]{2,1,0:T(8,128)(2,1)}), bf16[32,8,128]{2,1,0:T(8,128)(2,1)S(1)}, u32[]{:S(2)}, u32[]{:S(2)}) %all-to-all-start.1) | async-done | bytes 65568 | tf_op jit(solution)/shard_map/all_to_all | solution.py:495
  55.5 7.8 %shard_map.53 = f32[64,2,512]{2,1,0:T(2,128)} custom-call(bf16[64,512,256]{2,1,0:T(8,128)(2,1)} %table_hbm.3, bf16[256,128]{1,0:T(8,128)(2,1)S(1)} %bitcast.11), custom_call_target="tpu_custom_call" | custom-call | flops 268435456 | bytes 16777216 | tf_op jit(solution)/shard_map/pallas_call | solution.py:423
  (4 shorter events, 0.1 us)
Async XLA Ops:
  0.6 16.5 %copy-start = (s32[1024]{0:T(1024)S(1)}, s32[1024]{0:T(1024)}, u32[]{:S(2)}) copy-start(s32[1024]{0:T(1024)} %param.5) | copy-start | bytes 12292
  9.9 23.7 %all-to-all-start = ((bf16[32,72,128]{2,1,0:T(8,128)(2,1)}), bf16[32,72,128]{2,1,0:T(8,128)(2,1)S(1)}, u32[]{:S(2)}, u32[]{:S(2)}) async-start(bf16[32,72,128]{2,1,0:T(8,128)(2,1)} %shard_map.50), calls=%async_computation | async-start | bytes 1179648 | tf_op jit(solution)/shard_map/all_to_all | solution.py:475
  43.6 6.4 %collective-permute-start = (f32[32,8,128]{2,1,0:T(8,128)S(1)}, f32[32,8,128]{2,1,0:T(8,128)S(1)}, u32[]{:S(2)}, u32[]{:S(2)}) collective-permute-start(f32[32,8,128]{2,1,0:T(8,128)S(1)} %get-tuple-element.7), channel_id=1, source_target_pairs={{0,1},{1,0},{2,3},{3,2},{4,5},{5,4},{6,7},{7,6},{8,9},{9,8},{10,11... | collective-permute-start | bytes 393224 | tf_op jit(solution)/shard_map/ppermute | solution.py:446
  45.3 10.2 %all-to-all-start.1 = ((bf16[32,8,128]{2,1,0:T(8,128)(2,1)}), bf16[32,8,128]{2,1,0:T(8,128)(2,1)S(1)}, u32[]{:S(2)}, u32[]{:S(2)}) async-start(bf16[32,8,128]{2,1,0:T(8,128)(2,1)} %bitcast.2), calls=%async_computation.1 | async-start | bytes 131072 | tf_op jit(solution)/shard_map/all_to_all | solution.py:495

commit v11 on v10

--- a/solution.py
+++ b/solution.py
@@ -95,10 +95,17 @@
         part_copy(source, target, sems, part).start()
 
 
-def next_part(source, target, sems, part):
+def next_part(source, target, sems, part, ahead):
     part_copy(source, target, sems, part).wait()
-    if part + IN_FLIGHT < sems.shape[0]:
-        part_copy(source, target, sems, part + IN_FLIGHT).start()
+    more = part + ahead < sems.shape[0]
+    if isinstance(part, int):
+        if more:
+            part_copy(source, target, sems, part + ahead).start()
+    else:
+
+        @pl.when(more)
+        def _():
+            part_copy(source, target, sems, part + ahead).start()
 
 
 def reciprocal(value):
@@ -146,11 +153,12 @@
     groups, shares, rows, width = modes_ref.shape
     columns = basis_ref.shape[2]
     depth = lhs_ref.shape[1]
-    pieces = depth // basis_ref.shape[1]
+    pieces, share_rows = found_ref.shape[0], found_ref.shape[2]
     chunks = basis_ref.shape[0] // pieces
     cycles = rows // C
     second = round_up(rows, 16)
-    start_parts(basis_hbm, basis_ref, sems, IN_FLIGHT)
+    ahead = 2 * pieces
+    start_parts(basis_hbm, basis_ref, sems, ahead)
     for group in range(groups):
         span = slice(group * width, (group + 1) * width)
         odd = odd_ref[:, span]
@@ -161,6 +169,8 @@
         lhs_ref[second : second + rows, span] = (values * odd).astype(jnp.bfloat16)
     low_half = lax.broadcasted_iota(jnp.int32, (cycles, LANES), 1) < HALF
     sums_ref[...] = jnp.zeros_like(sums_ref)
+    found_ref[...] = jnp.zeros_like(found_ref)
+    low_ref[0] = jnp.zeros_like(low_ref[0])
 
     def store_maps(at, maps):
         squares = maps[0] * maps[0]
@@ -170,10 +180,10 @@
         maps_ref[at, REST] = maps[0]
         maps_ref[at, C] = squares
 
-    def maps_of_chunk(chunk):
+    def maps_of_chunk(chunk, carry):
         for piece in range(pieces):
-            next_part(basis_hbm, basis_ref, sems, chunk * pieces + piece)
-        basis = basis_ref[chunk * pieces : (chunk + 1) * pieces].reshape(depth, columns)
+            next_part(basis_hbm, basis_ref, sems, chunk * pieces + piece, ahead)
+        basis = basis_ref[pl.ds(chunk * pieces, pieces)].reshape(depth, columns)
         result = jnp.dot(lhs_ref[...], basis, preferred_element_type=jnp.float32)
         for part in range(CHUNK // 2):
             at = CHUNK * chunk + 2 * part
@@ -188,80 +198,67 @@
                 right.append(jnp.where(low_half, pltpu.roll(near, HALF, 1), far))
             store_maps(at, left)
             store_maps(at + 1, right)
-
-    def product(at, pair):
-        if pair == SUMS - 1:
-            return maps_ref[at, C]
-        a_at, b_at = PAIRS[pair]
-        return maps_ref[at, a_at] * maps_ref[at, b_at]
-
-    def add_totals(chunk):
-        for pair in range(SUMS):
-            total = sums_ref[pair]
-            for at in range(CHUNK * chunk, CHUNK * (chunk + 1)):
-                total = total + product(at, pair)
-            sums_ref[pair] = total
-
-    maps_of_chunk(0)
-    for chunk in range(1, chunks):
-        maps_of_chunk(chunk)
-        add_totals(chunk - 1)
-    add_totals(chunks - 1)
+        vectors = [CHUNK * chunk + part for part in range(CHUNK)]
+        for a_at in range(C):
+            own = [maps_ref[at, a_at] for at in vectors]
+            for b_at in range(a_at, C):
+                if (a_at, b_at) == (REST, REST):
+                    continue
+                pair = PAIRS.index((a_at, b_at))
+                total = sums_ref[pair]
+                for at, value in zip(vectors, own):
+                    total = total + value * (value if a_at == b_at else maps_ref[at, b_at])
+                sums_ref[pair] = total
+        total = sums_ref[SUMS - 1]
+        for at in vectors:
+            total = total + maps_ref[at, C]
+        sums_ref[SUMS - 1] = total
+        return carry
+
+    lax.fori_loop(0, chunks, maps_of_chunk, 0)
     for pair in range(SUMS):
         total = sums_ref[pair]
         sums_ref[pair] = pltpu.roll(total, 1, 1) + pltpu.roll(total, 2, 1)
 
     def solve_steps(at):
+        maps = [maps_ref[at, chan] for chan in range(C + 1)]
+
         def sum_of(pair):
-            own = product(at, pair)
+            own = maps[C] if pair == SUMS - 1 else maps[PAIRS[pair][0]] * maps[PAIRS[pair][1]]
             total = sums_ref[pair] + own
             sums_ref[pair] = total - pltpu.roll(own, 2, 1)
             return total
 
-        return combine_steps(sum_of, lambda chan: pltpu.roll(maps_ref[at, chan], 1, 1))
-
-    def two_vectors(at, beside):
-        found = in_step([solve_steps(at), solve_steps(at + 1), beside])[:2]
+        return combine_steps(sum_of, lambda chan: pltpu.roll(maps[chan], 1, 1))
+
+    def add_spectra(chunk, part, low):
+        lhs = jnp.concatenate([low_ref[low, at] for at in range(pieces)], axis=1)
+        found_ref[part] += lax.dot_general(
+            lhs, basis_ref[chunk * pieces + part], (((1,), (1,)), ((), ())), preferred_element_type=jnp.float32
+        )
+
+    def two_vectors(pair_at, carry):
+        at = 2 * pair_at
+        chunk, part = pair_at // pieces, pair_at % pieces
+        add_spectra(jnp.maximum(chunk - 1, 0), part, chunk)
+        found = in_step([solve_steps(at), solve_steps(at + 1)])
         found = [pltpu.roll(value, LANES - 1, 1) for value in found]
         ilc_ref[at] = found[0]
         ilc_ref[at + 1] = found[1]
         near = jnp.where(low_half, found[0], pltpu.roll(found[1], HALF, 1))
         far = jnp.where(low_half, pltpu.roll(found[0], HALF, 1), found[1])
-        return jnp.concatenate([near, far], axis=0).astype(jnp.bfloat16)
-
-    share_rows = depth // (CHUNK // 2)
-    per_piece = depth // pieces // share_rows
-
-    def add_spectra(chunk, part):
-        first = part % per_piece * share_rows
-        basis = basis_ref[chunk * pieces + part // per_piece, first : first + share_rows, :]
-        found_ref[:, part * share_rows : (part + 1) * share_rows] += lax.dot_general(
-            low_ref[chunk], basis, (((1,), (1,)), ((), ())), preferred_element_type=jnp.float32
-        )
-
-    def spectra_steps(chunk, part):
-        for _ in range(8):
-            yield None
-        add_spectra(chunk, part)
-        while True:
-            yield None
-
-    found_ref[...] = jnp.zeros_like(found_ref)
-    low_ref[...] = jnp.zeros_like(low_ref)
-
-    def solve_chunk(chunk, carry):
-        before = jnp.maximum(chunk - 1, 0)
-        found = [two_vectors(CHUNK * chunk + 2 * part, spectra_steps(before, part)) for part in range(CHUNK // 2)]
-        low_ref[chunk] = jnp.concatenate(found, axis=1)
+        low_ref[chunk + 1, part] = jnp.concatenate([near, far], axis=0).astype(jnp.bfloat16)
         return carry
 
-    lax.fori_loop(0, chunks, solve_chunk, 0)
-    for part in range(CHUNK // 2):
-        add_spectra(chunks - 1, part)
+    lax.fori_loop(0, HALO // 2, two_vectors, 0)
+    for part in range(pieces):
+        add_spectra(chunks - 1, part, chunks)
     for group in range(groups):
         span = slice(group * width, (group + 1) * width)
         sign = 1.0 - 2.0 * odd_ref[:, span]
-        value = (found_ref[0:cycles, span] + sign * found_ref[cycles:, span]).astype(jnp.bfloat16)
+        part, first = group * width // share_rows, group * width % share_rows
+        result = found_ref[part, :, first : first + width]
+        value = (result[0:cycles] + sign * result[cycles:]).astype(jnp.bfloat16)
         for share in range(shares):
             spectra_ref[group, share] = value
 
@@ -269,7 +266,7 @@
 def run_ilc(modes, odd, basis):
     groups, shares, rows, width = modes.shape
     chunks, depth, columns = basis.shape
-    pieces = 2
+    pieces = CHUNK // 2
     basis = basis.reshape(chunks * pieces, depth // pieces, columns)
     cycles = rows // C
     vmem = pl.BlockSpec(memory_space=pltpu.VMEM)
@@ -286,8 +283,8 @@
             pltpu.VMEM((2 * round_up(rows, 16), depth), jnp.bfloat16),
             pltpu.VMEM((HALO, C + 1, cycles, LANES), jnp.float32),
             pltpu.VMEM((SUMS, cycles, LANES), jnp.float32),
-            pltpu.VMEM((chunks, 2 * cycles, columns), jnp.bfloat16),
-            pltpu.VMEM((2 * cycles, depth), jnp.float32),
+            pltpu.VMEM((chunks + 1, pieces, 2 * cycles, LANES), jnp.bfloat16),
+            pltpu.VMEM((pieces, 2 * cycles, depth // pieces), jnp.float32),
             pltpu.SemaphoreType.DMA((chunks * pieces,)),
         ],
         cost_estimate=pl.CostEstimate(
@@ -325,32 +322,39 @@
         lhs = lhs_ref[part % 2, pair].astype(jnp.bfloat16)
         result = jnp.dot(lhs, both, preferred_element_type=jnp.float32)
         for slot in range(2):
-            rows = slice((at + slot) * height, (at + slot + 1) * height)
+            rows = pl.ds(pl.multiple_of((at + slot) * height, 8), height)
             own = result[slot * height : (slot + 1) * height, slot * total : (slot + 1) * total]
             for lanes in range(held_ref.shape[0]):
                 held_ref[lanes, rows, :] = own[:, lanes * LANES : (lanes + 1) * LANES]
 
+    def some_slots(part, carry):
+        next_part(table_hbm, table_ref, sems, part, IN_FLIGHT)
+        for pair in range(slots // 2):
+            two_slots(part, pair)
+            stack_rows(jnp.minimum(part + 1, parts - 1), pair)
+        return carry
+
     def turn(half):
         count = total_slots // HALVES
         first = half * count * height
-        for chan in range(C):
+
+        def turn_channel(chan, carry):
             for lanes in range(held_ref.shape[0]):
-                both = [held_ref[lanes, pl.ds(first + 2 * chan + part, count, stride=height), :] for part in range(2)]
+                at = first + 2 * chan
+                both = [held_ref[lanes, pl.ds(at + part, count, stride=height), :] for part in range(2)]
                 span = slice(half * 2 * count, (half + 1) * 2 * count)
                 turned_ref[chan, lanes * LANES : (lanes + 1) * LANES, span] = jnp.concatenate(both, axis=0).T
-
-    for part in range(-1, parts):
-        if part + 1 < parts:
-            part_copy(alm_hbm, alm_ref, alm_sems, part + 1).wait()
-        if part >= 0:
-            next_part(table_hbm, table_ref, sems, part)
-        for pair in range(slots // 2):
-            if part >= 0:
-                two_slots(part, pair)
-            if part + 1 < parts:
-                stack_rows(part + 1, pair)
-        if (part + 1) * HALVES % parts == 0 and part >= 0:
-            turn((part + 1) * HALVES // parts - 1)
+            return carry
+
+        lax.fori_loop(0, C, turn_channel, 0)
+
+    for part in range(parts):
+        part_copy(alm_hbm, alm_ref, alm_sems, part).wait()
+    for pair in range(slots // 2):
+        stack_rows(0, pair)
+    for half in range(HALVES):
+        lax.fori_loop(half * parts // HALVES, (half + 1) * parts // HALVES, some_slots, 0)
+        turn(half)
     each = targets // out_sems.shape[0]
     for target in range(targets):
         span = slice(target * cycles, (target + 1) * cycles)
@@ -406,7 +410,7 @@
         rows = [turned_ref[row + share * count : row + share * count + slots, :] for share in range(2)]
         lhs = jnp.concatenate(rows, axis=0).astype(jnp.bfloat16)
         for piece in range(pieces):
-            next_part(table_hbm, table_ref, sems, first // slots * pieces + piece)
+            next_part(table_hbm, table_ref, sems, first // slots * pieces + piece, IN_FLIGHT)
         table = table_ref[first : first + slots].reshape(slots * degrees, total)
         result = lax.dot_general(lhs, table, (((1,), (1,)), ((), ())), preferred_element_type=jnp.float32)
         for slot in range(slots):

time: 63.7 us -> 68.4 us (1.074)
  Pallas kernels: 34.2 us -> 39 us
    pallas_call x1, Pallas kernels: 9.21 us -> 12.1 us  [make_modes(): pl.pallas_call(modes_kernel, in_specs=[pl.BlockSpec(memory_space=pl.ANY)]...]
    pallas_call x1, Pallas kernels: 9.98 us -> 11.9 us  [run_ilc(): pl.pallas_call(ilc_kernel, in_specs=[vmem, vmem, pl.BlockSpec(memory_spac...]
where the time goes in v11:
time: 68.4 us; the launch traced here: 68.1 us
  Pallas kernels  39 us (57%)
  waiting for transfers between devices  14.2 us (21%)
  starting transfers between devices  11.6 us (17%)
  local copies, waits for them, and re-layouts  2.42 us (4%)
  between operations  0.72 us (1%)
    pallas_call x1, Pallas kernels, make_modes(): pl.pallas_call(modes_kernel, in_specs=[pl.BlockSpec(memory_space=pl.ANY)]...  12.1 us
    pallas_call x1, Pallas kernels, run_ilc(): pl.pallas_call(ilc_kernel, in_specs=[vmem, vmem, pl.BlockSpec(memory_spac...  11.9 us
    all_to_all x1, waiting for transfers between devices, body(): lax.all_to_all(partial, axes, split_axis=0, concat_axis=0, tiled=True)  7.87 us
    pallas_call x1, Pallas kernels, analyse(): pl.pallas_call(analysis_kernel, in_specs=[pl.BlockSpec(memory_space=pl.AN...  7.82 us
    all_to_all x1, starting transfers between devices, body(): lax.all_to_all(partial, axes, split_axis=0, concat_axis=0, tiled=True)  7.3 us
    pallas_call x1, Pallas kernels, make_basis(): pl.pallas_call(functools.partial(basis_kernel, slots), grid=(rows // bloc...  7.17 us
    all_to_all x1, waiting for transfers between devices, body(): lax.all_to_all(spectra, axes, split_axis=0, concat_axis=0, tiled=True)  4.18 us
    all_to_all x1, starting transfers between devices, body(): lax.all_to_all(spectra, axes, split_axis=0, concat_axis=0, tiled=True)  2.57 us
  transfers between devices with their start and end apart: 3, of which 3 were waited for; matrix products, arithmetic and copies ran while one was open for 4% of the time, Pallas kernels for 11%

profile of v11, /device:TPU:0, one launch (start us, length us, event | category | flops | bytes accessed | tf_op | source)
XLA Modules:
  0.0 68.1 jit_solution(77857868121446132)
XLA Ops:
  0.6 0.0 copy-start
  0.6 12.1 %shard_map.50 = bf16[32,72,128]{2,1,0:T(8,128)(2,1)} custom-call(bf16[64,9,2,512]{3,2,1,0:T(2,128)(2,1)} %alm_hbm.1, bf16[64,512,256]{2,1,0:T(8,128)(2,1)} %table_hbm.3), custom_call_target="tpu_custom_call" | custom-call | flops 301989888 | bytes 17956864 | tf_op jit(solution)/shard_map/pallas_call | solution.py:376
  12.8 7.3 %all-to-all-start = ((bf16[32,72,128]{2,1,0:T(8,128)(2,1)}), bf16[32,72,128]{2,1,0:T(8,128)(2,1)S(1)}, u32[]{:S(2)}, u32[]{:S(2)}) async-start(bf16[32,72,128]{2,1,0:T(8,128)(2,1)} %shard_map.50), calls=%async_computation | async-start | bytes 1179648 | tf_op jit(solution)/shard_map/all_to_all | solution.py:479
  20.1 0.0 copy-done
  20.1 0.1 broadcast_in_dim.11
  20.2 1.1 %convert_element_type.27.order_ref = f32[2048,1]{1,0:T(8,128)S(1)} reshape(f32[32,2,32]{2,1,0:T(2,128)S(1)} %broadcast_in_dim.13) | data formatting | bytes 16384 | tf_op jit(solution)/shard_map/convert_element_type | solution.py:490
  21.3 0.1 reshape.91
  21.4 7.2 %shard_map.51 = bf16[4,2048,512]{2,1,0:T(8,128)(2,1)} custom-call(f32[2048,1]{1,0:T(8,128)S(1)} %convert_element_type.27.order_ref), custom_call_target="tpu_custom_call" | custom-call | flops 33554432 | bytes 8388608 | tf_op jit(solution)/shard_map/pallas_call | solution.py:74
  28.6 7.9 %all-to-all-done = bf16[32,72,128]{2,1,0:T(8,128)(2,1)S(1)} async-done(((bf16[32,72,128]{2,1,0:T(8,128)(2,1)}), bf16[32,72,128]{2,1,0:T(8,128)(2,1)S(1)}, u32[]{:S(2)}, u32[]{:S(2)}) %all-to-all-start) | async-done | bytes 589856 | tf_op jit(solution)/shard_map/all_to_all | solution.py:479
  36.5 11.9 %shard_map.52 = (f32[32,8,128]{2,1,0:T(8,128)S(1)}, bf16[16,2,8,128]{3,2,1,0:T(8,128)(2,1)}) custom-call(bf16[16,2,72,128]{3,2,1,0:T(8,128)(2,1)S(1)} %bitcast.10, f32[1,2048]{1,0:T(1,128)S(1)} %fusion.3.odd_ref, bf16[16,512,512]{2,1,0:T(8,128)(2,1)} %bitcast.13), custom_call_target="tpu_custom_call" | custom-call | flops 1342177280 | bytes 8388608 | tf_op jit(solution)/shard_map/pallas_call | solution.py:273
  48.4 1.7 %collective-permute-start = (f32[32,8,128]{2,1,0:T(8,128)S(1)}, f32[32,8,128]{2,1,0:T(8,128)S(1)}, u32[]{:S(2)}, u32[]{:S(2)}) collective-permute-start(f32[32,8,128]{2,1,0:T(8,128)S(1)} %get-tuple-element.7), channel_id=1, source_target_pairs={{0,1},{1,0},{2,3},{3,2},{4,5},{5,4},{6,7},{7,6},{8,9},{9,8},{10,11... | collective-permute-start | bytes 393224 | tf_op jit(solution)/shard_map/ppermute | solution.py:450
  50.1 2.6 %all-to-all-start.1 = ((bf16[32,8,128]{2,1,0:T(8,128)(2,1)}), bf16[32,8,128]{2,1,0:T(8,128)(2,1)S(1)}, u32[]{:S(2)}, u32[]{:S(2)}) async-start(bf16[32,8,128]{2,1,0:T(8,128)(2,1)} %bitcast.2), calls=%async_computation.1 | async-start | bytes 131072 | tf_op jit(solution)/shard_map/all_to_all | solution.py:499
  52.7 2.1 %collective-permute-done = f32[32,8,128]{2,1,0:T(8,128)S(1)} collective-permute-done((f32[32,8,128]{2,1,0:T(8,128)S(1)}, f32[32,8,128]{2,1,0:T(8,128)S(1)}, u32[]{:S(2)}, u32[]{:S(2)}) %collective-permute-start) | collective-permute-done | bytes 131104 | tf_op jit(solution)/shard_map/ppermute | solution.py:450
  54.8 0.1 fusion.2
  54.8 0.1 fusion
  55.0 0.2 copy.6
  55.2 0.9 %reshape.94 = f32[16,2048]{1,0:T(8,128)} reshape(f32[2,8,64,32]{3,2,1,0:T(8,128)S(1)} %copy.6) | data formatting | bytes 262144 | tf_op jit(solution)/shard_map/reshape | solution.py:503
  56.1 4.2 %all-to-all-done.1 = bf16[32,8,128]{2,1,0:T(8,128)(2,1)S(1)} async-done(((bf16[32,8,128]{2,1,0:T(8,128)(2,1)}), bf16[32,8,128]{2,1,0:T(8,128)(2,1)S(1)}, u32[]{:S(2)}, u32[]{:S(2)}) %all-to-all-start.1) | async-done | bytes 65568 | tf_op jit(solution)/shard_map/all_to_all | solution.py:499
  60.3 7.8 %shard_map.53 = f32[64,2,512]{2,1,0:T(2,128)} custom-call(bf16[64,512,256]{2,1,0:T(8,128)(2,1)} %table_hbm.3, bf16[256,128]{1,0:T(8,128)(2,1)S(1)} %bitcast.11), custom_call_target="tpu_custom_call" | custom-call | flops 268435456 | bytes 16777216 | tf_op jit(solution)/shard_map/pallas_call | solution.py:427
  (4 shorter events, 0.1 us)
Async XLA Ops:
  0.6 19.5 %copy-start = (s32[1024]{0:T(1024)S(1)}, s32[1024]{0:T(1024)}, u32[]{:S(2)}) copy-start(s32[1024]{0:T(1024)} %param.5) | copy-start | bytes 12292
  12.8 23.7 %all-to-all-start = ((bf16[32,72,128]{2,1,0:T(8,128)(2,1)}), bf16[32,72,128]{2,1,0:T(8,128)(2,1)S(1)}, u32[]{:S(2)}, u32[]{:S(2)}) async-start(bf16[32,72,128]{2,1,0:T(8,128)(2,1)} %shard_map.50), calls=%async_computation | async-start | bytes 1179648 | tf_op jit(solution)/shard_map/all_to_all | solution.py:479
  48.4 6.4 %collective-permute-start = (f32[32,8,128]{2,1,0:T(8,128)S(1)}, f32[32,8,128]{2,1,0:T(8,128)S(1)}, u32[]{:S(2)}, u32[]{:S(2)}) collective-permute-start(f32[32,8,128]{2,1,0:T(8,128)S(1)} %get-tuple-element.7), channel_id=1, source_target_pairs={{0,1},{1,0},{2,3},{3,2},{4,5},{5,4},{6,7},{7,6},{8,9},{9,8},{10,11... | collective-permute-start | bytes 393224 | tf_op jit(solution)/shard_map/ppermute | solution.py:450
  50.1 10.2 %all-to-all-start.1 = ((bf16[32,8,128]{2,1,0:T(8,128)(2,1)}), bf16[32,8,128]{2,1,0:T(8,128)(2,1)S(1)}, u32[]{:S(2)}, u32[]{:S(2)}) async-start(bf16[32,8,128]{2,1,0:T(8,128)(2,1)} %bitcast.2), calls=%async_computation.1 | async-start | bytes 131072 | tf_op jit(solution)/shard_map/all_to_all | solution.py:499

commit v12 on v11

--- a/solution.py
+++ b/solution.py
@@ -169,8 +169,6 @@
         lhs_ref[second : second + rows, span] = (values * odd).astype(jnp.bfloat16)
     low_half = lax.broadcasted_iota(jnp.int32, (cycles, LANES), 1) < HALF
     sums_ref[...] = jnp.zeros_like(sums_ref)
-    found_ref[...] = jnp.zeros_like(found_ref)
-    low_ref[0] = jnp.zeros_like(low_ref[0])
 
     def store_maps(at, maps):
         squares = maps[0] * maps[0]
@@ -180,10 +178,10 @@
         maps_ref[at, REST] = maps[0]
         maps_ref[at, C] = squares
 
-    def maps_of_chunk(chunk, carry):
+    def maps_of_chunk(chunk):
         for piece in range(pieces):
             next_part(basis_hbm, basis_ref, sems, chunk * pieces + piece, ahead)
-        basis = basis_ref[pl.ds(chunk * pieces, pieces)].reshape(depth, columns)
+        basis = basis_ref[chunk * pieces : (chunk + 1) * pieces].reshape(depth, columns)
         result = jnp.dot(lhs_ref[...], basis, preferred_element_type=jnp.float32)
         for part in range(CHUNK // 2):
             at = CHUNK * chunk + 2 * part
@@ -198,6 +196,8 @@
                 right.append(jnp.where(low_half, pltpu.roll(near, HALF, 1), far))
             store_maps(at, left)
             store_maps(at + 1, right)
+
+    def add_totals(chunk):
         vectors = [CHUNK * chunk + part for part in range(CHUNK)]
         for a_at in range(C):
             own = [maps_ref[at, a_at] for at in vectors]
@@ -213,9 +213,12 @@
         for at in vectors:
             total = total + maps_ref[at, C]
         sums_ref[SUMS - 1] = total
-        return carry
-
-    lax.fori_loop(0, chunks, maps_of_chunk, 0)
+
+    maps_of_chunk(0)
+    for chunk in range(1, chunks):
+        maps_of_chunk(chunk)
+        add_totals(chunk - 1)
+    add_totals(chunks - 1)
     for pair in range(SUMS):
         total = sums_ref[pair]
         sums_ref[pair] = pltpu.roll(total, 1, 1) + pltpu.roll(total, 2, 1)
@@ -231,28 +234,26 @@
 
         return combine_steps(sum_of, lambda chan: pltpu.roll(maps[chan], 1, 1))
 
-    def add_spectra(chunk, part, low):
-        lhs = jnp.concatenate([low_ref[low, at] for at in range(pieces)], axis=1)
-        found_ref[part] += lax.dot_general(
-            lhs, basis_ref[chunk * pieces + part], (((1,), (1,)), ((), ())), preferred_element_type=jnp.float32
-        )
-
-    def two_vectors(pair_at, carry):
+    def add_spectra(chunk):
+        lhs = jnp.concatenate([low_ref[chunk, part] for part in range(pieces)], axis=1)
+        for part in range(pieces):
+            term = lax.dot_general(
+                lhs, basis_ref[chunk * pieces + part], (((1,), (1,)), ((), ())), preferred_element_type=jnp.float32
+            )
+            found_ref[part] = term if chunk == 0 else found_ref[part] + term
+
+    for pair_at in range(HALO // 2):
         at = 2 * pair_at
         chunk, part = pair_at // pieces, pair_at % pieces
-        add_spectra(jnp.maximum(chunk - 1, 0), part, chunk)
         found = in_step([solve_steps(at), solve_steps(at + 1)])
         found = [pltpu.roll(value, LANES - 1, 1) for value in found]
         ilc_ref[at] = found[0]
         ilc_ref[at + 1] = found[1]
         near = jnp.where(low_half, found[0], pltpu.roll(found[1], HALF, 1))
         far = jnp.where(low_half, pltpu.roll(found[0], HALF, 1), found[1])
-        low_ref[chunk + 1, part] = jnp.concatenate([near, far], axis=0).astype(jnp.bfloat16)
-        return carry
-
-    lax.fori_loop(0, HALO // 2, two_vectors, 0)
-    for part in range(pieces):
-        add_spectra(chunks - 1, part, chunks)
+        low_ref[chunk, part] = jnp.concatenate([near, far], axis=0).astype(jnp.bfloat16)
+        if part == pieces - 1:
+            add_spectra(chunk)
     for group in range(groups):
         span = slice(group * width, (group + 1) * width)
         sign = 1.0 - 2.0 * odd_ref[:, span]
@@ -283,7 +284,7 @@
             pltpu.VMEM((2 * round_up(rows, 16), depth), jnp.bfloat16),
             pltpu.VMEM((HALO, C + 1, cycles, LANES), jnp.float32),
             pltpu.VMEM((SUMS, cycles, LANES), jnp.float32),
-            pltpu.VMEM((chunks + 1, pieces, 2 * cycles, LANES), jnp.bfloat16),
+            pltpu.VMEM((chunks, pieces, 2 * cycles, LANES), jnp.bfloat16),
             pltpu.VMEM((pieces, 2 * cycles, depth // pieces), jnp.float32),
             pltpu.SemaphoreType.DMA((chunks * pieces,)),
         ],
@@ -296,65 +297,42 @@
     )(modes, odd, basis)
 
 
-def modes_kernel(
-    alm_hbm, table_hbm, out_hbm, alm_ref, table_ref, lhs_ref, held_ref, turned_ref, out_ref, alm_sems, sems, out_sems
-):
+def modes_kernel(alm_hbm, table_hbm, out_hbm, alm_ref, table_ref, held_ref, turned_ref, out_ref, alm_sems, sems, out_sems):
     parts = sems.shape[0]
-    total_slots, _, total = table_ref.shape
+    total_slots, degrees, total = table_ref.shape
     slots = total_slots // parts
     targets, rows = out_ref.shape[:2]
     cycles = rows // C
-    height = held_ref.shape[1] // total_slots
+    height = 2 * C
     start_parts(alm_hbm, alm_ref, alm_sems, parts)
     start_parts(table_hbm, table_ref, sems, IN_FLIGHT)
-    lhs_ref[...] = jnp.zeros_like(lhs_ref)
-
-    def stack_rows(part, pair):
-        for slot in range(2):
-            for chan in range(C):
-                span = slice(slot * height + 2 * chan, slot * height + 2 * chan + 2)
-                own = alm_ref[part * slots + 2 * pair + slot, chan]
-                lhs_ref[part % 2, pair, span, :] = own.astype(jnp.float32)
-
-    def two_slots(part, pair):
-        at = part * slots + 2 * pair
-        both = jnp.concatenate([table_ref[at], table_ref[at + 1]], axis=1)
-        lhs = lhs_ref[part % 2, pair].astype(jnp.bfloat16)
-        result = jnp.dot(lhs, both, preferred_element_type=jnp.float32)
-        for slot in range(2):
-            rows = pl.ds(pl.multiple_of((at + slot) * height, 8), height)
+
+    def some_slots(part):
+        part_copy(alm_hbm, alm_ref, alm_sems, part).wait()
+        next_part(table_hbm, table_ref, sems, part, IN_FLIGHT)
+        first = part * slots
+        lhs = alm_ref[first : first + slots].reshape(slots * height, degrees)
+        rhs = jnp.concatenate([table_ref[first + slot] for slot in range(slots)], axis=1)
+        result = jnp.dot(lhs, rhs, preferred_element_type=jnp.float32)
+        for slot in range(slots):
             own = result[slot * height : (slot + 1) * height, slot * total : (slot + 1) * total]
             for lanes in range(held_ref.shape[0]):
-                held_ref[lanes, rows, :] = own[:, lanes * LANES : (lanes + 1) * LANES]
-
-    def some_slots(part, carry):
-        next_part(table_hbm, table_ref, sems, part, IN_FLIGHT)
-        for pair in range(slots // 2):
-            two_slots(part, pair)
-            stack_rows(jnp.minimum(part + 1, parts - 1), pair)
-        return carry
+                span = slice((first + slot) * height, (first + slot + 1) * height)
+                held_ref[lanes, span, :] = own[:, lanes * LANES : (lanes + 1) * LANES]
 
     def turn(half):
         count = total_slots // HALVES
         first = half * count * height
-
-        def turn_channel(chan, carry):
+        for chan in range(C):
             for lanes in range(held_ref.shape[0]):
-                at = first + 2 * chan
-                both = [held_ref[lanes, pl.ds(at + part, count, stride=height), :] for part in range(2)]
+                both = [held_ref[lanes, pl.ds(first + 2 * chan + part, count, stride=height), :] for part in range(2)]
                 span = slice(half * 2 * count, (half + 1) * 2 * count)
                 turned_ref[chan, lanes * LANES : (lanes + 1) * LANES, span] = jnp.concatenate(both, axis=0).T
-            return carry
-
-        lax.fori_loop(0, C, turn_channel, 0)
 
     for part in range(parts):
-        part_copy(alm_hbm, alm_ref, alm_sems, part).wait()
-    for pair in range(slots // 2):
-        stack_rows(0, pair)
-    for half in range(HALVES):
-        lax.fori_loop(half * parts // HALVES, (half + 1) * parts // HALVES, some_slots, 0)
-        turn(half)
+        some_slots(part)
+        if (part + 1) * HALVES % parts == 0:
+            turn((part + 1) * HALVES // parts - 1)
     each = targets // out_sems.shape[0]
     for target in range(targets):
         span = slice(target * cycles, (target + 1) * cycles)
@@ -371,7 +349,7 @@
     slots = 4
     parts = slot_count // slots
     width = 2 * slot_count
-    height = round_up(2 * C, 8)
+    height = 2 * C
     out = jax.ShapeDtypeStruct((targets, C * (total // targets), width), jnp.bfloat16)
     return pl.pallas_call(
         modes_kernel,
@@ -381,7 +359,6 @@
         scratch_shapes=[
             pltpu.VMEM(alm.shape, jnp.bfloat16),
             pltpu.VMEM(legendre.shape, jnp.bfloat16),
-            pltpu.VMEM((2, slots // 2, 2 * height, degrees), jnp.float32),
             pltpu.VMEM((total // LANES, slot_count * height, LANES), jnp.float32),
             pltpu.VMEM((C, total, width), jnp.float32),
             pltpu.VMEM(out.shape, out.dtype),

time: 68.4 us -> 62.7 us (0.917)
  Pallas kernels: 39 us -> 33.2 us
    pallas_call x1, Pallas kernels: 12.1 us -> 9.16 us  [make_modes(): pl.pallas_call(modes_kernel, in_specs=[pl.BlockSpec(memory_space=pl.ANY)]...]
    pallas_call x1, Pallas kernels: 11.9 us -> 9.07 us  [run_ilc(): pl.pallas_call(ilc_kernel, in_specs=[vmem, vmem, pl.BlockSpec(memory_spac...]
where the time goes in v12:
time: 62.7 us; the launch traced here: 62.5 us
  Pallas kernels  33.2 us (53%)
  waiting for transfers between devices  14 us (22%)
  starting transfers between devices  11.8 us (19%)
  local copies, waits for them, and re-layouts  2.42 us (4%)
  between operations  0.88 us (1%)
    pallas_call x1, Pallas kernels, make_modes(): pl.pallas_call(modes_kernel, in_specs=[pl.BlockSpec(memory_space=pl.ANY)]...  9.16 us
    pallas_call x1, Pallas kernels, run_ilc(): pl.pallas_call(ilc_kernel, in_specs=[vmem, vmem, pl.BlockSpec(memory_spac...  9.07 us
    all_to_all x1, waiting for transfers between devices, body(): lax.all_to_all(partial, axes, split_axis=0, concat_axis=0, tiled=True)  7.87 us
    pallas_call x1, Pallas kernels, analyse(): pl.pallas_call(analysis_kernel, in_specs=[pl.BlockSpec(memory_space=pl.AN...  7.82 us
    all_to_all x1, starting transfers between devices, body(): lax.all_to_all(partial, axes, split_axis=0, concat_axis=0, tiled=True)  7.3 us
    pallas_call x1, Pallas kernels, make_basis(): pl.pallas_call(functools.partial(basis_kernel, slots), grid=(rows // bloc...  7.17 us
    all_to_all x1, waiting for transfers between devices, body(): lax.all_to_all(spectra, axes, split_axis=0, concat_axis=0, tiled=True)  4.18 us
    all_to_all x1, starting transfers between devices, body(): lax.all_to_all(spectra, axes, split_axis=0, concat_axis=0, tiled=True)  2.75 us
  transfers between devices with their start and end apart: 3, of which 3 were waited for; matrix products, arithmetic and copies ran while one was open for 4% of the time, Pallas kernels for 11%

profile of v12, /device:TPU:0, one launch (start us, length us, event | category | flops | bytes accessed | tf_op | source)
XLA Modules:
  0.0 62.5 jit_solution(6333586848642197096)
XLA Ops:
  0.6 0.0 copy-start
  0.6 9.2 %shard_map.50 = bf16[32,72,128]{2,1,0:T(8,128)(2,1)} custom-call(bf16[64,9,2,512]{3,2,1,0:T(2,128)(2,1)} %alm_hbm.1, bf16[64,512,256]{2,1,0:T(8,128)(2,1)} %table_hbm.3), custom_call_target="tpu_custom_call" | custom-call | flops 301989888 | bytes 17956864 | tf_op jit(solution)/shard_map/pallas_call | solution.py:354
  9.8 7.3 %all-to-all-start = ((bf16[32,72,128]{2,1,0:T(8,128)(2,1)}), bf16[32,72,128]{2,1,0:T(8,128)(2,1)S(1)}, u32[]{:S(2)}, u32[]{:S(2)}) async-start(bf16[32,72,128]{2,1,0:T(8,128)(2,1)} %shard_map.50), calls=%async_computation | async-start | bytes 1179648 | tf_op jit(solution)/shard_map/all_to_all | solution.py:456
  17.1 0.0 copy-done
  17.1 0.1 broadcast_in_dim.11
  17.2 1.1 %convert_element_type.27.order_ref = f32[2048,1]{1,0:T(8,128)S(1)} reshape(f32[32,2,32]{2,1,0:T(2,128)S(1)} %broadcast_in_dim.13) | data formatting | bytes 16384 | tf_op jit(solution)/shard_map/convert_element_type | solution.py:467
  18.4 0.1 reshape.91
  18.5 7.2 %shard_map.51 = bf16[4,2048,512]{2,1,0:T(8,128)(2,1)} custom-call(f32[2048,1]{1,0:T(8,128)S(1)} %convert_element_type.27.order_ref), custom_call_target="tpu_custom_call" | custom-call | flops 33554432 | bytes 8388608 | tf_op jit(solution)/shard_map/pallas_call | solution.py:74
  25.7 7.9 %all-to-all-done = bf16[32,72,128]{2,1,0:T(8,128)(2,1)S(1)} async-done(((bf16[32,72,128]{2,1,0:T(8,128)(2,1)}), bf16[32,72,128]{2,1,0:T(8,128)(2,1)S(1)}, u32[]{:S(2)}, u32[]{:S(2)}) %all-to-all-start) | async-done | bytes 589856 | tf_op jit(solution)/shard_map/all_to_all | solution.py:456
  33.5 9.1 %shard_map.52 = (f32[32,8,128]{2,1,0:T(8,128)S(1)}, bf16[16,2,8,128]{3,2,1,0:T(8,128)(2,1)}) custom-call(bf16[16,2,72,128]{3,2,1,0:T(8,128)(2,1)S(1)} %bitcast.10, f32[1,2048]{1,0:T(1,128)S(1)} %fusion.3.odd_ref, bf16[16,512,512]{2,1,0:T(8,128)(2,1)} %bitcast.13), custom_call_target="tpu_custom_call" | custom-call | flops 1342177280 | bytes 8388608 | tf_op jit(solution)/shard_map/pallas_call | solution.py:274
  42.6 1.7 %collective-permute-start = (f32[32,8,128]{2,1,0:T(8,128)S(1)}, f32[32,8,128]{2,1,0:T(8,128)S(1)}, u32[]{:S(2)}, u32[]{:S(2)}) collective-permute-start(f32[32,8,128]{2,1,0:T(8,128)S(1)} %get-tuple-element.7), channel_id=1, source_target_pairs={{0,1},{1,0},{2,3},{3,2},{4,5},{5,4},{6,7},{7,6},{8,9},{9,8},{10,11... | collective-permute-start | bytes 393224 | tf_op jit(solution)/shard_map/ppermute | solution.py:427
  44.3 2.8 %all-to-all-start.1 = ((bf16[32,8,128]{2,1,0:T(8,128)(2,1)}), bf16[32,8,128]{2,1,0:T(8,128)(2,1)S(1)}, u32[]{:S(2)}, u32[]{:S(2)}) async-start(bf16[32,8,128]{2,1,0:T(8,128)(2,1)} %bitcast.2), calls=%async_computation.1 | async-start | bytes 131072 | tf_op jit(solution)/shard_map/all_to_all | solution.py:476
  47.1 1.9 %collective-permute-done = f32[32,8,128]{2,1,0:T(8,128)S(1)} collective-permute-done((f32[32,8,128]{2,1,0:T(8,128)S(1)}, f32[32,8,128]{2,1,0:T(8,128)S(1)}, u32[]{:S(2)}, u32[]{:S(2)}) %collective-permute-start) | collective-permute-done | bytes 131104 | tf_op jit(solution)/shard_map/ppermute | solution.py:427
  49.0 0.1 fusion.2
  49.1 0.1 fusion
  49.2 0.2 copy.6
  49.4 0.9 %reshape.94 = f32[16,2048]{1,0:T(8,128)} reshape(f32[2,8,64,32]{3,2,1,0:T(8,128)S(1)} %copy.6) | data formatting | bytes 262144 | tf_op jit(solution)/shard_map/reshape | solution.py:480
  50.3 4.2 %all-to-all-done.1 = bf16[32,8,128]{2,1,0:T(8,128)(2,1)S(1)} async-done(((bf16[32,8,128]{2,1,0:T(8,128)(2,1)}), bf16[32,8,128]{2,1,0:T(8,128)(2,1)S(1)}, u32[]{:S(2)}, u32[]{:S(2)}) %all-to-all-start.1) | async-done | bytes 65568 | tf_op jit(solution)/shard_map/all_to_all | solution.py:476
  54.5 7.8 %shard_map.53 = f32[64,2,512]{2,1,0:T(2,128)} custom-call(bf16[64,512,256]{2,1,0:T(8,128)(2,1)} %table_hbm.3, bf16[256,128]{1,0:T(8,128)(2,1)S(1)} %bitcast.11), custom_call_target="tpu_custom_call" | custom-call | flops 268435456 | bytes 16777216 | tf_op jit(solution)/shard_map/pallas_call | solution.py:404
  (4 shorter events, 0.1 us)
Async XLA Ops:
  0.6 16.5 %copy-start = (s32[1024]{0:T(1024)S(1)}, s32[1024]{0:T(1024)}, u32[]{:S(2)}) copy-start(s32[1024]{0:T(1024)} %param.5) | copy-start | bytes 12292
  9.8 23.7 %all-to-all-start = ((bf16[32,72,128]{2,1,0:T(8,128)(2,1)}), bf16[32,72,128]{2,1,0:T(8,128)(2,1)S(1)}, u32[]{:S(2)}, u32[]{:S(2)}) async-start(bf16[32,72,128]{2,1,0:T(8,128)(2,1)} %shard_map.50), calls=%async_computation | async-start | bytes 1179648 | tf_op jit(solution)/shard_map/all_to_all | solution.py:456
  42.6 6.4 %collective-permute-start = (f32[32,8,128]{2,1,0:T(8,128)S(1)}, f32[32,8,128]{2,1,0:T(8,128)S(1)}, u32[]{:S(2)}, u32[]{:S(2)}) collective-permute-start(f32[32,8,128]{2,1,0:T(8,128)S(1)} %get-tuple-element.7), channel_id=1, source_target_pairs={{0,1},{1,0},{2,3},{3,2},{4,5},{5,4},{6,7},{7,6},{8,9},{9,8},{10,11... | collective-permute-start | bytes 393224 | tf_op jit(solution)/shard_map/ppermute | solution.py:427
  44.3 10.2 %all-to-all-start.1 = ((bf16[32,8,128]{2,1,0:T(8,128)(2,1)}), bf16[32,8,128]{2,1,0:T(8,128)(2,1)S(1)}, u32[]{:S(2)}, u32[]{:S(2)}) async-start(bf16[32,8,128]{2,1,0:T(8,128)(2,1)} %bitcast.2), calls=%async_computation.1 | async-start | bytes 131072 | tf_op jit(solution)/shard_map/all_to_all | solution.py:476

commit v13 on v12

--- a/solution.py
+++ b/solution.py
@@ -149,8 +149,9 @@
     return found
 
 
-def ilc_kernel(modes_ref, odd_ref, basis_hbm, ilc_ref, spectra_ref, basis_ref, lhs_ref, maps_ref, sums_ref, low_ref, found_ref, sems):
-    groups, shares, rows, width = modes_ref.shape
+def ilc_kernel(places, modes_ref, odd_ref, basis_hbm, ilc_ref, spectra_ref, basis_ref, lhs_ref, maps_ref, sums_ref, low_ref, found_ref, sems):
+    _, rows, width = modes_ref.shape
+    groups, shares = len(places), len(places[0])
     columns = basis_ref.shape[2]
     depth = lhs_ref.shape[1]
     pieces, share_rows = found_ref.shape[0], found_ref.shape[2]
@@ -162,9 +163,9 @@
     for group in range(groups):
         span = slice(group * width, (group + 1) * width)
         odd = odd_ref[:, span]
-        values = modes_ref[group, 0].astype(jnp.float32)
-        for share in range(1, shares):
-            values = values + modes_ref[group, share].astype(jnp.float32)
+        values = modes_ref[places[group][0]].astype(jnp.float32)
+        for place in places[group][1:]:
+            values = values + modes_ref[place].astype(jnp.float32)
         lhs_ref[0:rows, span] = (values * (1.0 - odd)).astype(jnp.bfloat16)
         lhs_ref[second : second + rows, span] = (values * odd).astype(jnp.bfloat16)
     low_half = lax.broadcasted_iota(jnp.int32, (cycles, LANES), 1) < HALF
@@ -264,15 +265,16 @@
             spectra_ref[group, share] = value
 
 
-def run_ilc(modes, odd, basis):
-    groups, shares, rows, width = modes.shape
+def run_ilc(modes, odd, basis, places):
+    _, rows, width = modes.shape
+    groups, shares = len(places), len(places[0])
     chunks, depth, columns = basis.shape
     pieces = CHUNK // 2
     basis = basis.reshape(chunks * pieces, depth // pieces, columns)
     cycles = rows // C
     vmem = pl.BlockSpec(memory_space=pltpu.VMEM)
     return pl.pallas_call(
-        ilc_kernel,
+        functools.partial(ilc_kernel, places),
         in_specs=[vmem, vmem, pl.BlockSpec(memory_space=pl.ANY)],
         out_specs=[vmem, vmem],
         out_shape=[
@@ -297,7 +299,7 @@
     )(modes, odd, basis)
 
 
-def modes_kernel(alm_hbm, table_hbm, out_hbm, alm_ref, table_ref, held_ref, turned_ref, out_ref, alm_sems, sems, out_sems):
+def modes_kernel(order, alm_hbm, table_hbm, out_hbm, alm_ref, table_ref, held_ref, turned_ref, out_ref, alm_sems, sems, out_sems):
     parts = sems.shape[0]
     total_slots, degrees, total = table_ref.shape
     slots = total_slots // parts
@@ -334,17 +336,18 @@
         if (part + 1) * HALVES % parts == 0:
             turn((part + 1) * HALVES // parts - 1)
     each = targets // out_sems.shape[0]
-    for target in range(targets):
+    for at, target in enumerate(order):
         span = slice(target * cycles, (target + 1) * cycles)
         block = jnp.concatenate([turned_ref[chan, span, :] for chan in range(C)], axis=0)
-        out_ref[target] = block.astype(jnp.bfloat16)
-        if (target + 1) % each == 0:
-            part_copy(out_ref, out_hbm, out_sems, target // each).start()
+        out_ref[at] = block.astype(jnp.bfloat16)
+        if (at + 1) % each == 0:
+            part_copy(out_ref, out_hbm, out_sems, at // each).start()
     for part in range(out_sems.shape[0]):
         part_copy(out_ref, out_hbm, out_sems, part).wait()
 
 
-def make_modes(alm, legendre, targets):
+def make_modes(alm, legendre, order):
+    targets = len(order)
     slot_count, degrees, total = legendre.shape
     slots = 4
     parts = slot_count // slots
@@ -352,7 +355,7 @@
     height = 2 * C
     out = jax.ShapeDtypeStruct((targets, C * (total // targets), width), jnp.bfloat16)
     return pl.pallas_call(
-        modes_kernel,
+        functools.partial(modes_kernel, order),
         in_specs=[pl.BlockSpec(memory_space=pl.ANY)] * 2,
         out_specs=pl.BlockSpec(memory_space=pl.ANY),
         out_shape=out,
@@ -439,7 +442,8 @@
 
 def body(alm, legendre, order_of_slot):
     tile_count = lax.axis_size("tile")
-    band_count = lax.axis_size("band")
+    chip_count, core_count = lax.axis_size("chip"), lax.axis_size("core")
+    band_count = chip_count * core_count
     tile_at = lax.axis_index("tile")
     slot_count = alm.shape[0]
     targets = band_count * tile_count
@@ -450,30 +454,37 @@
     group_width = math.lcm(width, LANES)
     groups = depth // group_width
     plain = group_width == width and padded == cycles
-    axes = ("band", "tile")
-
-    partial = make_modes(alm, legendre, targets)
-    partial = lax.all_to_all(partial, axes, split_axis=0, concat_axis=0, tiled=True)
-    modes = partial.reshape(band_count, tile_count, C * cycles, width)
-    if not plain:
-        modes = jnp.sum(modes.astype(jnp.float32), axis=1).astype(jnp.bfloat16)
+    order = [
+        (chip * core_count + core) * tile_count + tile
+        for core in range(core_count)
+        for tile in range(tile_count)
+        for chip in range(chip_count)
+    ]
+    partial = make_modes(alm, legendre, order)
+    modes = lax.all_to_all(partial, ("core", "tile", "chip"), split_axis=0, concat_axis=0, tiled=True)
+    if plain:
+        places = [[order.index(band * tile_count + tile) for tile in range(tile_count)] for band in range(band_count)]
+    else:
+        places = [[group] for group in range(groups)]
+        modes = modes.reshape(core_count, tile_count, chip_count, C * cycles, width)
+        modes = jnp.sum(modes.astype(jnp.float32), axis=1).astype(jnp.bfloat16).transpose(1, 0, 2, 3)
         modes = modes.reshape(groups, group_width // width, C, cycles, width)
         modes = modes.transpose(0, 2, 3, 1, 4).reshape(groups, C, cycles, group_width)
         modes = jnp.pad(modes, ((0, 0), (0, 0), (0, padded - cycles), (0, 0)))
-        modes = modes.reshape(groups, 1, C * padded, group_width)
+        modes = modes.reshape(groups, C * padded, group_width)
 
     order_rows = order_of_slot.reshape(band_count * HALVES, 1, slot_count // HALVES)
     order_rows = jnp.broadcast_to(order_rows, (band_count * HALVES, 2, slot_count // HALVES)).reshape(depth)
     basis = make_basis(order_rows.astype(jnp.float32)[:, None], slot_count)
     odd = (order_rows % 2).astype(jnp.float32)[None, :]
-    vectors, spectra = run_ilc(modes, odd, basis)
+    vectors, spectra = run_ilc(modes, odd, basis, places)
 
     if not plain:
         spectra = spectra[:, 0, :cycles].reshape(groups, cycles, group_width // width, width)
         spectra = spectra.transpose(0, 2, 1, 3).reshape(band_count, 1, cycles, width)
         spectra = jnp.broadcast_to(spectra, (band_count, tile_count, cycles, width))
     spectra = spectra.reshape(targets, cycles, width)
-    routed = lax.all_to_all(spectra, axes, split_axis=0, concat_axis=0, tiled=True)
+    routed = lax.all_to_all(spectra, ("chip", "core", "tile"), split_axis=0, concat_axis=0, tiled=True)
     found = in_tile_order(from_other_tiles([vectors[:, :cycles]] * tile_count))
     lanes = LANES // tile_count
     found = lax.dynamic_slice_in_dim(found, tile_at * lanes, lanes, axis=3)
@@ -484,11 +495,16 @@
 
 
 def solution(mesh):
-    placed = (P("band", None, None, "tile"), P("band", "tile", None), P())
+    band_count, tile_count = mesh.shape["band"], mesh.shape["tile"]
+    core_count = 2 if band_count % 2 == 0 else 1
+    fine = jax.sharding.Mesh(
+        mesh.devices.reshape(band_count // core_count, core_count, tile_count), ("chip", "core", "tile")
+    )
+    band = ("chip", "core")
     return jax.shard_map(
         body,
-        mesh=mesh,
-        in_specs=placed,
-        out_specs=(P("band", "tile"), P("band", None, "tile")),
+        mesh=fine,
+        in_specs=(P(band, None, None, "tile"), P(band, "tile", None), P()),
+        out_specs=(P(band, "tile"), P(band, None, "tile")),
         check_vma=False,
     )

time: 62.7 us -> 63.5 us (1.013)
  waiting for transfers between devices: 14 us -> 15.3 us
  starting transfers between devices: 11.8 us -> 11.1 us
    all_to_all x2, waiting for transfers between devices: 12 us -> 13.4 us  [the longest x1 9.22 us: body(): lax.all_to_all(partial, ('core', 'tile', 'chip'), split_axis=0, concat_ax...]
    ppermute x1, starting transfers between devices: 1.71 us -> 1.08 us  [from_other_tiles(): lax.ppermute(sends[hop], 'tile', [(at, (at + hop) % count) for at in rang...]
where the time goes in v13:
time: 63.5 us; the launch traced here: 63.2 us
  Pallas kernels  33.2 us (52%)
  waiting for transfers between devices  15.3 us (24%)
  starting transfers between devices  11.1 us (17%)
  local copies, waits for them, and re-layouts  2.42 us (4%)
  between operations  0.88 us (1%)
    all_to_all x1, waiting for transfers between devices, body(): lax.all_to_all(partial, ('core', 'tile', 'chip'), split_axis=0, concat_ax...  9.22 us
    pallas_call x1, Pallas kernels, make_modes(): pl.pallas_call(functools.partial(modes_kernel, order), in_specs=[pl.Block...  9.15 us
    pallas_call x1, Pallas kernels, run_ilc(): pl.pallas_call(functools.partial(ilc_kernel, places), in_specs=[vmem, vme...  9.08 us
    pallas_call x1, Pallas kernels, analyse(): pl.pallas_call(analysis_kernel, in_specs=[pl.BlockSpec(memory_space=pl.AN...  7.82 us
    all_to_all x1, starting transfers between devices, body(): lax.all_to_all(partial, ('core', 'tile', 'chip'), split_axis=0, concat_ax...  7.3 us
    pallas_call x1, Pallas kernels, make_basis(): pl.pallas_call(functools.partial(basis_kernel, slots), grid=(rows // bloc...  7.17 us
    all_to_all x1, waiting for transfers between devices, body(): lax.all_to_all(spectra, ('chip', 'core', 'tile'), split_axis=0, concat_ax...  4.2 us
    all_to_all x1, starting transfers between devices, body(): lax.all_to_all(spectra, ('chip', 'core', 'tile'), split_axis=0, concat_ax...  2.75 us
  transfers between devices with their start and end apart: 3, of which 3 were waited for; matrix products, arithmetic and copies ran while one was open for 4% of the time, Pallas kernels for 11%

profile of v13, /device:TPU:0, one launch (start us, length us, event | category | flops | bytes accessed | tf_op | source)
XLA Modules:
  0.0 63.2 jit_solution(10051481951008613753)
XLA Ops:
  0.6 0.0 copy-start
  0.6 9.2 %shard_map.50 = bf16[32,72,128]{2,1,0:T(8,128)(2,1)} custom-call(bf16[64,9,2,512]{3,2,1,0:T(2,128)(2,1)} %alm_hbm.1, bf16[64,512,256]{2,1,0:T(8,128)(2,1)} %table_hbm.3), custom_call_target="tpu_custom_call" | custom-call | flops 301989888 | bytes 17956864 | tf_op jit(solution)/shard_map/pallas_call | solution.py:357
  9.8 7.3 %all-to-all-start = ((bf16[32,72,128]{2,1,0:T(8,128)(2,1)}), bf16[32,72,128]{2,1,0:T(8,128)(2,1)S(1)}, u32[]{:S(2)}, u32[]{:S(2)}) async-start(bf16[32,72,128]{2,1,0:T(8,128)(2,1)} %shard_map.50), calls=%async_computation | async-start | bytes 1179648 | tf_op jit(solution)/shard_map/all_to_all | solution.py:464
  17.1 0.0 copy-done
  17.1 0.1 broadcast_in_dim.11
  17.2 1.1 %convert_element_type.27.order_ref = f32[2048,1]{1,0:T(8,128)S(1)} reshape(f32[32,2,32]{2,1,0:T(2,128)S(1)} %broadcast_in_dim.13) | data formatting | bytes 16384 | tf_op jit(solution)/shard_map/convert_element_type | solution.py:478
  18.3 0.1 reshape.87
  18.4 7.2 %shard_map.51 = bf16[4,2048,512]{2,1,0:T(8,128)(2,1)} custom-call(f32[2048,1]{1,0:T(8,128)S(1)} %convert_element_type.27.order_ref), custom_call_target="tpu_custom_call" | custom-call | flops 33554432 | bytes 8388608 | tf_op jit(solution)/shard_map/pallas_call | solution.py:74
  25.6 9.2 %all-to-all-done.modes_ref = bf16[32,72,128]{2,1,0:T(8,128)(2,1)S(1)} async-done(((bf16[32,72,128]{2,1,0:T(8,128)(2,1)}), bf16[32,72,128]{2,1,0:T(8,128)(2,1)S(1)}, u32[]{:S(2)}, u32[]{:S(2)}) %all-to-all-start) | async-done | bytes 589856 | tf_op jit(solution)/shard_map/all_to_all | solution.py:464
  34.9 9.1 %shard_map.52 = (f32[32,8,128]{2,1,0:T(8,128)S(1)}, bf16[16,2,8,128]{3,2,1,0:T(8,128)(2,1)}) custom-call(bf16[32,72,128]{2,1,0:T(8,128)(2,1)S(1)} %all-to-all-done.modes_ref, f32[1,2048]{1,0:T(1,128)S(1)} %fusion.3.odd_ref, bf16[16,512,512]{2,1,0:T(8,128)(2,1)} %bitcast.11), custom_call_target="tpu_custom_call" | custom-call | flops 1342177280 | bytes 8388608 | tf_op jit(solution)/shard_map/pallas_call | solution.py:276
  44.0 1.1 %collective-permute-start = (f32[32,8,128]{2,1,0:T(8,128)S(1)}, f32[32,8,128]{2,1,0:T(8,128)S(1)}, u32[]{:S(2)}, u32[]{:S(2)}) collective-permute-start(f32[32,8,128]{2,1,0:T(8,128)S(1)} %get-tuple-element.7), channel_id=1, source_target_pairs={{0,1},{1,0},{2,3},{3,2},{4,5},{5,4},{6,7},{7,6},{8,9},{9,8},{10,11... | collective-permute-start | bytes 393224 | tf_op jit(solution)/shard_map/ppermute | solution.py:430
  45.0 2.8 %all-to-all-start.1 = ((bf16[32,8,128]{2,1,0:T(8,128)(2,1)}), bf16[32,8,128]{2,1,0:T(8,128)(2,1)S(1)}, u32[]{:S(2)}, u32[]{:S(2)}) async-start(bf16[32,8,128]{2,1,0:T(8,128)(2,1)} %bitcast.1), calls=%async_computation.1 | async-start | bytes 131072 | tf_op jit(solution)/shard_map/all_to_all | solution.py:487
  47.8 1.9 %collective-permute-done = f32[32,8,128]{2,1,0:T(8,128)S(1)} collective-permute-done((f32[32,8,128]{2,1,0:T(8,128)S(1)}, f32[32,8,128]{2,1,0:T(8,128)S(1)}, u32[]{:S(2)}, u32[]{:S(2)}) %collective-permute-start) | collective-permute-done | bytes 131104 | tf_op jit(solution)/shard_map/ppermute | solution.py:430
  49.7 0.1 fusion.2
  49.8 0.1 fusion
  49.9 0.2 copy.6
  50.1 0.9 %reshape.90 = f32[16,2048]{1,0:T(8,128)} reshape(f32[2,8,64,32]{3,2,1,0:T(8,128)S(1)} %copy.6) | data formatting | bytes 262144 | tf_op jit(solution)/shard_map/reshape | solution.py:491
  51.0 4.2 %all-to-all-done.1 = bf16[32,8,128]{2,1,0:T(8,128)(2,1)S(1)} async-done(((bf16[32,8,128]{2,1,0:T(8,128)(2,1)}), bf16[32,8,128]{2,1,0:T(8,128)(2,1)S(1)}, u32[]{:S(2)}, u32[]{:S(2)}) %all-to-all-start.1) | async-done | bytes 65568 | tf_op jit(solution)/shard_map/all_to_all | solution.py:487
  55.2 7.8 %shard_map.53 = f32[64,2,512]{2,1,0:T(2,128)} custom-call(bf16[64,512,256]{2,1,0:T(8,128)(2,1)} %table_hbm.3, bf16[256,128]{1,0:T(8,128)(2,1)S(1)} %bitcast.9), custom_call_target="tpu_custom_call" | custom-call | flops 268435456 | bytes 16777216 | tf_op jit(solution)/shard_map/pallas_call | solution.py:407
  (4 shorter events, 0.1 us)
Async XLA Ops:
  0.6 16.5 %copy-start = (s32[1024]{0:T(1024)S(1)}, s32[1024]{0:T(1024)}, u32[]{:S(2)}) copy-start(s32[1024]{0:T(1024)} %param.5) | copy-start | bytes 12292
  9.8 25.1 %all-to-all-start = ((bf16[32,72,128]{2,1,0:T(8,128)(2,1)}), bf16[32,72,128]{2,1,0:T(8,128)(2,1)S(1)}, u32[]{:S(2)}, u32[]{:S(2)}) async-start(bf16[32,72,128]{2,1,0:T(8,128)(2,1)} %shard_map.50), calls=%async_computation | async-start | bytes 1179648 | tf_op jit(solution)/shard_map/all_to_all | solution.py:464
  44.0 5.8 %collective-permute-start = (f32[32,8,128]{2,1,0:T(8,128)S(1)}, f32[32,8,128]{2,1,0:T(8,128)S(1)}, u32[]{:S(2)}, u32[]{:S(2)}) collective-permute-start(f32[32,8,128]{2,1,0:T(8,128)S(1)} %get-tuple-element.7), channel_id=1, source_target_pairs={{0,1},{1,0},{2,3},{3,2},{4,5},{5,4},{6,7},{7,6},{8,9},{9,8},{10,11... | collective-permute-start | bytes 393224 | tf_op jit(solution)/shard_map/ppermute | solution.py:430
  45.0 10.2 %all-to-all-start.1 = ((bf16[32,8,128]{2,1,0:T(8,128)(2,1)}), bf16[32,8,128]{2,1,0:T(8,128)(2,1)S(1)}, u32[]{:S(2)}, u32[]{:S(2)}) async-start(bf16[32,8,128]{2,1,0:T(8,128)(2,1)} %bitcast.1), calls=%async_computation.1 | async-start | bytes 131072 | tf_op jit(solution)/shard_map/all_to_all | solution.py:487

commit v14 on v12

--- a/solution.py
+++ b/solution.py
@@ -24,6 +24,7 @@
 SUMS = len(PAIRS) + 1
 VMEM_LIMIT = 48 * 1024 * 1024
 IN_FLIGHT = 6
+FIRST = 3
 HALVES = 2
 CHUNK = 8
 
@@ -90,22 +91,20 @@
     return pltpu.make_async_copy(source.at[span], target.at[span], sems.at[part])
 
 
-def start_parts(source, target, sems, count):
-    for part in range(min(count, sems.shape[0])):
+def started(parts, done, most):
+    return min(parts, done + min(most, FIRST + done))
+
+
+def start_parts(source, target, sems, most):
+    for part in range(started(sems.shape[0], 0, most)):
         part_copy(source, target, sems, part).start()
 
 
-def next_part(source, target, sems, part, ahead):
+def next_part(source, target, sems, part, most):
+    parts = sems.shape[0]
     part_copy(source, target, sems, part).wait()
-    more = part + ahead < sems.shape[0]
-    if isinstance(part, int):
-        if more:
-            part_copy(source, target, sems, part + ahead).start()
-    else:
-
-        @pl.when(more)
-        def _():
-            part_copy(source, target, sems, part + ahead).start()
+    for later in range(started(parts, part, most), started(parts, part + 1, most)):
+        part_copy(source, target, sems, later).start()
 
 
 def reciprocal(value):
@@ -179,10 +178,12 @@
         maps_ref[at, C] = squares
 
     def maps_of_chunk(chunk):
+        result = None
         for piece in range(pieces):
             next_part(basis_hbm, basis_ref, sems, chunk * pieces + piece, ahead)
-        basis = basis_ref[chunk * pieces : (chunk + 1) * pieces].reshape(depth, columns)
-        result = jnp.dot(lhs_ref[...], basis, preferred_element_type=jnp.float32)
+            lhs = lhs_ref[:, piece * share_rows : (piece + 1) * share_rows]
+            term = jnp.dot(lhs, basis_ref[chunk * pieces + piece], preferred_element_type=jnp.float32)
+            result = term if result is None else result + term
         for part in range(CHUNK // 2):
             at = CHUNK * chunk + 2 * part
             lanes = slice(part * LANES, (part + 1) * LANES)
@@ -304,7 +305,8 @@
     targets, rows = out_ref.shape[:2]
     cycles = rows // C
     height = 2 * C
-    start_parts(alm_hbm, alm_ref, alm_sems, parts)
+    for part in range(parts):
+        part_copy(alm_hbm, alm_ref, alm_sems, part).start()
     start_parts(table_hbm, table_ref, sems, IN_FLIGHT)
 
     def some_slots(part):
@@ -375,7 +377,7 @@
     )(alm, legendre)
 
 
-def analysis_kernel(table_hbm, spectra_ref, out_ref, table_ref, turned_ref, sems):
+def analysis_kernel(table_hbm, spectra_ref, out_hbm, table_ref, turned_ref, out_ref, sems, out_sems):
     total_slots, degrees, total = table_ref.shape
     slots = 8
     pieces = sems.shape[0] * slots // total_slots
@@ -394,6 +396,9 @@
             span = slice(slot * degrees, (slot + 1) * degrees)
             out_ref[first + slot, 0:1, :] = result[slot : slot + 1, span]
             out_ref[first + slot, 1:2, :] = result[slots + slot : slots + slot + 1, span]
+        part_copy(out_ref, out_hbm, out_sems, first // slots).start()
+    for part in range(out_sems.shape[0]):
+        part_copy(out_ref, out_hbm, out_sems, part).wait()
 
 
 def analyse(legendre, spectra):
@@ -404,12 +409,14 @@
     return pl.pallas_call(
         analysis_kernel,
         in_specs=[pl.BlockSpec(memory_space=pl.ANY), vmem],
-        out_specs=vmem,
+        out_specs=pl.BlockSpec(memory_space=pl.ANY),
         out_shape=jax.ShapeDtypeStruct((slot_count, 2, degrees), jnp.float32),
         scratch_shapes=[
             pltpu.VMEM(legendre.shape, jnp.bfloat16),
             pltpu.VMEM((width, total), jnp.float32),
+            pltpu.VMEM((slot_count, 2, degrees), jnp.float32),
             pltpu.SemaphoreType.DMA((slot_count // 4,)),
+            pltpu.SemaphoreType.DMA((slot_count // slots,)),
         ],
         cost_estimate=pl.CostEstimate(
             flops=2 * slot_count * degrees * total * 2 * slots,

time: 62.7 us -> 63.8 us (1.018)
  Pallas kernels: 33.2 us -> 34.3 us
where the time goes in v14:
time: 63.8 us; the launch traced here: 63.6 us
  Pallas kernels  34.3 us (54%)
  waiting for transfers between devices  14 us (22%)
  starting transfers between devices  11.8 us (18%)
  local copies, waits for them, and re-layouts  2.42 us (4%)
  between operations  0.88 us (1%)
    pallas_call x1, Pallas kernels, run_ilc(): pl.pallas_call(ilc_kernel, in_specs=[vmem, vmem, pl.BlockSpec(memory_spac...  9.64 us
    pallas_call x1, Pallas kernels, make_modes(): pl.pallas_call(modes_kernel, in_specs=[pl.BlockSpec(memory_space=pl.ANY)]...  9.38 us
    pallas_call x1, Pallas kernels, analyse(): pl.pallas_call(analysis_kernel, in_specs=[pl.BlockSpec(memory_space=pl.AN...  8.11 us
    all_to_all x1, waiting for transfers between devices, body(): lax.all_to_all(partial, axes, split_axis=0, concat_axis=0, tiled=True)  7.87 us
    all_to_all x1, starting transfers between devices, body(): lax.all_to_all(partial, axes, split_axis=0, concat_axis=0, tiled=True)  7.3 us
    pallas_call x1, Pallas kernels, make_basis(): pl.pallas_call(functools.partial(basis_kernel, slots), grid=(rows // bloc...  7.17 us
    all_to_all x1, waiting for transfers between devices, body(): lax.all_to_all(spectra, axes, split_axis=0, concat_axis=0, tiled=True)  4.18 us
    all_to_all x1, starting transfers between devices, body(): lax.all_to_all(spectra, axes, split_axis=0, concat_axis=0, tiled=True)  2.75 us
  transfers between devices with their start and end apart: 3, of which 3 were waited for; matrix products, arithmetic and copies ran while one was open for 4% of the time, Pallas kernels for 11%

profile of v14, /device:TPU:0, one launch (start us, length us, event | category | flops | bytes accessed | tf_op | source)
XLA Modules:
  0.0 63.6 jit_solution(416240496389457690)
XLA Ops:
  0.6 0.0 copy-start
  0.6 9.4 %shard_map.50 = bf16[32,72,128]{2,1,0:T(8,128)(2,1)} custom-call(bf16[64,9,2,512]{3,2,1,0:T(2,128)(2,1)} %alm_hbm.1, bf16[64,512,256]{2,1,0:T(8,128)(2,1)} %table_hbm.3), custom_call_target="tpu_custom_call" | custom-call | flops 301989888 | bytes 17956864 | tf_op jit(solution)/shard_map/pallas_call | solution.py:356
  10.0 7.3 %all-to-all-start = ((bf16[32,72,128]{2,1,0:T(8,128)(2,1)}), bf16[32,72,128]{2,1,0:T(8,128)(2,1)S(1)}, u32[]{:S(2)}, u32[]{:S(2)}) async-start(bf16[32,72,128]{2,1,0:T(8,128)(2,1)} %shard_map.50), calls=%async_computation | async-start | bytes 1179648 | tf_op jit(solution)/shard_map/all_to_all | solution.py:463
  17.3 0.0 copy-done
  17.3 0.1 broadcast_in_dim.11
  17.4 1.1 %convert_element_type.27.order_ref = f32[2048,1]{1,0:T(8,128)S(1)} reshape(f32[32,2,32]{2,1,0:T(2,128)S(1)} %broadcast_in_dim.13) | data formatting | bytes 16384 | tf_op jit(solution)/shard_map/convert_element_type | solution.py:474
  18.6 0.1 reshape.91
  18.7 7.2 %shard_map.51 = bf16[4,2048,512]{2,1,0:T(8,128)(2,1)} custom-call(f32[2048,1]{1,0:T(8,128)S(1)} %convert_element_type.27.order_ref), custom_call_target="tpu_custom_call" | custom-call | flops 33554432 | bytes 8388608 | tf_op jit(solution)/shard_map/pallas_call | solution.py:75
  25.9 7.9 %all-to-all-done = bf16[32,72,128]{2,1,0:T(8,128)(2,1)S(1)} async-done(((bf16[32,72,128]{2,1,0:T(8,128)(2,1)}), bf16[32,72,128]{2,1,0:T(8,128)(2,1)S(1)}, u32[]{:S(2)}, u32[]{:S(2)}) %all-to-all-start) | async-done | bytes 589856 | tf_op jit(solution)/shard_map/all_to_all | solution.py:463
  33.7 9.6 %shard_map.52 = (f32[32,8,128]{2,1,0:T(8,128)S(1)}, bf16[16,2,8,128]{3,2,1,0:T(8,128)(2,1)}) custom-call(bf16[16,2,72,128]{3,2,1,0:T(8,128)(2,1)S(1)} %bitcast.10, f32[1,2048]{1,0:T(1,128)S(1)} %fusion.3.odd_ref, bf16[16,512,512]{2,1,0:T(8,128)(2,1)} %bitcast.13), custom_call_target="tpu_custom_call" | custom-call | flops 1342177280 | bytes 8388608 | tf_op jit(solution)/shard_map/pallas_call | solution.py:275
  43.4 1.7 %collective-permute-start = (f32[32,8,128]{2,1,0:T(8,128)S(1)}, f32[32,8,128]{2,1,0:T(8,128)S(1)}, u32[]{:S(2)}, u32[]{:S(2)}) collective-permute-start(f32[32,8,128]{2,1,0:T(8,128)S(1)} %get-tuple-element.7), channel_id=1, source_target_pairs={{0,1},{1,0},{2,3},{3,2},{4,5},{5,4},{6,7},{7,6},{8,9},{9,8},{10,11... | collective-permute-start | bytes 393224 | tf_op jit(solution)/shard_map/ppermute | solution.py:434
  45.1 2.8 %all-to-all-start.1 = ((bf16[32,8,128]{2,1,0:T(8,128)(2,1)}), bf16[32,8,128]{2,1,0:T(8,128)(2,1)S(1)}, u32[]{:S(2)}, u32[]{:S(2)}) async-start(bf16[32,8,128]{2,1,0:T(8,128)(2,1)} %bitcast.2), calls=%async_computation.1 | async-start | bytes 131072 | tf_op jit(solution)/shard_map/all_to_all | solution.py:483
  47.9 1.9 %collective-permute-done = f32[32,8,128]{2,1,0:T(8,128)S(1)} collective-permute-done((f32[32,8,128]{2,1,0:T(8,128)S(1)}, f32[32,8,128]{2,1,0:T(8,128)S(1)}, u32[]{:S(2)}, u32[]{:S(2)}) %collective-permute-start) | collective-permute-done | bytes 131104 | tf_op jit(solution)/shard_map/ppermute | solution.py:434
  49.8 0.1 fusion.2
  49.9 0.1 fusion
  50.0 0.2 copy.6
  50.2 0.9 %reshape.94 = f32[16,2048]{1,0:T(8,128)} reshape(f32[2,8,64,32]{3,2,1,0:T(8,128)S(1)} %copy.6) | data formatting | bytes 262144 | tf_op jit(solution)/shard_map/reshape | solution.py:487
  51.1 4.2 %all-to-all-done.1 = bf16[32,8,128]{2,1,0:T(8,128)(2,1)S(1)} async-done(((bf16[32,8,128]{2,1,0:T(8,128)(2,1)}), bf16[32,8,128]{2,1,0:T(8,128)(2,1)S(1)}, u32[]{:S(2)}, u32[]{:S(2)}) %all-to-all-start.1) | async-done | bytes 65568 | tf_op jit(solution)/shard_map/all_to_all | solution.py:483
  55.3 8.1 %shard_map.53 = f32[64,2,512]{2,1,0:T(2,128)} custom-call(bf16[64,512,256]{2,1,0:T(8,128)(2,1)} %table_hbm.3, bf16[256,128]{1,0:T(8,128)(2,1)S(1)} %bitcast.11), custom_call_target="tpu_custom_call" | custom-call | flops 268435456 | bytes 16777216 | tf_op jit(solution)/shard_map/pallas_call | solution.py:409
  (4 shorter events, 0.1 us)
Async XLA Ops:
  0.6 16.7 %copy-start = (s32[1024]{0:T(1024)S(1)}, s32[1024]{0:T(1024)}, u32[]{:S(2)}) copy-start(s32[1024]{0:T(1024)} %param.5) | copy-start | bytes 12292
  10.0 23.7 %all-to-all-start = ((bf16[32,72,128]{2,1,0:T(8,128)(2,1)}), bf16[32,72,128]{2,1,0:T(8,128)(2,1)S(1)}, u32[]{:S(2)}, u32[]{:S(2)}) async-start(bf16[32,72,128]{2,1,0:T(8,128)(2,1)} %shard_map.50), calls=%async_computation | async-start | bytes 1179648 | tf_op jit(solution)/shard_map/all_to_all | solution.py:463
  43.4 6.4 %collective-permute-start = (f32[32,8,128]{2,1,0:T(8,128)S(1)}, f32[32,8,128]{2,1,0:T(8,128)S(1)}, u32[]{:S(2)}, u32[]{:S(2)}) collective-permute-start(f32[32,8,128]{2,1,0:T(8,128)S(1)} %get-tuple-element.7), channel_id=1, source_target_pairs={{0,1},{1,0},{2,3},{3,2},{4,5},{5,4},{6,7},{7,6},{8,9},{9,8},{10,11... | collective-permute-start | bytes 393224 | tf_op jit(solution)/shard_map/ppermute | solution.py:434
  45.1 10.2 %all-to-all-start.1 = ((bf16[32,8,128]{2,1,0:T(8,128)(2,1)}), bf16[32,8,128]{2,1,0:T(8,128)(2,1)S(1)}, u32[]{:S(2)}, u32[]{:S(2)}) async-start(bf16[32,8,128]{2,1,0:T(8,128)(2,1)} %bitcast.2), calls=%async_computation.1 | async-start | bytes 131072 | tf_op jit(solution)/shard_map/all_to_all | solution.py:483

commit v15 on v12

--- a/solution.py
+++ b/solution.py
@@ -23,7 +23,7 @@
 PAIRS = [(a_at, b_at) for a_at in range(REST) for b_at in range(a_at, REST)] + [(a_at, REST) for a_at in range(REST)]
 SUMS = len(PAIRS) + 1
 VMEM_LIMIT = 48 * 1024 * 1024
-IN_FLIGHT = 6
+IN_FLIGHT = 4
 HALVES = 2
 CHUNK = 8
 
@@ -157,7 +157,7 @@
     chunks = basis_ref.shape[0] // pieces
     cycles = rows // C
     second = round_up(rows, 16)
-    ahead = 2 * pieces
+    ahead = 3
     start_parts(basis_hbm, basis_ref, sems, ahead)
     for group in range(groups):
         span = slice(group * width, (group + 1) * width)
@@ -179,8 +179,7 @@
         maps_ref[at, C] = squares
 
     def maps_of_chunk(chunk):
-        for piece in range(pieces):
-            next_part(basis_hbm, basis_ref, sems, chunk * pieces + piece, ahead)
+        next_part(basis_hbm, basis_ref, sems, chunk, ahead)
         basis = basis_ref[chunk * pieces : (chunk + 1) * pieces].reshape(depth, columns)
         result = jnp.dot(lhs_ref[...], basis, preferred_element_type=jnp.float32)
         for part in range(CHUNK // 2):
@@ -286,7 +285,7 @@
             pltpu.VMEM((SUMS, cycles, LANES), jnp.float32),
             pltpu.VMEM((chunks, pieces, 2 * cycles, LANES), jnp.bfloat16),
             pltpu.VMEM((pieces, 2 * cycles, depth // pieces), jnp.float32),
-            pltpu.SemaphoreType.DMA((chunks * pieces,)),
+            pltpu.SemaphoreType.DMA((chunks,)),
         ],
         cost_estimate=pl.CostEstimate(
             flops=2 * chunks * depth * columns * (2 * rows + 2 * cycles),
@@ -297,20 +296,18 @@
     )(modes, odd, basis)
 
 
-def modes_kernel(alm_hbm, table_hbm, out_hbm, alm_ref, table_ref, held_ref, turned_ref, out_ref, alm_sems, sems, out_sems):
+def modes_kernel(alm_hbm, table_hbm, out_hbm, alm_ref, table_ref, held_ref, turned_ref, out_ref, alm_sem, sems, out_sems):
     parts = sems.shape[0]
     total_slots, degrees, total = table_ref.shape
-    slots = total_slots // parts
+    each, slots = total_slots // parts, 4
     targets, rows = out_ref.shape[:2]
     cycles = rows // C
     height = 2 * C
-    start_parts(alm_hbm, alm_ref, alm_sems, parts)
+    alm_copy = pltpu.make_async_copy(alm_hbm, alm_ref, alm_sem)
+    alm_copy.start()
     start_parts(table_hbm, table_ref, sems, IN_FLIGHT)
 
-    def some_slots(part):
-        part_copy(alm_hbm, alm_ref, alm_sems, part).wait()
-        next_part(table_hbm, table_ref, sems, part, IN_FLIGHT)
-        first = part * slots
+    def some_slots(first):
         lhs = alm_ref[first : first + slots].reshape(slots * height, degrees)
         rhs = jnp.concatenate([table_ref[first + slot] for slot in range(slots)], axis=1)
         result = jnp.dot(lhs, rhs, preferred_element_type=jnp.float32)
@@ -329,8 +326,11 @@
                 span = slice(half * 2 * count, (half + 1) * 2 * count)
                 turned_ref[chan, lanes * LANES : (lanes + 1) * LANES, span] = jnp.concatenate(both, axis=0).T
 
+    alm_copy.wait()
     for part in range(parts):
-        some_slots(part)
+        next_part(table_hbm, table_ref, sems, part, IN_FLIGHT)
+        for first in range(part * each, (part + 1) * each, slots):
+            some_slots(first)
         if (part + 1) * HALVES % parts == 0:
             turn((part + 1) * HALVES // parts - 1)
     each = targets // out_sems.shape[0]
@@ -346,8 +346,7 @@
 
 def make_modes(alm, legendre, targets):
     slot_count, degrees, total = legendre.shape
-    slots = 4
-    parts = slot_count // slots
+    parts = slot_count // 8
     width = 2 * slot_count
     height = 2 * C
     out = jax.ShapeDtypeStruct((targets, C * (total // targets), width), jnp.bfloat16)
@@ -362,7 +361,7 @@
             pltpu.VMEM((total // LANES, slot_count * height, LANES), jnp.float32),
             pltpu.VMEM((C, total, width), jnp.float32),
             pltpu.VMEM(out.shape, out.dtype),
-            pltpu.SemaphoreType.DMA((parts,)),
+            pltpu.SemaphoreType.DMA,
             pltpu.SemaphoreType.DMA((parts,)),
             pltpu.SemaphoreType.DMA((4,)),
         ],
@@ -378,7 +377,6 @@
 def analysis_kernel(table_hbm, spectra_ref, out_ref, table_ref, turned_ref, sems):
     total_slots, degrees, total = table_ref.shape
     slots = 8
-    pieces = sems.shape[0] * slots // total_slots
     start_parts(table_hbm, table_ref, sems, IN_FLIGHT)
     turned_ref[...] = spectra_ref[...].astype(jnp.float32).T
     count = total_slots // HALVES
@@ -386,8 +384,7 @@
         row = first // count * 2 * count + first % count
         rows = [turned_ref[row + share * count : row + share * count + slots, :] for share in range(2)]
         lhs = jnp.concatenate(rows, axis=0).astype(jnp.bfloat16)
-        for piece in range(pieces):
-            next_part(table_hbm, table_ref, sems, first // slots * pieces + piece, IN_FLIGHT)
+        next_part(table_hbm, table_ref, sems, first // slots, IN_FLIGHT)
         table = table_ref[first : first + slots].reshape(slots * degrees, total)
         result = lax.dot_general(lhs, table, (((1,), (1,)), ((), ())), preferred_element_type=jnp.float32)
         for slot in range(slots):
@@ -409,7 +406,7 @@
         scratch_shapes=[
             pltpu.VMEM(legendre.shape, jnp.bfloat16),
             pltpu.VMEM((width, total), jnp.float32),
-            pltpu.SemaphoreType.DMA((slot_count // 4,)),
+            pltpu.SemaphoreType.DMA((slot_count // slots,)),
         ],
         cost_estimate=pl.CostEstimate(
             flops=2 * slot_count * degrees * total * 2 * slots,

time: 62.7 us -> 62.4 us (level)
  transfers between devices with their start and end apart: 3 -> 3, of which waited for: 3 -> 3; matrix products, arithmetic and copies ran while one was open for 4% -> 4% of each run, Pallas kernels for 11% -> 12%
where the time goes in v15:
time: 62.4 us; the launch traced here: 62.1 us
  Pallas kernels  32.9 us (53%)
  waiting for transfers between devices  14 us (22%)
  starting transfers between devices  11.8 us (19%)
  local copies, waits for them, and re-layouts  2.42 us (4%)
  between operations  0.88 us (1%)
    pallas_call x1, Pallas kernels, make_modes(): pl.pallas_call(modes_kernel, in_specs=[pl.BlockSpec(memory_space=pl.ANY)]...  9.14 us
    pallas_call x1, Pallas kernels, run_ilc(): pl.pallas_call(ilc_kernel, in_specs=[vmem, vmem, pl.BlockSpec(memory_spac...  8.83 us
    all_to_all x1, waiting for transfers between devices, body(): lax.all_to_all(partial, axes, split_axis=0, concat_axis=0, tiled=True)  7.87 us
    pallas_call x1, Pallas kernels, analyse(): pl.pallas_call(analysis_kernel, in_specs=[pl.BlockSpec(memory_space=pl.AN...  7.73 us
    all_to_all x1, starting transfers between devices, body(): lax.all_to_all(partial, axes, split_axis=0, concat_axis=0, tiled=True)  7.3 us
    pallas_call x1, Pallas kernels, make_basis(): pl.pallas_call(functools.partial(basis_kernel, slots), grid=(rows // bloc...  7.17 us
    all_to_all x1, waiting for transfers between devices, body(): lax.all_to_all(spectra, axes, split_axis=0, concat_axis=0, tiled=True)  4.18 us
    all_to_all x1, starting transfers between devices, body(): lax.all_to_all(spectra, axes, split_axis=0, concat_axis=0, tiled=True)  2.75 us
  transfers between devices with their start and end apart: 3, of which 3 were waited for; matrix products, arithmetic and copies ran while one was open for 4% of the time, Pallas kernels for 12%

profile of v15, /device:TPU:0, one launch (start us, length us, event | category | flops | bytes accessed | tf_op | source)
XLA Modules:
  0.0 62.1 jit_solution(16819994364390939577)
XLA Ops:
  0.6 0.0 copy-start
  0.6 9.1 %shard_map.50 = bf16[32,72,128]{2,1,0:T(8,128)(2,1)} custom-call(bf16[64,9,2,512]{3,2,1,0:T(2,128)(2,1)} %alm_hbm.1, bf16[64,512,256]{2,1,0:T(8,128)(2,1)} %table_hbm.3), custom_call_target="tpu_custom_call" | custom-call | flops 301989888 | bytes 17956864 | tf_op jit(solution)/shard_map/pallas_call | solution.py:353
  9.8 7.3 %all-to-all-start = ((bf16[32,72,128]{2,1,0:T(8,128)(2,1)}), bf16[32,72,128]{2,1,0:T(8,128)(2,1)S(1)}, u32[]{:S(2)}, u32[]{:S(2)}) async-start(bf16[32,72,128]{2,1,0:T(8,128)(2,1)} %shard_map.50), calls=%async_computation | async-start | bytes 1179648 | tf_op jit(solution)/shard_map/all_to_all | solution.py:453
  17.1 0.0 copy-done
  17.1 0.1 broadcast_in_dim.11
  17.2 1.1 %convert_element_type.27.order_ref = f32[2048,1]{1,0:T(8,128)S(1)} reshape(f32[32,2,32]{2,1,0:T(2,128)S(1)} %broadcast_in_dim.13) | data formatting | bytes 16384 | tf_op jit(solution)/shard_map/convert_element_type | solution.py:464
  18.3 0.1 reshape.91
  18.4 7.2 %shard_map.51 = bf16[4,2048,512]{2,1,0:T(8,128)(2,1)} custom-call(f32[2048,1]{1,0:T(8,128)S(1)} %convert_element_type.27.order_ref), custom_call_target="tpu_custom_call" | custom-call | flops 33554432 | bytes 8388608 | tf_op jit(solution)/shard_map/pallas_call | solution.py:74
  25.6 7.9 %all-to-all-done = bf16[32,72,128]{2,1,0:T(8,128)(2,1)S(1)} async-done(((bf16[32,72,128]{2,1,0:T(8,128)(2,1)}), bf16[32,72,128]{2,1,0:T(8,128)(2,1)S(1)}, u32[]{:S(2)}, u32[]{:S(2)}) %all-to-all-start) | async-done | bytes 589856 | tf_op jit(solution)/shard_map/all_to_all | solution.py:453
  33.5 8.8 %shard_map.52 = (f32[32,8,128]{2,1,0:T(8,128)S(1)}, bf16[16,2,8,128]{3,2,1,0:T(8,128)(2,1)}) custom-call(bf16[16,2,72,128]{3,2,1,0:T(8,128)(2,1)S(1)} %bitcast.10, f32[1,2048]{1,0:T(1,128)S(1)} %fusion.3.odd_ref, bf16[16,512,512]{2,1,0:T(8,128)(2,1)} %bitcast.13), custom_call_target="tpu_custom_call" | custom-call | flops 1342177280 | bytes 8388608 | tf_op jit(solution)/shard_map/pallas_call | solution.py:273
  42.3 1.7 %collective-permute-start = (f32[32,8,128]{2,1,0:T(8,128)S(1)}, f32[32,8,128]{2,1,0:T(8,128)S(1)}, u32[]{:S(2)}, u32[]{:S(2)}) collective-permute-start(f32[32,8,128]{2,1,0:T(8,128)S(1)} %get-tuple-element.7), channel_id=1, source_target_pairs={{0,1},{1,0},{2,3},{3,2},{4,5},{5,4},{6,7},{7,6},{8,9},{9,8},{10,11... | collective-permute-start | bytes 393224 | tf_op jit(solution)/shard_map/ppermute | solution.py:424
  44.1 2.8 %all-to-all-start.1 = ((bf16[32,8,128]{2,1,0:T(8,128)(2,1)}), bf16[32,8,128]{2,1,0:T(8,128)(2,1)S(1)}, u32[]{:S(2)}, u32[]{:S(2)}) async-start(bf16[32,8,128]{2,1,0:T(8,128)(2,1)} %bitcast.2), calls=%async_computation.1 | async-start | bytes 131072 | tf_op jit(solution)/shard_map/all_to_all | solution.py:473
  46.8 1.9 %collective-permute-done = f32[32,8,128]{2,1,0:T(8,128)S(1)} collective-permute-done((f32[32,8,128]{2,1,0:T(8,128)S(1)}, f32[32,8,128]{2,1,0:T(8,128)S(1)}, u32[]{:S(2)}, u32[]{:S(2)}) %collective-permute-start) | collective-permute-done | bytes 131104 | tf_op jit(solution)/shard_map/ppermute | solution.py:424
  48.7 0.1 fusion.2
  48.8 0.1 fusion
  48.9 0.2 copy.6
  49.2 0.9 %reshape.94 = f32[16,2048]{1,0:T(8,128)} reshape(f32[2,8,64,32]{3,2,1,0:T(8,128)S(1)} %copy.6) | data formatting | bytes 262144 | tf_op jit(solution)/shard_map/reshape | solution.py:477
  50.1 4.2 %all-to-all-done.1 = bf16[32,8,128]{2,1,0:T(8,128)(2,1)S(1)} async-done(((bf16[32,8,128]{2,1,0:T(8,128)(2,1)}), bf16[32,8,128]{2,1,0:T(8,128)(2,1)S(1)}, u32[]{:S(2)}, u32[]{:S(2)}) %all-to-all-start.1) | async-done | bytes 65568 | tf_op jit(solution)/shard_map/all_to_all | solution.py:473
  54.2 7.7 %shard_map.53 = f32[64,2,512]{2,1,0:T(2,128)} custom-call(bf16[64,512,256]{2,1,0:T(8,128)(2,1)} %table_hbm.3, bf16[256,128]{1,0:T(8,128)(2,1)S(1)} %bitcast.11), custom_call_target="tpu_custom_call" | custom-call | flops 268435456 | bytes 16777216 | tf_op jit(solution)/shard_map/pallas_call | solution.py:401
  (4 shorter events, 0.1 us)
Async XLA Ops:
  0.6 16.5 %copy-start = (s32[1024]{0:T(1024)S(1)}, s32[1024]{0:T(1024)}, u32[]{:S(2)}) copy-start(s32[1024]{0:T(1024)} %param.5) | copy-start | bytes 12292
  9.8 23.7 %all-to-all-start = ((bf16[32,72,128]{2,1,0:T(8,128)(2,1)}), bf16[32,72,128]{2,1,0:T(8,128)(2,1)S(1)}, u32[]{:S(2)}, u32[]{:S(2)}) async-start(bf16[32,72,128]{2,1,0:T(8,128)(2,1)} %shard_map.50), calls=%async_computation | async-start | bytes 1179648 | tf_op jit(solution)/shard_map/all_to_all | solution.py:453
  42.3 6.4 %collective-permute-start = (f32[32,8,128]{2,1,0:T(8,128)S(1)}, f32[32,8,128]{2,1,0:T(8,128)S(1)}, u32[]{:S(2)}, u32[]{:S(2)}) collective-permute-start(f32[32,8,128]{2,1,0:T(8,128)S(1)} %get-tuple-element.7), channel_id=1, source_target_pairs={{0,1},{1,0},{2,3},{3,2},{4,5},{5,4},{6,7},{7,6},{8,9},{9,8},{10,11... | collective-permute-start | bytes 393224 | tf_op jit(solution)/shard_map/ppermute | solution.py:424
  44.1 10.2 %all-to-all-start.1 = ((bf16[32,8,128]{2,1,0:T(8,128)(2,1)}), bf16[32,8,128]{2,1,0:T(8,128)(2,1)S(1)}, u32[]{:S(2)}, u32[]{:S(2)}) async-start(bf16[32,8,128]{2,1,0:T(8,128)(2,1)} %bitcast.2), calls=%async_computation.1 | async-start | bytes 131072 | tf_op jit(solution)/shard_map/all_to_all | solution.py:473

commit v16 on v15

--- a/solution.py
+++ b/solution.py
@@ -24,6 +24,7 @@
 SUMS = len(PAIRS) + 1
 VMEM_LIMIT = 48 * 1024 * 1024
 IN_FLIGHT = 4
+BUNDLES = 2
 HALVES = 2
 CHUNK = 8
 
@@ -149,8 +150,11 @@
     return found
 
 
-def ilc_kernel(modes_ref, odd_ref, basis_hbm, ilc_ref, spectra_ref, basis_ref, lhs_ref, maps_ref, sums_ref, low_ref, found_ref, sems):
-    groups, shares, rows, width = modes_ref.shape
+def ilc_kernel(bundles, *refs):
+    modes_refs, refs = refs[:bundles], refs[bundles:]
+    odd_ref, basis_hbm, ilc_ref, spectra_ref, basis_ref, lhs_ref, maps_ref, sums_ref, low_ref, found_ref, sems = refs
+    groups, shares, _, width = modes_refs[0].shape
+    rows = sum(modes_ref.shape[2] for modes_ref in modes_refs)
     columns = basis_ref.shape[2]
     depth = lhs_ref.shape[1]
     pieces, share_rows = found_ref.shape[0], found_ref.shape[2]
@@ -162,9 +166,13 @@
     for group in range(groups):
         span = slice(group * width, (group + 1) * width)
         odd = odd_ref[:, span]
-        values = modes_ref[group, 0].astype(jnp.float32)
-        for share in range(1, shares):
-            values = values + modes_ref[group, share].astype(jnp.float32)
+        values = []
+        for modes_ref in modes_refs:
+            value = modes_ref[group, 0].astype(jnp.float32)
+            for share in range(1, shares):
+                value = value + modes_ref[group, share].astype(jnp.float32)
+            values.append(value)
+        values = jnp.concatenate(values, axis=0)
         lhs_ref[0:rows, span] = (values * (1.0 - odd)).astype(jnp.bfloat16)
         lhs_ref[second : second + rows, span] = (values * odd).astype(jnp.bfloat16)
     low_half = lax.broadcasted_iota(jnp.int32, (cycles, LANES), 1) < HALF
@@ -264,15 +272,16 @@
 
 
 def run_ilc(modes, odd, basis):
-    groups, shares, rows, width = modes.shape
+    groups, shares, _, width = modes[0].shape
+    rows = sum(each.shape[2] for each in modes)
     chunks, depth, columns = basis.shape
     pieces = CHUNK // 2
     basis = basis.reshape(chunks * pieces, depth // pieces, columns)
     cycles = rows // C
     vmem = pl.BlockSpec(memory_space=pltpu.VMEM)
     return pl.pallas_call(
-        ilc_kernel,
-        in_specs=[vmem, vmem, pl.BlockSpec(memory_space=pl.ANY)],
+        functools.partial(ilc_kernel, len(modes)),
+        in_specs=[vmem] * (len(modes) + 1) + [pl.BlockSpec(memory_space=pl.ANY)],
         out_specs=[vmem, vmem],
         out_shape=[
             jax.ShapeDtypeStruct((HALO, cycles, LANES), jnp.float32),
@@ -293,15 +302,17 @@
             transcendentals=0,
         ),
         compiler_params=pltpu.CompilerParams(vmem_limit_bytes=VMEM_LIMIT),
-    )(modes, odd, basis)
-
-
-def modes_kernel(alm_hbm, table_hbm, out_hbm, alm_ref, table_ref, held_ref, turned_ref, out_ref, alm_sem, sems, out_sems):
+    )(*modes, odd, basis)
+
+
+def modes_kernel(alm_hbm, table_hbm, *refs):
+    out_hbms, (alm_ref, table_ref, held_ref, turned_ref) = refs[:BUNDLES], refs[BUNDLES : BUNDLES + 4]
+    out_refs, (alm_sem, sems, out_sems) = refs[BUNDLES + 4 : -3], refs[-3:]
     parts = sems.shape[0]
     total_slots, degrees, total = table_ref.shape
     each, slots = total_slots // parts, 4
-    targets, rows = out_ref.shape[:2]
-    cycles = rows // C
+    targets = out_refs[0].shape[0]
+    cycles = total // targets
     height = 2 * C
     alm_copy = pltpu.make_async_copy(alm_hbm, alm_ref, alm_sem)
     alm_copy.start()
@@ -333,15 +344,18 @@
             some_slots(first)
         if (part + 1) * HALVES % parts == 0:
             turn((part + 1) * HALVES // parts - 1)
-    each = targets // out_sems.shape[0]
-    for target in range(targets):
-        span = slice(target * cycles, (target + 1) * cycles)
-        block = jnp.concatenate([turned_ref[chan, span, :] for chan in range(C)], axis=0)
-        out_ref[target] = block.astype(jnp.bfloat16)
-        if (target + 1) % each == 0:
-            part_copy(out_ref, out_hbm, out_sems, target // each).start()
-    for part in range(out_sems.shape[0]):
-        part_copy(out_ref, out_hbm, out_sems, part).wait()
+    for at, (out_ref, out_hbm) in enumerate(zip(out_refs, out_hbms)):
+        for target in range(targets):
+            span = slice(target * cycles, (target + 1) * cycles)
+            block = jnp.concatenate([turned_ref[chan, span, :] for chan in bundle(at)], axis=0)
+            out_ref[target] = block.astype(jnp.bfloat16)
+        pltpu.make_async_copy(out_ref, out_hbm, out_sems.at[at]).start()
+    for at, (out_ref, out_hbm) in enumerate(zip(out_refs, out_hbms)):
+        pltpu.make_async_copy(out_ref, out_hbm, out_sems.at[at]).wait()
+
+
+def bundle(at):
+    return range(at * C // BUNDLES, (at + 1) * C // BUNDLES)
 
 
 def make_modes(alm, legendre, targets):
@@ -349,21 +363,24 @@
     parts = slot_count // 8
     width = 2 * slot_count
     height = 2 * C
-    out = jax.ShapeDtypeStruct((targets, C * (total // targets), width), jnp.bfloat16)
+    outs = [
+        jax.ShapeDtypeStruct((targets, len(bundle(at)) * (total // targets), width), jnp.bfloat16)
+        for at in range(BUNDLES)
+    ]
     return pl.pallas_call(
         modes_kernel,
         in_specs=[pl.BlockSpec(memory_space=pl.ANY)] * 2,
-        out_specs=pl.BlockSpec(memory_space=pl.ANY),
-        out_shape=out,
+        out_specs=[pl.BlockSpec(memory_space=pl.ANY)] * BUNDLES,
+        out_shape=outs,
         scratch_shapes=[
             pltpu.VMEM(alm.shape, jnp.bfloat16),
             pltpu.VMEM(legendre.shape, jnp.bfloat16),
             pltpu.VMEM((total // LANES, slot_count * height, LANES), jnp.float32),
             pltpu.VMEM((C, total, width), jnp.float32),
-            pltpu.VMEM(out.shape, out.dtype),
+            *[pltpu.VMEM(out.shape, out.dtype) for out in outs],
             pltpu.SemaphoreType.DMA,
             pltpu.SemaphoreType.DMA((parts,)),
-            pltpu.SemaphoreType.DMA((4,)),
+            pltpu.SemaphoreType.DMA((BUNDLES,)),
         ],
         cost_estimate=pl.CostEstimate(
             flops=2 * slot_count * degrees * total * 2 * C,
@@ -449,15 +466,16 @@
     plain = group_width == width and padded == cycles
     axes = ("band", "tile")
 
-    partial = make_modes(alm, legendre, targets)
-    partial = lax.all_to_all(partial, axes, split_axis=0, concat_axis=0, tiled=True)
-    modes = partial.reshape(band_count, tile_count, C * cycles, width)
+    modes = [
+        lax.all_to_all(each, axes, split_axis=0, concat_axis=0, tiled=True).reshape(band_count, tile_count, -1, width)
+        for each in make_modes(alm, legendre, targets)
+    ]
     if not plain:
-        modes = jnp.sum(modes.astype(jnp.float32), axis=1).astype(jnp.bfloat16)
+        modes = jnp.sum(jnp.concatenate(modes, axis=2).astype(jnp.float32), axis=1).astype(jnp.bfloat16)
         modes = modes.reshape(groups, group_width // width, C, cycles, width)
         modes = modes.transpose(0, 2, 3, 1, 4).reshape(groups, C, cycles, group_width)
         modes = jnp.pad(modes, ((0, 0), (0, 0), (0, padded - cycles), (0, 0)))
-        modes = modes.reshape(groups, 1, C * padded, group_width)
+        modes = [modes.reshape(groups, 1, C * padded, group_width)]
 
     order_rows = order_of_slot.reshape(band_count * HALVES, 1, slot_count // HALVES)
     order_rows = jnp.broadcast_to(order_rows, (band_count * HALVES, 2, slot_count // HALVES)).reshape(depth)

time: 62.4 us -> 70.5 us (1.13)
  blocking collectives: 0 us -> 18 us
  starting transfers between devices: 11.8 us -> 6.5 us
  waiting for transfers between devices: 14 us -> 9.3 us
    all_to_all x0 -> x1, blocking collectives: none -> 18 us  [body(): lax.all_to_all(each, axes, split_axis=0, concat_axis=0, tiled=True)]
    all_to_all x1, starting transfers between devices: 7.3 us -> 2.59 us  [body(): lax.all_to_all(each, axes, split_axis=0, concat_axis=0, tiled=True)]
    all_to_all x1, waiting for transfers between devices: 7.87 us -> 3.19 us  [body(): lax.all_to_all(each, axes, split_axis=0, concat_axis=0, tiled=True)]
  transfers between devices with their start and end apart: 3 -> 3, of which waited for: 3 -> 3; matrix products, arithmetic and copies ran while one was open for 4% -> 4% of each run, Pallas kernels for 12% -> 10%
where the time goes in v16:
time: 70.5 us; the launch traced here: 70.2 us
  Pallas kernels  32.8 us (47%)
  blocking collectives  18 us (26%)
  waiting for transfers between devices  9.3 us (13%)
  starting transfers between devices  6.5 us (9%)
  local copies, waits for them, and re-layouts  2.42 us (3%)
  between operations  0.88 us (1%)
    all_to_all x1, blocking collectives, body(): lax.all_to_all(each, axes, split_axis=0, concat_axis=0, tiled=True)  18 us
    pallas_call x1, Pallas kernels, make_modes(): pl.pallas_call(modes_kernel, in_specs=[pl.BlockSpec(memory_space=pl.ANY)]...  9.12 us
    pallas_call x1, Pallas kernels, run_ilc(): pl.pallas_call(functools.partial(ilc_kernel, len(modes)), in_specs=[vmem]...  8.83 us
    pallas_call x1, Pallas kernels, analyse(): pl.pallas_call(analysis_kernel, in_specs=[pl.BlockSpec(memory_space=pl.AN...  7.73 us
    pallas_call x1, Pallas kernels, make_basis(): pl.pallas_call(functools.partial(basis_kernel, slots), grid=(rows // bloc...  7.16 us
    all_to_all x1, waiting for transfers between devices, body(): lax.all_to_all(spectra, axes, split_axis=0, concat_axis=0, tiled=True)  4.17 us
    all_to_all x1, waiting for transfers between devices, body(): lax.all_to_all(each, axes, split_axis=0, concat_axis=0, tiled=True)  3.19 us
    all_to_all x1, starting transfers between devices, body(): lax.all_to_all(spectra, axes, split_axis=0, concat_axis=0, tiled=True)  2.75 us
  transfers between devices with their start and end apart: 3, of which 3 were waited for; matrix products, arithmetic and copies ran while one was open for 4% of the time, Pallas kernels for 10%

profile of v16, /device:TPU:0, one launch (start us, length us, event | category | flops | bytes accessed | tf_op | source)
XLA Modules:
  0.0 70.2 jit_solution(8260964421293686433)
XLA Ops:
  0.6 0.0 copy-start
  0.6 9.1 %shard_map.50 = (bf16[32,32,128]{2,1,0:T(8,128)(2,1)}, bf16[32,40,128]{2,1,0:T(8,128)(2,1)}) custom-call(bf16[64,9,2,512]{3,2,1,0:T(2,128)(2,1)} %alm_hbm.1, bf16[64,512,256]{2,1,0:T(8,128)(2,1)} %table_hbm.3), custom_call_target="tpu_custom_call" | custom-call | flops 301989888 | bytes 17956864 | tf_op jit(solution)/shard_map/pallas_call | solution.py:370
  9.8 18.0 %all_to_all.15 = bf16[32,32,128]{2,1,0:T(8,128)(2,1)S(1)} all-to-all(bf16[32,32,128]{2,1,0:T(8,128)(2,1)} %get-tuple-element.8), channel_id=1, replica_groups=mesh['band'=16,'tile'=2] {'band','tile'}, dimensions={0} | all-to-all | bytes 524288 | tf_op jit(solution)/shard_map/all_to_all | solution.py:470
  27.8 2.6 %all-to-all-start.1 = ((bf16[32,40,128]{2,1,0:T(8,128)(2,1)}), bf16[32,40,128]{2,1,0:T(8,128)(2,1)S(1)}, u32[]{:S(2)}, u32[]{:S(2)}) async-start(bf16[32,40,128]{2,1,0:T(8,128)(2,1)} %get-tuple-element.9), calls=%async_computation.1 | async-start | bytes 655360 | tf_op jit(solution)/shard_map/all_to_all | solution.py:470
  30.4 0.0 copy-done
  30.4 0.1 broadcast_in_dim.11
  30.5 1.1 %convert_element_type.27.order_ref = f32[2048,1]{1,0:T(8,128)S(1)} reshape(f32[32,2,32]{2,1,0:T(2,128)S(1)} %broadcast_in_dim.13) | data formatting | bytes 16384 | tf_op jit(solution)/shard_map/convert_element_type | solution.py:482
  31.6 0.1 reshape.95
  31.7 7.2 %shard_map.51 = bf16[4,2048,512]{2,1,0:T(8,128)(2,1)} custom-call(f32[2048,1]{1,0:T(8,128)S(1)} %convert_element_type.27.order_ref), custom_call_target="tpu_custom_call" | custom-call | flops 33554432 | bytes 8388608 | tf_op jit(solution)/shard_map/pallas_call | solution.py:75
  38.9 3.2 %all-to-all-done.1 = bf16[32,40,128]{2,1,0:T(8,128)(2,1)S(1)} async-done(((bf16[32,40,128]{2,1,0:T(8,128)(2,1)}), bf16[32,40,128]{2,1,0:T(8,128)(2,1)S(1)}, u32[]{:S(2)}, u32[]{:S(2)}) %all-to-all-start.1) | async-done | bytes 327712 | tf_op jit(solution)/shard_map/all_to_all | solution.py:470
  42.1 8.8 %shard_map.52 = (f32[32,8,128]{2,1,0:T(8,128)S(1)}, bf16[16,2,8,128]{3,2,1,0:T(8,128)(2,1)}) custom-call(bf16[16,2,32,128]{3,2,1,0:T(8,128)(2,1)S(1)} %bitcast.12, bf16[16,2,40,128]{3,2,1,0:T(8,128)(2,1)S(1)} %bitcast.11, f32[1,2048]{1,0:T(1,128)S(1)} %fusion.3.refs_2_, bf16[16,512,512]{2,1,0:T(8,128)(2,1)} %bitcast.15), custom_call_target="tpu_custom_call" | custom-call | flops 1342177280 | bytes 8388608 | tf_op jit(solution)/shard_map/pallas_call | solution.py:282
  50.9 1.2 %collective-permute-start = (f32[32,8,128]{2,1,0:T(8,128)S(1)}, f32[32,8,128]{2,1,0:T(8,128)S(1)}, u32[]{:S(2)}, u32[]{:S(2)}) collective-permute-start(f32[32,8,128]{2,1,0:T(8,128)S(1)} %get-tuple-element.11), channel_id=1, source_target_pairs={{0,1},{1,0},{2,3},{3,2},{4,5},{5,4},{6,7},{7,6},{8,9},{9,8},{10,11... | collective-permute-start | bytes 393224 | tf_op jit(solution)/shard_map/ppermute | solution.py:441
  52.1 2.8 %all-to-all-start.2 = ((bf16[32,8,128]{2,1,0:T(8,128)(2,1)}), bf16[32,8,128]{2,1,0:T(8,128)(2,1)S(1)}, u32[]{:S(2)}, u32[]{:S(2)}) async-start(bf16[32,8,128]{2,1,0:T(8,128)(2,1)} %bitcast.3), calls=%async_computation.2 | async-start | bytes 131072 | tf_op jit(solution)/shard_map/all_to_all | solution.py:491
  54.8 1.9 %collective-permute-done = f32[32,8,128]{2,1,0:T(8,128)S(1)} collective-permute-done((f32[32,8,128]{2,1,0:T(8,128)S(1)}, f32[32,8,128]{2,1,0:T(8,128)S(1)}, u32[]{:S(2)}, u32[]{:S(2)}) %collective-permute-start) | collective-permute-done | bytes 131104 | tf_op jit(solution)/shard_map/ppermute | solution.py:441
  56.8 0.1 fusion.2
  56.8 0.1 fusion
  57.0 0.2 copy.6
  57.2 0.9 %reshape.98 = f32[16,2048]{1,0:T(8,128)} reshape(f32[2,8,64,32]{3,2,1,0:T(8,128)S(1)} %copy.6) | data formatting | bytes 262144 | tf_op jit(solution)/shard_map/reshape | solution.py:495
  58.1 4.2 %all-to-all-done.2 = bf16[32,8,128]{2,1,0:T(8,128)(2,1)S(1)} async-done(((bf16[32,8,128]{2,1,0:T(8,128)(2,1)}), bf16[32,8,128]{2,1,0:T(8,128)(2,1)S(1)}, u32[]{:S(2)}, u32[]{:S(2)}) %all-to-all-start.2) | async-done | bytes 65568 | tf_op jit(solution)/shard_map/all_to_all | solution.py:491
  62.3 7.7 %shard_map.53 = f32[64,2,512]{2,1,0:T(2,128)} custom-call(bf16[64,512,256]{2,1,0:T(8,128)(2,1)} %table_hbm.3, bf16[256,128]{1,0:T(8,128)(2,1)S(1)} %bitcast.13), custom_call_target="tpu_custom_call" | custom-call | flops 268435456 | bytes 16777216 | tf_op jit(solution)/shard_map/pallas_call | solution.py:418
  (4 shorter events, 0.1 us)
Async XLA Ops:
  0.6 29.7 %copy-start = (s32[1024]{0:T(1024)S(1)}, s32[1024]{0:T(1024)}, u32[]{:S(2)}) copy-start(s32[1024]{0:T(1024)} %param.5) | copy-start | bytes 12292
  27.8 14.3 %all-to-all-start.1 = ((bf16[32,40,128]{2,1,0:T(8,128)(2,1)}), bf16[32,40,128]{2,1,0:T(8,128)(2,1)S(1)}, u32[]{:S(2)}, u32[]{:S(2)}) async-start(bf16[32,40,128]{2,1,0:T(8,128)(2,1)} %get-tuple-element.9), calls=%async_computation.1 | async-start | bytes 655360 | tf_op jit(solution)/shard_map/all_to_all | solution.py:470
  50.9 5.9 %collective-permute-start = (f32[32,8,128]{2,1,0:T(8,128)S(1)}, f32[32,8,128]{2,1,0:T(8,128)S(1)}, u32[]{:S(2)}, u32[]{:S(2)}) collective-permute-start(f32[32,8,128]{2,1,0:T(8,128)S(1)} %get-tuple-element.11), channel_id=1, source_target_pairs={{0,1},{1,0},{2,3},{3,2},{4,5},{5,4},{6,7},{7,6},{8,9},{9,8},{10,11... | collective-permute-start | bytes 393224 | tf_op jit(solution)/shard_map/ppermute | solution.py:441
  52.1 10.2 %all-to-all-start.2 = ((bf16[32,8,128]{2,1,0:T(8,128)(2,1)}), bf16[32,8,128]{2,1,0:T(8,128)(2,1)S(1)}, u32[]{:S(2)}, u32[]{:S(2)}) async-start(bf16[32,8,128]{2,1,0:T(8,128)(2,1)} %bitcast.3), calls=%async_computation.2 | async-start | bytes 131072 | tf_op jit(solution)/shard_map/all_to_all | solution.py:491

commit v17 on v15

--- a/solution.py
+++ b/solution.py
@@ -24,7 +24,7 @@
 SUMS = len(PAIRS) + 1
 VMEM_LIMIT = 48 * 1024 * 1024
 IN_FLIGHT = 4
-HALVES = 2
+HALVES = 1
 CHUNK = 8
 
 
@@ -153,7 +153,7 @@
     groups, shares, rows, width = modes_ref.shape
     columns = basis_ref.shape[2]
     depth = lhs_ref.shape[1]
-    pieces, share_rows = found_ref.shape[0], found_ref.shape[2]
+    pieces = depth // basis_ref.shape[1]
     chunks = basis_ref.shape[0] // pieces
     cycles = rows // C
     second = round_up(rows, 16)
@@ -235,11 +235,9 @@
 
     def add_spectra(chunk):
         lhs = jnp.concatenate([low_ref[chunk, part] for part in range(pieces)], axis=1)
-        for part in range(pieces):
-            term = lax.dot_general(
-                lhs, basis_ref[chunk * pieces + part], (((1,), (1,)), ((), ())), preferred_element_type=jnp.float32
-            )
-            found_ref[part] = term if chunk == 0 else found_ref[part] + term
+        basis = basis_ref[chunk * pieces : (chunk + 1) * pieces].reshape(depth, columns)
+        term = lax.dot_general(lhs, basis, (((1,), (1,)), ((), ())), preferred_element_type=jnp.float32)
+        found_ref[...] = term if chunk == 0 else found_ref[...] + term
 
     for pair_at in range(HALO // 2):
         at = 2 * pair_at
@@ -256,8 +254,7 @@
     for group in range(groups):
         span = slice(group * width, (group + 1) * width)
         sign = 1.0 - 2.0 * odd_ref[:, span]
-        part, first = group * width // share_rows, group * width % share_rows
-        result = found_ref[part, :, first : first + width]
+        result = found_ref[:, span]
         value = (result[0:cycles] + sign * result[cycles:]).astype(jnp.bfloat16)
         for share in range(shares):
             spectra_ref[group, share] = value
@@ -284,7 +281,7 @@
             pltpu.VMEM((HALO, C + 1, cycles, LANES), jnp.float32),
             pltpu.VMEM((SUMS, cycles, LANES), jnp.float32),
             pltpu.VMEM((chunks, pieces, 2 * cycles, LANES), jnp.bfloat16),
-            pltpu.VMEM((pieces, 2 * cycles, depth // pieces), jnp.float32),
+            pltpu.VMEM((2 * cycles, depth), jnp.float32),
             pltpu.SemaphoreType.DMA((chunks,)),
         ],
         cost_estimate=pl.CostEstimate(
@@ -317,22 +314,33 @@
                 span = slice((first + slot) * height, (first + slot + 1) * height)
                 held_ref[lanes, span, :] = own[:, lanes * LANES : (lanes + 1) * LANES]
 
-    def turn(half):
-        count = total_slots // HALVES
-        first = half * count * height
-        for chan in range(C):
-            for lanes in range(held_ref.shape[0]):
-                both = [held_ref[lanes, pl.ds(first + 2 * chan + part, count, stride=height), :] for part in range(2)]
-                span = slice(half * 2 * count, (half + 1) * 2 * count)
-                turned_ref[chan, lanes * LANES : (lanes + 1) * LANES, span] = jnp.concatenate(both, axis=0).T
+    def rows_of(chan):
+        both = [
+            jnp.concatenate(
+                [
+                    held_ref[lanes, pl.ds(2 * chan + part, total_slots, stride=height), :].astype(jnp.bfloat16)
+                    for lanes in range(held_ref.shape[0])
+                ],
+                axis=1,
+            )
+            for part in range(2)
+        ]
+        return jnp.concatenate(both, axis=0)
 
     alm_copy.wait()
     for part in range(parts):
         next_part(table_hbm, table_ref, sems, part, IN_FLIGHT)
         for first in range(part * each, (part + 1) * each, slots):
             some_slots(first)
-        if (part + 1) * HALVES % parts == 0:
-            turn((part + 1) * HALVES // parts - 1)
+    one = lax.broadcasted_iota(jnp.int32, (total, total), 0) == lax.broadcasted_iota(jnp.int32, (total, total), 1)
+    one = one.astype(jnp.float32).astype(jnp.bfloat16)
+    width = 2 * total_slots
+    together = C if width % LANES == 0 else 1
+    for chan in range(0, C, together):
+        rows = jnp.concatenate([rows_of(chan + at) for at in range(together)], axis=0)
+        turned = lax.dot_general(one, rows, (((1,), (1,)), ((), ())), preferred_element_type=jnp.float32)
+        for at in range(together):
+            turned_ref[chan + at] = turned[:, at * width : (at + 1) * width]
     each = targets // out_sems.shape[0]
     for target in range(targets):
         span = slice(target * cycles, (target + 1) * cycles)

time: 62.4 us -> 61.8 us (level)
  no operation moved by 1% of the time
where the time goes in v17:
time: 61.8 us; the launch traced here: 61.6 us
  Pallas kernels  32.3 us (52%)
  waiting for transfers between devices  14.1 us (23%)
  starting transfers between devices  11.8 us (19%)
  local copies, waits for them, and re-layouts  2.31 us (4%)
  between operations  0.88 us (1%)
    pallas_call x1, Pallas kernels, run_ilc(): pl.pallas_call(ilc_kernel, in_specs=[vmem, vmem, pl.BlockSpec(memory_spac...  8.83 us
    pallas_call x1, Pallas kernels, make_modes(): pl.pallas_call(modes_kernel, in_specs=[pl.BlockSpec(memory_space=pl.ANY)]...  8.59 us
    all_to_all x1, waiting for transfers between devices, body(): lax.all_to_all(partial, axes, split_axis=0, concat_axis=0, tiled=True)  8 us
    pallas_call x1, Pallas kernels, analyse(): pl.pallas_call(analysis_kernel, in_specs=[pl.BlockSpec(memory_space=pl.AN...  7.73 us
    all_to_all x1, starting transfers between devices, body(): lax.all_to_all(partial, axes, split_axis=0, concat_axis=0, tiled=True)  7.3 us
    pallas_call x1, Pallas kernels, make_basis(): pl.pallas_call(functools.partial(basis_kernel, slots), grid=(rows // bloc...  7.15 us
    all_to_all x1, waiting for transfers between devices, body(): lax.all_to_all(spectra, axes, split_axis=0, concat_axis=0, tiled=True)  4.18 us
    all_to_all x1, starting transfers between devices, body(): lax.all_to_all(spectra, axes, split_axis=0, concat_axis=0, tiled=True)  2.75 us
  transfers between devices with their start and end apart: 3, of which 3 were waited for; matrix products, arithmetic and copies ran while one was open for 4% of the time, Pallas kernels for 12%

profile of v17, /device:TPU:0, one launch (start us, length us, event | category | flops | bytes accessed | tf_op | source)
XLA Modules:
  0.0 61.6 jit_solution(6354213536790217510)
XLA Ops:
  0.6 0.0 copy-start
  0.6 8.6 %shard_map.50 = bf16[32,72,128]{2,1,0:T(8,128)(2,1)} custom-call(bf16[64,9,2,512]{3,2,1,0:T(2,128)(2,1)} %alm_hbm.1, bf16[64,512,256]{2,1,0:T(8,128)(2,1)} %table_hbm.3), custom_call_target="tpu_custom_call" | custom-call | flops 301989888 | bytes 17956864 | tf_op jit(solution)/shard_map/pallas_call | solution.py:361
  9.2 7.3 %all-to-all-start = ((bf16[32,72,128]{2,1,0:T(8,128)(2,1)}), bf16[32,72,128]{2,1,0:T(8,128)(2,1)S(1)}, u32[]{:S(2)}, u32[]{:S(2)}) async-start(bf16[32,72,128]{2,1,0:T(8,128)(2,1)} %shard_map.50), calls=%async_computation | async-start | bytes 1179648 | tf_op jit(solution)/shard_map/all_to_all | solution.py:461
  16.6 0.0 copy-done
  16.6 0.1 broadcast_in_dim.11
  16.6 1.0 %convert_element_type.27.order_ref = f32[2048,1]{1,0:T(8,128)S(1)} reshape(f32[16,2,64]{2,1,0:T(2,128)S(1)} %broadcast_in_dim.13) | data formatting | bytes 16384 | tf_op jit(solution)/shard_map/convert_element_type | solution.py:472
  17.7 0.1 reshape.91
  17.8 7.2 %shard_map.51 = bf16[4,2048,512]{2,1,0:T(8,128)(2,1)} custom-call(f32[2048,1]{1,0:T(8,128)S(1)} %convert_element_type.27.order_ref), custom_call_target="tpu_custom_call" | custom-call | flops 33554432 | bytes 8388608 | tf_op jit(solution)/shard_map/pallas_call | solution.py:74
  25.0 8.0 %all-to-all-done = bf16[32,72,128]{2,1,0:T(8,128)(2,1)S(1)} async-done(((bf16[32,72,128]{2,1,0:T(8,128)(2,1)}), bf16[32,72,128]{2,1,0:T(8,128)(2,1)S(1)}, u32[]{:S(2)}, u32[]{:S(2)}) %all-to-all-start) | async-done | bytes 589856 | tf_op jit(solution)/shard_map/all_to_all | solution.py:461
  33.0 8.8 %shard_map.52 = (f32[32,8,128]{2,1,0:T(8,128)S(1)}, bf16[16,2,8,128]{3,2,1,0:T(8,128)(2,1)}) custom-call(bf16[16,2,72,128]{3,2,1,0:T(8,128)(2,1)S(1)} %bitcast.10, f32[1,2048]{1,0:T(1,128)S(1)} %fusion.3.odd_ref, bf16[16,512,512]{2,1,0:T(8,128)(2,1)} %bitcast.13), custom_call_target="tpu_custom_call" | custom-call | flops 1342177280 | bytes 8388608 | tf_op jit(solution)/shard_map/pallas_call | solution.py:270
  41.8 1.7 %collective-permute-start = (f32[32,8,128]{2,1,0:T(8,128)S(1)}, f32[32,8,128]{2,1,0:T(8,128)S(1)}, u32[]{:S(2)}, u32[]{:S(2)}) collective-permute-start(f32[32,8,128]{2,1,0:T(8,128)S(1)} %get-tuple-element.7), channel_id=1, source_target_pairs={{0,1},{1,0},{2,3},{3,2},{4,5},{5,4},{6,7},{7,6},{8,9},{9,8},{10,11... | collective-permute-start | bytes 393224 | tf_op jit(solution)/shard_map/ppermute | solution.py:432
  43.5 2.8 %all-to-all-start.1 = ((bf16[32,8,128]{2,1,0:T(8,128)(2,1)}), bf16[32,8,128]{2,1,0:T(8,128)(2,1)S(1)}, u32[]{:S(2)}, u32[]{:S(2)}) async-start(bf16[32,8,128]{2,1,0:T(8,128)(2,1)} %bitcast.2), calls=%async_computation.1 | async-start | bytes 131072 | tf_op jit(solution)/shard_map/all_to_all | solution.py:481
  46.3 1.9 %collective-permute-done = f32[32,8,128]{2,1,0:T(8,128)S(1)} collective-permute-done((f32[32,8,128]{2,1,0:T(8,128)S(1)}, f32[32,8,128]{2,1,0:T(8,128)S(1)}, u32[]{:S(2)}, u32[]{:S(2)}) %collective-permute-start) | collective-permute-done | bytes 131104 | tf_op jit(solution)/shard_map/ppermute | solution.py:432
  48.2 0.1 fusion.2
  48.3 0.1 fusion
  48.4 0.2 copy.6
  48.6 0.9 %reshape.94 = f32[16,2048]{1,0:T(8,128)} reshape(f32[2,8,64,32]{3,2,1,0:T(8,128)S(1)} %copy.6) | data formatting | bytes 262144 | tf_op jit(solution)/shard_map/reshape | solution.py:485
  49.5 4.2 %all-to-all-done.1 = bf16[32,8,128]{2,1,0:T(8,128)(2,1)S(1)} async-done(((bf16[32,8,128]{2,1,0:T(8,128)(2,1)}), bf16[32,8,128]{2,1,0:T(8,128)(2,1)S(1)}, u32[]{:S(2)}, u32[]{:S(2)}) %all-to-all-start.1) | async-done | bytes 65568 | tf_op jit(solution)/shard_map/all_to_all | solution.py:481
  53.7 7.7 %shard_map.53 = f32[64,2,512]{2,1,0:T(2,128)} custom-call(bf16[64,512,256]{2,1,0:T(8,128)(2,1)} %table_hbm.3, bf16[256,128]{1,0:T(8,128)(2,1)S(1)} %bitcast.11), custom_call_target="tpu_custom_call" | custom-call | flops 268435456 | bytes 16777216 | tf_op jit(solution)/shard_map/pallas_call | solution.py:409
  (4 shorter events, 0.1 us)
Async XLA Ops:
  0.6 15.9 %copy-start = (s32[1024]{0:T(1024)S(1)}, s32[1024]{0:T(1024)}, u32[]{:S(2)}) copy-start(s32[1024]{0:T(1024)} %param.5) | copy-start | bytes 12292
  9.2 23.7 %all-to-all-start = ((bf16[32,72,128]{2,1,0:T(8,128)(2,1)}), bf16[32,72,128]{2,1,0:T(8,128)(2,1)S(1)}, u32[]{:S(2)}, u32[]{:S(2)}) async-start(bf16[32,72,128]{2,1,0:T(8,128)(2,1)} %shard_map.50), calls=%async_computation | async-start | bytes 1179648 | tf_op jit(solution)/shard_map/all_to_all | solution.py:461
  41.8 6.4 %collective-permute-start = (f32[32,8,128]{2,1,0:T(8,128)S(1)}, f32[32,8,128]{2,1,0:T(8,128)S(1)}, u32[]{:S(2)}, u32[]{:S(2)}) collective-permute-start(f32[32,8,128]{2,1,0:T(8,128)S(1)} %get-tuple-element.7), channel_id=1, source_target_pairs={{0,1},{1,0},{2,3},{3,2},{4,5},{5,4},{6,7},{7,6},{8,9},{9,8},{10,11... | collective-permute-start | bytes 393224 | tf_op jit(solution)/shard_map/ppermute | solution.py:432
  43.5 10.2 %all-to-all-start.1 = ((bf16[32,8,128]{2,1,0:T(8,128)(2,1)}), bf16[32,8,128]{2,1,0:T(8,128)(2,1)S(1)}, u32[]{:S(2)}, u32[]{:S(2)}) async-start(bf16[32,8,128]{2,1,0:T(8,128)(2,1)} %bitcast.2), calls=%async_computation.1 | async-start | bytes 131072 | tf_op jit(solution)/shard_map/all_to_all | solution.py:481

commit v18 on v17

--- a/solution.py
+++ b/solution.py
@@ -23,7 +23,7 @@
 PAIRS = [(a_at, b_at) for a_at in range(REST) for b_at in range(a_at, REST)] + [(a_at, REST) for a_at in range(REST)]
 SUMS = len(PAIRS) + 1
 VMEM_LIMIT = 48 * 1024 * 1024
-IN_FLIGHT = 4
+IN_FLIGHT = 2
 HALVES = 1
 CHUNK = 8
 
@@ -153,12 +153,11 @@
     groups, shares, rows, width = modes_ref.shape
     columns = basis_ref.shape[2]
     depth = lhs_ref.shape[1]
-    pieces = depth // basis_ref.shape[1]
+    pieces, share_rows = found_ref.shape[0], found_ref.shape[2]
     chunks = basis_ref.shape[0] // pieces
     cycles = rows // C
     second = round_up(rows, 16)
-    ahead = 3
-    start_parts(basis_hbm, basis_ref, sems, ahead)
+    start_parts(basis_hbm, basis_ref, sems, IN_FLIGHT)
     for group in range(groups):
         span = slice(group * width, (group + 1) * width)
         odd = odd_ref[:, span]
@@ -179,7 +178,7 @@
         maps_ref[at, C] = squares
 
     def maps_of_chunk(chunk):
-        next_part(basis_hbm, basis_ref, sems, chunk, ahead)
+        next_part(basis_hbm, basis_ref, sems, chunk, IN_FLIGHT)
         basis = basis_ref[chunk * pieces : (chunk + 1) * pieces].reshape(depth, columns)
         result = jnp.dot(lhs_ref[...], basis, preferred_element_type=jnp.float32)
         for part in range(CHUNK // 2):
@@ -235,9 +234,11 @@
 
     def add_spectra(chunk):
         lhs = jnp.concatenate([low_ref[chunk, part] for part in range(pieces)], axis=1)
-        basis = basis_ref[chunk * pieces : (chunk + 1) * pieces].reshape(depth, columns)
-        term = lax.dot_general(lhs, basis, (((1,), (1,)), ((), ())), preferred_element_type=jnp.float32)
-        found_ref[...] = term if chunk == 0 else found_ref[...] + term
+        for part in range(pieces):
+            term = lax.dot_general(
+                lhs, basis_ref[chunk * pieces + part], (((1,), (1,)), ((), ())), preferred_element_type=jnp.float32
+            )
+            found_ref[part] = term if chunk == 0 else found_ref[part] + term
 
     for pair_at in range(HALO // 2):
         at = 2 * pair_at
@@ -254,7 +255,8 @@
     for group in range(groups):
         span = slice(group * width, (group + 1) * width)
         sign = 1.0 - 2.0 * odd_ref[:, span]
-        result = found_ref[:, span]
+        part, first = group * width // share_rows, group * width % share_rows
+        result = found_ref[part, :, first : first + width]
         value = (result[0:cycles] + sign * result[cycles:]).astype(jnp.bfloat16)
         for share in range(shares):
             spectra_ref[group, share] = value
@@ -281,7 +283,7 @@
             pltpu.VMEM((HALO, C + 1, cycles, LANES), jnp.float32),
             pltpu.VMEM((SUMS, cycles, LANES), jnp.float32),
             pltpu.VMEM((chunks, pieces, 2 * cycles, LANES), jnp.bfloat16),
-            pltpu.VMEM((2 * cycles, depth), jnp.float32),
+            pltpu.VMEM((pieces, 2 * cycles, depth // pieces), jnp.float32),
             pltpu.SemaphoreType.DMA((chunks,)),
         ],
         cost_estimate=pl.CostEstimate(
@@ -293,7 +295,7 @@
     )(modes, odd, basis)
 
 
-def modes_kernel(alm_hbm, table_hbm, out_hbm, alm_ref, table_ref, held_ref, turned_ref, out_ref, alm_sem, sems, out_sems):
+def modes_kernel(alm_hbm, table_hbm, out_hbm, alm_ref, table_ref, held_ref, out_ref, alm_sem, sems, out_sems):
     parts = sems.shape[0]
     total_slots, degrees, total = table_ref.shape
     each, slots = total_slots // parts, 4
@@ -336,15 +338,15 @@
     one = one.astype(jnp.float32).astype(jnp.bfloat16)
     width = 2 * total_slots
     together = C if width % LANES == 0 else 1
+    turned = []
     for chan in range(0, C, together):
         rows = jnp.concatenate([rows_of(chan + at) for at in range(together)], axis=0)
-        turned = lax.dot_general(one, rows, (((1,), (1,)), ((), ())), preferred_element_type=jnp.float32)
-        for at in range(together):
-            turned_ref[chan + at] = turned[:, at * width : (at + 1) * width]
+        both = lax.dot_general(one, rows, (((1,), (1,)), ((), ())), preferred_element_type=jnp.float32)
+        turned += [both[:, at * width : (at + 1) * width] for at in range(together)]
     each = targets // out_sems.shape[0]
     for target in range(targets):
         span = slice(target * cycles, (target + 1) * cycles)
-        block = jnp.concatenate([turned_ref[chan, span, :] for chan in range(C)], axis=0)
+        block = jnp.concatenate([turned[chan][span] for chan in range(C)], axis=0)
         out_ref[target] = block.astype(jnp.bfloat16)
         if (target + 1) % each == 0:
             part_copy(out_ref, out_hbm, out_sems, target // each).start()
@@ -367,7 +369,6 @@
             pltpu.VMEM(alm.shape, jnp.bfloat16),
             pltpu.VMEM(legendre.shape, jnp.bfloat16),
             pltpu.VMEM((total // LANES, slot_count * height, LANES), jnp.float32),
-            pltpu.VMEM((C, total, width), jnp.float32),
             pltpu.VMEM(out.shape, out.dtype),
             pltpu.SemaphoreType.DMA,
             pltpu.SemaphoreType.DMA((parts,)),

time: 61.8 us -> 64.4 us (1.042)
  Pallas kernels: 32.3 us -> 34.8 us
    pallas_call x1, Pallas kernels: 7.73 us -> 8.94 us  [analyse(): pl.pallas_call(analysis_kernel, in_specs=[pl.BlockSpec(memory_space=pl.AN...]
    pallas_call x1, Pallas kernels: 8.59 us -> 9.53 us  [make_modes(): pl.pallas_call(modes_kernel, in_specs=[pl.BlockSpec(memory_space=pl.ANY)]...]
  transfers between devices with their start and end apart: 3 -> 3, of which waited for: 3 -> 3; matrix products, arithmetic and copies ran while one was open for 4% -> 4% of each run, Pallas kernels for 12% -> 11%
where the time goes in v18:
time: 64.4 us; the launch traced here: 64.1 us
  Pallas kernels  34.8 us (54%)
  waiting for transfers between devices  14.1 us (22%)
  starting transfers between devices  11.8 us (18%)
  local copies, waits for them, and re-layouts  2.31 us (4%)
  between operations  0.88 us (1%)
    pallas_call x1, Pallas kernels, make_modes(): pl.pallas_call(modes_kernel, in_specs=[pl.BlockSpec(memory_space=pl.ANY)]...  9.53 us
    pallas_call x1, Pallas kernels, run_ilc(): pl.pallas_call(ilc_kernel, in_specs=[vmem, vmem, pl.BlockSpec(memory_spac...  9.2 us
    pallas_call x1, Pallas kernels, analyse(): pl.pallas_call(analysis_kernel, in_specs=[pl.BlockSpec(memory_space=pl.AN...  8.94 us
    all_to_all x1, waiting for transfers between devices, body(): lax.all_to_all(partial, axes, split_axis=0, concat_axis=0, tiled=True)  8 us
    all_to_all x1, starting transfers between devices, body(): lax.all_to_all(partial, axes, split_axis=0, concat_axis=0, tiled=True)  7.3 us
    pallas_call x1, Pallas kernels, make_basis(): pl.pallas_call(functools.partial(basis_kernel, slots), grid=(rows // bloc...  7.15 us
    all_to_all x1, waiting for transfers between devices, body(): lax.all_to_all(spectra, axes, split_axis=0, concat_axis=0, tiled=True)  4.18 us
    all_to_all x1, starting transfers between devices, body(): lax.all_to_all(spectra, axes, split_axis=0, concat_axis=0, tiled=True)  2.75 us
  transfers between devices with their start and end apart: 3, of which 3 were waited for; matrix products, arithmetic and copies ran while one was open for 4% of the time, Pallas kernels for 11%

profile of v18, /device:TPU:0, one launch (start us, length us, event | category | flops | bytes accessed | tf_op | source)
XLA Modules:
  0.0 64.1 jit_solution(16915415931124635461)
XLA Ops:
  0.6 0.0 copy-start
  0.6 9.5 %shard_map.50 = bf16[32,72,128]{2,1,0:T(8,128)(2,1)} custom-call(bf16[64,9,2,512]{3,2,1,0:T(2,128)(2,1)} %alm_hbm.1, bf16[64,512,256]{2,1,0:T(8,128)(2,1)} %table_hbm.3), custom_call_target="tpu_custom_call" | custom-call | flops 301989888 | bytes 17956864 | tf_op jit(solution)/shard_map/pallas_call | solution.py:363
  10.2 7.3 %all-to-all-start = ((bf16[32,72,128]{2,1,0:T(8,128)(2,1)}), bf16[32,72,128]{2,1,0:T(8,128)(2,1)S(1)}, u32[]{:S(2)}, u32[]{:S(2)}) async-start(bf16[32,72,128]{2,1,0:T(8,128)(2,1)} %shard_map.50), calls=%async_computation | async-start | bytes 1179648 | tf_op jit(solution)/shard_map/all_to_all | solution.py:462
  17.5 0.0 copy-done
  17.5 0.1 broadcast_in_dim.11
  17.6 1.0 %convert_element_type.27.order_ref = f32[2048,1]{1,0:T(8,128)S(1)} reshape(f32[16,2,64]{2,1,0:T(2,128)S(1)} %broadcast_in_dim.13) | data formatting | bytes 16384 | tf_op jit(solution)/shard_map/convert_element_type | solution.py:473
  18.6 0.1 reshape.91
  18.7 7.2 %shard_map.51 = bf16[4,2048,512]{2,1,0:T(8,128)(2,1)} custom-call(f32[2048,1]{1,0:T(8,128)S(1)} %convert_element_type.27.order_ref), custom_call_target="tpu_custom_call" | custom-call | flops 33554432 | bytes 8388608 | tf_op jit(solution)/shard_map/pallas_call | solution.py:74
  25.9 8.0 %all-to-all-done = bf16[32,72,128]{2,1,0:T(8,128)(2,1)S(1)} async-done(((bf16[32,72,128]{2,1,0:T(8,128)(2,1)}), bf16[32,72,128]{2,1,0:T(8,128)(2,1)S(1)}, u32[]{:S(2)}, u32[]{:S(2)}) %all-to-all-start) | async-done | bytes 589856 | tf_op jit(solution)/shard_map/all_to_all | solution.py:462
  33.9 9.2 %shard_map.52 = (f32[32,8,128]{2,1,0:T(8,128)S(1)}, bf16[16,2,8,128]{3,2,1,0:T(8,128)(2,1)}) custom-call(bf16[16,2,72,128]{3,2,1,0:T(8,128)(2,1)S(1)} %bitcast.10, f32[1,2048]{1,0:T(1,128)S(1)} %fusion.3.odd_ref, bf16[16,512,512]{2,1,0:T(8,128)(2,1)} %bitcast.13), custom_call_target="tpu_custom_call" | custom-call | flops 1342177280 | bytes 8388608 | tf_op jit(solution)/shard_map/pallas_call | solution.py:272
  43.1 1.7 %collective-permute-start = (f32[32,8,128]{2,1,0:T(8,128)S(1)}, f32[32,8,128]{2,1,0:T(8,128)S(1)}, u32[]{:S(2)}, u32[]{:S(2)}) collective-permute-start(f32[32,8,128]{2,1,0:T(8,128)S(1)} %get-tuple-element.7), channel_id=1, source_target_pairs={{0,1},{1,0},{2,3},{3,2},{4,5},{5,4},{6,7},{7,6},{8,9},{9,8},{10,11... | collective-permute-start | bytes 393224 | tf_op jit(solution)/shard_map/ppermute | solution.py:433
  44.8 2.8 %all-to-all-start.1 = ((bf16[32,8,128]{2,1,0:T(8,128)(2,1)}), bf16[32,8,128]{2,1,0:T(8,128)(2,1)S(1)}, u32[]{:S(2)}, u32[]{:S(2)}) async-start(bf16[32,8,128]{2,1,0:T(8,128)(2,1)} %bitcast.2), calls=%async_computation.1 | async-start | bytes 131072 | tf_op jit(solution)/shard_map/all_to_all | solution.py:482
  47.6 1.9 %collective-permute-done = f32[32,8,128]{2,1,0:T(8,128)S(1)} collective-permute-done((f32[32,8,128]{2,1,0:T(8,128)S(1)}, f32[32,8,128]{2,1,0:T(8,128)S(1)}, u32[]{:S(2)}, u32[]{:S(2)}) %collective-permute-start) | collective-permute-done | bytes 131104 | tf_op jit(solution)/shard_map/ppermute | solution.py:433
  49.5 0.1 fusion.2
  49.6 0.1 fusion
  49.7 0.2 copy.6
  49.9 0.9 %reshape.94 = f32[16,2048]{1,0:T(8,128)} reshape(f32[2,8,64,32]{3,2,1,0:T(8,128)S(1)} %copy.6) | data formatting | bytes 262144 | tf_op jit(solution)/shard_map/reshape | solution.py:486
  50.8 4.2 %all-to-all-done.1 = bf16[32,8,128]{2,1,0:T(8,128)(2,1)S(1)} async-done(((bf16[32,8,128]{2,1,0:T(8,128)(2,1)}), bf16[32,8,128]{2,1,0:T(8,128)(2,1)S(1)}, u32[]{:S(2)}, u32[]{:S(2)}) %all-to-all-start.1) | async-done | bytes 65568 | tf_op jit(solution)/shard_map/all_to_all | solution.py:482
  55.0 8.9 %shard_map.53 = f32[64,2,512]{2,1,0:T(2,128)} custom-call(bf16[64,512,256]{2,1,0:T(8,128)(2,1)} %table_hbm.3, bf16[256,128]{1,0:T(8,128)(2,1)S(1)} %bitcast.11), custom_call_target="tpu_custom_call" | custom-call | flops 268435456 | bytes 16777216 | tf_op jit(solution)/shard_map/pallas_call | solution.py:410
  (4 shorter events, 0.1 us)
Async XLA Ops:
  0.6 16.9 %copy-start = (s32[1024]{0:T(1024)S(1)}, s32[1024]{0:T(1024)}, u32[]{:S(2)}) copy-start(s32[1024]{0:T(1024)} %param.5) | copy-start | bytes 12292
  10.2 23.7 %all-to-all-start = ((bf16[32,72,128]{2,1,0:T(8,128)(2,1)}), bf16[32,72,128]{2,1,0:T(8,128)(2,1)S(1)}, u32[]{:S(2)}, u32[]{:S(2)}) async-start(bf16[32,72,128]{2,1,0:T(8,128)(2,1)} %shard_map.50), calls=%async_computation | async-start | bytes 1179648 | tf_op jit(solution)/shard_map/all_to_all | solution.py:462
  43.1 6.4 %collective-permute-start = (f32[32,8,128]{2,1,0:T(8,128)S(1)}, f32[32,8,128]{2,1,0:T(8,128)S(1)}, u32[]{:S(2)}, u32[]{:S(2)}) collective-permute-start(f32[32,8,128]{2,1,0:T(8,128)S(1)} %get-tuple-element.7), channel_id=1, source_target_pairs={{0,1},{1,0},{2,3},{3,2},{4,5},{5,4},{6,7},{7,6},{8,9},{9,8},{10,11... | collective-permute-start | bytes 393224 | tf_op jit(solution)/shard_map/ppermute | solution.py:433
  44.8 10.2 %all-to-all-start.1 = ((bf16[32,8,128]{2,1,0:T(8,128)(2,1)}), bf16[32,8,128]{2,1,0:T(8,128)(2,1)S(1)}, u32[]{:S(2)}, u32[]{:S(2)}) async-start(bf16[32,8,128]{2,1,0:T(8,128)(2,1)} %bitcast.2), calls=%async_computation.1 | async-start | bytes 131072 | tf_op jit(solution)/shard_map/all_to_all | solution.py:482

commit v19 on v18

--- a/solution.py
+++ b/solution.py
@@ -23,7 +23,7 @@
 PAIRS = [(a_at, b_at) for a_at in range(REST) for b_at in range(a_at, REST)] + [(a_at, REST) for a_at in range(REST)]
 SUMS = len(PAIRS) + 1
 VMEM_LIMIT = 48 * 1024 * 1024
-IN_FLIGHT = 2
+IN_FLIGHT = 6
 HALVES = 1
 CHUNK = 8
 
@@ -295,7 +295,7 @@
     )(modes, odd, basis)
 
 
-def modes_kernel(alm_hbm, table_hbm, out_hbm, alm_ref, table_ref, held_ref, out_ref, alm_sem, sems, out_sems):
+def modes_kernel(alm_hbm, table_hbm, out_hbm, alm_ref, table_ref, held_ref, turned_ref, out_ref, alm_sem, sems, out_sems):
     parts = sems.shape[0]
     total_slots, degrees, total = table_ref.shape
     each, slots = total_slots // parts, 4
@@ -338,15 +338,15 @@
     one = one.astype(jnp.float32).astype(jnp.bfloat16)
     width = 2 * total_slots
     together = C if width % LANES == 0 else 1
-    turned = []
     for chan in range(0, C, together):
         rows = jnp.concatenate([rows_of(chan + at) for at in range(together)], axis=0)
-        both = lax.dot_general(one, rows, (((1,), (1,)), ((), ())), preferred_element_type=jnp.float32)
-        turned += [both[:, at * width : (at + 1) * width] for at in range(together)]
+        turned = lax.dot_general(one, rows, (((1,), (1,)), ((), ())), preferred_element_type=jnp.float32)
+        for at in range(together):
+            turned_ref[chan + at] = turned[:, at * width : (at + 1) * width]
     each = targets // out_sems.shape[0]
     for target in range(targets):
         span = slice(target * cycles, (target + 1) * cycles)
-        block = jnp.concatenate([turned[chan][span] for chan in range(C)], axis=0)
+        block = jnp.concatenate([turned_ref[chan, span, :] for chan in range(C)], axis=0)
         out_ref[target] = block.astype(jnp.bfloat16)
         if (target + 1) % each == 0:
             part_copy(out_ref, out_hbm, out_sems, target // each).start()
@@ -369,6 +369,7 @@
             pltpu.VMEM(alm.shape, jnp.bfloat16),
             pltpu.VMEM(legendre.shape, jnp.bfloat16),
             pltpu.VMEM((total // LANES, slot_count * height, LANES), jnp.float32),
+            pltpu.VMEM((C, total, width), jnp.float32),
             pltpu.VMEM(out.shape, out.dtype),
             pltpu.SemaphoreType.DMA,
             pltpu.SemaphoreType.DMA((parts,)),

time: 64.4 us -> 62.8 us (0.975)
  Pallas kernels: 34.8 us -> 33.2 us
    pallas_call x1, Pallas kernels: 8.94 us -> 7.7 us  [analyse(): pl.pallas_call(analysis_kernel, in_specs=[pl.BlockSpec(memory_space=pl.AN...]
where the time goes in v19:
time: 62.8 us; the launch traced here: 62.5 us
  Pallas kernels  33.2 us (53%)
  waiting for transfers between devices  14.1 us (22%)
  starting transfers between devices  11.8 us (19%)
  local copies, waits for them, and re-layouts  2.31 us (4%)
  between operations  0.88 us (1%)
    pallas_call x1, Pallas kernels, make_modes(): pl.pallas_call(modes_kernel, in_specs=[pl.BlockSpec(memory_space=pl.ANY)]...  9.59 us
    pallas_call x1, Pallas kernels, run_ilc(): pl.pallas_call(ilc_kernel, in_specs=[vmem, vmem, pl.BlockSpec(memory_spac...  8.81 us
    all_to_all x1, waiting for transfers between devices, body(): lax.all_to_all(partial, axes, split_axis=0, concat_axis=0, tiled=True)  8 us
    pallas_call x1, Pallas kernels, analyse(): pl.pallas_call(analysis_kernel, in_specs=[pl.BlockSpec(memory_space=pl.AN...  7.7 us
    all_to_all x1, starting transfers between devices, body(): lax.all_to_all(partial, axes, split_axis=0, concat_axis=0, tiled=True)  7.3 us
    pallas_call x1, Pallas kernels, make_basis(): pl.pallas_call(functools.partial(basis_kernel, slots), grid=(rows // bloc...  7.15 us
    all_to_all x1, waiting for transfers between devices, body(): lax.all_to_all(spectra, axes, split_axis=0, concat_axis=0, tiled=True)  4.18 us
    all_to_all x1, starting transfers between devices, body(): lax.all_to_all(spectra, axes, split_axis=0, concat_axis=0, tiled=True)  2.75 us
  transfers between devices with their start and end apart: 3, of which 3 were waited for; matrix products, arithmetic and copies ran while one was open for 4% of the time, Pallas kernels for 11%

profile of v19, /device:TPU:0, one launch (start us, length us, event | category | flops | bytes accessed | tf_op | source)
XLA Modules:
  0.0 62.5 jit_solution(10363688089236110969)
XLA Ops:
  0.6 0.0 copy-start
  0.6 9.6 %shard_map.50 = bf16[32,72,128]{2,1,0:T(8,128)(2,1)} custom-call(bf16[64,9,2,512]{3,2,1,0:T(2,128)(2,1)} %alm_hbm.1, bf16[64,512,256]{2,1,0:T(8,128)(2,1)} %table_hbm.3), custom_call_target="tpu_custom_call" | custom-call | flops 301989888 | bytes 17956864 | tf_op jit(solution)/shard_map/pallas_call | solution.py:363
  10.2 7.3 %all-to-all-start = ((bf16[32,72,128]{2,1,0:T(8,128)(2,1)}), bf16[32,72,128]{2,1,0:T(8,128)(2,1)S(1)}, u32[]{:S(2)}, u32[]{:S(2)}) async-start(bf16[32,72,128]{2,1,0:T(8,128)(2,1)} %shard_map.50), calls=%async_computation | async-start | bytes 1179648 | tf_op jit(solution)/shard_map/all_to_all | solution.py:463
  17.5 0.0 copy-done
  17.6 0.1 broadcast_in_dim.11
  17.6 1.0 %convert_element_type.27.order_ref = f32[2048,1]{1,0:T(8,128)S(1)} reshape(f32[16,2,64]{2,1,0:T(2,128)S(1)} %broadcast_in_dim.13) | data formatting | bytes 16384 | tf_op jit(solution)/shard_map/convert_element_type | solution.py:474
  18.7 0.1 reshape.91
  18.8 7.2 %shard_map.51 = bf16[4,2048,512]{2,1,0:T(8,128)(2,1)} custom-call(f32[2048,1]{1,0:T(8,128)S(1)} %convert_element_type.27.order_ref), custom_call_target="tpu_custom_call" | custom-call | flops 33554432 | bytes 8388608 | tf_op jit(solution)/shard_map/pallas_call | solution.py:74
  26.0 8.0 %all-to-all-done = bf16[32,72,128]{2,1,0:T(8,128)(2,1)S(1)} async-done(((bf16[32,72,128]{2,1,0:T(8,128)(2,1)}), bf16[32,72,128]{2,1,0:T(8,128)(2,1)S(1)}, u32[]{:S(2)}, u32[]{:S(2)}) %all-to-all-start) | async-done | bytes 589856 | tf_op jit(solution)/shard_map/all_to_all | solution.py:463
  34.0 8.8 %shard_map.52 = (f32[32,8,128]{2,1,0:T(8,128)S(1)}, bf16[16,2,8,128]{3,2,1,0:T(8,128)(2,1)}) custom-call(bf16[16,2,72,128]{3,2,1,0:T(8,128)(2,1)S(1)} %bitcast.10, f32[1,2048]{1,0:T(1,128)S(1)} %fusion.3.odd_ref, bf16[16,512,512]{2,1,0:T(8,128)(2,1)} %bitcast.13), custom_call_target="tpu_custom_call" | custom-call | flops 1342177280 | bytes 8388608 | tf_op jit(solution)/shard_map/pallas_call | solution.py:272
  42.8 1.7 %collective-permute-start = (f32[32,8,128]{2,1,0:T(8,128)S(1)}, f32[32,8,128]{2,1,0:T(8,128)S(1)}, u32[]{:S(2)}, u32[]{:S(2)}) collective-permute-start(f32[32,8,128]{2,1,0:T(8,128)S(1)} %get-tuple-element.7), channel_id=1, source_target_pairs={{0,1},{1,0},{2,3},{3,2},{4,5},{5,4},{6,7},{7,6},{8,9},{9,8},{10,11... | collective-permute-start | bytes 393224 | tf_op jit(solution)/shard_map/ppermute | solution.py:434
  44.5 2.8 %all-to-all-start.1 = ((bf16[32,8,128]{2,1,0:T(8,128)(2,1)}), bf16[32,8,128]{2,1,0:T(8,128)(2,1)S(1)}, u32[]{:S(2)}, u32[]{:S(2)}) async-start(bf16[32,8,128]{2,1,0:T(8,128)(2,1)} %bitcast.2), calls=%async_computation.1 | async-start | bytes 131072 | tf_op jit(solution)/shard_map/all_to_all | solution.py:483
  47.2 1.9 %collective-permute-done = f32[32,8,128]{2,1,0:T(8,128)S(1)} collective-permute-done((f32[32,8,128]{2,1,0:T(8,128)S(1)}, f32[32,8,128]{2,1,0:T(8,128)S(1)}, u32[]{:S(2)}, u32[]{:S(2)}) %collective-permute-start) | collective-permute-done | bytes 131104 | tf_op jit(solution)/shard_map/ppermute | solution.py:434
  49.2 0.1 fusion.2
  49.2 0.1 fusion
  49.4 0.2 copy.6
  49.6 0.9 %reshape.94 = f32[16,2048]{1,0:T(8,128)} reshape(f32[2,8,64,32]{3,2,1,0:T(8,128)S(1)} %copy.6) | data formatting | bytes 262144 | tf_op jit(solution)/shard_map/reshape | solution.py:487
  50.5 4.2 %all-to-all-done.1 = bf16[32,8,128]{2,1,0:T(8,128)(2,1)S(1)} async-done(((bf16[32,8,128]{2,1,0:T(8,128)(2,1)}), bf16[32,8,128]{2,1,0:T(8,128)(2,1)S(1)}, u32[]{:S(2)}, u32[]{:S(2)}) %all-to-all-start.1) | async-done | bytes 65568 | tf_op jit(solution)/shard_map/all_to_all | solution.py:483
  54.7 7.7 %shard_map.53 = f32[64,2,512]{2,1,0:T(2,128)} custom-call(bf16[64,512,256]{2,1,0:T(8,128)(2,1)} %table_hbm.3, bf16[256,128]{1,0:T(8,128)(2,1)S(1)} %bitcast.11), custom_call_target="tpu_custom_call" | custom-call | flops 268435456 | bytes 16777216 | tf_op jit(solution)/shard_map/pallas_call | solution.py:411
  (4 shorter events, 0.1 us)
Async XLA Ops:
  0.6 16.9 %copy-start = (s32[1024]{0:T(1024)S(1)}, s32[1024]{0:T(1024)}, u32[]{:S(2)}) copy-start(s32[1024]{0:T(1024)} %param.5) | copy-start | bytes 12292
  10.2 23.7 %all-to-all-start = ((bf16[32,72,128]{2,1,0:T(8,128)(2,1)}), bf16[32,72,128]{2,1,0:T(8,128)(2,1)S(1)}, u32[]{:S(2)}, u32[]{:S(2)}) async-start(bf16[32,72,128]{2,1,0:T(8,128)(2,1)} %shard_map.50), calls=%async_computation | async-start | bytes 1179648 | tf_op jit(solution)/shard_map/all_to_all | solution.py:463
  42.8 6.4 %collective-permute-start = (f32[32,8,128]{2,1,0:T(8,128)S(1)}, f32[32,8,128]{2,1,0:T(8,128)S(1)}, u32[]{:S(2)}, u32[]{:S(2)}) collective-permute-start(f32[32,8,128]{2,1,0:T(8,128)S(1)} %get-tuple-element.7), channel_id=1, source_target_pairs={{0,1},{1,0},{2,3},{3,2},{4,5},{5,4},{6,7},{7,6},{8,9},{9,8},{10,11... | collective-permute-start | bytes 393224 | tf_op jit(solution)/shard_map/ppermute | solution.py:434
  44.5 10.2 %all-to-all-start.1 = ((bf16[32,8,128]{2,1,0:T(8,128)(2,1)}), bf16[32,8,128]{2,1,0:T(8,128)(2,1)S(1)}, u32[]{:S(2)}, u32[]{:S(2)}) async-start(bf16[32,8,128]{2,1,0:T(8,128)(2,1)} %bitcast.2), calls=%async_computation.1 | async-start | bytes 131072 | tf_op jit(solution)/shard_map/all_to_all | solution.py:483

commit v20 on v18

--- a/solution.py
+++ b/solution.py
@@ -23,7 +23,7 @@
 PAIRS = [(a_at, b_at) for a_at in range(REST) for b_at in range(a_at, REST)] + [(a_at, REST) for a_at in range(REST)]
 SUMS = len(PAIRS) + 1
 VMEM_LIMIT = 48 * 1024 * 1024
-IN_FLIGHT = 2
+IN_FLIGHT = 4
 HALVES = 1
 CHUNK = 8
 
@@ -157,7 +157,7 @@
     chunks = basis_ref.shape[0] // pieces
     cycles = rows // C
     second = round_up(rows, 16)
-    start_parts(basis_hbm, basis_ref, sems, IN_FLIGHT)
+    start_parts(basis_hbm, basis_ref, sems, IN_FLIGHT - 1)
     for group in range(groups):
         span = slice(group * width, (group + 1) * width)
         odd = odd_ref[:, span]
@@ -178,7 +178,7 @@
         maps_ref[at, C] = squares
 
     def maps_of_chunk(chunk):
-        next_part(basis_hbm, basis_ref, sems, chunk, IN_FLIGHT)
+        next_part(basis_hbm, basis_ref, sems, chunk, IN_FLIGHT - 1)
         basis = basis_ref[chunk * pieces : (chunk + 1) * pieces].reshape(depth, columns)
         result = jnp.dot(lhs_ref[...], basis, preferred_element_type=jnp.float32)
         for part in range(CHUNK // 2):

time: 64.4 us -> 61.8 us (0.960)
  Pallas kernels: 34.8 us -> 32.3 us
    pallas_call x1, Pallas kernels: 8.94 us -> 7.73 us  [analyse(): pl.pallas_call(analysis_kernel, in_specs=[pl.BlockSpec(memory_space=pl.AN...]
    pallas_call x1, Pallas kernels: 9.53 us -> 8.59 us  [make_modes(): pl.pallas_call(modes_kernel, in_specs=[pl.BlockSpec(memory_space=pl.ANY)]...]
  transfers between devices with their start and end apart: 3 -> 3, of which waited for: 3 -> 3; matrix products, arithmetic and copies ran while one was open for 4% -> 4% of each run, Pallas kernels for 11% -> 12%
where the time goes in v20:
time: 61.8 us; the launch traced here: 61.6 us
  Pallas kernels  32.3 us (52%)
  waiting for transfers between devices  14.1 us (23%)
  starting transfers between devices  11.8 us (19%)
  local copies, waits for them, and re-layouts  2.31 us (4%)
  between operations  0.88 us (1%)
    pallas_call x1, Pallas kernels, run_ilc(): pl.pallas_call(ilc_kernel, in_specs=[vmem, vmem, pl.BlockSpec(memory_spac...  8.83 us
    pallas_call x1, Pallas kernels, make_modes(): pl.pallas_call(modes_kernel, in_specs=[pl.BlockSpec(memory_space=pl.ANY)]...  8.59 us
    all_to_all x1, waiting for transfers between devices, body(): lax.all_to_all(partial, axes, split_axis=0, concat_axis=0, tiled=True)  8 us
    pallas_call x1, Pallas kernels, analyse(): pl.pallas_call(analysis_kernel, in_specs=[pl.BlockSpec(memory_space=pl.AN...  7.73 us
    all_to_all x1, starting transfers between devices, body(): lax.all_to_all(partial, axes, split_axis=0, concat_axis=0, tiled=True)  7.3 us
    pallas_call x1, Pallas kernels, make_basis(): pl.pallas_call(functools.partial(basis_kernel, slots), grid=(rows // bloc...  7.15 us
    all_to_all x1, waiting for transfers between devices, body(): lax.all_to_all(spectra, axes, split_axis=0, concat_axis=0, tiled=True)  4.18 us
    all_to_all x1, starting transfers between devices, body(): lax.all_to_all(spectra, axes, split_axis=0, concat_axis=0, tiled=True)  2.75 us
  transfers between devices with their start and end apart: 3, of which 3 were waited for; matrix products, arithmetic and copies ran while one was open for 4% of the time, Pallas kernels for 12%

profile of v20, /device:TPU:0, one launch (start us, length us, event | category | flops | bytes accessed | tf_op | source)
XLA Modules:
  0.0 61.6 jit_solution(6354213536790217510)
XLA Ops:
  0.6 0.0 copy-start
  0.6 8.6 %shard_map.50 = bf16[32,72,128]{2,1,0:T(8,128)(2,1)} custom-call(bf16[64,9,2,512]{3,2,1,0:T(2,128)(2,1)} %alm_hbm.1, bf16[64,512,256]{2,1,0:T(8,128)(2,1)} %table_hbm.3), custom_call_target="tpu_custom_call" | custom-call | flops 301989888 | bytes 17956864 | tf_op jit(solution)/shard_map/pallas_call | solution.py:363
  9.2 7.3 %all-to-all-start = ((bf16[32,72,128]{2,1,0:T(8,128)(2,1)}), bf16[32,72,128]{2,1,0:T(8,128)(2,1)S(1)}, u32[]{:S(2)}, u32[]{:S(2)}) async-start(bf16[32,72,128]{2,1,0:T(8,128)(2,1)} %shard_map.50), calls=%async_computation | async-start | bytes 1179648 | tf_op jit(solution)/shard_map/all_to_all | solution.py:462
  16.6 0.0 copy-done
  16.6 0.1 broadcast_in_dim.11
  16.6 1.0 %convert_element_type.27.order_ref = f32[2048,1]{1,0:T(8,128)S(1)} reshape(f32[16,2,64]{2,1,0:T(2,128)S(1)} %broadcast_in_dim.13) | data formatting | bytes 16384 | tf_op jit(solution)/shard_map/convert_element_type | solution.py:473
  17.7 0.1 reshape.91
  17.8 7.2 %shard_map.51 = bf16[4,2048,512]{2,1,0:T(8,128)(2,1)} custom-call(f32[2048,1]{1,0:T(8,128)S(1)} %convert_element_type.27.order_ref), custom_call_target="tpu_custom_call" | custom-call | flops 33554432 | bytes 8388608 | tf_op jit(solution)/shard_map/pallas_call | solution.py:74
  25.0 8.0 %all-to-all-done = bf16[32,72,128]{2,1,0:T(8,128)(2,1)S(1)} async-done(((bf16[32,72,128]{2,1,0:T(8,128)(2,1)}), bf16[32,72,128]{2,1,0:T(8,128)(2,1)S(1)}, u32[]{:S(2)}, u32[]{:S(2)}) %all-to-all-start) | async-done | bytes 589856 | tf_op jit(solution)/shard_map/all_to_all | solution.py:462
  33.0 8.8 %shard_map.52 = (f32[32,8,128]{2,1,0:T(8,128)S(1)}, bf16[16,2,8,128]{3,2,1,0:T(8,128)(2,1)}) custom-call(bf16[16,2,72,128]{3,2,1,0:T(8,128)(2,1)S(1)} %bitcast.10, f32[1,2048]{1,0:T(1,128)S(1)} %fusion.3.odd_ref, bf16[16,512,512]{2,1,0:T(8,128)(2,1)} %bitcast.13), custom_call_target="tpu_custom_call" | custom-call | flops 1342177280 | bytes 8388608 | tf_op jit(solution)/shard_map/pallas_call | solution.py:272
  41.8 1.7 %collective-permute-start = (f32[32,8,128]{2,1,0:T(8,128)S(1)}, f32[32,8,128]{2,1,0:T(8,128)S(1)}, u32[]{:S(2)}, u32[]{:S(2)}) collective-permute-start(f32[32,8,128]{2,1,0:T(8,128)S(1)} %get-tuple-element.7), channel_id=1, source_target_pairs={{0,1},{1,0},{2,3},{3,2},{4,5},{5,4},{6,7},{7,6},{8,9},{9,8},{10,11... | collective-permute-start | bytes 393224 | tf_op jit(solution)/shard_map/ppermute | solution.py:433
  43.5 2.8 %all-to-all-start.1 = ((bf16[32,8,128]{2,1,0:T(8,128)(2,1)}), bf16[32,8,128]{2,1,0:T(8,128)(2,1)S(1)}, u32[]{:S(2)}, u32[]{:S(2)}) async-start(bf16[32,8,128]{2,1,0:T(8,128)(2,1)} %bitcast.2), calls=%async_computation.1 | async-start | bytes 131072 | tf_op jit(solution)/shard_map/all_to_all | solution.py:482
  46.3 1.9 %collective-permute-done = f32[32,8,128]{2,1,0:T(8,128)S(1)} collective-permute-done((f32[32,8,128]{2,1,0:T(8,128)S(1)}, f32[32,8,128]{2,1,0:T(8,128)S(1)}, u32[]{:S(2)}, u32[]{:S(2)}) %collective-permute-start) | collective-permute-done | bytes 131104 | tf_op jit(solution)/shard_map/ppermute | solution.py:433
  48.2 0.1 fusion.2
  48.3 0.1 fusion
  48.4 0.2 copy.6
  48.6 0.9 %reshape.94 = f32[16,2048]{1,0:T(8,128)} reshape(f32[2,8,64,32]{3,2,1,0:T(8,128)S(1)} %copy.6) | data formatting | bytes 262144 | tf_op jit(solution)/shard_map/reshape | solution.py:486
  49.5 4.2 %all-to-all-done.1 = bf16[32,8,128]{2,1,0:T(8,128)(2,1)S(1)} async-done(((bf16[32,8,128]{2,1,0:T(8,128)(2,1)}), bf16[32,8,128]{2,1,0:T(8,128)(2,1)S(1)}, u32[]{:S(2)}, u32[]{:S(2)}) %all-to-all-start.1) | async-done | bytes 65568 | tf_op jit(solution)/shard_map/all_to_all | solution.py:482
  53.7 7.7 %shard_map.53 = f32[64,2,512]{2,1,0:T(2,128)} custom-call(bf16[64,512,256]{2,1,0:T(8,128)(2,1)} %table_hbm.3, bf16[256,128]{1,0:T(8,128)(2,1)S(1)} %bitcast.11), custom_call_target="tpu_custom_call" | custom-call | flops 268435456 | bytes 16777216 | tf_op jit(solution)/shard_map/pallas_call | solution.py:410
  (4 shorter events, 0.1 us)
Async XLA Ops:
  0.6 15.9 %copy-start = (s32[1024]{0:T(1024)S(1)}, s32[1024]{0:T(1024)}, u32[]{:S(2)}) copy-start(s32[1024]{0:T(1024)} %param.5) | copy-start | bytes 12292
  9.2 23.7 %all-to-all-start = ((bf16[32,72,128]{2,1,0:T(8,128)(2,1)}), bf16[32,72,128]{2,1,0:T(8,128)(2,1)S(1)}, u32[]{:S(2)}, u32[]{:S(2)}) async-start(bf16[32,72,128]{2,1,0:T(8,128)(2,1)} %shard_map.50), calls=%async_computation | async-start | bytes 1179648 | tf_op jit(solution)/shard_map/all_to_all | solution.py:462
  41.8 6.4 %collective-permute-start = (f32[32,8,128]{2,1,0:T(8,128)S(1)}, f32[32,8,128]{2,1,0:T(8,128)S(1)}, u32[]{:S(2)}, u32[]{:S(2)}) collective-permute-start(f32[32,8,128]{2,1,0:T(8,128)S(1)} %get-tuple-element.7), channel_id=1, source_target_pairs={{0,1},{1,0},{2,3},{3,2},{4,5},{5,4},{6,7},{7,6},{8,9},{9,8},{10,11... | collective-permute-start | bytes 393224 | tf_op jit(solution)/shard_map/ppermute | solution.py:433
  43.5 10.2 %all-to-all-start.1 = ((bf16[32,8,128]{2,1,0:T(8,128)(2,1)}), bf16[32,8,128]{2,1,0:T(8,128)(2,1)S(1)}, u32[]{:S(2)}, u32[]{:S(2)}) async-start(bf16[32,8,128]{2,1,0:T(8,128)(2,1)} %bitcast.2), calls=%async_computation.1 | async-start | bytes 131072 | tf_op jit(solution)/shard_map/all_to_all | solution.py:482
